TPU v7x, 32 devices: a whole 2x2x4 slice. The times are simulated.
32 devices in a mesh: dp: 16 (over z, y, x), tensor: 2 (over core).
Axes of the slice: x: 2, y: 2, z: 4, core: 2. Of those that a mesh axis runs over, the one named last changes fastest.
Arguments:
- tokens: bfloat16 [16384, 1024], P(('dp', 'tensor')), may hold values from -6 to 6
- cont_prompt: int32 [16], replicated, may hold values from 0 to 1
- routes: int32 [16384, 1], P(('dp', 'tensor')), may hold values from 0 to 15, as said below
- norm1_gain: bfloat16 [1024], P('dp'), may hold values from 0.5 to 1.5
- w_query: bfloat16 [1024, 1024], P('dp', 'tensor'), may hold values from -0.1875 to 0.1875
- w_key: bfloat16 [1024, 1024], P('dp', 'tensor'), may hold values from -0.1875 to 0.1875
- w_value: bfloat16 [1024, 1024], P('dp', 'tensor'), may hold values from -0.1875 to 0.1875
- w_attn_out: bfloat16 [1024, 1024], P('tensor', 'dp'), may hold values from -3 to 3
- norm2_gain: bfloat16 [1024], P('dp'), may hold values from 0.5 to 1.5
- w_ffn_in: bfloat16 [1024, 4096], P('dp', 'tensor'), may hold values from -0.1875 to 0.1875
- w_ffn_out: bfloat16 [4096, 1024], P('tensor', 'dp'), may hold values from -0.09375 to 0.09375
- centroids: bfloat16 [16, 1024], P('dp'), may hold values from -0.09375 to 0.09375
- expert_in_a: bfloat16 [16, 1024, 4096], P('dp', None, 'tensor'), may hold values from -0.1875 to 0.1875
- expert_out_a: bfloat16 [16, 4096, 1024], P('dp', 'tensor'), may hold values from -0.09375 to 0.09375
- expert_in_b: bfloat16 [16, 1024, 4096], P('dp', None, 'tensor'), may hold values from -0.1875 to 0.1875
- expert_out_b: bfloat16 [16, 4096, 1024], P('dp', 'tensor'), may hold values from -0.09375 to 0.09375
- grad_out: bfloat16 [16384, 1024], P(('dp', 'tensor')), may hold values from -6 to 6
Outputs:
- out: bfloat16 [16384, 1024], P(('dp', 'tensor'))
- grad_tokens: bfloat16 [16384, 1024], P(('dp', 'tensor'))
- grad_norm1_gain: float32 [1024], P('dp')
- grad_w_query: float32 [1024, 1024], P('dp', 'tensor')
- grad_w_key: float32 [1024, 1024], P('dp', 'tensor')
- grad_w_value: float32 [1024, 1024], P('dp', 'tensor')
- grad_w_attn_out: float32 [1024, 1024], P('tensor', 'dp')
- grad_norm2_gain: float32 [1024], P('dp')
- grad_w_ffn_in: float32 [1024, 4096], P('dp', 'tensor')
- grad_w_ffn_out: float32 [4096, 1024], P('tensor', 'dp')
- grad_centroids: float32 [16, 1024], P('dp')
- grad_expert_in_a: float32 [16, 1024, 4096], P('dp', None, 'tensor')
- grad_expert_out_a: float32 [16, 4096, 1024], P('dp', 'tensor')
- grad_expert_in_b: float32 [16, 1024, 4096], P('dp', None, 'tensor')
- grad_expert_out_b: float32 [16, 4096, 1024], P('dp', 'tensor')
Inputs may be any that keep to these rules, and one draw needn't show every extreme that they name: Continuation j follows prompt cont_prompt[j]. `routes`: each row names one expert; among the 512 rows of one device at most 48 name the same expert, and in every draw some device has exactly 48 rows naming one expert.
All inputs are finite; a program needn't handle non-finite values.
Results may differ from a plain program's by a relative error of at most 0.03.
Values may be sent and summed in bfloat16 or wider, within the bound.
No kernel may reach another device: no remote copies, remote signals or barrier semaphores. Data moves between devices by JAX's collectives and lax.ppermute only.
A program may use at most 384 MiB of HBM per device.

v0:
```python
import jax
import jax.numpy as jnp
from jax import lax
from jax.sharding import PartitionSpec as P

HEAD = 64
PLEN = 4096
CONT = 512


def shortened(value):

    def short(part):
        return part.astype(jnp.bfloat16) if part.dtype == jnp.float32 else part

    return jax.tree.map(short, value)


def carried_in(value, axis, combine, identity):
    peers, place = (lax.axis_size(axis), lax.axis_index(axis))
    everything = lax.all_gather(value, axis)
    start = jnp.broadcast_to(jnp.asarray(identity, value.dtype), value.shape)

    def turn(k, before):
        reached = k < place
        new = combine(before, everything[k])
        return jnp.where(reached, new, before)

    return lax.fori_loop(0, peers, turn, start)


def rows_gather(value):
    return lax.all_gather(value, "tensor", axis=0, tiled=True)


def rows_scatter(value):
    return lax.psum_scatter(
        value.astype(jnp.bfloat16), "tensor", scatter_dimension=0, tiled=True
    ).astype(jnp.float32)


def pair_total(value):
    return jax.tree.map(lambda part: part.astype(jnp.float32), lax.psum(shortened(value), "tensor"))


def to_experts(value):
    return lax.all_to_all(value, "dp", split_axis=0, concat_axis=0, tiled=True)


def matmul(left, right):
    return jnp.dot(left, right, preferred_element_type=jnp.float32)


def matmul_tn(left, right):
    return lax.dot_general(
        left, right, (((0,), (0,)), ((), ())), preferred_element_type=jnp.float32
    )


def matmul_nt(left, right):
    return lax.dot_general(
        left, right, (((1,), (1,)), ((), ())), preferred_element_type=jnp.float32
    )


def norm_forward(hidden, gain):
    mean_row = jnp.mean(hidden, -1, keepdims=True)
    centred = hidden - mean_row
    scale_inv = lax.rsqrt(jnp.mean(centred * centred, -1, keepdims=True) + 1e-05)
    normed = centred * scale_inv
    return (normed * gain, normed, scale_inv)


def norm_backward(grad_m, normed, scale_inv, gain):
    grad_hat = grad_m * gain
    inner = (
        grad_hat
        - jnp.mean(grad_hat, -1, keepdims=True)
        - normed * jnp.mean(grad_hat * normed, -1, keepdims=True)
    )
    return (inner * scale_inv, jnp.sum(grad_m * normed, 0))


def gelu_grad(preact, grad):
    unused, pull = jax.vjp(jax.nn.gelu, preact)
    return pull(grad)[0]


def add_counts(first, second):
    return first + second


def attend(queries, keys, values, allowed, heads):
    scale = HEAD ** (-0.5)

    def head_step(head, carry):
        outputs, log_sums = carry
        query_h = lax.dynamic_slice_in_dim(queries, head * HEAD, HEAD, 1)
        key_h = lax.dynamic_slice_in_dim(keys, head * HEAD, HEAD, 1)
        value_h = lax.dynamic_slice_in_dim(values, head * HEAD, HEAD, 1)
        scores = jnp.where(allowed, matmul_nt(query_h, key_h) * scale, -1e30)
        top_score = jnp.max(scores, 1, keepdims=True)
        expo = jnp.exp(scores - top_score)
        total = jnp.sum(expo, 1, keepdims=True)
        probs = (expo / total).astype(jnp.bfloat16)
        outputs = lax.dynamic_update_slice_in_dim(outputs, matmul(probs, value_h), head * HEAD, 1)
        log_sums = lax.dynamic_update_index_in_dim(
            log_sums, top_score[:, 0] + jnp.log(total[:, 0]), head, 0
        )
        return (outputs, log_sums)

    start_state = (
        jnp.zeros((queries.shape[0], heads * HEAD), jnp.float32),
        jnp.zeros((heads, queries.shape[0]), jnp.float32),
    )
    return lax.fori_loop(0, heads, head_step, start_state)


def attend_back(queries, keys, values, allowed, log_sums, grad_attended, heads):
    scale = HEAD ** (-0.5)

    def head_step(head, carry):
        grad_q, grad_k, grad_v = carry
        query_h = lax.dynamic_slice_in_dim(queries, head * HEAD, HEAD, 1)
        key_h = lax.dynamic_slice_in_dim(keys, head * HEAD, HEAD, 1)
        value_h = lax.dynamic_slice_in_dim(values, head * HEAD, HEAD, 1)
        grad_o = lax.dynamic_slice_in_dim(grad_attended, head * HEAD, HEAD, 1)
        scores = jnp.where(allowed, matmul_nt(query_h, key_h) * scale, -1e30)
        probs = jnp.exp(
            scores - lax.dynamic_index_in_dim(log_sums, head, 0, keepdims=False)[:, None]
        )
        grad_p = matmul_nt(grad_o, value_h)
        grad_s = (probs * (grad_p - jnp.sum(probs * grad_p, 1, keepdims=True))).astype(jnp.bfloat16)
        grad_q = lax.dynamic_update_slice_in_dim(
            grad_q, matmul(grad_s, key_h) * scale, head * HEAD, 1
        )
        grad_k = lax.dynamic_update_slice_in_dim(
            grad_k, matmul_tn(grad_s, query_h) * scale, head * HEAD, 1
        )
        grad_v = lax.dynamic_update_slice_in_dim(
            grad_v, matmul_tn(probs.astype(jnp.bfloat16), grad_o), head * HEAD, 1
        )
        return (grad_q, grad_k, grad_v)

    start_state = (
        jnp.zeros(queries.shape, jnp.float32),
        jnp.zeros(keys.shape, jnp.float32),
        jnp.zeros(values.shape, jnp.float32),
    )
    return lax.fori_loop(0, heads, head_step, start_state)


def add_block(buffer, block, start):
    length = block.shape[0]
    current = lax.dynamic_slice_in_dim(buffer, start, length, 0)
    return lax.dynamic_update_slice_in_dim(buffer, current + block, start, 0)


def body(
    tokens,
    cont_prompt,
    routes,
    norm1_gain,
    w_query,
    w_key,
    w_value,
    w_attn_out,
    norm2_gain,
    w_ffn_in,
    w_ffn_out,
    centroids,
    expert_in_a,
    expert_out_a,
    expert_in_b,
    expert_out_b,
    grad_out,
):
    experts = lax.axis_size("dp")
    pair_size = lax.axis_size("tensor")
    dp_index = lax.axis_index("dp")
    tensor_index = lax.axis_index("tensor")
    rows_dev = tokens.shape[0]
    rows_dp = rows_dev * pair_size
    prm_dev = rows_dp - CONT
    pkeys = experts * prm_dev
    heads = w_query.shape[1] // HEAD
    width = tokens.shape[1]
    span = PLEN // prm_dev
    owner_start = dp_index // span * PLEN
    mapped_start = cont_prompt[dp_index] * PLEN
    gain_one, query_full, key_full, value_full, attn_full, gain_two, ffn_in_full, ffn_out_full = (
        lax.all_gather(norm1_gain, "dp", axis=0, tiled=True),
        lax.all_gather(w_query, "dp", axis=0, tiled=True),
        lax.all_gather(w_key, "dp", axis=0, tiled=True),
        lax.all_gather(w_value, "dp", axis=0, tiled=True),
        lax.all_gather(w_attn_out, "dp", axis=1, tiled=True),
        lax.all_gather(norm2_gain, "dp", axis=0, tiled=True),
        lax.all_gather(w_ffn_in, "dp", axis=0, tiled=True),
        lax.all_gather(w_ffn_out, "dp", axis=1, tiled=True),
    )
    inputs = tokens.astype(jnp.float32)
    normed_one, hat_one, inv_one = norm_forward(inputs, gain_one.astype(jnp.float32))
    rows_one = rows_gather(normed_one.astype(jnp.bfloat16))
    queries = matmul(rows_one, query_full).astype(jnp.bfloat16)
    keys_own = matmul(rows_one, key_full).astype(jnp.bfloat16)
    values_own = matmul(rows_one, value_full).astype(jnp.bfloat16)
    prompt_keys, prompt_values = (
        lax.all_gather(keys_own[:prm_dev], "dp", axis=0, tiled=True),
        lax.all_gather(values_own[:prm_dev], "dp", axis=0, tiled=True),
    )
    keys_first = lax.dynamic_slice_in_dim(prompt_keys, owner_start, PLEN, 0)
    values_first = lax.dynamic_slice_in_dim(prompt_values, owner_start, PLEN, 0)
    first_row = lax.broadcasted_iota(jnp.int32, (prm_dev, 1), 0)
    first_column = lax.broadcasted_iota(jnp.int32, (1, PLEN), 1)
    allowed_first = first_column <= dp_index % span * prm_dev + first_row
    keys_second = jnp.concatenate(
        [lax.dynamic_slice_in_dim(prompt_keys, mapped_start, PLEN, 0), keys_own[prm_dev:]], 0
    )
    values_second = jnp.concatenate(
        [lax.dynamic_slice_in_dim(prompt_values, mapped_start, PLEN, 0), values_own[prm_dev:]], 0
    )
    second_row = lax.broadcasted_iota(jnp.int32, (CONT, 1), 0)
    second_column = lax.broadcasted_iota(jnp.int32, (1, PLEN + CONT), 1)
    allowed_second = (second_column < PLEN) | (second_column - PLEN <= second_row)
    attn_first, sums_first = attend(
        queries[:prm_dev], keys_first, values_first, allowed_first, heads
    )
    attn_second, sums_second = attend(
        queries[prm_dev:], keys_second, values_second, allowed_second, heads
    )
    attn_low = jnp.concatenate([attn_first, attn_second], 0).astype(jnp.bfloat16)
    hidden_one = inputs + rows_scatter(matmul(attn_low, attn_full))
    normed_two, hat_two, inv_two = norm_forward(hidden_one, gain_two.astype(jnp.float32))
    rows_two = rows_gather(normed_two.astype(jnp.bfloat16))
    ffn_pre = matmul(rows_two, ffn_in_full)
    ffn_act = jax.nn.gelu(ffn_pre).astype(jnp.bfloat16)
    hidden_two = hidden_one + rows_scatter(matmul(ffn_act, ffn_out_full))
    route = routes[:, 0]
    slots_per = max(2, (3 * rows_dev + 2 * experts - 1) // (2 * experts))
    capacity = 5 * rows_dp // 4
    expert_ids = lax.broadcasted_iota(jnp.int32, (1, experts), 1)
    onehot = (route[:, None] == expert_ids).astype(jnp.int32)
    offsets = carried_in(
        jnp.sum(onehot, 0), ("dp", "tensor"), add_counts, jnp.zeros((experts,), jnp.int32)
    )
    local_rank = jnp.sum((jnp.cumsum(onehot, 0) - 1) * onehot, 1)
    global_slot = local_rank + jnp.sum(onehot * offsets[None, :], 1)
    kept = global_slot < capacity
    target = route * slots_per + local_rank
    columns = lax.broadcasted_iota(jnp.int32, (1, experts * slots_per), 1)
    placer = ((columns == target[:, None]) & kept[:, None]).astype(jnp.bfloat16)
    sent_rows = (
        matmul_tn(placer, hidden_two.astype(jnp.bfloat16))
        .astype(jnp.bfloat16)
        .reshape(experts, slots_per, width)
    )
    expert_rows = rows_gather(to_experts(sent_rows)).reshape(-1, width)
    centre = centroids[0]
    gate_value = jax.nn.sigmoid(matmul(expert_rows, centre))
    pre_a = matmul(expert_rows, expert_in_a[0])
    act_a = jax.nn.gelu(pre_a).astype(jnp.bfloat16)
    branch_a = pair_total(matmul(act_a, expert_out_a[0]))
    middle = (expert_rows.astype(jnp.float32) + branch_a).astype(jnp.bfloat16)
    pre_b = matmul(middle, expert_in_b[0])
    act_b = jax.nn.gelu(pre_b).astype(jnp.bfloat16)
    branch_b = rows_scatter(matmul(act_b, expert_out_b[0]))
    half_rows = expert_rows.shape[0] // pair_size
    start_row = tensor_index * half_rows
    branch_half = lax.dynamic_slice_in_dim(branch_a, start_row, half_rows, 0) + branch_b
    gate_half = lax.dynamic_slice_in_dim(gate_value, start_row, half_rows, 0)
    returned = (
        (gate_half[:, None] * branch_half).astype(jnp.bfloat16).reshape(experts, slots_per, width)
    )
    came_back = to_experts(returned).reshape(experts * slots_per, width)
    output = hidden_two + matmul(placer, came_back)
    cotangent = grad_out.astype(jnp.float32)
    sent_grad = matmul_tn(placer, grad_out).astype(jnp.bfloat16).reshape(experts, slots_per, width)
    grad_half = to_experts(sent_grad).reshape(half_rows, width)
    grad_returned = rows_gather(grad_half).astype(jnp.float32)
    grad_gate_half = jnp.sum(grad_half.astype(jnp.float32) * branch_half, 1)
    grad_logit_half = grad_gate_half * gate_half * (1.0 - gate_half)
    rows_half = lax.dynamic_slice_in_dim(expert_rows, start_row, half_rows, 0)
    centre_part = matmul(grad_logit_half, rows_half.astype(jnp.float32))
    grad_branch = gate_value[:, None] * grad_returned
    grad_b = grad_branch.astype(jnp.bfloat16)
    grad_pre_b = gelu_grad(pre_b, matmul_nt(grad_b, expert_out_b[0])).astype(jnp.bfloat16)
    grad_out_b = matmul_tn(act_b, grad_b)
    grad_in_b = matmul_tn(middle, grad_pre_b)
    grad_middle = pair_total(matmul_nt(grad_pre_b, expert_in_b[0]))
    grad_a = (grad_branch + grad_middle).astype(jnp.bfloat16)
    grad_pre_a = gelu_grad(pre_a, matmul_nt(grad_a, expert_out_a[0])).astype(jnp.bfloat16)
    grad_out_a = matmul_tn(act_a, grad_a)
    grad_in_a = matmul_tn(expert_rows, grad_pre_a)
    grad_rows = (
        rows_scatter(matmul_nt(grad_pre_a, expert_in_a[0]))
        + lax.dynamic_slice_in_dim(grad_middle, start_row, half_rows, 0)
        + grad_logit_half[:, None] * centre.astype(jnp.float32)[None, :]
    )
    grad_back = to_experts(
        grad_rows.astype(jnp.bfloat16).reshape(experts, slots_per, width)
    ).reshape(experts * slots_per, width)
    grad_two = cotangent + matmul(placer, grad_back)
    gain_one, query_full, key_full, value_full, attn_full, gain_two, ffn_in_full, ffn_out_full = (
        lax.all_gather(norm1_gain, "dp", axis=0, tiled=True),
        lax.all_gather(w_query, "dp", axis=0, tiled=True),
        lax.all_gather(w_key, "dp", axis=0, tiled=True),
        lax.all_gather(w_value, "dp", axis=0, tiled=True),
        lax.all_gather(w_attn_out, "dp", axis=1, tiled=True),
        lax.all_gather(norm2_gain, "dp", axis=0, tiled=True),
        lax.all_gather(w_ffn_in, "dp", axis=0, tiled=True),
        lax.all_gather(w_ffn_out, "dp", axis=1, tiled=True),
    )
    rows_down = rows_gather(grad_two.astype(jnp.bfloat16))
    grad_ffn_pre = gelu_grad(ffn_pre, matmul_nt(rows_down, ffn_out_full)).astype(jnp.bfloat16)
    grad_ffn_out = matmul_tn(ffn_act, rows_down)
    grad_ffn_in = matmul_tn(rows_two, grad_ffn_pre)
    grad_norm_two = rows_scatter(matmul_nt(grad_ffn_pre, ffn_in_full))
    back_two, grad_gain_two = norm_backward(
        grad_norm_two, hat_two, inv_two, gain_two.astype(jnp.float32)
    )
    grad_one = grad_two + back_two
    rows_attn = rows_gather(grad_one.astype(jnp.bfloat16))
    grad_attn_out = matmul_tn(attn_low, rows_attn)
    grad_attended = matmul_nt(rows_attn, attn_full).astype(jnp.bfloat16)
    grad_q_first, grad_k_first, grad_v_first = attend_back(
        queries[:prm_dev],
        keys_first,
        values_first,
        allowed_first,
        sums_first,
        grad_attended[:prm_dev],
        heads,
    )
    grad_q_second, grad_k_second, grad_v_second = attend_back(
        queries[prm_dev:],
        keys_second,
        values_second,
        allowed_second,
        sums_second,
        grad_attended[prm_dev:],
        heads,
    )
    local_width = keys_own.shape[1]
    buffer_k = jnp.zeros((pkeys, local_width), jnp.float32)
    buffer_v = jnp.zeros((pkeys, local_width), jnp.float32)
    buffer_k = add_block(
        add_block(buffer_k, grad_k_first, owner_start), grad_k_second[:PLEN], mapped_start
    )
    buffer_v = add_block(
        add_block(buffer_v, grad_v_first, owner_start), grad_v_second[:PLEN], mapped_start
    )
    prompt_grad_k, prompt_grad_v = (
        lax.psum_scatter(buffer_k, "dp", scatter_dimension=0, tiled=True),
        lax.psum_scatter(buffer_v, "dp", scatter_dimension=0, tiled=True),
    )
    grad_keys = jnp.concatenate([prompt_grad_k, grad_k_second[PLEN:]], 0).astype(jnp.bfloat16)
    grad_values = jnp.concatenate([prompt_grad_v, grad_v_second[PLEN:]], 0).astype(jnp.bfloat16)
    grad_queries = jnp.concatenate([grad_q_first, grad_q_second], 0).astype(jnp.bfloat16)
    grad_query = matmul_tn(rows_one, grad_queries)
    grad_key = matmul_tn(rows_one, grad_keys)
    grad_value = matmul_tn(rows_one, grad_values)
    grad_norm_one = rows_scatter(
        matmul_nt(grad_queries, query_full)
        + matmul_nt(grad_keys, key_full)
        + matmul_nt(grad_values, value_full)
    )
    back_one, grad_gain_one = norm_backward(
        grad_norm_one, hat_one, inv_one, gain_one.astype(jnp.float32)
    )
    grad_input = grad_one + back_one
    (
        gain_one_part,
        query_shard,
        key_shard,
        value_shard,
        attn_shard,
        gain_two_part,
        ffn_in_shard,
        ffn_out_shard,
    ) = (
        lax.psum_scatter(grad_gain_one, "dp", scatter_dimension=0, tiled=True),
        lax.psum_scatter(grad_query, "dp", scatter_dimension=0, tiled=True),
        lax.psum_scatter(grad_key, "dp", scatter_dimension=0, tiled=True),
        lax.psum_scatter(grad_value, "dp", scatter_dimension=0, tiled=True),
        lax.psum_scatter(grad_attn_out, "dp", scatter_dimension=1, tiled=True),
        lax.psum_scatter(grad_gain_two, "dp", scatter_dimension=0, tiled=True),
        lax.psum_scatter(grad_ffn_in, "dp", scatter_dimension=0, tiled=True),
        lax.psum_scatter(grad_ffn_out, "dp", scatter_dimension=1, tiled=True),
    )
    gain_one_shard, gain_two_shard, centre_grad = pair_total(
        (gain_one_part, gain_two_part, centre_part)
    )
    return (
        output.astype(jnp.bfloat16),
        grad_input.astype(jnp.bfloat16),
        gain_one_shard,
        query_shard,
        key_shard,
        value_shard,
        attn_shard,
        gain_two_shard,
        ffn_in_shard,
        ffn_out_shard,
        centre_grad[None, :],
        grad_in_a[None],
        grad_out_a[None],
        grad_in_b[None],
        grad_out_b[None],
    )


def solution(mesh):
    return jax.shard_map(
        body,
        mesh=mesh,
        in_specs=(
            P(("dp", "tensor"), None),
            P(),
            P(("dp", "tensor"), None),
            P("dp"),
            P("dp", "tensor"),
            P("dp", "tensor"),
            P("dp", "tensor"),
            P("tensor", "dp"),
            P("dp"),
            P("dp", "tensor"),
            P("tensor", "dp"),
            P("dp", None),
            P("dp", None, "tensor"),
            P("dp", "tensor", None),
            P("dp", None, "tensor"),
            P("dp", "tensor", None),
            P(("dp", "tensor"), None),
        ),
        out_specs=(
            P(("dp", "tensor"), None),
            P(("dp", "tensor"), None),
            P("dp"),
            P("dp", "tensor"),
            P("dp", "tensor"),
            P("dp", "tensor"),
            P("tensor", "dp"),
            P("dp"),
            P("dp", "tensor"),
            P("tensor", "dp"),
            P("dp", None),
            P("dp", None, "tensor"),
            P("dp", "tensor", None),
            P("dp", None, "tensor"),
            P("dp", "tensor", None),
        ),
        check_vma=False,
    )
```

profile of v0, /device:TPU:9, one launch (start us, length us, event | category | flops | bytes accessed | tf_op | source)
XLA Modules:
  0.0 3098.8 jit_solution(9611729205401209624)
XLA Ops:
  11.6 29.1 all-reduce.6
  48.4 16.6 all-gather.24.cloned.1.call-done
  65.1 14.5 all-gather.16.cloned.1.call-done
  83.6 52.3 %all-gather.20.cloned.1.call-done = bf16[1024,512]{1,0:T(8,128)(2,1)} async-done(((bf16[64,512]{1,0:T(8,128)(2,1)}), bf16[1024,512]{1,0:T(8,128)(2,1)}) %all-gather.20.cloned.1.call-update) | async-done | bytes 1048592 | tf_op jit(solution)/shard_map/all_gather | solution.py:194
  142.1 50.4 %all-gather.18.cloned.1.call-done = bf16[1024,512]{1,0:T(8,128)(2,1)} async-done(((bf16[64,512]{1,0:T(8,128)(2,1)}), bf16[1024,512]{1,0:T(8,128)(2,1)}) %all-gather.18.cloned.1.call-update) | async-done | bytes 1048592 | tf_op jit(solution)/shard_map/all_gather | solution.py:193
  195.8 111.7 %all-gather.26.cloned.1.call-done = bf16[8192,512]{1,0:T(8,128)(2,1)} async-done(((bf16[512,512]{1,0:T(8,128)(2,1)}), bf16[8192,512]{1,0:T(8,128)(2,1)}) %all-gather.26.cloned.1.call-update) | async-done | bytes 8388624 | tf_op jit(solution)/shard_map/all_gather | solution.py:209
  314.9 106.7 %all-gather.22.cloned.1.call-done = bf16[8192,512]{1,0:T(8,128)(2,1)} async-done(((bf16[512,512]{1,0:T(8,128)(2,1)}), bf16[8192,512]{1,0:T(8,128)(2,1)}) %all-gather.22.cloned.1.call-update) | async-done | bytes 8388624 | tf_op jit(solution)/shard_map/all_gather | solution.py:208
  437.0 75.2 %while.83 = (s32[]{:T(128)}, bf16[512,512]{0,1:T(8,128)(2,1)S(1)}, f32[8,512]{1,0:T(8,128)S(1)}, bf16[512,512]{1,0:T(8,128)(2,1)S(1)}, bf16[4608,512]{1,0:T(8,12...) while((s32[]{:T(128)}, bf16[512,512]{0,1:T(8,128)(2,1)S(1)}, ...), condition=%wide.region_9.10_spmd.clone, body=%wide.region_6.9_spmd.clone.sunk | while | flops 627572224 | bytes 30981296 | solution.py:116
  513.0 64.3 %while.82 = (s32[]{:T(128)}, bf16[512,512]{0,1:T(8,128)(2,1)S(1)}, f32[8,512]{1,0:T(8,128)S(1)}, bf16[512,512]{1,0:T(8,128)(2,1)S(1)}, bf16[4096,512]{1,0:T(8,12...) while((s32[]{:T(128)}, bf16[512,512]{0,1:T(8,128)(2,1)S(1)}, ...), condition=%wide.region_5.6_spmd.clone, body=%wide.region_2.5_spmd.clone.sunk | while | flops 555744768 | bytes 27549864 | solution.py:116
  599.6 40.6 %all-reduce.2 = s32[512]{0:T(512)S(1)} all-reduce(s32[512]{0:T(512)S(1)} %dynamic-update-slice.2), channel_id=2, replica_groups=mesh['dp'=16,'tensor'=2] {'dp','tensor'}, use_global_device_ids=true, to_apply=%add.2 | all-reduce | flops 512 | bytes 4096
  641.7 29.7 all-gather.32.cloned.1.call-done
  671.4 13.1 all-gather.30.cloned.1.call-done
  695.3 67.8 %all-gather.34.cloned.1.call-done = bf16[2048,1024]{0,1:T(8,128)(2,1)} async-done(((bf16[2048,64]{0,1:T(8,128)(2,1)}), bf16[2048,1024]{0,1:T(8,128)(2,1)}) %all-gather.34.cloned.1.call-update) | async-done | bytes 4194320 | tf_op jit(solution)/shard_map/all_gather | solution.py:199
  763.1 11.0 convolution_convert_fusion.1
  786.8 42.5 %all_to_all.20 = bf16[16,48,1024]{2,1,0:T(8,128)(2,1)} all-to-all(bf16[16,48,1024]{2,1,0:T(8,128)(2,1)S(1)} %bitcast.156), channel_id=1, replica_groups=mesh['dp'=16,'tensor'=2] {'dp'}, dimensions={0} | all-to-all | bytes 3145728 | tf_op jit(solution)/shard_map/all_to_all | solution.py:47
  829.4 12.8 all-gather.36.cloned.1.call-done
  868.3 42.5 %all_to_all.21 = bf16[16,48,1024]{2,1,0:T(8,128)(2,1)} all-to-all(bf16[16,48,1024]{2,1,0:T(8,128)(2,1)S(1)} %bitcast.157), channel_id=1, replica_groups=mesh['dp'=16,'tensor'=2] {'dp'}, dimensions={0} | all-to-all | bytes 3145728 | tf_op jit(solution)/shard_map/all_to_all | solution.py:47
  911.9 12.4 fusion.90
  924.3 17.7 fusion.73
  952.8 13.1 fusion.111
  976.7 20.4 fusion.66
  1023.5 42.6 %all_to_all.22 = bf16[16,48,1024]{2,1,0:T(8,128)(2,1)S(1)} all-to-all(bf16[16,48,1024]{2,1,0:T(8,128)(2,1)S(1)} %bitcast.154), channel_id=1, replica_groups=mesh['dp'=16,'tensor'=2] {'dp'}, dimensions={0} | all-to-all | bytes 3145728 | tf_op jit(solution)/shard_map/all_to_all | solution.py:47
  1068.9 11.2 all-gather.40.cloned.1.call-done
  1080.1 12.5 fusion.80
  1118.8 11.9 all-gather.42.cloned.1.call-done
  1142.5 233.1 %while.84 = (s32[]{:T(128)}, bf16[512,512]{0,1:T(8,128)(2,1)S(1)}, f32[4096,512]{0,1:T(8,128)}, f32[4096,512]{0,1:T(8,128)}, bf16[512,512]{1,0:T(8,128)(2,1)S(1)...) while((s32[]{:T(128)}, bf16[512,512]{0,1:T(8,128)(2,1)S(1)}, ...), condition=%wide.region_31.32_spmd.clone, body=%wide.region_29.31_spmd.clone.sunk | while | flops 1363443200 | bytes 102384856 | solution.py:150
  1385.2 278.0 %while.85 = (s32[]{:T(128)}, bf16[512,512]{0,1:T(8,128)(2,1)S(1)}, f32[4608,512]{0,1:T(8,128)}, f32[4608,512]{0,1:T(8,128)}, bf16[512,512]{1,0:T(8,128)(2,1)S(1)...) while((s32[]{:T(128)}, bf16[512,512]{0,1:T(8,128)(2,1)S(1)}, ...), condition=%wide.region_34.35_spmd.clone, body=%wide.region_32.34_spmd.clone.sunk | while | flops 1536228864 | bytes 133996792 | solution.py:150
  1398.2 10.9 multiply_convert_fusion.16
  1432.9 10.9 multiply_convert_fusion.16
  1467.5 10.9 multiply_convert_fusion.16
  1502.1 10.9 multiply_convert_fusion.16
  1536.8 10.9 multiply_convert_fusion.16
  1571.5 10.9 multiply_convert_fusion.16
  1606.2 10.9 multiply_convert_fusion.16
  1675.0 11.2 add_dynamic-update-slice_fusion.1
  1698.9 11.2 add_dynamic-update-slice_fusion
  1717.8 315.4 %reduce-scatter.25.cloned.1.call-done = f32[512,512]{0,1:T(8,128)} async-done(((f32[8192,512]{0,1:T(8,128)}), f32[512,512]{0,1:T(8,128)}) %reduce-scatter.25.cloned.1.call-update) | async-done | bytes 1048592 | tf_op jit(solution)/shard_map/reduce_scatter | solution.py:353
  2034.5 353.2 %reduce-scatter.27.cloned.1.call-done = f32[512,512]{0,1:T(8,128)} async-done(((f32[8192,512]{0,1:T(8,128)}), f32[512,512]{0,1:T(8,128)}) %reduce-scatter.27.cloned.1.call-update) | async-done | bytes 1048592 | tf_op jit(solution)/shard_map/reduce_scatter | solution.py:354
  2403.6 12.5 fusion.176
  2432.5 12.5 convolution_bitcast_fusion.1
  2445.0 14.1 convolution_bitcast_fusion
  2476.0 11.0 convolution_bitcast_fusion.3
  2487.1 15.3 convolution_bitcast_fusion.2
  2518.9 28.3 all-reduce.5
  2564.5 193.3 %reduce-scatter.41.cloned.1.call-done = f32[2048,64]{0,1:T(8,128)} async-done(((f32[2048,1024]{0,1:T(8,128)}), f32[2048,64]{0,1:T(8,128)}) %reduce-scatter.41.cloned.1.call-update) | async-done | bytes 524304 | tf_op jit(solution)/shard_map/reduce_scatter | solution.py:388
  2757.8 183.1 %reduce-scatter.39.cloned.1.call-done = f32[64,2048]{1,0:T(8,128)} async-done(((f32[1024,2048]{1,0:T(8,128)}), f32[64,2048]{1,0:T(8,128)}) %reduce-scatter.39.cloned.1.call-update) | async-done | bytes 524304 | tf_op jit(solution)/shard_map/reduce_scatter | solution.py:387
  2940.9 70.2 %reduce-scatter.33.cloned.1.call-done = f32[64,512]{1,0:T(8,128)} async-done(((f32[1024,512]{1,0:T(8,128)}), f32[64,512]{1,0:T(8,128)}) %reduce-scatter.33.cloned.1.call-update) | async-done | bytes 131088 | tf_op jit(solution)/shard_map/reduce_scatter | solution.py:383
  3011.1 80.7 %reduce-scatter.35.cloned.1.call-done = f32[64,512]{1,0:T(8,128)} async-done(((f32[1024,512]{1,0:T(8,128)}), f32[64,512]{1,0:T(8,128)}) %reduce-scatter.35.cloned.1.call-update) | async-done | bytes 131088 | tf_op jit(solution)/shard_map/reduce_scatter | solution.py:384
  (624 shorter events, 907.5 us)
Async XLA Ops:
  7.2 57.9 %all-gather.24.cloned.1.call-start = ((), (), s32[]{:S(2)}) async-start(), calls=%async_computation.22 | async-start | bytes 1114112 | tf_op jit(solution)/shard_map/all_gather | solution.py:195
  7.9 71.6 %all-gather.16.cloned.1.call-start = ((), (), s32[]{:S(2)}) async-start(), calls=%async_computation.18 | async-start | bytes 3145728 | tf_op jit(solution)/shard_map/all_gather | solution.py:33
  47.1 88.8 %all-gather.20.cloned.1.call-start = ((), (), s32[]{:S(2)}) async-start(), calls=%async_computation.20 | async-start | bytes 1114112 | tf_op jit(solution)/shard_map/all_gather | solution.py:194
  47.8 144.8 %all-gather.18.cloned.1.call-start = ((), (), s32[]{:S(2)}) async-start(), calls=%async_computation.19 | async-start | bytes 1114112 | tf_op jit(solution)/shard_map/all_gather | solution.py:193
  48.4 259.1 %all-gather.26.cloned.1.call-start = ((), (), s32[]{:S(2)}) async-start(), calls=%async_computation.23 | async-start | bytes 8912896 | tf_op jit(solution)/shard_map/all_gather | solution.py:209
  83.5 57.3 %copy-start.78 = (s32[16]{0:T(128)S(1)}, s32[16]{0:T(128)}, u32[]{:S(2)}) copy-start(s32[16]{0:T(128)} %param.28) | copy-start | bytes 196
  83.5 338.2 %all-gather.22.cloned.1.call-start = ((), (), s32[]{:S(2)}) async-start(), calls=%async_computation.21 | async-start | bytes 8912896 | tf_op jit(solution)/shard_map/all_gather | solution.py:208
  139.8 437.5 %all-gather.28.cloned.1.call-start = ((), (), s32[]{:S(2)}) async-start(), calls=%async_computation.24 | async-start | bytes 1114112 | tf_op jit(solution)/shard_map/all_gather | solution.py:196
  140.6 452.4 %reduce-scatter.15.cloned.1.call-start = ((), (), s32[]{:S(2)}) async-start(), calls=%async_computation.25 | async-start | bytes 3145728 | tf_op jit(solution)/shard_map/reduce_scatter | solution.py:37
  512.2 65.9 %copy-start.29 = (bf16[512,512]{0,1:T(8,128)(2,1)}, bf16[512,512]{0,1:T(8,128)(2,1)S(1)}, u32[]{:S(2)}) copy-start(bf16[512,512]{0,1:T(8,128)(2,1)S(1)} %get-tuple-element.687) | copy-start | bytes 1572868
  582.1 89.3 %all-gather.32.cloned.1.call-start = ((), (), s32[]{:S(2)}) async-start(), calls=%async_computation.27 | async-start | bytes 4456448 | tf_op jit(solution)/shard_map/all_gather | solution.py:198
  582.8 101.7 %all-gather.30.cloned.1.call-start = ((), (), s32[]{:S(2)}) async-start(), calls=%async_computation.26 | async-start | bytes 3145728 | tf_op jit(solution)/shard_map/all_gather | solution.py:33
  582.9 57.4 %copy-start.36 = (f32[1024]{0:T(1024)}, f32[1024]{0:T(1024)S(1)}, u32[]{:S(2)}) copy-start(f32[1024]{0:T(1024)S(1)} %convert_element_type.224) | copy-start | bytes 12292
  598.4 164.7 %all-gather.34.cloned.1.call-start = ((), (), s32[]{:S(2)}) async-start(), calls=%async_computation.28 | async-start | bytes 4456448 | tf_op jit(solution)/shard_map/all_gather | solution.py:199
  599.1 185.3 %reduce-scatter.17.cloned.1.call-start = ((), (), s32[]{:S(2)}) async-start(), calls=%async_computation.29 | async-start | bytes 3145728 | tf_op jit(solution)/shard_map/reduce_scatter | solution.py:37
  641.7 53.6 %copy-start.60 = (s32[16,5]{0,1:T(8,128)}, s32[16,5]{0,1:T(8,128)S(1)}, u32[]{:S(2)}) copy-start(s32[16,5]{0,1:T(8,128)S(1)} %reduce-window.9) | copy-start | bytes 964
  774.2 68.0 %all-gather.36.cloned.1.call-start = ((), (), s32[]{:S(2)}) async-start(), calls=%async_computation.30 | async-start | bytes 4718592 | tf_op jit(solution)/shard_map/all_gather | solution.py:33
  775.6 290.4 %copy-start.66 = (pred[512]{0:T(512)(128)(4,1)}, pred[512]{0:T(512)(128)(4,1)S(1)}, u32[]{:S(2)}) copy-start(pred[512]{0:T(512)(128)(4,1)S(1)} %add_compare_fusion) | copy-start | bytes 1540
  775.7 290.4 %copy-start.63 = (s32[512,1]{0,1:T(1,128)}, s32[512,1]{0,1:T(1,128)S(1)}, u32[]{:S(2)}) copy-start(s32[512,1]{0,1:T(1,128)S(1)} %multiply_add_fusion) | copy-start | bytes 6148
  829.4 82.6 %all-reduce.11.cloned.1.call-start = ((), (), s32[]{:S(2)}) async-start(), calls=%async_computation.31 | async-start | bytes 6291456 | tf_op jit(solution)/shard_map/psum | solution.py:43
  865.7 45.2 %copy-start.10 = (bf16[32,48,1024]{2,1,0:T(8,128)(2,1)S(1)}, bf16[32,48,1024]{2,1,0:T(8,128)(2,1)}, u32[]{:S(2)}) copy-start(bf16[32,48,1024]{2,1,0:T(8,128)(2,1)} %all-gather.36.cloned.1.call-done) | copy-start | bytes 9437188
  865.7 45.2 %copy-start.58 = (bf16[1,1024]{1,0:T(2,128)(2,1)S(1)}, bf16[1,1024]{1,0:T(2,128)(2,1)}, u32[]{:S(2)}) copy-start(bf16[1,1024]{1,0:T(2,128)(2,1)} %param.38) | copy-start | bytes 6148
  865.7 58.6 %all-gather.38.cloned.1.call-start = ((), (), s32[]{:S(2)}) async-start(), calls=%async_computation.33 | async-start | bytes 4718592 | tf_op jit(solution)/shard_map/all_gather | solution.py:33
  910.9 65.8 %all-reduce.13.cloned.1.call-start = ((), (), s32[]{:S(2)}) async-start(), calls=%async_computation.34 | async-start | bytes 6291456 | tf_op jit(solution)/shard_map/psum | solution.py:43
  911.9 108.0 %copy-start.55 = (f32[1536]{0:T(1024)}, f32[1536]{0:T(1024)S(1)}, u32[]{:S(2)}) copy-start(f32[1536]{0:T(1024)S(1)} %add_divide_fusion) | copy-start | bytes 18436
  952.8 63.8 %reduce-scatter.19.cloned.1.call-start = ((), (), s32[]{:S(2)}) async-start(), calls=%async_computation.32 | async-start | bytes 4718592 | tf_op jit(solution)/shard_map/reduce_scatter | solution.py:37
  966.0 54.6 %reduce-scatter.21.cloned.1.call-start = ((), (), s32[]{:S(2)}) async-start(), calls=%async_computation.35 | async-start | bytes 4718592 | tf_op jit(solution)/shard_map/reduce_scatter | solution.py:37
  1007.3 72.8 %all-gather.40.cloned.1.call-start = ((), (), s32[]{:S(2)}) async-start(), calls=%async_computation.36 | async-start | bytes 3145728 | tf_op jit(solution)/shard_map/all_gather | solution.py:33
  1020.5 45.5 %copy-start.46 = (f32[768]{0:T(1024)}, f32[768]{0:T(1024)S(1)}, u32[]{:S(2)}) copy-start(f32[768]{0:T(1024)S(1)} %get-tuple-element.895) | copy-start | bytes 9220
  1020.5 45.5 %copy-start.76 = (bf16[512,1024]{1,0:T(8,128)(2,1)S(1)}, bf16[512,1024]{1,0:T(8,128)(2,1)}, u32[]{:S(2)}) copy-start(bf16[512,1024]{1,0:T(8,128)(2,1)} %param.43) | copy-start | bytes 3145732
  1068.8 42.4 %reduce-scatter.23.cloned.1.call-start = ((), (), s32[]{:S(2)}) async-start(), calls=%async_computation.37 | async-start | bytes 3145728 | tf_op jit(solution)/shard_map/reduce_scatter | solution.py:37
  1100.3 30.3 all-gather.42.cloned.1.call-start
  1118.8 914.4 %reduce-scatter.25.cloned.1.call-start = ((), (), s32[]{:S(2)}) async-start(), calls=%async_computation.39 | async-start | bytes 17825792 | tf_op jit(solution)/shard_map/reduce_scatter | solution.py:353
  1686.2 701.4 %reduce-scatter.27.cloned.1.call-start = ((), (), s32[]{:S(2)}) async-start(), calls=%async_computation.40 | async-start | bytes 17825792 | tf_op jit(solution)/shard_map/reduce_scatter | solution.py:354
  1710.2 806.6 %reduce-scatter.29.cloned.1.call-start = ((), (), s32[]{:S(2)}) async-start(), calls=%async_computation.41 | async-start | bytes 3145728 | tf_op jit(solution)/shard_map/reduce_scatter | solution.py:37
  1711.6 680.2 %copy-start.24 = (bf16[512,512]{0,1:T(8,128)(2,1)}, bf16[512,512]{0,1:T(8,128)(2,1)S(1)}, u32[]{:S(2)}) copy-start(bf16[512,512]{0,1:T(8,128)(2,1)S(1)} %slice.76) | copy-start | bytes 1572868
  1713.0 675.9 %copy-start.33 = (bf16[512,512]{0,1:T(8,128)(2,1)}, bf16[512,512]{0,1:T(8,128)(2,1)S(1)}, u32[]{:S(2)}) copy-start(bf16[512,512]{0,1:T(8,128)(2,1)S(1)} %slice.77) | copy-start | bytes 1572868
  2034.5 357.3 %copy-start.26 = (bf16[512,512]{0,1:T(8,128)(2,1)}, bf16[512,512]{0,1:T(8,128)(2,1)S(1)}, u32[]{:S(2)}) copy-start(bf16[512,512]{0,1:T(8,128)(2,1)S(1)} %convert.32) | copy-start | bytes 1572868
  2394.7 168.0 %reduce-scatter.37.cloned.1.call-start = ((), (), s32[]{:S(2)}) async-start(), calls=%async_computation.45 | async-start | bytes 2228224 | tf_op jit(solution)/shard_map/reduce_scatter | solution.py:385
  2399.2 165.3 %reduce-scatter.31.cloned.1.call-start = ((), (), s32[]{:S(2)}) async-start(), calls=%async_computation.42 | async-start | bytes 2228224 | tf_op jit(solution)/shard_map/reduce_scatter | solution.py:382
  2403.5 354.2 %reduce-scatter.41.cloned.1.call-start = ((), (), s32[]{:S(2)}) async-start(), calls=%async_computation.47 | async-start | bytes 8912896 | tf_op jit(solution)/shard_map/reduce_scatter | solution.py:388
  2416.1 524.7 %reduce-scatter.39.cloned.1.call-start = ((), (), s32[]{:S(2)}) async-start(), calls=%async_computation.46 | async-start | bytes 8912896 | tf_op jit(solution)/shard_map/reduce_scatter | solution.py:387
  2426.7 584.4 %reduce-scatter.33.cloned.1.call-start = ((), (), s32[]{:S(2)}) async-start(), calls=%async_computation.43 | async-start | bytes 2228224 | tf_op jit(solution)/shard_map/reduce_scatter | solution.py:383
  2432.5 26.7 slice-start.4
  2460.8 52.1 %all-to-all-start.1 = ((bf16[16,48,1024]{2,1,0:T(8,128)(2,1)}), bf16[16,48,1024]{2,1,0:T(8,128)(2,1)}, u32[]{:S(2)}, u32[]{:S(2)}) async-start(bf16[16,48,1024]{2,1,0:T(8,128)(2,1)} %bitcast.153), calls=%async_computation.4 | async-start | bytes 3145728 | tf_op jit(solution)/shard_map/all_to_all | solution.py:47
  2471.3 620.5 %reduce-scatter.35.cloned.1.call-start = ((), (), s32[]{:S(2)}) async-start(), calls=%async_computation.44 | async-start | bytes 2228224 | tf_op jit(solution)/shard_map/reduce_scatter | solution.py:384
  2487.1 25.8 copy-start.5
  2487.1 25.8 copy-start.8
  (93 other events, 785.7 us)
Sparse Core Ops, SparseCore 0:
  10.8 54.2 all-gather.23
  67.2 12.2 all-gather.15
  82.3 53.5 all-gather.19
  138.5 54.0 all-gather.17
  195.8 111.6 all-gather.25
  310.6 111.0 all-gather.21
  424.5 53.5 all-gather.27
  582.2 10.6 reduce-scatter.14
  596.1 75.2 all-gather.31
  673.5 11.0 all-gather.29
  687.7 75.3 all-gather.33
  774.3 10.0 reduce-scatter.16
  829.5 12.6 all-gather.35
  865.8 24.3 all-reduce.10
  911.0 12.6 all-gather.37
  952.9 23.7 all-reduce.12
  979.3 12.0 reduce-scatter.18
  1007.4 12.0 reduce-scatter.20
  1069.0 11.0 all-gather.39
  1100.5 10.7 reduce-scatter.22
  1118.9 11.7 all-gather.41
  1686.3 346.7 reduce-scatter.24
  2035.6 352.0 reduce-scatter.26
  2394.8 15.8 reduce-scatter.28
  2413.5 66.3 reduce-scatter.36
  2482.7 81.7 reduce-scatter.30
  2567.2 190.4 reduce-scatter.40
  2760.6 180.2 reduce-scatter.38
  2943.7 67.2 reduce-scatter.32
  3013.8 77.9 reduce-scatter.34
where the time goes:
time: 3120 us; the launch traced here: 3100 us
  waiting for transfers between devices  1750 us (56%)
  matrix products  735 us (24%)
  other arithmetic  250 us (8%)
  blocking collectives  236 us (8%)
  local copies, waits for them, and re-layouts  93.9 us (3%)
    reduce_scatter x1, waiting for transfers between devices, body(): lax.psum_scatter(buffer_v, 'dp', scatter_dimension=0, tiled=True)  353 us
    dot_general x58, matrix products, matmul_nt(): lax.dot_general(left, right, (((1,), (1,)), ((), ())), preferred_element_...  326 us
    reduce_scatter x1, waiting for transfers between devices, body(): lax.psum_scatter(buffer_k, 'dp', scatter_dimension=0, tiled=True)  315 us
    dot_general x44, matrix products, matmul_tn(): lax.dot_general(left, right, (((0,), (0,)), ((), ())), preferred_element_...  219 us
    reduce_scatter x1, waiting for transfers between devices, body(): lax.psum_scatter(grad_ffn_out, 'dp', scatter_dimension=1, tiled=True)  193 us
    dot_general x46, matrix products, matmul(): return jnp.dot(left, right, preferred_element_type=jnp.float32)  190 us
    reduce_scatter x1, waiting for transfers between devices, body(): lax.psum_scatter(grad_ffn_in, 'dp', scatter_dimension=0, tiled=True)  183 us
    convert_element_type x16, other arithmetic, head_step(): (probs * (grad_p - jnp.sum(probs * grad_p, 1, keepdims=True))).astype(jnp...  151 us
  transfers between devices with their start and end apart: 31, of which 24 were waited for; matrix products, arithmetic and copies ran while one was open for 13% of the time, Pallas kernels for 0%

commit v1 on v0

--- a/solution.py
+++ b/solution.py
@@ -1,6 +1,10 @@
+import functools
+
 import jax
 import jax.numpy as jnp
 from jax import lax
+from jax.experimental import pallas as pl
+from jax.experimental.pallas import tpu as pltpu
 from jax.sharding import PartitionSpec as P
 
 HEAD = 64
@@ -156,7 +160,7 @@
     return lax.dynamic_update_slice_in_dim(buffer, current + block, start, 0)
 
 
-def body(
+def body_general(
     tokens,
     cont_prompt,
     routes,
@@ -409,7 +413,477 @@
     )
 
 
+LOG2E = 1.4426950408889634
+BF16 = jnp.bfloat16
+F32 = jnp.float32
+
+
+def dot_tt(left, right):
+    return lax.dot_general(left, right, (((0,), (0,)), ((), ())), preferred_element_type=F32)
+
+
+def attn_fwd_kernel(plan, own, prompts, out, log_sums, *, head, factor):
+    step_id = pl.program_id(0)
+    block, full, first = plan[0, step_id], plan[1, step_id], plan[2, step_id]
+
+    @pl.when(plan[3, step_id] > 0)
+    def _():
+        query = own[block, 0:head, :]
+
+        def tile(key, value, carry, diagonal):
+            scores = dot_tt(key, query) * factor
+            if diagonal:
+                key_at = lax.broadcasted_iota(jnp.int32, scores.shape, 0)
+                query_at = lax.broadcasted_iota(jnp.int32, scores.shape, 1)
+                scores = jnp.where(key_at <= query_at, scores, -1e30)
+            top = jnp.max(scores, 0, keepdims=True)
+            if carry is None:
+                expo = jnp.exp2(scores - top)
+                return top, jnp.sum(expo, 0, keepdims=True), matmul(value, expo.astype(BF16))
+            before, total, result = carry
+            top = jnp.maximum(before, top)
+            expo = jnp.exp2(scores - top)
+            shrink = jnp.exp2(before - top)
+            return (
+                top,
+                total * shrink + jnp.sum(expo, 0, keepdims=True),
+                result * shrink + matmul(value, expo.astype(BF16)),
+            )
+
+        carry = tile(own[block, head : 2 * head, :], own[block, 2 * head : 3 * head, :], None, True)
+
+        def step(k, carry):
+            at = first + k
+            return tile(prompts[at, 0:head, :], prompts[at, head : 2 * head, :], carry, False)
+
+        top, total, result = lax.fori_loop(0, full, step, carry)
+        out[block] = (result / total).astype(BF16)
+        log_sums[block] = top + jnp.log2(total)
+
+
+def attn_bwd_kernel(
+    plan, own, prompts, grad, out, log_sums, grad_own, grad_prompts, sum_k, sum_v, *, head, factor, scale
+):
+    step_id = pl.program_id(0)
+    block, full, first = plan[0, step_id], plan[1, step_id], plan[2, step_id]
+
+    @pl.when(step_id == 0)
+    def _():
+        sum_k[...] = jnp.zeros_like(sum_k)
+        sum_v[...] = jnp.zeros_like(sum_v)
+
+    @pl.when(plan[3, step_id] > 0)
+    def _():
+        query_t, grad_t, log_sum = own[block, 0:head, :], grad[block], log_sums[block]
+        inner = jnp.sum(grad_t.astype(F32) * out[block].astype(F32), 0, keepdims=True)
+        query, grad_o = query_t.T, grad_t.T
+
+        def tile(key, value, diagonal):
+            probs = jnp.exp2(dot_tt(key, query_t) * factor - log_sum)
+            if diagonal:
+                key_at = lax.broadcasted_iota(jnp.int32, probs.shape, 0)
+                query_at = lax.broadcasted_iota(jnp.int32, probs.shape, 1)
+                probs = jnp.where(key_at <= query_at, probs, 0.0)
+            grad_s = (probs * (dot_tt(value, grad_t) - inner)).astype(BF16)
+            return matmul(grad_s, query), matmul(probs.astype(BF16), grad_o), matmul(key, grad_s)
+
+        grad_k, grad_v, grad_q = tile(
+            own[block, head : 2 * head, :], own[block, 2 * head : 3 * head, :], True
+        )
+        grad_own[block, head : 2 * head, :] = (grad_k * scale).T.astype(BF16)
+        grad_own[block, 2 * head : 3 * head, :] = grad_v.T.astype(BF16)
+
+        def step(k, grad_q):
+            at = first + k
+            more_k, more_v, more_q = tile(
+                prompts[at, 0:head, :], prompts[at, head : 2 * head, :], False
+            )
+            sum_k[at] += more_k
+            sum_v[at] += more_v
+            return grad_q + more_q
+
+        grad_q = lax.fori_loop(0, full, step, grad_q)
+        grad_own[block, 0:head, :] = (grad_q * scale).astype(BF16)
+
+    @pl.when(step_id == pl.num_programs(0) - 1)
+    def _():
+        def finish(k, carry):
+            grad_prompts[k, 0:head, :] = (sum_k[k] * scale).T.astype(BF16)
+            grad_prompts[k, head : 2 * head, :] = sum_v[k].T.astype(BF16)
+            return carry
+
+        lax.fori_loop(0, sum_k.shape[0], finish, 0)
+
+
+def attn_forward(plan, own, prompts):
+    blocks, triple, length = own.shape
+    head = triple // 3
+    whole = pl.BlockSpec(memory_space=pltpu.VMEM)
+    return pl.pallas_call(
+        functools.partial(attn_fwd_kernel, head=head, factor=head**-0.5 * LOG2E),
+        grid_spec=pltpu.PrefetchScalarGridSpec(
+            num_scalar_prefetch=1,
+            grid=(plan.shape[1],),
+            in_specs=[whole, whole],
+            out_specs=[whole, whole],
+        ),
+        out_shape=[
+            jax.ShapeDtypeStruct((blocks, head, length), BF16),
+            jax.ShapeDtypeStruct((blocks, 1, length), F32),
+        ],
+        compiler_params=pltpu.CompilerParams(vmem_limit_bytes=40 * 2**20),
+        cost_estimate=pl.CostEstimate(
+            flops=100 * length * length * 256 * 4,
+            bytes_accessed=8 * 2**20,
+            transcendentals=100 * length * length,
+        ),
+        name="attn_fwd",
+    )(plan, own, prompts)
+
+
+def attn_backward(plan, own, prompts, grad, out, log_sums):
+    blocks, triple, length = own.shape
+    head = triple // 3
+    whole = pl.BlockSpec(memory_space=pltpu.VMEM)
+    return pl.pallas_call(
+        functools.partial(
+            attn_bwd_kernel, head=head, factor=head**-0.5 * LOG2E, scale=head**-0.5
+        ),
+        grid_spec=pltpu.PrefetchScalarGridSpec(
+            num_scalar_prefetch=1,
+            grid=(plan.shape[1],),
+            in_specs=[whole] * 5,
+            out_specs=[whole, whole],
+            scratch_shapes=[pltpu.VMEM((prompts.shape[0], length, head), F32)] * 2,
+        ),
+        out_shape=[
+            jax.ShapeDtypeStruct(own.shape, BF16),
+            jax.ShapeDtypeStruct(prompts.shape, BF16),
+        ],
+        compiler_params=pltpu.CompilerParams(vmem_limit_bytes=48 * 2**20),
+        cost_estimate=pl.CostEstimate(
+            flops=100 * length * length * 256 * 10,
+            bytes_accessed=16 * 2**20,
+            transcendentals=100 * length * length,
+        ),
+        name="attn_bwd",
+    )(plan, own, prompts, grad, out, log_sums)
+
+
+def swap(value):
+    return lax.ppermute(value, "tensor", [(0, 1), (1, 0)])
+
+
+def to_core_one(value):
+    return lax.ppermute(value, "tensor", [(0, 1)])
+
+
+def to_core_zero(value):
+    return lax.ppermute(value, "tensor", [(1, 0)])
+
+
+def with_other(value):
+    return jnp.concatenate([value, swap(value)], 0)
+
+
+def keep_rows(value):
+    half = value.shape[0] // 2
+    return value[:half] + swap(value[half:].astype(BF16)).astype(F32)
+
+
+def pair_sum(value):
+    half = value.shape[0] // 2
+    other = swap(value.astype(BF16)).astype(F32)
+    return value + jnp.concatenate([other[half:], other[:half]], 0)
+
+
+def fits_paired(mesh):
+    return mesh.shape["tensor"] == 2 and mesh.shape["dp"] == 16
+
+
+def body_paired(
+    tokens,
+    cont_prompt,
+    routes,
+    norm1_gain,
+    w_query,
+    w_key,
+    w_value,
+    w_attn_out,
+    norm2_gain,
+    w_ffn_in,
+    w_ffn_out,
+    centroids,
+    expert_in_a,
+    expert_out_a,
+    expert_in_b,
+    expert_out_b,
+    grad_out,
+):
+    experts = lax.axis_size("dp")
+    dp_index = lax.axis_index("dp")
+    core_zero = lax.axis_index("tensor") == 0
+    rows, width = tokens.shape
+    rows_dp = 2 * rows
+    shard = w_query.shape[0]
+    half_heads = w_query.shape[1] // HEAD
+    hidden = w_ffn_in.shape[1]
+    triple = 3 * HEAD
+    heads = 2 * half_heads
+    both = lambda lower, upper: (jnp.where(core_zero, lower, upper), jnp.where(core_zero, upper, lower))
+
+    route = routes[:, 0]
+    slots_per = max(2, (3 * rows + 2 * experts - 1) // (2 * experts))
+    capacity = 5 * rows_dp // 4
+    onehot = route[:, None] == lax.broadcasted_iota(jnp.int32, (1, experts), 1)
+    onehot_low = onehot.astype(BF16)
+    below = lax.broadcasted_iota(jnp.int32, (rows, rows), 0) > lax.broadcasted_iota(
+        jnp.int32, (rows, rows), 1
+    )
+    earlier = matmul(below.astype(BF16), onehot_low)
+    local_rank = jnp.sum(jnp.where(onehot, earlier, 0.0), 1).astype(jnp.int32)
+    target = route * slots_per + local_rank
+    columns = lax.broadcasted_iota(jnp.int32, (1, experts * slots_per), 1)
+    placer = (columns == target[:, None]).astype(BF16)
+    counts = jnp.sum(onehot_low.astype(F32), 0).astype(BF16)
+    counts_pair = jnp.concatenate(both(counts, swap(counts)), 0)
+
+    qkv_shard = jnp.stack(
+        [part.reshape(shard, half_heads, HEAD) for part in (w_query, w_key, w_value)], 2
+    ).reshape(shard, half_heads * triple)
+    extra = jnp.concatenate([norm1_gain, norm2_gain, counts_pair], 0)
+    extra = jnp.pad(extra[None, :], ((0, 7), (0, half_heads * triple - extra.shape[0])))
+    first_all = lax.all_gather(jnp.concatenate([qkv_shard, extra], 0), "dp")
+    qkv_full = first_all[:, :shard].reshape(width, half_heads * triple)
+    gain_one = first_all[:, shard, :shard].reshape(width).astype(F32)
+    gain_two = first_all[:, shard, shard : 2 * shard].reshape(width).astype(F32)
+    counts_all = first_all[:, shard, 2 * shard : 2 * shard + 2 * experts].reshape(experts, 2, experts)
+    second_all = lax.all_gather(
+        jnp.concatenate([w_ffn_in, w_ffn_out.T, w_attn_out.T], 1), "dp", axis=0, tiled=True
+    )
+    ffn_in = second_all[:, :hidden]
+    ffn_out_t = second_all[:, hidden : 2 * hidden]
+    attn_half = second_all[:, 2 * hidden :]
+
+    sent_grad = matmul_tn(placer, grad_out).astype(BF16).reshape(experts, slots_per, width)
+    grad_own = to_experts(sent_grad).reshape(-1, width)
+
+    mine = jnp.sum(
+        jnp.where(lax.broadcasted_iota(jnp.int32, (1, 1, experts), 2) == dp_index, counts_all.astype(F32), 0.0),
+        2,
+    )
+    per_chip = jnp.sum(mine, 1)
+    chip_before = jnp.sum(
+        jnp.where(
+            lax.broadcasted_iota(jnp.int32, (experts, experts), 1)
+            < lax.broadcasted_iota(jnp.int32, (experts, experts), 0),
+            per_chip[None, :],
+            0.0,
+        ),
+        1,
+    )
+    starts = both(chip_before, chip_before + mine[:, 0])
+    slot_at = lax.broadcasted_iota(jnp.int32, (1, slots_per), 1).astype(F32)
+    kept = jnp.concatenate(
+        [(start[:, None] + slot_at < capacity).reshape(-1, 1) for start in starts], 0
+    )
+    half_rows = experts * slots_per
+    grad_returned = jnp.where(kept, with_other(grad_own).astype(F32), 0.0)
+
+    pair_tokens = with_other(tokens).astype(F32)
+    normed_one, hat_pair, inv_pair = norm_forward(pair_tokens, gain_one)
+    inputs, hat_one, inv_one = pair_tokens[:rows], hat_pair[:rows], inv_pair[:rows]
+    rows_one = normed_one.astype(BF16)
+    other_t = lax.dot_general(
+        qkv_full, rows_one[rows:], (((0,), (1,)), ((), ())), preferred_element_type=F32
+    ).astype(BF16)
+    own_t = lax.dot_general(
+        qkv_full, rows_one[:rows], (((0,), (1,)), ((), ())), preferred_element_type=F32
+    ).astype(BF16)
+    qkv_t = jnp.concatenate(both(own_t, swap(other_t)), 0).reshape(heads, triple, rows)
+    by_head = lax.all_to_all(qkv_t, "dp", split_axis=0, concat_axis=0, tiled=True)
+
+    lent = experts // 4
+    span = PLEN // rows
+    own_blocks = jnp.concatenate([by_head, to_core_zero(by_head[:lent])], 0)
+    prompt_kv = jnp.where(core_zero, by_head[:, HEAD:], to_core_one(by_head[:, HEAD:]))
+    places = jnp.arange(experts + lent, dtype=jnp.int32)
+    follows = cont_prompt * span
+    plan_zero = jnp.stack(
+        [
+            places,
+            jnp.where(places < experts, places % span, span),
+            jnp.concatenate([places[:experts] // span * span, follows[:lent]], 0),
+            jnp.ones_like(places),
+        ]
+    )
+    plan_one = jnp.stack(
+        [
+            jnp.minimum(places + lent, experts - 1),
+            jnp.full_like(places, span),
+            jnp.concatenate([follows[lent:], jnp.zeros((2 * lent,), jnp.int32)], 0),
+            (places < experts - lent).astype(jnp.int32),
+        ]
+    )
+    plan = jnp.where(core_zero, plan_zero, plan_one)
+    attn_blocks, log_sums = attn_forward(plan, own_blocks, prompt_kv)
+    lent_back = to_core_one(attn_blocks[experts:])
+    attn_own = jnp.concatenate(
+        [jnp.where(core_zero, attn_blocks[:lent], lent_back), attn_blocks[lent:experts]], 0
+    )
+    attn_t = lax.all_to_all(attn_own, "dp", split_axis=0, concat_axis=0, tiled=True).reshape(
+        width, rows
+    )
+
+    attn_out_t = jnp.concatenate(both(attn_half, swap(attn_half)), 1)
+    hidden_one = inputs + lax.dot_general(
+        attn_t, attn_out_t, (((0,), (1,)), ((), ())), preferred_element_type=F32
+    )
+    normed_two, hat_two, inv_two = norm_forward(hidden_one, gain_two)
+    rows_two = with_other(normed_two.astype(BF16))
+    ffn_pre = matmul(rows_two, ffn_in).astype(BF16)
+    ffn_act = jax.nn.gelu(ffn_pre.astype(F32)).astype(BF16)
+    hidden_two = hidden_one + keep_rows(matmul_nt(ffn_act, ffn_out_t))
+
+    sent_rows = (
+        matmul_tn(placer, hidden_two.astype(BF16)).astype(BF16).reshape(experts, slots_per, width)
+    )
+    expert_rows = with_other(to_experts(sent_rows).reshape(-1, width))
+    centre = centroids[0]
+    gate_value = jax.nn.sigmoid(matmul(expert_rows, centre))
+    pre_a = matmul(expert_rows, expert_in_a[0]).astype(BF16)
+    act_a = jax.nn.gelu(pre_a.astype(F32)).astype(BF16)
+    branch_a = pair_sum(matmul(act_a, expert_out_a[0]))
+    middle = (expert_rows.astype(F32) + branch_a).astype(BF16)
+    pre_b = matmul(middle, expert_in_b[0]).astype(BF16)
+    act_b = jax.nn.gelu(pre_b.astype(F32)).astype(BF16)
+    branch_half = branch_a[:half_rows] + keep_rows(matmul(act_b, expert_out_b[0]))
+    gate_half = gate_value[:half_rows]
+    returned = (
+        jnp.where(kept[:half_rows], gate_half[:, None] * branch_half, 0.0)
+        .astype(BF16)
+        .reshape(experts, slots_per, width)
+    )
+    came_back = to_experts(returned).reshape(half_rows, width)
+    output = hidden_two + matmul(placer, came_back)
+
+    grad_half = grad_returned[:half_rows]
+    grad_logit_half = jnp.sum(grad_half * branch_half, 1) * gate_half * (1.0 - gate_half)
+    centre_part = matmul(grad_logit_half, expert_rows[:half_rows].astype(F32))
+    grad_branch = gate_value[:, None] * grad_returned
+    grad_b = grad_branch.astype(BF16)
+    grad_pre_b = gelu_grad(pre_b.astype(F32), matmul_nt(grad_b, expert_out_b[0])).astype(BF16)
+    grad_middle = pair_sum(matmul_nt(grad_pre_b, expert_in_b[0]))
+    grad_a = (grad_branch + grad_middle).astype(BF16)
+    grad_pre_a = gelu_grad(pre_a.astype(F32), matmul_nt(grad_a, expert_out_a[0])).astype(BF16)
+    grad_rows = (
+        keep_rows(matmul_nt(grad_pre_a, expert_in_a[0]))
+        + grad_middle[:half_rows]
+        + grad_logit_half[:, None] * centre.astype(F32)[None, :]
+    )
+    grad_back = to_experts(grad_rows.astype(BF16).reshape(experts, slots_per, width)).reshape(
+        half_rows, width
+    )
+    grad_out_b = matmul_tn(act_b, grad_b)
+    grad_in_b = matmul_tn(middle, grad_pre_b)
+    grad_out_a = matmul_tn(act_a, grad_a)
+    grad_in_a = matmul_tn(expert_rows, grad_pre_a)
+    grad_two = grad_out.astype(F32) + matmul(placer, grad_back)
+
+    rows_down = with_other(grad_two.astype(BF16))
+    grad_ffn_pre = gelu_grad(ffn_pre.astype(F32), matmul(rows_down, ffn_out_t)).astype(BF16)
+    grad_ffn_out_t = matmul_tn(rows_down, ffn_act)
+    grad_ffn_in = matmul_tn(rows_two, grad_ffn_pre)
+    grad_norm_two = keep_rows(matmul_nt(grad_ffn_pre, ffn_in))
+    back_two, grad_gain_two = norm_backward(grad_norm_two, hat_two, inv_two, gain_two)
+    grad_one = grad_two + back_two
+
+    grad_branch_one = grad_one.astype(BF16)
+    grad_attn_t = lax.dot_general(
+        attn_out_t, grad_branch_one, (((0,), (1,)), ((), ())), preferred_element_type=F32
+    ).astype(BF16)
+    grad_by_head = lax.all_to_all(
+        grad_attn_t.reshape(heads, HEAD, rows), "dp", split_axis=0, concat_axis=0, tiled=True
+    )
+    grad_attn_out = lax.dot_general(
+        grad_branch_one, attn_t, (((0,), (1,)), ((), ())), preferred_element_type=F32
+    )
+    half_width = width // 2
+    part_own, part_other = both(grad_attn_out[:, :half_width], grad_attn_out[:, half_width:])
+    grad_attn_half = part_own + swap(part_other.astype(BF16)).astype(F32)
+    second_sum = lax.psum_scatter(
+        jnp.concatenate(
+            [grad_ffn_in.astype(BF16), grad_ffn_out_t.astype(BF16), grad_attn_half.astype(BF16)], 1
+        ),
+        "dp",
+        scatter_dimension=0,
+        tiled=True,
+    ).astype(F32)
+    grad_blocks = jnp.concatenate([grad_by_head, to_core_zero(grad_by_head[:lent])], 0)
+    grad_own_blocks, grad_prompts = attn_backward(
+        plan, own_blocks, prompt_kv, grad_blocks, attn_blocks, log_sums
+    )
+    lent_grad = to_core_one(grad_own_blocks[experts:])
+    prompt_sum = grad_prompts.astype(F32) + to_core_zero(grad_prompts).astype(F32)
+    prompt_part = jnp.concatenate(
+        [
+            grad_own_blocks[:experts, :HEAD],
+            (grad_own_blocks[:experts, HEAD:].astype(F32) + prompt_sum).astype(BF16),
+        ],
+        1,
+    )
+    cont_part = jnp.concatenate([lent_grad, grad_own_blocks[lent:experts]], 0)
+    grad_qkv = lax.all_to_all(
+        jnp.where(core_zero, prompt_part, cont_part), "dp", split_axis=0, concat_axis=0, tiled=True
+    ).reshape(2, half_heads * triple, rows)
+    keep_half, send_half = both(grad_qkv[0], grad_qkv[1])
+    grad_qkv_t = jnp.concatenate([keep_half, swap(send_half)], 1)
+    grad_qkv_w = lax.dot_general(
+        rows_one, grad_qkv_t, (((0,), (1,)), ((), ())), preferred_element_type=F32
+    )
+    grad_norm_one = keep_rows(
+        lax.dot_general(
+            grad_qkv_t, qkv_full, (((0,), (1,)), ((), ())), preferred_element_type=F32
+        )
+    )
+    back_one, grad_gain_one = norm_backward(grad_norm_one, hat_one, inv_one, gain_one)
+    grad_input = grad_one + back_one
+
+    gains = jnp.stack([grad_gain_one, grad_gain_two], 0)
+    gains = (gains + swap(gains)).reshape(2, experts, shard).transpose(1, 0, 2).reshape(experts, 1, 2 * shard)
+    gains = jnp.pad(gains.astype(BF16), ((0, 0), (0, 7), (0, half_heads * triple - 2 * shard)))
+    first_sum = lax.psum_scatter(
+        jnp.concatenate([grad_qkv_w.astype(BF16).reshape(experts, shard, -1), gains], 1),
+        "dp",
+        scatter_dimension=0,
+        tiled=False,
+    ).astype(F32)
+    qkv_sum = first_sum[:shard].reshape(shard, half_heads, 3, HEAD)
+    query_shard, key_shard, value_shard = (
+        qkv_sum[:, :, part].reshape(shard, half_heads * HEAD) for part in range(3)
+    )
+    centre_grad = centre_part + swap(centre_part)
+    return (
+        output.astype(BF16),
+        grad_input.astype(BF16),
+        first_sum[shard, :shard],
+        query_shard,
+        key_shard,
+        value_shard,
+        second_sum[:, 2 * hidden :].T,
+        first_sum[shard, shard : 2 * shard],
+        second_sum[:, :hidden],
+        second_sum[:, hidden : 2 * hidden].T,
+        centre_grad[None, :],
+        grad_in_a[None],
+        grad_out_a[None],
+        grad_in_b[None],
+        grad_out_b[None],
+    )
+
+
 def solution(mesh):
+    body = body_paired if fits_paired(mesh) else body_general
     return jax.shard_map(
         body,
         mesh=mesh,

time: 3120 us -> 1120 us (0.36)
  waiting for transfers between devices: 1750 us -> 213 us
  matrix products: 735 us -> 236 us
  other arithmetic: 250 us -> 68.3 us
  Pallas kernels: 0 us -> 167 us
  blocking collectives: 236 us -> 322 us
  local copies, waits for them, and re-layouts: 93.9 us -> 38.8 us
  starting transfers between devices: 12.7 us -> 49.6 us
    reduce_scatter x14 -> x2, waiting for transfers between devices: 1230 us -> 70.1 us  [the longest x1 70.1 us: body_paired(): lax.psum_scatter(jnp.concatenate([grad_qkv_w.astype(BF16).reshape(experts...]
    all_gather x14 -> x2, waiting for transfers between devices: 499 us -> 65.2 us  [the longest x1 65.1 us: body_paired(): first_all = lax.all_gather(jnp.concatenate([qkv_shard, extra], 0), 'dp')]
    dot_general x58 -> x6, matrix products: 326 us -> 66.6 us  [matmul_nt(): lax.dot_general(left, right, (((1,), (1,)), ((), ())), preferred_element_...]
    all_to_all x0 -> x2, blocking collectives: none -> 239 us  [the longest x1 127 us: body_paired(): lax.all_to_all(qkv_t, 'dp', split_axis=0, concat_axis=0, tiled=True)]
    pallas_call x0 -> x2, Pallas kernels: none -> 167 us  [the longest x1 93.7 us: attn_backward(): pl.pallas_call(functools.partial(attn_bwd_kernel, head=head, factor=head...]
    convert_element_type x30 -> x16, other arithmetic: 176 us -> 25 us  [the longest x1 7.76 us: body_paired(): grad_a = (grad_branch + grad_middle).astype(BF16)]
    dot_general x44 -> x8, matrix products: 219 us -> 75.9 us  [matmul_tn(): lax.dot_general(left, right, (((0,), (0,)), ((), ())), preferred_element_...]
    dot_general x46 -> x11, matrix products: 190 us -> 72.6 us  [matmul(): return jnp.dot(left, right, preferred_element_type=jnp.float32)]
  transfers between devices with their start and end apart: 31 -> 33, of which waited for: 24 -> 16; matrix products, arithmetic and copies ran while one was open for 13% -> 22% of each run, Pallas kernels for 0% -> 15%
where the time goes in v1:
time: 1120 us; the launch traced here: 1110 us
  blocking collectives  322 us (29%)
  matrix products  236 us (21%)
  waiting for transfers between devices  213 us (19%)
  Pallas kernels  167 us (15%)
  other arithmetic  68.3 us (6%)
  starting transfers between devices  49.6 us (4%)
  local copies, waits for them, and re-layouts  38.8 us (3%)
  between operations  15.5 us (1%)
    all_to_all x1, blocking collectives, body_paired(): lax.all_to_all(qkv_t, 'dp', split_axis=0, concat_axis=0, tiled=True)  127 us
    all_to_all x1, blocking collectives, body_paired(): lax.all_to_all(jnp.where(core_zero, prompt_part, cont_part), 'dp', split_...  112 us
    pallas_call x1, Pallas kernels, attn_backward(): pl.pallas_call(functools.partial(attn_bwd_kernel, head=head, factor=head...  93.7 us
    all_to_all x2, blocking collectives, to_experts(): return lax.all_to_all(value, 'dp', split_axis=0, concat_axis=0, tiled=True)  83 us
    dot_general x8, matrix products, matmul_tn(): lax.dot_general(left, right, (((0,), (0,)), ((), ())), preferred_element_...  75.9 us
    pallas_call x1, Pallas kernels, attn_forward(): pl.pallas_call(functools.partial(attn_fwd_kernel, head=head, factor=head...  73.3 us
    dot_general x11, matrix products, matmul(): return jnp.dot(left, right, preferred_element_type=jnp.float32)  72.6 us
    reduce_scatter x1, waiting for transfers between devices, body_paired(): lax.psum_scatter(jnp.concatenate([grad_qkv_w.astype(BF16).reshape(experts...  70.1 us
  transfers between devices with their start and end apart: 33, of which 16 were waited for; matrix products, arithmetic and copies ran while one was open for 22% of the time, Pallas kernels for 15%

profile of v1, /device:TPU:9, one launch (start us, length us, event | category | flops | bytes accessed | tf_op | source)
XLA Modules:
  0.0 1110.0 jit_solution(2595394129274477858)
XLA Ops:
  20.7 65.1 %all-gather.6.cloned.1.call-done = bf16[1152,1536]{1,0:T(8,128)(2,1)} async-done(((bf16[72,1536]{1,0:T(8,128)(2,1)}), bf16[1152,1536]{1,0:T(8,128)(2,1)}) %all-gather.6.cloned.1.call-update) | async-done | bytes 3538960 | tf_op jit(solution)/shard_map/all_gather | solution.py:656
  85.9 3.8 slice.239
  102.7 126.8 %all_to_all.40 = bf16[16,192,512]{2,1,0:T(8,128)(2,1)S(1)} all-to-all(bf16[16,192,512]{2,1,0:T(8,128)(2,1)S(1)} %bitcast.101), channel_id=1, replica_groups=mesh['dp'=16,'tensor'=2] {'dp'}, dimensions={0} | all-to-all | bytes 6291456 | tf_op jit(solution)/shard_map/all_to_all | solution.py:704
  231.0 3.3 collective-permute-start.3
  236.5 73.3 %attn_fwd.1 = (bf16[20,64,512]{2,1,0:T(8,128)(2,1)S(1)}, f32[20,1,512]{2,1,0:T(1,128)S(1)}) custom-call(s32[4,20]{1,0:T(4,128)S(1)} %add_select_fusion.2.plan, bf16[20,192,512]{2,1,0:T(8,128)(2,1)S(1)} %constant_dynamic-update-slice_fusion.own, bf16[16,128,512]{2,1,0:T(8,128)(2,1)S(1)} %broadcast_select_fusion.prompts), custom_call_target="tpu_custom_call" | custom-call | flops 26843545600 | bytes 8388608 | tf_op jit(solution)/shard_map/attn_fwd/pallas_call | solution.py:522
  314.4 6.4 all-to-all-start.1
  328.2 17.0 %all-to-all-done.1 = bf16[16,64,512]{2,1,0:T(8,128)(2,1)S(1)} async-done(((bf16[16,64,512]{2,1,0:T(8,128)(2,1)}), bf16[16,64,512]{2,1,0:T(8,128)(2,1)S(1)}, u32[]{:S(2)}, u32[]{:S(2)}) %all-to-all-start.1) | async-done | bytes 1048608 | tf_op jit(solution)/shard_map/all_to_all | solution.py:734
  345.2 3.3 fusion.108
  354.9 7.8 convolution_convert_fusion.5
  362.8 9.1 fusion.51
  375.9 40.7 %all_to_all.41 = bf16[16,48,1024]{2,1,0:T(8,128)(2,1)S(1)} all-to-all(bf16[16,48,1024]{2,1,0:T(8,128)(2,1)S(1)} %bitcast.109), channel_id=1, replica_groups=mesh['dp'=16,'tensor'=2] {'dp'}, dimensions={0} | all-to-all | bytes 3145728 | tf_op jit(solution)/shard_map/all_to_all | solution.py:51
  421.0 4.8 all-to-all-start.4
  425.8 11.2 %convolution_convert_fusion.1 = bf16[1536,2048]{1,0:T(8,128)(2,1)S(1)} fusion(bf16[1,1024,2048]{2,1,0:T(8,128)(2,1)} %param.29, bf16[768,1024]{1,0:T(8,128)(2,1)S(1)} %collective-permute-done.9, bf16[768,1024]{1,0:T(8,128)(2,1)S(1)} %bitcast.103), kind=kOutput, calls=%fused_computation.47 | convolution fusion | flops 6451888128 | bytes 13631488 | tf_op jit(solution)/shard_map/dot_general | solution.py:55
  437.1 10.4 fusion.109
  447.9 14.2 %all-to-all-done.4 = bf16[16,48,1024]{2,1,0:T(8,128)(2,1)} async-done(((bf16[16,48,1024]{2,1,0:T(8,128)(2,1)}), bf16[16,48,1024]{2,1,0:T(8,128)(2,1)}, u32[]{:S(2)}, u32[]{:S(2)}) %all-to-all-start.4) | async-done | bytes 1572896 | tf_op jit(solution)/shard_map/all_to_all | solution.py:51
  470.4 6.0 maximum_add_fusion
  476.5 14.6 %convolution_convert_fusion = bf16[1536,2048]{1,0:T(8,128)(2,1)} fusion(bf16[1,1024,2048]{2,1,0:T(8,128)(2,1)} %param.31, f32[1536,1024]{1,0:T(8,128)S(1)} %maximum_add_fusion, bf16[768,1024]{1,0:T(8,128)(2,1)S(1)} %copy-done.65, bf16[768,1024]{1,0:T(8,128)(2,1)S(1)} %bitcast.105), kind=kOutput, calls=%fused_computation.46 | convolution fusion | flops 6455033856 | bytes 19922944 | tf_op jit(solution)/shard_map/dot_general | solution.py:55
  491.1 19.3 %fusion.4 = bf16[1536,2048]{1,0:T(8,128)(2,1)} fusion(bf16[1536,2048]{1,0:T(8,128)(2,1)} %convolution_convert_fusion, bf16[1,2048,1024]{2,1,0:T(8,128)(2,1)S(1)} %copy-done.61, f32[1536]{0:T(1024)S(1)} %add_divide_fusion, bf16[768,1024]{1,0:T(8,128)(2,1)} %collective-permute-done.12, bf16[768,1024]{1,0:T(8,128)(2,1)} %bitcast.21, ...), kind=kOutput, calls=%fused_computation.19 | convolution fusion | flops 6519521280 | bytes 19930624 | tf_op jit(solution)/shard_map/dot_general | solution.py:65
  510.4 8.8 fusion.110
  519.3 10.0 fusion.33
  531.9 7.8 add_convert_fusion
  539.7 18.1 %fusion.7 = bf16[1536,2048]{1,0:T(8,128)(2,1)S(1)} fusion(bf16[1536,2048]{1,0:T(8,128)(2,1)} %copy-done.79, bf16[1536,1024]{1,0:T(8,128)(2,1)S(1)} %get-tuple-element.38, bf16[1,2048,1024]{2,1,0:T(8,128)(2,1)} %param.30), kind=kOutput, calls=%fused_computation.22 | convolution fusion | flops 6508511232 | bytes 19922944 | tf_op jit(solution)/shard_map/dot_general | solution.py:65
  557.8 6.8 fusion.46
  568.2 6.0 fusion.59
  578.0 42.2 %all_to_all.42 = bf16[16,48,1024]{2,1,0:T(8,128)(2,1)S(1)} all-to-all(bf16[16,48,1024]{2,1,0:T(8,128)(2,1)S(1)} %bitcast.110), channel_id=1, replica_groups=mesh['dp'=16,'tensor'=2] {'dp'}, dimensions={0} | all-to-all | bytes 3145728 | tf_op jit(solution)/shard_map/all_to_all | solution.py:51
  626.4 9.5 fusion.23
  636.0 4.5 fusion.55
  648.2 3.3 fusion.74
  651.6 4.0 all-to-all-start.6
  659.2 10.1 convolution_convert_fusion.3
  669.3 6.3 convolution_convert_fusion.4
  676.2 3.6 all-to-all-done.6
  679.8 4.3 collective-permute-start.17
  684.2 8.9 pad_maximum_fusion
  694.4 93.7 %attn_bwd.1 = (bf16[20,192,512]{2,1,0:T(8,128)(2,1)}, bf16[16,128,512]{2,1,0:T(8,128)(2,1)S(1)}) custom-call(s32[4,20]{1,0:T(4,128)S(1)} %copy-done.5, bf16[20,192,512]{2,1,0:T(8,128)(2,1)} %copy-done, bf16[16,128,512]{2,1,0:T(8,128)(2,1)} %copy-done.1, bf16[20,64,512]{2,1,0:T(8,128)(2,1)S(1)} %pad_maximum_fusion.18.grad, ...), custom_call_target="tpu_custom_call" | custom-call | flops 67108864000 | bytes 16777216 | tf_op jit(solution)/shard_map/attn_bwd/pallas_call | solution.py:548
  798.1 112.3 %all_to_all.43 = bf16[16,192,512]{2,1,0:T(8,128)(2,1)S(1)} all-to-all(bf16[16,192,512]{2,1,0:T(8,128)(2,1)S(1)} %maximum_select_fusion), channel_id=1, replica_groups=mesh['dp'=16,'tensor'=2] {'dp'}, dimensions={0} | all-to-all | bytes 6291456 | tf_op jit(solution)/shard_map/all_to_all | solution.py:836
  914.7 3.5 fusion.64
  918.8 17.8 %convolution_bitcast_fusion = f32[1,2048,1024]{2,1,0:T(8,128)} fusion(f32[1536]{0:T(1024)S(1)} %copy-done.41, bf16[1536,2048]{1,0:T(8,128)(2,1)S(1)} %bitcast.146, bf16[768,1024]{1,0:T(8,128)(2,1)} %collective-permute-done.12, bf16[768,1024]{1,0:T(8,128)(2,1)} %bitcast.21, pred[1536]{0:T(1024)(128)(4,1)S(1)} %copy-done.57), kind=kOutput, calls=%fused_computation.56 | convolution fusion | flops 6484918272 | bytes 17833472 | tf_op jit(solution)/shard_map/dot_general | solution.py:59
  938.2 4.9 convolution_convert_fusion.2
  943.2 4.1 fusion.58
  947.4 13.3 %convolution_bitcast_fusion.1 = f32[1,1024,2048]{2,1,0:T(8,128)} fusion(bf16[1536,2048]{1,0:T(8,128)(2,1)} %fusion.4, f32[1536,1024]{1,0:T(8,128)} %copy-done.15, bf16[768,1024]{1,0:T(8,128)(2,1)} %copy-done.64, bf16[768,1024]{1,0:T(8,128)(2,1)S(1)} %bitcast.106), kind=kOutput, calls=%fused_computation.57 | convolution fusion | flops 6451888128 | bytes 24117248 | tf_op jit(solution)/shard_map/dot_general | solution.py:59
  960.7 4.5 all-to-all-start.3
  965.2 13.9 %convolution_bitcast_fusion.2 = f32[1,2048,1024]{2,1,0:T(8,128)} fusion(bf16[1536,1024]{1,0:T(8,128)(2,1)} %copy-done.27, bf16[1536,2048]{1,0:T(8,128)(2,1)} %copy-done.79), kind=kOutput, calls=%fused_computation.58 | convolution fusion | flops 6473908224 | bytes 17825792 | tf_op jit(solution)/shard_map/dot_general | solution.py:59
  979.9 11.3 %convolution_bitcast_fusion.3 = f32[1,1024,2048]{2,1,0:T(8,128)} fusion(bf16[1536,2048]{1,0:T(8,128)(2,1)} %copy-done.74, bf16[768,1024]{1,0:T(8,128)(2,1)S(1)} %copy-done.66, bf16[768,1024]{1,0:T(8,128)(2,1)S(1)} %bitcast.108), kind=kOutput, calls=%fused_computation.59 | convolution fusion | flops 6448742400 | bytes 17825792 | tf_op jit(solution)/shard_map/dot_general | solution.py:59
  991.8 21.4 %all-to-all-done.3 = bf16[16,48,1024]{2,1,0:T(8,128)(2,1)} async-done(((bf16[16,48,1024]{2,1,0:T(8,128)(2,1)}), bf16[16,48,1024]{2,1,0:T(8,128)(2,1)}, u32[]{:S(2)}, u32[]{:S(2)}) %all-to-all-start.3) | async-done | bytes 1572896 | tf_op jit(solution)/shard_map/all_to_all | solution.py:51
  1013.2 4.6 add_convert_fusion.5
  1017.8 3.2 add_convert_fusion.4
  1025.4 70.1 %reduce-scatter.3.cloned.1.call-done = bf16[1,72,1536]{2,1,0:T(8,128)(2,1)} async-done(((bf16[16,72,1536]{2,1,0:T(8,128)(2,1)}), bf16[1,72,1536]{2,1,0:T(8,128)(2,1)}) %reduce-scatter.3.cloned.1.call-update) | async-done | bytes 221200 | tf_op jit(solution)/shard_map/reduce_scatter | solution.py:855
  (354 shorter events, 124.5 us)
Async XLA Ops:
  7.2 78.7 %all-gather.6.cloned.1.call-start = ((), (), s32[]{:S(2)}) async-start(), calls=%async_computation.13 | async-start | bytes 3760128 | tf_op jit(solution)/shard_map/all_gather | solution.py:656
  8.1 5.3 collective-permute-start.1
  14.9 305.9 %all-gather.4.cloned.1.call-start = ((), (), s32[]{:S(2)}) async-start(), calls=%async_computation.10 | async-start | bytes 10027008 | tf_op jit(solution)/shard_map/all_gather | solution.py:661
  16.9 2.7 collective-permute-start
  20.7 73.0 %copy-start.52 = (f32[1024]{0:T(1024)}, f32[1024]{0:T(1024)S(1)}, u32[]{:S(2)}) copy-start(f32[1024]{0:T(1024)S(1)} %add_rsqrt_fusion) | copy-start | bytes 12292
  95.7 4.8 collective-permute-start.2
  102.6 128.3 %copy-start.73 = (s32[16]{0:T(128)S(1)}, s32[16]{0:T(128)}, u32[]{:S(2)}) copy-start(s32[16]{0:T(128)} %param.18) | copy-start | bytes 196
  229.6 6.6 collective-permute-start.4
  231.0 5.2 collective-permute-start.3
  236.3 73.6 %copy-start = (bf16[20,192,512]{2,1,0:T(8,128)(2,1)}, bf16[20,192,512]{2,1,0:T(8,128)(2,1)S(1)}, u32[]{:S(2)}) copy-start(bf16[20,192,512]{2,1,0:T(8,128)(2,1)S(1)} %constant_dynamic-update-slice_fusion.own) | copy-start | bytes 11796484
  236.5 73.3 %copy-start.1 = (bf16[16,128,512]{2,1,0:T(8,128)(2,1)}, bf16[16,128,512]{2,1,0:T(8,128)(2,1)S(1)}, u32[]{:S(2)}) copy-start(bf16[16,128,512]{2,1,0:T(8,128)(2,1)S(1)} %broadcast_select_fusion.prompts) | copy-start | bytes 6291460
  309.9 3.4 collective-permute-start.5
  314.4 30.7 %all-to-all-start.1 = ((bf16[16,64,512]{2,1,0:T(8,128)(2,1)}), bf16[16,64,512]{2,1,0:T(8,128)(2,1)S(1)}, u32[]{:S(2)}, u32[]{:S(2)}) async-start(bf16[16,64,512]{2,1,0:T(8,128)(2,1)} %pad_maximum_fusion.19), calls=%async_computation.1 | async-start | bytes 2097152 | tf_op jit(solution)/shard_map/all_to_all | solution.py:734
  323.1 3.3 collective-permute-start.6
  349.3 4.6 collective-permute-start.7
  372.1 2.7 collective-permute-start.8
  372.8 45.9 %copy-start.53 = (s32[512,1]{0,1:T(1,128)}, s32[512,1]{0,1:T(1,128)S(1)}, u32[]{:S(2)}) copy-start(s32[512,1]{0,1:T(1,128)S(1)} %multiply_add_fusion.1) | copy-start | bytes 6148
  374.8 41.9 %copy-start.33 = (bf16[512,1024]{1,0:T(8,128)(2,1)}, bf16[512,1024]{1,0:T(8,128)(2,1)S(1)}, u32[]{:S(2)}) copy-start(bf16[512,1024]{1,0:T(8,128)(2,1)S(1)} %collective-permute-done.8) | copy-start | bytes 3145732
  374.8 43.9 %copy-start.67 = (bf16[512,1024]{1,0:T(8,128)(2,1)S(1)}, bf16[512,1024]{1,0:T(8,128)(2,1)}, u32[]{:S(2)}) copy-start(bf16[512,1024]{1,0:T(8,128)(2,1)} %param.33) | copy-start | bytes 3145732
  416.7 9.1 collective-permute-start.9
  421.0 41.2 %all-to-all-start.4 = ((bf16[16,48,1024]{2,1,0:T(8,128)(2,1)}), bf16[16,48,1024]{2,1,0:T(8,128)(2,1)}, u32[]{:S(2)}, u32[]{:S(2)}) async-start(bf16[16,48,1024]{2,1,0:T(8,128)(2,1)} %bitcast.20), calls=%async_computation.4 | async-start | bytes 3145728 | tf_op jit(solution)/shard_map/all_to_all | solution.py:51
  447.5 20.5 %collective-permute-start.10 = (bf16[1536,1024]{1,0:T(8,128)(2,1)}, bf16[1536,1024]{1,0:T(8,128)(2,1)S(1)}, u32[]{:S(2)}, u32[]{:S(2)}) collective-permute-start(bf16[1536,1024]{1,0:T(8,128)(2,1)} %get-tuple-element.63), channel_id=1, source_target_pairs={{0,1},{1,0},{2,3},{3,2},{4,5},{5,4},{6,7},{7,6},{8,9},{9,8},{10,11... | collective-permute-start | bytes 9437192 | tf_op jit(solution)/shard_map/ppermute | solution.py:574
  462.2 28.9 %collective-permute-start.12 = (bf16[768,1024]{1,0:T(8,128)(2,1)}, bf16[768,1024]{1,0:T(8,128)(2,1)}, u32[]{:S(2)}, u32[]{:S(2)}) collective-permute-start(bf16[768,1024]{1,0:T(8,128)(2,1)} %bitcast.21), channel_id=1, source_target_pairs={{0,1},{1,0},{2,3},{3,2},{4,5},{5,4},{6,7},{7,6},{8,9},{9,8},{10,11... | collective-permute-start | bytes 4718600 | tf_op jit(solution)/shard_map/ppermute | solution.py:574
  465.1 66.8 %copy-start.56 = (pred[1536]{0:T(1024)(128)(4,1)}, pred[1536]{0:T(1024)(128)(4,1)S(1)}, u32[]{:S(2)}) copy-start(pred[1536]{0:T(1024)(128)(4,1)S(1)} %add_reduce_fusion) | copy-start | bytes 4612
  468.0 106.2 %copy-start.40 = (f32[1536]{0:T(1024)}, f32[1536]{0:T(1024)S(1)}, u32[]{:S(2)}) copy-start(f32[1536]{0:T(1024)S(1)} %add_divide_fusion) | copy-start | bytes 18436
  519.2 10.9 collective-permute-start.13
  529.5 38.6 %collective-permute-start.11 = (bf16[768,1024]{1,0:T(8,128)(2,1)S(1)}, bf16[768,1024]{1,0:T(8,128)(2,1)}, u32[]{:S(2)}, u32[]{:S(2)}) collective-permute-start(bf16[768,1024]{1,0:T(8,128)(2,1)S(1)} %slice.392), channel_id=1, source_target_pairs={{0,1},{1,0},{2,3},{3,2},{4,5},{5,4},{6,7},{7,6},{8,9},{9,8},{10,11... | collective-permute-start | bytes 4718600 | tf_op jit(solution)/shard_map/ppermute | solution.py:574
  567.5 6.7 collective-permute-start.14
  574.7 45.4 %copy-start.54 = (s32[512,1]{0,1:T(1,128)S(1)}, s32[512,1]{0,1:T(1,128)}, u32[]{:S(2)}) copy-start(s32[512,1]{0,1:T(1,128)} %copy-done.53) | copy-start | bytes 6148
  574.7 45.4 %copy-start.68 = (bf16[512,1024]{1,0:T(8,128)(2,1)S(1)}, bf16[512,1024]{1,0:T(8,128)(2,1)}, u32[]{:S(2)}) copy-start(bf16[512,1024]{1,0:T(8,128)(2,1)} %param.33) | copy-start | bytes 3145732
  574.7 51.6 %slice-start = ((s8[9437184]{0:T(1024)(128)(4,1)}), s8[4194304]{0:T(1024)(128)(4,1)S(1)}, s32[]{:S(2)}) async-start(s8[9437184]{0:T(1024)(128)(4,1)} %bitcast.124), calls=%async_computation.14 | async-start | bytes 8388608
  574.7 51.6 %slice-start.1 = ((s8[9437184]{0:T(1024)(128)(4,1)}), s8[4194304]{0:T(1024)(128)(4,1)S(1)}, s32[]{:S(2)}) async-start(s8[9437184]{0:T(1024)(128)(4,1)} %bitcast.124), calls=%async_computation.15 | async-start | bytes 8388608
  577.9 48.4 %slice-start.2 = ((s8[9437184]{0:T(1024)(128)(4,1)}), s8[1048576]{0:T(1024)(128)(4,1)S(1)}, s32[]{:S(2)}) async-start(s8[9437184]{0:T(1024)(128)(4,1)} %bitcast.124), calls=%async_computation.16 | async-start | bytes 2097152
  577.9 48.4 %copy-start.78 = (bf16[1024,2048]{1,0:T(8,128)(2,1)S(1)}, bf16[1024,2048]{1,0:T(8,128)(2,1)}, u32[]{:S(2)}) copy-start(bf16[1024,2048]{1,0:T(8,128)(2,1)} %copy-done.77) | copy-start | bytes 12582916
  621.2 4.1 collective-permute-start.15
  640.7 2.7 collective-permute-start.16
  651.6 28.3 %all-to-all-start.6 = ((bf16[16,64,512]{2,1,0:T(8,128)(2,1)}), bf16[16,64,512]{2,1,0:T(8,128)(2,1)S(1)}, u32[]{:S(2)}, u32[]{:S(2)}) async-start(bf16[16,64,512]{2,1,0:T(8,128)(2,1)} %bitcast.24), calls=%async_computation.6 | async-start | bytes 2097152 | tf_op jit(solution)/shard_map/all_to_all | solution.py:805
  655.6 365.5 %reduce-scatter.5.cloned.1.call-start = ((), (), s32[]{:S(2)}) async-start(), calls=%async_computation.12 | async-start | bytes 10027008 | tf_op jit(solution)/shard_map/reduce_scatter | solution.py:814
  658.2 17.3 %collective-permute-start.23 = (bf16[1024,512]{1,0:T(8,128)(2,1)S(1)}, bf16[1024,512]{1,0:T(8,128)(2,1)S(1)}, u32[]{:S(2)}, u32[]{:S(2)}) collective-permute-start(bf16[1024,512]{1,0:T(8,128)(2,1)S(1)} %select_convert_fusion.1), channel_id=1, source_target_pairs={{0,1},{1,0},{2,3},{3,2},{4,5},{5,4},{6,7},{7,6},{8,9},{9,8},{10,11... | collective-permute-start | bytes 3145736 | tf_op jit(solution)/shard_map/ppermute | solution.py:574
  679.8 13.3 %collective-permute-start.17 = (bf16[4,64,512]{2,1,0:T(8,128)(2,1)S(1)}, bf16[4,64,512]{2,1,0:T(8,128)(2,1)S(1)}, u32[]{:S(2)}, u32[]{:S(2)}) collective-permute-start(bf16[4,64,512]{2,1,0:T(8,128)(2,1)S(1)} %slice.267), channel_id=1, source_target_pairs={{1,0},{3,2},{5,4},{7,6},{9,8},{11,10},{13,12},{15,14},{17,16},{19,... | collective-permute-start | bytes 786440 | tf_op jit(solution)/shard_map/ppermute | solution.py:582
  693.1 402.4 %reduce-scatter.3.cloned.1.call-start = ((), (), s32[]{:S(2)}) async-start(), calls=%async_computation.11 | async-start | bytes 3760128 | tf_op jit(solution)/shard_map/reduce_scatter | solution.py:855
  788.1 7.8 collective-permute-start.18
  791.3 5.6 collective-permute-start.19
  910.6 4.1 collective-permute-start.20
  918.4 18.2 %collective-permute-start.21 = (bf16[512,1024]{1,0:T(8,128)(2,1)S(1)}, bf16[512,1024]{1,0:T(8,128)(2,1)S(1)}, u32[]{:S(2)}, u32[]{:S(2)}) collective-permute-start(bf16[512,1024]{1,0:T(8,128)(2,1)S(1)} %slice.393), channel_id=1, source_target_pairs={{0,1},{1,0},{2,3},{3,2},{4,5},{5,4},{6,7},{7,6},{8,9},{9,8},{10,11... | collective-permute-start | bytes 3145736 | tf_op jit(solution)/shard_map/ppermute | solution.py:574
  937.4 5.7 collective-permute-start.22
  960.7 52.5 %all-to-all-start.3 = ((bf16[16,48,1024]{2,1,0:T(8,128)(2,1)}), bf16[16,48,1024]{2,1,0:T(8,128)(2,1)}, u32[]{:S(2)}, u32[]{:S(2)}) async-start(bf16[16,48,1024]{2,1,0:T(8,128)(2,1)} %bitcast.18), calls=%async_computation.3 | async-start | bytes 3145728 | tf_op jit(solution)/shard_map/all_to_all | solution.py:51
  979.4 11.8 %collective-permute-start.24 = (f32[1024]{0:T(1024)S(1)}, f32[1024]{0:T(1024)S(1)}, u32[]{:S(2)}, u32[]{:S(2)}) collective-permute-start(f32[1024]{0:T(1024)S(1)} %bitcast.133), channel_id=1, source_target_pairs={{0,1},{1,0},{2,3},{3,2},{4,5},{5,4},{6,7},{7,6},{8,9},{9,8},{10,11... | collective-permute-start | bytes 12296 | tf_op jit(solution)/shard_map/ppermute | solution.py:574
  (71 other events, 694.0 us)
Sparse Core Ops, SparseCore 0:
  15.1 70.7 all-gather.5
  89.3 165.7 all-gather.3
  693.2 210.0 reduce-scatter.4
  947.5 147.9 reduce-scatter.2

commit v2 on v1

--- a/solution.py
+++ b/solution.py
@@ -654,19 +654,14 @@
     extra = jnp.concatenate([norm1_gain, norm2_gain, counts_pair], 0)
     extra = jnp.pad(extra[None, :], ((0, 7), (0, half_heads * triple - extra.shape[0])))
     first_all = lax.all_gather(jnp.concatenate([qkv_shard, extra], 0), "dp")
+    sent_grad = matmul_tn(placer, grad_out).astype(BF16).reshape(experts, slots_per, width)
+    grad_own, first_all = lax.optimization_barrier((to_experts(sent_grad), first_all))
+    grad_own = grad_own.reshape(-1, width)
+
     qkv_full = first_all[:, :shard].reshape(width, half_heads * triple)
     gain_one = first_all[:, shard, :shard].reshape(width).astype(F32)
     gain_two = first_all[:, shard, shard : 2 * shard].reshape(width).astype(F32)
     counts_all = first_all[:, shard, 2 * shard : 2 * shard + 2 * experts].reshape(experts, 2, experts)
-    second_all = lax.all_gather(
-        jnp.concatenate([w_ffn_in, w_ffn_out.T, w_attn_out.T], 1), "dp", axis=0, tiled=True
-    )
-    ffn_in = second_all[:, :hidden]
-    ffn_out_t = second_all[:, hidden : 2 * hidden]
-    attn_half = second_all[:, 2 * hidden :]
-
-    sent_grad = matmul_tn(placer, grad_out).astype(BF16).reshape(experts, slots_per, width)
-    grad_own = to_experts(sent_grad).reshape(-1, width)
 
     mine = jnp.sum(
         jnp.where(lax.broadcasted_iota(jnp.int32, (1, 1, experts), 2) == dp_index, counts_all.astype(F32), 0.0),
@@ -702,6 +697,16 @@
     ).astype(BF16)
     qkv_t = jnp.concatenate(both(own_t, swap(other_t)), 0).reshape(heads, triple, rows)
     by_head = lax.all_to_all(qkv_t, "dp", split_axis=0, concat_axis=0, tiled=True)
+
+    second_shard = jnp.concatenate([w_ffn_in, w_ffn_out.T, w_attn_out.T], 1)
+    by_head, second_shard = lax.optimization_barrier((by_head, second_shard))
+    second_all = lax.all_gather(
+        second_shard, "dp", axis=0, tiled=True
+    )
+    ffn_in = second_all[:, :hidden]
+    ffn_out_t = second_all[:, hidden : 2 * hidden]
+    attn_half = second_all[:, 2 * hidden :]
+
 
     lent = experts // 4
     span = PLEN // rows
@@ -748,7 +753,9 @@
     sent_rows = (
         matmul_tn(placer, hidden_two.astype(BF16)).astype(BF16).reshape(experts, slots_per, width)
     )
-    expert_rows = with_other(to_experts(sent_rows).reshape(-1, width))
+    own_rows, normed_own = lax.optimization_barrier((to_experts(sent_rows), rows_one[:rows]))
+    normed_all = lax.all_gather(normed_own, "dp")
+    expert_rows = with_other(own_rows.reshape(-1, width))
     centre = centroids[0]
     gate_value = jax.nn.sigmoid(matmul(expert_rows, centre))
     pre_a = matmul(expert_rows, expert_in_a[0]).astype(BF16)
@@ -765,7 +772,6 @@
         .reshape(experts, slots_per, width)
     )
     came_back = to_experts(returned).reshape(half_rows, width)
-    output = hidden_two + matmul(placer, came_back)
 
     grad_half = grad_returned[:half_rows]
     grad_logit_half = jnp.sum(grad_half * branch_half, 1) * gate_half * (1.0 - gate_half)
@@ -781,13 +787,17 @@
         + grad_middle[:half_rows]
         + grad_logit_half[:, None] * centre.astype(F32)[None, :]
     )
-    grad_back = to_experts(grad_rows.astype(BF16).reshape(experts, slots_per, width)).reshape(
-        half_rows, width
-    )
     grad_out_b = matmul_tn(act_b, grad_b)
     grad_in_b = matmul_tn(middle, grad_pre_b)
     grad_out_a = matmul_tn(act_a, grad_a)
     grad_in_a = matmul_tn(expert_rows, grad_pre_a)
+    grad_rows, came_back = lax.optimization_barrier((grad_rows.astype(BF16), came_back))
+    output = hidden_two + matmul(placer, came_back)
+    grad_back = to_experts(grad_rows.reshape(experts, slots_per, width))
+    grad_back, grad_out_b, grad_in_b, grad_out_a, grad_in_a = lax.optimization_barrier(
+        (grad_back, grad_out_b, grad_in_b, grad_out_a, grad_in_a)
+    )
+    grad_back = grad_back.reshape(half_rows, width)
     grad_two = grad_out.astype(F32) + matmul(placer, grad_back)
 
     rows_down = with_other(grad_two.astype(BF16))
@@ -795,7 +805,7 @@
     grad_ffn_out_t = matmul_tn(rows_down, ffn_act)
     grad_ffn_in = matmul_tn(rows_two, grad_ffn_pre)
     grad_norm_two = keep_rows(matmul_nt(grad_ffn_pre, ffn_in))
-    back_two, grad_gain_two = norm_backward(grad_norm_two, hat_two, inv_two, gain_two)
+    back_two = norm_backward(grad_norm_two, hat_two, inv_two, gain_two)[0]
     grad_one = grad_two + back_two
 
     grad_branch_one = grad_one.astype(BF16)
@@ -833,46 +843,52 @@
         1,
     )
     cont_part = jnp.concatenate([lent_grad, grad_own_blocks[lent:experts]], 0)
-    grad_qkv = lax.all_to_all(
-        jnp.where(core_zero, prompt_part, cont_part), "dp", split_axis=0, concat_axis=0, tiled=True
-    ).reshape(2, half_heads * triple, rows)
+    grad_head = jnp.where(core_zero, prompt_part, cont_part)
+    grad_qkv = lax.all_to_all(grad_head, "dp", split_axis=0, concat_axis=0, tiled=True)
+    grad_head_w = lax.dot_general(
+        normed_all, grad_head, (((0, 1), (0, 2)), ((), ())), preferred_element_type=F32
+    ).astype(BF16)
+    grad_head_w = (grad_head_w.astype(F32) + swap(grad_head_w).astype(F32)).astype(BF16)
+    grad_qkv, grad_head_w = lax.optimization_barrier((grad_qkv, grad_head_w))
+    by_row = lax.all_to_all(
+        grad_head_w.reshape(experts, shard, triple), "dp", split_axis=0, concat_axis=0, tiled=True
+    )
+    qkv_sum = jnp.where(core_zero, by_row[:half_heads], by_row[half_heads:]).astype(F32)
+    query_shard, key_shard, value_shard = (
+        qkv_sum[:, :, part * HEAD : (part + 1) * HEAD].transpose(1, 0, 2).reshape(shard, half_heads * HEAD)
+        for part in range(3)
+    )
+    grad_qkv = grad_qkv.reshape(2, half_heads * triple, rows)
     keep_half, send_half = both(grad_qkv[0], grad_qkv[1])
     grad_qkv_t = jnp.concatenate([keep_half, swap(send_half)], 1)
-    grad_qkv_w = lax.dot_general(
-        rows_one, grad_qkv_t, (((0,), (1,)), ((), ())), preferred_element_type=F32
-    )
     grad_norm_one = keep_rows(
         lax.dot_general(
             grad_qkv_t, qkv_full, (((0,), (1,)), ((), ())), preferred_element_type=F32
         )
     )
-    back_one, grad_gain_one = norm_backward(grad_norm_one, hat_one, inv_one, gain_one)
+    back_one = norm_backward(grad_norm_one, hat_one, inv_one, gain_one)[0]
     grad_input = grad_one + back_one
 
-    gains = jnp.stack([grad_gain_one, grad_gain_two], 0)
-    gains = (gains + swap(gains)).reshape(2, experts, shard).transpose(1, 0, 2).reshape(experts, 1, 2 * shard)
-    gains = jnp.pad(gains.astype(BF16), ((0, 0), (0, 7), (0, half_heads * triple - 2 * shard)))
-    first_sum = lax.psum_scatter(
-        jnp.concatenate([grad_qkv_w.astype(BF16).reshape(experts, shard, -1), gains], 1),
-        "dp",
-        scatter_dimension=0,
-        tiled=False,
-    ).astype(F32)
-    qkv_sum = first_sum[:shard].reshape(shard, half_heads, 3, HEAD)
-    query_shard, key_shard, value_shard = (
-        qkv_sum[:, :, part].reshape(shard, half_heads * HEAD) for part in range(3)
-    )
+    ffn_in_sum = second_sum[:, :hidden]
+    gains = jnp.stack(
+        [
+            jnp.sum(query_shard * w_query + key_shard * w_key + value_shard * w_value, 1)
+            / norm1_gain.astype(F32),
+            jnp.sum(ffn_in_sum * w_ffn_in, 1) / norm2_gain.astype(F32),
+        ]
+    )
+    gains = gains + swap(gains)
     centre_grad = centre_part + swap(centre_part)
     return (
         output.astype(BF16),
         grad_input.astype(BF16),
-        first_sum[shard, :shard],
+        gains[0],
         query_shard,
         key_shard,
         value_shard,
         second_sum[:, 2 * hidden :].T,
-        first_sum[shard, shard : 2 * shard],
-        second_sum[:, :hidden],
+        gains[1],
+        ffn_in_sum,
         second_sum[:, hidden : 2 * hidden].T,
         centre_grad[None, :],
         grad_in_a[None],

time: 1120 us -> 1060 us (0.946)
  blocking collectives: 322 us -> 0 us
  waiting for transfers between devices: 213 us -> 403 us
  starting transfers between devices: 49.6 us -> 92.2 us
  matrix products: 236 us -> 259 us
    all_to_all x4 -> x0, blocking collectives: 322 us -> none  [the longest x1 127 us: body_paired(): lax.all_to_all(qkv_t, 'dp', split_axis=0, concat_axis=0, tiled=True)]
    all_to_all x0 -> x3, waiting for transfers between devices: none -> 149 us  [the longest x1 83 us: body_paired(): lax.all_to_all(grad_head, 'dp', split_axis=0, concat_axis=0, tiled=True)]
    all_to_all x2 -> x4, waiting for transfers between devices: 35.6 us -> 146 us  [to_experts(): return lax.all_to_all(value, 'dp', split_axis=0, concat_axis=0, tiled=True)]
    reduce_scatter x1 -> x0, waiting for transfers between devices: 70.1 us -> none  [body_paired(): lax.psum_scatter(jnp.concatenate([grad_qkv_w.astype(BF16).reshape(experts...]
    all_gather x1 -> x2, waiting for transfers between devices: 0.02 us -> 49.3 us  [the longest x1 49.2 us: body_paired(): second_all = lax.all_gather(second_shard, 'dp', axis=0, tiled=True)]
    all_gather x1, waiting for transfers between devices: 65.1 us -> 28.5 us  [body_paired(): first_all = lax.all_gather(jnp.concatenate([qkv_shard, extra], 0), 'dp')]
    all_to_all x2 -> x4, starting transfers between devices: 9.28 us -> 26.9 us  [to_experts(): return lax.all_to_all(value, 'dp', split_axis=0, concat_axis=0, tiled=True)]
    all_to_all x1, waiting for transfers between devices: 17 us -> 0.01 us  [body_paired(): lax.all_to_all(attn_own, 'dp', split_axis=0, concat_axis=0, tiled=True)]
  transfers between devices with their start and end apart: 33 -> 39, of which waited for: 16 -> 21; matrix products, arithmetic and copies ran while one was open for 22% -> 28% of each run, Pallas kernels for 15% -> 16%
where the time goes in v2:
time: 1060 us; the launch traced here: 1050 us
  waiting for transfers between devices  403 us (38%)
  matrix products  259 us (24%)
  Pallas kernels  167 us (16%)
  starting transfers between devices  92.2 us (9%)
  other arithmetic  76.7 us (7%)
  local copies, waits for them, and re-layouts  40.5 us (4%)
  between operations  15.4 us (1%)
    all_to_all x4, waiting for transfers between devices, to_experts(): return lax.all_to_all(value, 'dp', split_axis=0, concat_axis=0, tiled=True)  146 us
    pallas_call x1, Pallas kernels, attn_backward(): pl.pallas_call(functools.partial(attn_bwd_kernel, head=head, factor=head...  93.8 us
    all_to_all x1, waiting for transfers between devices, body_paired(): lax.all_to_all(grad_head, 'dp', split_axis=0, concat_axis=0, tiled=True)  83 us
    dot_general x11, matrix products, matmul(): return jnp.dot(left, right, preferred_element_type=jnp.float32)  82.5 us
    dot_general x6, matrix products, matmul_nt(): lax.dot_general(left, right, (((1,), (1,)), ((), ())), preferred_element_...  73.6 us
    pallas_call x1, Pallas kernels, attn_forward(): pl.pallas_call(functools.partial(attn_fwd_kernel, head=head, factor=head...  73.3 us
    dot_general x8, matrix products, matmul_tn(): lax.dot_general(left, right, (((0,), (0,)), ((), ())), preferred_element_...  72.8 us
    all_to_all x1, waiting for transfers between devices, body_paired(): lax.all_to_all(qkv_t, 'dp', split_axis=0, concat_axis=0, tiled=True)  66.2 us
  transfers between devices with their start and end apart: 39, of which 21 were waited for; matrix products, arithmetic and copies ran while one was open for 28% of the time, Pallas kernels for 16%

profile of v2, /device:TPU:9, one launch (start us, length us, event | category | flops | bytes accessed | tf_op | source)
XLA Modules:
  0.0 1053.9 jit_solution(9726409252560234241)
XLA Ops:
  20.1 6.7 all-to-all-start
  30.8 44.5 %all-to-all-done = bf16[16,48,1024]{2,1,0:T(8,128)(2,1)} async-done(((bf16[16,48,1024]{2,1,0:T(8,128)(2,1)}), bf16[16,48,1024]{2,1,0:T(8,128)(2,1)}, u32[]{:S(2)}, u32[]{:S(2)}) %all-to-all-start) | async-done | bytes 1572896 | tf_op jit(solution)/shard_map/all_to_all | solution.py:51
  75.3 28.5 %all-gather.8.cloned.1.call-done = bf16[1152,1536]{1,0:T(8,128)(2,1)} async-done(((bf16[72,1536]{1,0:T(8,128)(2,1)}), bf16[1152,1536]{1,0:T(8,128)(2,1)}) %all-gather.8.cloned.1.call-update) | async-done | bytes 3538960 | tf_op jit(solution)/shard_map/all_gather | solution.py:656
  104.8 3.9 slice.188
  122.3 4.2 all-to-all-start.1
  128.4 66.2 %all-to-all-done.1 = bf16[16,192,512]{2,1,0:T(8,128)(2,1)S(1)} async-done(((bf16[16,192,512]{2,1,0:T(8,128)(2,1)}), bf16[16,192,512]{2,1,0:T(8,128)(2,1)S(1)}, u32[]{:S(2)}, u32[]{:S(2)}) %all-to-all-start.1) | async-done | bytes 3145760 | tf_op jit(solution)/shard_map/all_to_all | solution.py:699
  202.0 73.3 %attn_fwd.1 = (bf16[20,64,512]{2,1,0:T(8,128)(2,1)S(1)}, f32[20,1,512]{2,1,0:T(1,128)S(1)}) custom-call(s32[4,20]{1,0:T(4,128)S(1)} %add_select_fusion.2.plan, bf16[20,192,512]{2,1,0:T(8,128)(2,1)S(1)} %constant_dynamic-update-slice_fusion.own, bf16[16,128,512]{2,1,0:T(8,128)(2,1)S(1)} %broadcast_select_fusion.prompts), custom_call_target="tpu_custom_call" | custom-call | flops 26843545600 | bytes 8388608 | tf_op jit(solution)/shard_map/attn_fwd/pallas_call | solution.py:522
  280.2 7.6 all-to-all-start.2
  287.7 49.2 %all-gather.6.cloned.1.call-done = bf16[1024,4608]{1,0:T(8,128)(2,1)} async-done(((bf16[64,4608]{1,0:T(8,128)(2,1)}), bf16[1024,4608]{1,0:T(8,128)(2,1)}) %all-gather.6.cloned.1.call-update) | async-done | bytes 9437200 | tf_op jit(solution)/shard_map/all_gather | solution.py:703
  344.0 4.1 fusion.118
  351.6 8.1 convolution_convert_fusion.4
  359.8 9.1 fusion.50
  374.1 8.1 all-to-all-start.3
  384.5 33.3 %all-to-all-done.3 = bf16[16,48,1024]{2,1,0:T(8,128)(2,1)S(1)} async-done(((bf16[16,48,1024]{2,1,0:T(8,128)(2,1)}), bf16[16,48,1024]{2,1,0:T(8,128)(2,1)S(1)}, u32[]{:S(2)}, u32[]{:S(2)}) %all-to-all-start.3) | async-done | bytes 1572896 | tf_op jit(solution)/shard_map/all_to_all | solution.py:51
  423.3 19.0 %convolution_convert_fusion.1 = bf16[1536,2048]{1,0:T(8,128)(2,1)S(1)} fusion(bf16[1,1024,2048]{2,1,0:T(8,128)(2,1)} %param.29, bf16[768,1024]{1,0:T(8,128)(2,1)S(1)} %collective-permute-done.9, bf16[768,1024]{1,0:T(8,128)(2,1)S(1)} %bitcast.112), kind=kOutput, calls=%fused_computation.47 | convolution fusion | flops 6451888128 | bytes 13631488 | tf_op jit(solution)/shard_map/dot_general | solution.py:55
  442.4 10.4 fusion.119
  461.2 6.8 maximum_add_fusion
  468.1 14.6 %convolution_convert_fusion = bf16[1536,2048]{1,0:T(8,128)(2,1)} fusion(bf16[1,1024,2048]{2,1,0:T(8,128)(2,1)} %param.31, f32[1536,1024]{1,0:T(8,128)S(1)} %maximum_add_fusion, bf16[768,1024]{1,0:T(8,128)(2,1)S(1)} %copy-done.67, bf16[768,1024]{1,0:T(8,128)(2,1)S(1)} %bitcast.114), kind=kOutput, calls=%fused_computation.46 | convolution fusion | flops 6455033856 | bytes 19922944 | tf_op jit(solution)/shard_map/dot_general | solution.py:55
  482.7 19.0 %fusion.4 = bf16[1536,2048]{1,0:T(8,128)(2,1)} fusion(bf16[1536,2048]{1,0:T(8,128)(2,1)} %convolution_convert_fusion, bf16[1,2048,1024]{2,1,0:T(8,128)(2,1)S(1)} %copy-done.63, f32[1536]{0:T(1024)S(1)} %add_divide_fusion, bf16[768,1024]{1,0:T(8,128)(2,1)} %collective-permute-done.10, bf16[768,1024]{1,0:T(8,128)(2,1)} %bitcast.15, ...), kind=kOutput, calls=%fused_computation.19 | convolution fusion | flops 6519521280 | bytes 19930624 | tf_op jit(solution)/shard_map/dot_general | solution.py:65
  501.7 10.5 fusion.120
  512.6 10.4 fusion.42
  527.2 17.7 %fusion.109 = f32[2048,1024]{1,0:T(8,128)} fusion(f32[1536]{0:T(1024)S(1)} %add_divide_fusion, bf16[1536,2048]{1,0:T(8,128)(2,1)} %convolution_convert_fusion, bf16[768,1024]{1,0:T(8,128)(2,1)} %collective-permute-done.10, bf16[768,1024]{1,0:T(8,128)(2,1)} %bitcast.15, pred[1536]{0:T(1024)(128)(4,1)S(1)} %add_reduce_fusion.1), kind=kOutput, calls=%fused_computation.245 | convolution fusion | flops 6484918272 | bytes 17833472 | tf_op jit(solution)/shard_map/dot_general | solution.py:59
  547.1 9.4 add_convert_fusion
  556.6 4.0 select_convert_fusion
  560.6 4.5 all-to-all-start.4
  565.1 18.1 %fusion.7 = bf16[1536,2048]{1,0:T(8,128)(2,1)} fusion(bf16[1536,2048]{1,0:T(8,128)(2,1)} %copy-done.82, bf16[1536,1024]{1,0:T(8,128)(2,1)S(1)} %copy-done.27, bf16[1,2048,1024]{2,1,0:T(8,128)(2,1)} %param.30), kind=kOutput, calls=%fused_computation.22 | convolution fusion | flops 6508511232 | bytes 19922944 | tf_op jit(solution)/shard_map/dot_general | solution.py:65
  583.3 9.0 fusion.39
  593.5 11.8 %fusion.115 = f32[1024,2048]{1,0:T(8,128)} fusion(bf16[1536,2048]{1,0:T(8,128)(2,1)} %fusion.4, f32[1536,1024]{1,0:T(8,128)S(1)} %copy-done.16, bf16[768,1024]{1,0:T(8,128)(2,1)S(1)} %copy-done.68, bf16[768,1024]{1,0:T(8,128)(2,1)S(1)} %bitcast.115), kind=kOutput, calls=%fused_computation.247 | convolution fusion | flops 6451888128 | bytes 24117248 | tf_op jit(solution)/shard_map/dot_general | solution.py:59
  607.0 35.3 %all-to-all-done.4 = bf16[16,48,1024]{2,1,0:T(8,128)(2,1)} async-done(((bf16[16,48,1024]{2,1,0:T(8,128)(2,1)}), bf16[16,48,1024]{2,1,0:T(8,128)(2,1)}, u32[]{:S(2)}, u32[]{:S(2)}) %all-to-all-start.4) | async-done | bytes 1572896 | tf_op jit(solution)/shard_map/all_to_all | solution.py:51
  642.4 7.7 all-to-all-start.5
  650.1 11.5 %fusion.106 = f32[1024,2048]{1,0:T(8,128)} fusion(bf16[1536,2048]{1,0:T(8,128)(2,1)} %fusion.7, bf16[768,1024]{1,0:T(8,128)(2,1)} %copy-done.66, bf16[768,1024]{1,0:T(8,128)(2,1)S(1)} %bitcast.116), kind=kOutput, calls=%fused_computation.244 | convolution fusion | flops 6448742400 | bytes 17825792 | tf_op jit(solution)/shard_map/dot_general | solution.py:59
  661.6 13.0 %fusion.112 = f32[2048,1024]{1,0:T(8,128)} fusion(bf16[1536,1024]{1,0:T(8,128)(2,1)S(1)} %copy-done.28, bf16[1536,2048]{1,0:T(8,128)(2,1)} %copy-done.82), kind=kOutput, calls=%fused_computation.246 | convolution fusion | flops 6473908224 | bytes 17825792 | tf_op jit(solution)/shard_map/dot_general | solution.py:59
  674.6 33.2 %all-to-all-done.5 = bf16[16,48,1024]{2,1,0:T(8,128)(2,1)S(1)} async-done(((bf16[16,48,1024]{2,1,0:T(8,128)(2,1)}), bf16[16,48,1024]{2,1,0:T(8,128)(2,1)S(1)}, u32[]{:S(2)}, u32[]{:S(2)}) %all-to-all-start.5) | async-done | bytes 1572896 | tf_op jit(solution)/shard_map/all_to_all | solution.py:51
  714.4 11.1 %fusion.23 = bf16[1024,2048]{1,0:T(8,128)(2,1)S(1)} fusion(bf16[1024,2048]{1,0:T(8,128)(2,1)S(1)} %copy-done.80, bf16[1024,4608]{1,0:T(8,128)(2,1)} %all-gather.6.cloned.1.call-done, bf16[512,1024]{1,0:T(8,128)(2,1)S(1)} %collective-permute-done.15, bf16[512,1024]{1,0:T(8,128)(2,1)S(1)} %get-tuple-element.97), kind=kOutput, calls=%fused_computation.39 | convolution fusion | flops 4343201792 | bytes 14680064 | tf_op jit(solution)/shard_map/dot_general | solution.py:55
  725.6 7.9 fusion.54
  741.0 6.1 all-to-all-start.6
  751.7 6.8 convolution_convert_fusion.2
  758.5 6.3 convolution_convert_fusion.3
  766.4 4.9 all-to-all-done.6
  772.1 5.0 collective-permute-start.17
  777.2 9.1 pad_maximum_fusion
  788.0 93.8 %attn_bwd.1 = (bf16[20,192,512]{2,1,0:T(8,128)(2,1)}, bf16[16,128,512]{2,1,0:T(8,128)(2,1)S(1)}) custom-call(s32[4,20]{1,0:T(4,128)S(1)} %copy-done.5, bf16[20,192,512]{2,1,0:T(8,128)(2,1)} %copy-done, bf16[16,128,512]{2,1,0:T(8,128)(2,1)} %copy-done.1, bf16[20,64,512]{2,1,0:T(8,128)(2,1)S(1)} %pad_maximum_fusion.15.grad, ...), custom_call_target="tpu_custom_call" | custom-call | flops 67108864000 | bytes 16777216 | tf_op jit(solution)/shard_map/attn_bwd/pallas_call | solution.py:548
  891.2 4.8 all-to-all-start.7
  896.0 10.2 fusion.69
  909.5 83.0 %all-to-all-done.7 = bf16[16,192,512]{2,1,0:T(8,128)(2,1)} async-done(((bf16[16,192,512]{2,1,0:T(8,128)(2,1)}), bf16[16,192,512]{2,1,0:T(8,128)(2,1)}, u32[]{:S(2)}, u32[]{:S(2)}) %all-to-all-start.7) | async-done | bytes 3145760 | tf_op jit(solution)/shard_map/all_to_all | solution.py:847
  992.5 3.9 broadcast_select_fusion.2
  1003.8 8.0 all-to-all-start.8
  1011.9 6.4 fusion.61
  (364 shorter events, 158.5 us)
Async XLA Ops:
  7.2 96.7 %all-gather.8.cloned.1.call-start = ((), (), s32[]{:S(2)}) async-start(), calls=%async_computation.12 | async-start | bytes 3760128 | tf_op jit(solution)/shard_map/all_gather | solution.py:656
  8.0 5.3 collective-permute-start.1
  16.6 355.3 %copy-start.56 = (s32[512,1]{0,1:T(1,128)}, s32[512,1]{0,1:T(1,128)S(1)}, u32[]{:S(2)}) copy-start(s32[512,1]{0,1:T(1,128)S(1)} %multiply_add_fusion.1) | copy-start | bytes 6148
  20.1 55.2 %all-to-all-start = ((bf16[16,48,1024]{2,1,0:T(8,128)(2,1)}), bf16[16,48,1024]{2,1,0:T(8,128)(2,1)}, u32[]{:S(2)}, u32[]{:S(2)}) async-start(bf16[16,48,1024]{2,1,0:T(8,128)(2,1)} %bitcast.5), calls=%async_computation | async-start | bytes 3145728 | tf_op jit(solution)/shard_map/all_to_all | solution.py:51
  26.8 2.9 collective-permute-start
  29.7 79.0 %copy-start.13 = (bf16[512,1024]{1,0:T(8,128)(2,1)}, bf16[512,1024]{1,0:T(8,128)(2,1)S(1)}, u32[]{:S(2)}) copy-start(bf16[512,1024]{1,0:T(8,128)(2,1)S(1)} %collective-permute-done) | copy-start | bytes 3145732
  30.8 81.0 %copy-start.54 = (f32[1024]{0:T(1024)}, f32[1024]{0:T(1024)S(1)}, u32[]{:S(2)}) copy-start(f32[1024]{0:T(1024)S(1)} %add_rsqrt_fusion) | copy-start | bytes 12292
  113.7 4.8 collective-permute-start.2
  122.3 72.3 %all-to-all-start.1 = ((bf16[16,192,512]{2,1,0:T(8,128)(2,1)}), bf16[16,192,512]{2,1,0:T(8,128)(2,1)S(1)}, u32[]{:S(2)}, u32[]{:S(2)}) async-start(bf16[16,192,512]{2,1,0:T(8,128)(2,1)} %bitcast.110), calls=%async_computation.1 | async-start | bytes 6291456 | tf_op jit(solution)/shard_map/all_to_all | solution.py:699
  126.5 69.6 %copy-start.76 = (s32[16]{0:T(128)S(1)}, s32[16]{0:T(128)}, u32[]{:S(2)}) copy-start(s32[16]{0:T(128)} %param.18) | copy-start | bytes 196
  126.5 210.5 %all-gather.6.cloned.1.call-start = ((), (), s32[]{:S(2)}) async-start(), calls=%async_computation.10 | async-start | bytes 10027008 | tf_op jit(solution)/shard_map/all_gather | solution.py:703
  194.8 6.9 collective-permute-start.4
  196.2 5.5 collective-permute-start.3
  201.7 73.6 %copy-start = (bf16[20,192,512]{2,1,0:T(8,128)(2,1)}, bf16[20,192,512]{2,1,0:T(8,128)(2,1)S(1)}, u32[]{:S(2)}) copy-start(bf16[20,192,512]{2,1,0:T(8,128)(2,1)S(1)} %constant_dynamic-update-slice_fusion.own) | copy-start | bytes 11796484
  202.0 73.3 %copy-start.1 = (bf16[16,128,512]{2,1,0:T(8,128)(2,1)}, bf16[16,128,512]{2,1,0:T(8,128)(2,1)S(1)}, u32[]{:S(2)}) copy-start(bf16[16,128,512]{2,1,0:T(8,128)(2,1)S(1)} %broadcast_select_fusion.prompts) | copy-start | bytes 6291460
  275.3 64.3 %copy-start.12 = (bf16[512,1024]{1,0:T(8,128)(2,1)S(1)}, bf16[512,1024]{1,0:T(8,128)(2,1)}, u32[]{:S(2)}) copy-start(bf16[512,1024]{1,0:T(8,128)(2,1)} %param.17) | copy-start | bytes 3145732
  275.4 3.7 collective-permute-start.5
  280.2 63.8 %all-to-all-start.2 = ((bf16[16,64,512]{2,1,0:T(8,128)(2,1)}), bf16[16,64,512]{2,1,0:T(8,128)(2,1)S(1)}, u32[]{:S(2)}, u32[]{:S(2)}) async-start(bf16[16,64,512]{2,1,0:T(8,128)(2,1)} %pad_maximum_fusion.16), calls=%async_computation.2 | async-start | bytes 2097152 | tf_op jit(solution)/shard_map/all_to_all | solution.py:739
  339.2 3.1 collective-permute-start.6
  348.9 2.7 collective-permute-start.7
  369.1 2.7 collective-permute-start.8
  374.1 43.7 %all-to-all-start.3 = ((bf16[16,48,1024]{2,1,0:T(8,128)(2,1)}), bf16[16,48,1024]{2,1,0:T(8,128)(2,1)S(1)}, u32[]{:S(2)}, u32[]{:S(2)}) async-start(bf16[16,48,1024]{2,1,0:T(8,128)(2,1)} %bitcast.12), calls=%async_computation.3 | async-start | bytes 3145728 | tf_op jit(solution)/shard_map/all_to_all | solution.py:51
  382.2 513.8 %all-gather.10.cloned.1.call-start = ((), (), s32[]{:S(2)}) async-start(), calls=%async_computation.13 | async-start | bytes 17825792 | tf_op jit(solution)/shard_map/all_gather | solution.py:757
  417.8 5.5 collective-permute-start.9
  452.8 6.0 collective-permute-start.11
  455.7 27.0 %collective-permute-start.10 = (bf16[768,1024]{1,0:T(8,128)(2,1)}, bf16[768,1024]{1,0:T(8,128)(2,1)}, u32[]{:S(2)}, u32[]{:S(2)}) collective-permute-start(bf16[768,1024]{1,0:T(8,128)(2,1)} %bitcast.15), channel_id=1, source_target_pairs={{0,1},{1,0},{2,3},{3,2},{4,5},{5,4},{6,7},{7,6},{8,9},{9,8},{10,11... | collective-permute-start | bytes 4718600 | tf_op jit(solution)/shard_map/ppermute | solution.py:574
  468.0 88.5 %copy-start.15 = (f32[1536,1024]{1,0:T(8,128)}, f32[1536,1024]{1,0:T(8,128)S(1)}, u32[]{:S(2)}) copy-start(f32[1536,1024]{1,0:T(8,128)S(1)} %maximum_add_fusion) | copy-start | bytes 18874372
  512.2 32.7 %collective-permute-start.12 = (bf16[1536,1024]{1,0:T(8,128)(2,1)S(1)}, bf16[1536,1024]{1,0:T(8,128)(2,1)S(1)}, u32[]{:S(2)}, u32[]{:S(2)}) collective-permute-start(bf16[1536,1024]{1,0:T(8,128)(2,1)S(1)} %get-tuple-element.95), channel_id=1, source_target_pairs={{0,1},{1,0},{2,3},{3,2},{4,5},{5,4},{6,7},{7,6},{8,9},{9,8},{10,11... | collective-permute-start | bytes 9437192 | tf_op jit(solution)/shard_map/ppermute | solution.py:574
  527.1 29.5 %collective-permute-start.14 = (bf16[768,1024]{1,0:T(8,128)(2,1)}, bf16[768,1024]{1,0:T(8,128)(2,1)}, u32[]{:S(2)}, u32[]{:S(2)}) collective-permute-start(bf16[768,1024]{1,0:T(8,128)(2,1)} %slice.382), channel_id=1, source_target_pairs={{0,1},{1,0},{2,3},{3,2},{4,5},{5,4},{6,7},{7,6},{8,9},{9,8},{10,11... | collective-permute-start | bytes 4718600 | tf_op jit(solution)/shard_map/ppermute | solution.py:574
  560.6 81.8 %all-to-all-start.4 = ((bf16[16,48,1024]{2,1,0:T(8,128)(2,1)}), bf16[16,48,1024]{2,1,0:T(8,128)(2,1)}, u32[]{:S(2)}, u32[]{:S(2)}) async-start(bf16[16,48,1024]{2,1,0:T(8,128)(2,1)} %bitcast.20), calls=%async_computation.4 | async-start | bytes 3145728 | tf_op jit(solution)/shard_map/all_to_all | solution.py:51
  592.5 12.8 %collective-permute-start.13 = (bf16[768,1024]{1,0:T(8,128)(2,1)S(1)}, bf16[768,1024]{1,0:T(8,128)(2,1)S(1)}, u32[]{:S(2)}, u32[]{:S(2)}) collective-permute-start(bf16[768,1024]{1,0:T(8,128)(2,1)S(1)} %slice.383), channel_id=1, source_target_pairs={{0,1},{1,0},{2,3},{3,2},{4,5},{5,4},{6,7},{7,6},{8,9},{9,8},{10,11... | collective-permute-start | bytes 4718600 | tf_op jit(solution)/shard_map/ppermute | solution.py:574
  642.4 65.4 %all-to-all-start.5 = ((bf16[16,48,1024]{2,1,0:T(8,128)(2,1)}), bf16[16,48,1024]{2,1,0:T(8,128)(2,1)S(1)}, u32[]{:S(2)}, u32[]{:S(2)}) async-start(bf16[16,48,1024]{2,1,0:T(8,128)(2,1)} %bitcast.22), calls=%async_computation.5 | async-start | bytes 3145728 | tf_op jit(solution)/shard_map/all_to_all | solution.py:51
  708.8 4.5 collective-permute-start.15
  733.6 2.7 collective-permute-start.16
  741.0 30.4 %all-to-all-start.6 = ((bf16[16,64,512]{2,1,0:T(8,128)(2,1)}), bf16[16,64,512]{2,1,0:T(8,128)(2,1)S(1)}, u32[]{:S(2)}, u32[]{:S(2)}) async-start(bf16[16,64,512]{2,1,0:T(8,128)(2,1)} %bitcast.128), calls=%async_computation.6 | async-start | bytes 2097152 | tf_op jit(solution)/shard_map/all_to_all | solution.py:815
  747.1 293.3 %reduce-scatter.2.cloned.1.call-start = ((), (), s32[]{:S(2)}) async-start(), calls=%async_computation.11 | async-start | bytes 10027008 | tf_op jit(solution)/shard_map/reduce_scatter | solution.py:824
  750.7 14.1 %collective-permute-start.23 = (bf16[1024,512]{1,0:T(8,128)(2,1)S(1)}, bf16[1024,512]{1,0:T(8,128)(2,1)S(1)}, u32[]{:S(2)}, u32[]{:S(2)}) collective-permute-start(bf16[1024,512]{1,0:T(8,128)(2,1)S(1)} %select_convert_fusion.1), channel_id=1, source_target_pairs={{0,1},{1,0},{2,3},{3,2},{4,5},{5,4},{6,7},{7,6},{8,9},{9,8},{10,11... | collective-permute-start | bytes 3145736 | tf_op jit(solution)/shard_map/ppermute | solution.py:574
  772.1 14.2 %collective-permute-start.17 = (bf16[4,64,512]{2,1,0:T(8,128)(2,1)}, bf16[4,64,512]{2,1,0:T(8,128)(2,1)}, u32[]{:S(2)}, u32[]{:S(2)}) collective-permute-start(bf16[4,64,512]{2,1,0:T(8,128)(2,1)} %slice.265), channel_id=1, source_target_pairs={{1,0},{3,2},{5,4},{7,6},{9,8},{11,10},{13,12},{15,14},{17,16},{19,... | collective-permute-start | bytes 786440 | tf_op jit(solution)/shard_map/ppermute | solution.py:582
  881.8 6.1 collective-permute-start.18
  884.7 4.2 collective-permute-start.19
  891.2 101.3 %all-to-all-start.7 = ((bf16[16,192,512]{2,1,0:T(8,128)(2,1)}), bf16[16,192,512]{2,1,0:T(8,128)(2,1)}, u32[]{:S(2)}, u32[]{:S(2)}) async-start(bf16[16,192,512]{2,1,0:T(8,128)(2,1)} %maximum_select_fusion), calls=%async_computation.7 | async-start | bytes 6291456 | tf_op jit(solution)/shard_map/all_to_all | solution.py:847
  906.2 92.9 %copy-start.51 = (f32[768]{0:T(1024)S(1)}, f32[768]{0:T(1024)}, u32[]{:S(2)}) copy-start(f32[768]{0:T(1024)} %copy-done.50) | copy-start | bytes 9220
  906.3 3.1 collective-permute-start.20
  996.4 15.5 %collective-permute-start.21 = (bf16[1536,512]{1,0:T(8,128)(2,1)}, bf16[1536,512]{1,0:T(8,128)(2,1)}, u32[]{:S(2)}, u32[]{:S(2)}) collective-permute-start(bf16[1536,512]{1,0:T(8,128)(2,1)} %bitcast.28), channel_id=1, source_target_pairs={{0,1},{1,0},{2,3},{3,2},{4,5},{5,4},{6,7},{7,6},{8,9},{9,8},{10,11... | collective-permute-start | bytes 4718600 | tf_op jit(solution)/shard_map/ppermute | solution.py:574
  999.5 2.7 collective-permute-start.25
  1003.8 22.2 %all-to-all-start.8 = ((bf16[16,64,192]{2,1,0:T(8,128)(2,1)}), bf16[16,64,192]{2,1,0:T(8,128)(2,1)}, u32[]{:S(2)}, u32[]{:S(2)}) async-start(bf16[16,64,192]{2,1,0:T(8,128)(2,1)} %bitcast.29), calls=%async_computation.8 | async-start | bytes 1048576 | tf_op jit(solution)/shard_map/all_to_all | solution.py:853
  1021.5 12.6 %collective-permute-start.22 = (bf16[512,1024]{1,0:T(8,128)(2,1)}, bf16[512,1024]{1,0:T(8,128)(2,1)S(1)}, u32[]{:S(2)}, u32[]{:S(2)}) collective-permute-start(bf16[512,1024]{1,0:T(8,128)(2,1)} %slice.384), channel_id=1, source_target_pairs={{0,1},{1,0},{2,3},{3,2},{4,5},{5,4},{6,7},{7,6},{8,9},{9,8},{10,11... | collective-permute-start | bytes 3145736 | tf_op jit(solution)/shard_map/ppermute | solution.py:574
  1042.3 4.3 collective-permute-start.24
  (77 other events, 759.1 us)
Sparse Core Ops, SparseCore 0:
  15.0 88.8 all-gather.7
  194.7 142.2 all-gather.5
  456.1 250.9 all-gather.9
  786.4 216.9 reduce-scatter.1

commit v3 on v2

--- a/solution.py
+++ b/solution.py
@@ -414,6 +414,8 @@
 
 
 LOG2E = 1.4426950408889634
+GELU_A = 0.7978845608028654
+GELU_B = 0.044715
 BF16 = jnp.bfloat16
 F32 = jnp.float32
 
@@ -591,10 +593,69 @@
     return value[:half] + swap(value[half:].astype(BF16)).astype(F32)
 
 
-def pair_sum(value):
+def pair_parts(value):
     half = value.shape[0] // 2
-    other = swap(value.astype(BF16)).astype(F32)
-    return value + jnp.concatenate([other[half:], other[:half]], 0)
+    low = value.astype(BF16)
+    other = swap(low)
+    return low, jnp.concatenate([other[half:], other[:half]], 0)
+
+
+def gelu_pair(preact):
+    square = preact * preact
+    tanh = jnp.tanh(preact * (GELU_A + GELU_A * GELU_B * square))
+    half = 0.5 * preact
+    act = half + half * tanh
+    slope = 0.5 + 0.5 * tanh + half * (1.0 - tanh * tanh) * (GELU_A + 3.0 * GELU_A * GELU_B * square)
+    return lax.optimization_barrier((act.astype(BF16), slope.astype(BF16)))
+
+
+def from_bit(value, bit):
+    return lax.ppermute(value, "dp", [(i, i ^ bit) for i in range(lax.axis_size("dp"))])
+
+
+def chip_place():
+    place = lax.axis_index("dp")
+    return place // 4, place // 2 % 2, place % 2
+
+
+def ordered(bit, own, other, axis):
+    return jnp.where(
+        bit == 0, jnp.stack([own, other], axis), jnp.stack([other, own], axis)
+    )
+
+
+def gather_chips(value):
+    planes = lax.axis_size("dp") // 4
+    half = value.shape[1] // 2
+    z, y, x = chip_place()
+    blocks = jnp.stack([value] + [from_bit(value, 4 * k) for k in range(1, planes)])
+    line = jnp.stack(
+        [lax.dynamic_index_in_dim(blocks, z ^ k, 0, keepdims=False) for k in range(planes)]
+    )
+    first, second = line[:, :, :half], line[:, :, half:]
+    first = ordered(y, first, from_bit(first, 2), 1)
+    second = ordered(x, second, from_bit(second, 1), 1)
+    return ordered(x, first, from_bit(first, 1), 2), ordered(y, second, from_bit(second, 2), 1)
+
+
+def halve(value, bit, axis, partner):
+    lower = lax.index_in_dim(value, 0, axis, keepdims=False)
+    upper = lax.index_in_dim(value, 1, axis, keepdims=False)
+    keep, send = jnp.where(bit == 0, lower, upper), jnp.where(bit == 0, upper, lower)
+    return keep.astype(F32) + from_bit(send, partner).astype(F32)
+
+
+def scatter_chips(first, second):
+    planes = first.shape[0]
+    z, y, x = chip_place()
+    first = halve(first, x, 2, 1).astype(BF16)
+    second = halve(second, y, 1, 2).astype(BF16)
+    line = jnp.concatenate([halve(first, y, 1, 2), halve(second, x, 1, 1)], -1).astype(BF16)
+    total = lax.dynamic_index_in_dim(line, z, 0, keepdims=False).astype(F32)
+    for k in range(1, planes):
+        part = lax.dynamic_index_in_dim(line, z ^ k, 0, keepdims=False)
+        total = total + from_bit(part, 4 * k).astype(F32)
+    return total
 
 
 def fits_paired(mesh):
@@ -653,15 +714,14 @@
     ).reshape(shard, half_heads * triple)
     extra = jnp.concatenate([norm1_gain, norm2_gain, counts_pair], 0)
     extra = jnp.pad(extra[None, :], ((0, 7), (0, half_heads * triple - extra.shape[0])))
-    first_all = lax.all_gather(jnp.concatenate([qkv_shard, extra], 0), "dp")
-    sent_grad = matmul_tn(placer, grad_out).astype(BF16).reshape(experts, slots_per, width)
-    grad_own, first_all = lax.optimization_barrier((to_experts(sent_grad), first_all))
-    grad_own = grad_own.reshape(-1, width)
-
-    qkv_full = first_all[:, :shard].reshape(width, half_heads * triple)
-    gain_one = first_all[:, shard, :shard].reshape(width).astype(F32)
-    gain_two = first_all[:, shard, shard : 2 * shard].reshape(width).astype(F32)
-    counts_all = first_all[:, shard, 2 * shard : 2 * shard + 2 * experts].reshape(experts, 2, experts)
+    first_all, last_all = gather_chips(jnp.concatenate([qkv_shard, extra], 0))
+    qkv_full = jnp.concatenate([first_all[..., :shard, :], last_all[..., :shard, :]], -1).reshape(
+        width, half_heads * triple
+    )
+    extra_all = first_all[..., shard, :].reshape(experts, -1)
+    gain_one = extra_all[:, :shard].reshape(width).astype(F32)
+    gain_two = extra_all[:, shard : 2 * shard].reshape(width).astype(F32)
+    counts_all = extra_all[:, 2 * shard : 2 * shard + 2 * experts].reshape(experts, 2, experts)
 
     mine = jnp.sum(
         jnp.where(lax.broadcasted_iota(jnp.int32, (1, 1, experts), 2) == dp_index, counts_all.astype(F32), 0.0),
@@ -683,7 +743,6 @@
         [(start[:, None] + slot_at < capacity).reshape(-1, 1) for start in starts], 0
     )
     half_rows = experts * slots_per
-    grad_returned = jnp.where(kept, with_other(grad_own).astype(F32), 0.0)
 
     pair_tokens = with_other(tokens).astype(F32)
     normed_one, hat_pair, inv_pair = norm_forward(pair_tokens, gain_one)
@@ -746,25 +805,28 @@
     )
     normed_two, hat_two, inv_two = norm_forward(hidden_one, gain_two)
     rows_two = with_other(normed_two.astype(BF16))
-    ffn_pre = matmul(rows_two, ffn_in).astype(BF16)
-    ffn_act = jax.nn.gelu(ffn_pre.astype(F32)).astype(BF16)
+    ffn_act, ffn_slope = gelu_pair(matmul(rows_two, ffn_in))
     hidden_two = hidden_one + keep_rows(matmul_nt(ffn_act, ffn_out_t))
 
     sent_rows = (
         matmul_tn(placer, hidden_two.astype(BF16)).astype(BF16).reshape(experts, slots_per, width)
     )
-    own_rows, normed_own = lax.optimization_barrier((to_experts(sent_rows), rows_one[:rows]))
-    normed_all = lax.all_gather(normed_own, "dp")
+    sent_grad = matmul_tn(placer, grad_out).astype(BF16).reshape(experts, slots_per, width)
+    own_rows, sent_grad = lax.optimization_barrier((to_experts(sent_rows), sent_grad))
+    grad_own = to_experts(sent_grad)
     expert_rows = with_other(own_rows.reshape(-1, width))
     centre = centroids[0]
     gate_value = jax.nn.sigmoid(matmul(expert_rows, centre))
-    pre_a = matmul(expert_rows, expert_in_a[0]).astype(BF16)
-    act_a = jax.nn.gelu(pre_a.astype(F32)).astype(BF16)
-    branch_a = pair_sum(matmul(act_a, expert_out_a[0]))
-    middle = (expert_rows.astype(F32) + branch_a).astype(BF16)
-    pre_b = matmul(middle, expert_in_b[0]).astype(BF16)
-    act_b = jax.nn.gelu(pre_b.astype(F32)).astype(BF16)
-    branch_half = branch_a[:half_rows] + keep_rows(matmul(act_b, expert_out_b[0]))
+    act_a, slope_a = gelu_pair(matmul(expert_rows, expert_in_a[0]))
+    part_a, other_a = pair_parts(matmul(act_a, expert_out_a[0]))
+    middle = (expert_rows.astype(F32) + part_a.astype(F32) + other_a.astype(F32)).astype(BF16)
+    act_b, slope_b = gelu_pair(matmul(middle, expert_in_b[0]))
+    act_b, grad_own = lax.optimization_barrier((act_b, grad_own))
+    branch_half = (
+        part_a[:half_rows].astype(F32)
+        + other_a[:half_rows].astype(F32)
+        + keep_rows(matmul(act_b, expert_out_b[0]))
+    )
     gate_half = gate_value[:half_rows]
     returned = (
         jnp.where(kept[:half_rows], gate_half[:, None] * branch_half, 0.0)
@@ -773,18 +835,20 @@
     )
     came_back = to_experts(returned).reshape(half_rows, width)
 
-    grad_half = grad_returned[:half_rows]
+    grad_returned = jnp.where(kept, with_other(grad_own.reshape(-1, width)), 0.0).astype(BF16)
+    grad_half = grad_returned[:half_rows].astype(F32)
     grad_logit_half = jnp.sum(grad_half * branch_half, 1) * gate_half * (1.0 - gate_half)
     centre_part = matmul(grad_logit_half, expert_rows[:half_rows].astype(F32))
-    grad_branch = gate_value[:, None] * grad_returned
+    grad_branch = gate_value[:, None] * grad_returned.astype(F32)
     grad_b = grad_branch.astype(BF16)
-    grad_pre_b = gelu_grad(pre_b.astype(F32), matmul_nt(grad_b, expert_out_b[0])).astype(BF16)
-    grad_middle = pair_sum(matmul_nt(grad_pre_b, expert_in_b[0]))
-    grad_a = (grad_branch + grad_middle).astype(BF16)
-    grad_pre_a = gelu_grad(pre_a.astype(F32), matmul_nt(grad_a, expert_out_a[0])).astype(BF16)
+    grad_pre_b = (matmul_nt(grad_b, expert_out_b[0]) * slope_b.astype(F32)).astype(BF16)
+    part_m, other_m = pair_parts(matmul_nt(grad_pre_b, expert_in_b[0]))
+    grad_a = (grad_branch + part_m.astype(F32) + other_m.astype(F32)).astype(BF16)
+    grad_pre_a = (matmul_nt(grad_a, expert_out_a[0]) * slope_a.astype(F32)).astype(BF16)
     grad_rows = (
         keep_rows(matmul_nt(grad_pre_a, expert_in_a[0]))
-        + grad_middle[:half_rows]
+        + part_m[:half_rows].astype(F32)
+        + other_m[:half_rows].astype(F32)
         + grad_logit_half[:, None] * centre.astype(F32)[None, :]
     )
     grad_out_b = matmul_tn(act_b, grad_b)
@@ -801,7 +865,7 @@
     grad_two = grad_out.astype(F32) + matmul(placer, grad_back)
 
     rows_down = with_other(grad_two.astype(BF16))
-    grad_ffn_pre = gelu_grad(ffn_pre.astype(F32), matmul(rows_down, ffn_out_t)).astype(BF16)
+    grad_ffn_pre = (matmul(rows_down, ffn_out_t) * ffn_slope.astype(F32)).astype(BF16)
     grad_ffn_out_t = matmul_tn(rows_down, ffn_act)
     grad_ffn_in = matmul_tn(rows_two, grad_ffn_pre)
     grad_norm_two = keep_rows(matmul_nt(grad_ffn_pre, ffn_in))
@@ -843,24 +907,17 @@
         1,
     )
     cont_part = jnp.concatenate([lent_grad, grad_own_blocks[lent:experts]], 0)
-    grad_head = jnp.where(core_zero, prompt_part, cont_part)
-    grad_qkv = lax.all_to_all(grad_head, "dp", split_axis=0, concat_axis=0, tiled=True)
-    grad_head_w = lax.dot_general(
-        normed_all, grad_head, (((0, 1), (0, 2)), ((), ())), preferred_element_type=F32
-    ).astype(BF16)
-    grad_head_w = (grad_head_w.astype(F32) + swap(grad_head_w).astype(F32)).astype(BF16)
-    grad_qkv, grad_head_w = lax.optimization_barrier((grad_qkv, grad_head_w))
-    by_row = lax.all_to_all(
-        grad_head_w.reshape(experts, shard, triple), "dp", split_axis=0, concat_axis=0, tiled=True
-    )
-    qkv_sum = jnp.where(core_zero, by_row[:half_heads], by_row[half_heads:]).astype(F32)
-    query_shard, key_shard, value_shard = (
-        qkv_sum[:, :, part * HEAD : (part + 1) * HEAD].transpose(1, 0, 2).reshape(shard, half_heads * HEAD)
-        for part in range(3)
-    )
-    grad_qkv = grad_qkv.reshape(2, half_heads * triple, rows)
+    grad_qkv = lax.all_to_all(
+        jnp.where(core_zero, prompt_part, cont_part), "dp", split_axis=0, concat_axis=0, tiled=True
+    ).reshape(2, half_heads * triple, rows)
     keep_half, send_half = both(grad_qkv[0], grad_qkv[1])
     grad_qkv_t = jnp.concatenate([keep_half, swap(send_half)], 1)
+    grad_qkv_w = lax.dot_general(
+        rows_one, grad_qkv_t, (((0,), (1,)), ((), ())), preferred_element_type=F32
+    ).astype(BF16)
+    by_chip = grad_qkv_w.reshape(experts // 4, 2, 2, shard, half_heads * triple)
+    half_columns = half_heads * triple // 2
+    qkv_sum = scatter_chips(by_chip[..., :half_columns], by_chip[..., half_columns:])
     grad_norm_one = keep_rows(
         lax.dot_general(
             grad_qkv_t, qkv_full, (((0,), (1,)), ((), ())), preferred_element_type=F32
@@ -868,6 +925,10 @@
     )
     back_one = norm_backward(grad_norm_one, hat_one, inv_one, gain_one)[0]
     grad_input = grad_one + back_one
+    qkv_sum = qkv_sum.reshape(shard, half_heads, 3, HEAD)
+    query_shard, key_shard, value_shard = (
+        qkv_sum[:, :, part].reshape(shard, half_heads * HEAD) for part in range(3)
+    )
 
     ffn_in_sum = second_sum[:, :hidden]
     gains = jnp.stack(

time: 1060 us -> 998 us (0.942)
  waiting for transfers between devices: 403 us -> 266 us
  blocking collectives: 0 us -> 112 us
  matrix products: 259 us -> 226 us
    all_to_all x0 -> x1, blocking collectives: none -> 112 us  [body_paired(): lax.all_to_all(jnp.where(core_zero, prompt_part, cont_part), 'dp', split_...]
    all_to_all x4, waiting for transfers between devices: 146 us -> 54.3 us  [to_experts(): return lax.all_to_all(value, 'dp', split_axis=0, concat_axis=0, tiled=True)]
    all_to_all x2 -> x0, waiting for transfers between devices: 83 us -> none  [the longest x1 83 us: body_paired(): lax.all_to_all(grad_head, 'dp', split_axis=0, concat_axis=0, tiled=True)]
    ppermute x0 -> x14, waiting for transfers between devices: none -> 74 us  [from_bit(): lax.ppermute(value, 'dp', [(i, i ^ bit) for i in range(lax.axis_size('dp'...]
    all_gather x2 -> x0, waiting for transfers between devices: 28.5 us -> none  [the longest x1 28.5 us: body_paired(): first_all = lax.all_gather(jnp.concatenate([qkv_shard, extra], 0), 'dp')]
    dot_general x6, matrix products: 73.6 us -> 53.9 us  [matmul_nt(): lax.dot_general(left, right, (((1,), (1,)), ((), ())), preferred_element_...]
    all_to_all x2 -> x0, starting transfers between devices: 12.8 us -> none  [the longest x1 8.02 us: body_paired(): lax.all_to_all(grad_head_w.reshape(experts, shard, triple), 'dp', split_a...]
    ppermute x0 -> x14, starting transfers between devices: none -> 12.5 us  [from_bit(): lax.ppermute(value, 'dp', [(i, i ^ bit) for i in range(lax.axis_size('dp'...]
  transfers between devices with their start and end apart: 39 -> 48, of which waited for: 21 -> 28; matrix products, arithmetic and copies ran while one was open for 28% -> 23% of each run, Pallas kernels for 16% -> 17%
where the time goes in v3:
time: 998 us; the launch traced here: 988 us
  waiting for transfers between devices  266 us (27%)
  matrix products  226 us (23%)
  Pallas kernels  167 us (17%)
  blocking collectives  112 us (11%)
  starting transfers between devices  90.8 us (9%)
  other arithmetic  73 us (7%)
  local copies, waits for them, and re-layouts  36.6 us (4%)
  between operations  15.9 us (2%)
    all_to_all x1, blocking collectives, body_paired(): lax.all_to_all(jnp.where(core_zero, prompt_part, cont_part), 'dp', split_...  112 us
    pallas_call x1, Pallas kernels, attn_backward(): pl.pallas_call(functools.partial(attn_bwd_kernel, head=head, factor=head...  93.7 us
    dot_general x11, matrix products, matmul(): return jnp.dot(left, right, preferred_element_type=jnp.float32)  84.2 us
    ppermute x14, waiting for transfers between devices, from_bit(): lax.ppermute(value, 'dp', [(i, i ^ bit) for i in range(lax.axis_size('dp'...  74 us
    pallas_call x1, Pallas kernels, attn_forward(): pl.pallas_call(functools.partial(attn_fwd_kernel, head=head, factor=head...  73.3 us
    dot_general x8, matrix products, matmul_tn(): lax.dot_general(left, right, (((0,), (0,)), ((), ())), preferred_element_...  66.8 us
    all_to_all x1, waiting for transfers between devices, body_paired(): lax.all_to_all(qkv_t, 'dp', split_axis=0, concat_axis=0, tiled=True)  66 us
    all_to_all x4, waiting for transfers between devices, to_experts(): return lax.all_to_all(value, 'dp', split_axis=0, concat_axis=0, tiled=True)  54.3 us
  transfers between devices with their start and end apart: 48, of which 28 were waited for; matrix products, arithmetic and copies ran while one was open for 23% of the time, Pallas kernels for 17%

profile of v3, /device:TPU:9, one launch (start us, length us, event | category | flops | bytes accessed | tf_op | source)
XLA Modules:
  0.0 987.7 jit_solution(9473918534833502498)
XLA Ops:
  17.8 5.9 collective-permute-done.2
  23.6 7.0 collective-permute-done.3
  30.6 5.8 collective-permute-done.4
  40.4 8.4 collective-permute-done.5
  58.8 10.8 %collective-permute-done.6 = bf16[4,2,72,768]{3,2,0,1:T(8,128)(2,1)S(1)} collective-permute-done((bf16[4,2,72,768]{3,2,0,1:T(8,128)(2,1)S(1)}, bf16[4,2,72,768]{3,2,0,1:T(8,128)(2,1)S(1)}, u32[]{:S(2)}, u32[]{:S(2)}) %collective-permute-start.6) | collective-permute-done | bytes 884768 | tf_op jit(solution)/shard_map/ppermute | solution.py:613
  90.4 4.8 all-to-all-start
  97.3 66.0 %all-to-all-done = bf16[16,192,512]{2,1,0:T(8,128)(2,1)S(1)} async-done(((bf16[16,192,512]{2,1,0:T(8,128)(2,1)}), bf16[16,192,512]{2,1,0:T(8,128)(2,1)S(1)}, u32[]{:S(2)}, u32[]{:S(2)}) %all-to-all-start) | async-done | bytes 3145760 | tf_op jit(solution)/shard_map/all_to_all | solution.py:758
  172.4 73.3 %attn_fwd.1 = (bf16[20,64,512]{2,1,0:T(8,128)(2,1)S(1)}, f32[20,1,512]{2,1,0:T(1,128)S(1)}) custom-call(s32[4,20]{1,0:T(4,128)S(1)} %add_select_fusion.2.plan, bf16[20,192,512]{2,1,0:T(8,128)(2,1)S(1)} %constant_dynamic-update-slice_fusion.own, bf16[16,128,512]{2,1,0:T(8,128)(2,1)S(1)} %broadcast_select_fusion.prompts), custom_call_target="tpu_custom_call" | custom-call | flops 26843545600 | bytes 8388608 | tf_op jit(solution)/shard_map/attn_fwd/pallas_call | solution.py:524
  250.3 7.6 all-to-all-start.1
  257.8 47.8 %all-gather.2.cloned.1.call-done = bf16[1024,4608]{1,0:T(8,128)(2,1)} async-done(((bf16[64,4608]{1,0:T(8,128)(2,1)}), bf16[1024,4608]{1,0:T(8,128)(2,1)}) %all-gather.2.cloned.1.call-update) | async-done | bytes 9437200 | tf_op jit(solution)/shard_map/all_gather | solution.py:762
  312.8 4.1 fusion.101
  320.3 12.0 %add_convert_fusion.2 = (bf16[1024,2048]{1,0:T(8,128)(2,1)}, bf16[1024,2048]{1,0:T(8,128)(2,1)S(1)}) fusion(bf16[1024,4608]{1,0:T(8,128)(2,1)} %all-gather.2.cloned.1.call-done, bf16[512,1024]{1,0:T(8,128)(2,1)S(1)} %collective-permute-done.14, bf16[512,1024]{1,0:T(8,128)(2,1)S(1)} %multiply_convert_fusion.4), kind=kOutput, calls=%fused_computation.14 | convolution fusion | flops 4336910336 | bytes 14680064 | tf_op jit(solution)/shard_map/dot_general | solution.py:55
  332.3 7.9 fusion.25
  345.4 8.6 all-to-all-start.2
  356.3 33.2 %all-to-all-done.2 = bf16[16,48,1024]{2,1,0:T(8,128)(2,1)S(1)} async-done(((bf16[16,48,1024]{2,1,0:T(8,128)(2,1)}), bf16[16,48,1024]{2,1,0:T(8,128)(2,1)S(1)}, u32[]{:S(2)}, u32[]{:S(2)}) %all-to-all-start.2) | async-done | bytes 1572896 | tf_op jit(solution)/shard_map/all_to_all | solution.py:51
  394.9 18.3 %add_convert_fusion.1 = (bf16[1536,2048]{1,0:T(8,128)(2,1)}, bf16[1536,2048]{1,0:T(8,128)(2,1)S(1)}) fusion(bf16[1,1024,2048]{2,1,0:T(8,128)(2,1)} %param.29, bf16[768,1024]{1,0:T(8,128)(2,1)S(1)} %collective-permute-done.16, bf16[768,1024]{1,0:T(8,128)(2,1)S(1)} %bitcast.155), kind=kOutput, calls=%fused_computation.8 | convolution fusion | flops 6505365504 | bytes 19922944 | tf_op jit(solution)/shard_map/dot_general | solution.py:55
  413.3 8.0 fusion.18
  422.7 5.2 all-to-all-start.3
  435.9 19.4 %add_convert_fusion = (bf16[1536,2048]{1,0:T(8,128)(2,1)}, bf16[1536,2048]{1,0:T(8,128)(2,1)}) fusion(bf16[1,1024,2048]{2,1,0:T(8,128)(2,1)S(1)} %copy-done.74, bf16[1536,1024]{1,0:T(8,128)(2,1)} %fusion.18, bf16[768,1024]{1,0:T(8,128)(2,1)S(1)} %get-tuple-element.91, bf16[768,1024]{1,0:T(8,128)(2,1)S(1)} %get-tuple-element.90, ...), kind=kOutput, calls=%fused_computation.6 | convolution fusion | flops 6517948416 | bytes 26214400 | tf_op jit(solution)/shard_map/dot_general | solution.py:55
  455.3 8.2 all-to-all-done.3
  465.6 10.0 %fusion.4 = f32[1536,1024]{1,0:T(8,128)S(1)} fusion(bf16[1536,2048]{1,0:T(8,128)(2,1)} %get-tuple-element.49, bf16[1,2048,1024]{2,1,0:T(8,128)(2,1)} %param.32), kind=kOutput, calls=%fused_computation.20 | convolution fusion | flops 6442450944 | bytes 16777216 | tf_op jit(solution)/shard_map/dot_general | solution.py:55
  478.8 4.1 maximum_select_fusion
  483.0 9.4 multiply_convert_fusion.1
  492.4 8.4 fusion.21
  500.9 4.9 select_convert_fusion
  505.8 5.2 all-to-all-start.4
  511.0 11.3 %fusion.44 = f32[2048,1024]{1,0:T(8,128)} fusion(bf16[1536,2048]{1,0:T(8,128)(2,1)} %get-tuple-element.49, bf16[1536,1024]{1,0:T(8,128)(2,1)S(1)} %maximum_select_fusion, f32[1536]{0:T(1024)S(1)} %add_divide_fusion), kind=kOutput, calls=%fused_computation.115 | convolution fusion | flops 6447169536 | bytes 17831936 | tf_op jit(solution)/shard_map/dot_general | solution.py:59
  524.6 7.2 add_convert_fusion.3
  533.4 10.8 %multiply_convert_fusion = bf16[1536,2048]{1,0:T(8,128)(2,1)} fusion(bf16[1536,2048]{1,0:T(8,128)(2,1)} %get-tuple-element.48, bf16[1536,1024]{1,0:T(8,128)(2,1)S(1)} %add_convert_fusion.3, bf16[1,2048,1024]{2,1,0:T(8,128)(2,1)S(1)} %copy-done.77), kind=kOutput, calls=%fused_computation.4 | convolution fusion | flops 6451888128 | bytes 19922944 | tf_op jit(solution)/shard_map/dot_general | solution.py:65
  544.2 9.4 fusion.14
  555.6 13.2 %fusion.96 = f32[1024,2048]{1,0:T(8,128)} fusion(bf16[1536,2048]{1,0:T(8,128)(2,1)} %copy-done.91, bf16[1536,1024]{1,0:T(8,128)(2,1)} %fusion.18, bf16[768,1024]{1,0:T(8,128)(2,1)S(1)} %copy-done.38, bf16[768,1024]{1,0:T(8,128)(2,1)S(1)} %copy-done.36, bf16[768,1024]{1,0:T(8,128)(2,1)S(1)} %copy-done.81, bf16[768,1024]{1,0:T(8,128)(2,1)S(1)} %bitcast.158), kind=kOutput, calls=%fused_computation.259 | convolution fusion | flops 6461325312 | bytes 24117248 | tf_op jit(solution)/shard_map/dot_general | solution.py:59
  572.7 6.6 all-to-all-start.5
  579.4 11.5 %fusion.95 = f32[1024,2048]{1,0:T(8,128)} fusion(bf16[1536,2048]{1,0:T(8,128)(2,1)} %multiply_convert_fusion, bf16[768,1024]{1,0:T(8,128)(2,1)} %copy-done.79, bf16[768,1024]{1,0:T(8,128)(2,1)S(1)} %bitcast.159), kind=kOutput, calls=%fused_computation.258 | convolution fusion | flops 6448742400 | bytes 17825792 | tf_op jit(solution)/shard_map/dot_general | solution.py:59
  590.9 11.1 %fusion.103 = f32[2048,1024]{1,0:T(8,128)} fusion(bf16[1536,2048]{1,0:T(8,128)(2,1)} %copy-done.96, bf16[1536,1024]{1,0:T(8,128)(2,1)S(1)} %copy-done.30), kind=kOutput, calls=%fused_computation.266 | convolution fusion | flops 6442450944 | bytes 17825792 | tf_op jit(solution)/shard_map/dot_general | solution.py:59
  602.0 12.8 %all-to-all-done.5 = bf16[16,48,1024]{2,1,0:T(8,128)(2,1)S(1)} async-done(((bf16[16,48,1024]{2,1,0:T(8,128)(2,1)}), bf16[16,48,1024]{2,1,0:T(8,128)(2,1)S(1)}, u32[]{:S(2)}, u32[]{:S(2)}) %all-to-all-start.5) | async-done | bytes 1572896 | tf_op jit(solution)/shard_map/all_to_all | solution.py:51
  621.1 8.2 multiply_convert_fusion.2
  629.4 8.1 fusion.27
  648.4 3.9 all-to-all-start.6
  656.0 8.8 convolution_convert_fusion.2
  664.8 6.3 convolution_convert_fusion.1
  672.7 3.9 all-to-all-done.6
  677.4 5.0 collective-permute-start.24
  682.4 9.4 pad_maximum_fusion
  693.6 93.7 %attn_bwd.1 = (bf16[20,192,512]{2,1,0:T(8,128)(2,1)}, bf16[16,128,512]{2,1,0:T(8,128)(2,1)S(1)}) custom-call(s32[4,20]{1,0:T(4,128)S(1)} %copy-done.5, bf16[20,192,512]{2,1,0:T(8,128)(2,1)} %copy-done, bf16[16,128,512]{2,1,0:T(8,128)(2,1)} %copy-done.1, bf16[20,64,512]{2,1,0:T(8,128)(2,1)S(1)} %pad_maximum_fusion.21.grad, ...), custom_call_target="tpu_custom_call" | custom-call | flops 67108864000 | bytes 16777216 | tf_op jit(solution)/shard_map/attn_bwd/pallas_call | solution.py:550
  795.5 112.5 %all_to_all.40 = bf16[16,192,512]{2,1,0:T(8,128)(2,1)S(1)} all-to-all(bf16[16,192,512]{2,1,0:T(8,128)(2,1)S(1)} %maximum_select_fusion.1), channel_id=1, replica_groups=mesh['dp'=16,'tensor'=2] {'dp'}, dimensions={0} | all-to-all | bytes 6291456 | tf_op jit(solution)/shard_map/all_to_all | solution.py:910
  927.2 12.9 %collective-permute-done.31 = bf16[4,2,64,768]{3,2,0,1:T(8,128)(2,1)S(1)} collective-permute-done((bf16[4,2,64,768]{3,2,0,1:T(8,128)(2,1)S(1)}, bf16[4,2,64,768]{3,2,0,1:T(8,128)(2,1)S(1)}, u32[]{:S(2)}, u32[]{:S(2)}) %collective-permute-start.31) | collective-permute-done | bytes 786464 | tf_op jit(solution)/shard_map/ppermute | solution.py:613
  943.3 6.7 collective-permute-done.32
  958.9 10.8 %collective-permute-done.35 = bf16[64,1536]{1,0:T(8,128)(2,1)S(1)} collective-permute-done((bf16[64,1536]{1,0:T(8,128)(2,1)S(1)}, bf16[64,1536]{1,0:T(8,128)(2,1)S(1)}, u32[]{:S(2)}, u32[]{:S(2)}) %collective-permute-start.35) | collective-permute-done | bytes 196640 | tf_op jit(solution)/shard_map/ppermute | solution.py:613
  (427 shorter events, 183.2 us)
Async XLA Ops:
  8.1 5.3 collective-permute-start.1
  14.2 9.4 collective-permute-start.2
  14.3 16.4 %collective-permute-start.3 = (bf16[72,1536]{1,0:T(8,128)(2,1)S(1)}, bf16[72,1536]{1,0:T(8,128)(2,1)S(1)}, u32[]{:S(2)}, u32[]{:S(2)}) collective-permute-start(bf16[72,1536]{1,0:T(8,128)(2,1)S(1)} %get-tuple-element.110), channel_id=1, source_target_pairs={{0,16},{2,18},{4,20},{6,22},{8,24},{10,26},{12,28},{14,30},{16,0},... | collective-permute-start | bytes 663560 | tf_op jit(solution)/shard_map/ppermute | solution.py:613
  16.7 19.7 %collective-permute-start.4 = (bf16[72,1536]{1,0:T(8,128)(2,1)S(1)}, bf16[72,1536]{1,0:T(8,128)(2,1)S(1)}, u32[]{:S(2)}, u32[]{:S(2)}) collective-permute-start(bf16[72,1536]{1,0:T(8,128)(2,1)S(1)} %get-tuple-element.110), channel_id=1, source_target_pairs={{0,24},{2,26},{4,28},{6,30},{8,16},{10,18},{12,20},{14,22},{16,8},... | collective-permute-start | bytes 663560 | tf_op jit(solution)/shard_map/ppermute | solution.py:613
  16.9 40.8 %collective-permute-start = (bf16[512,1024]{1,0:T(8,128)(2,1)S(1)}, bf16[512,1024]{1,0:T(8,128)(2,1)S(1)}, u32[]{:S(2)}, u32[]{:S(2)}) collective-permute-start(bf16[512,1024]{1,0:T(8,128)(2,1)S(1)} %copy-done.12), channel_id=1, source_target_pairs={{0,1},{1,0},{2,3},{3,2},{4,5},{5,4},{6,7},{7,6},{8,9},{9,8},{10,11... | collective-permute-start | bytes 3145736 | tf_op jit(solution)/shard_map/ppermute | solution.py:576
  37.9 10.9 %collective-permute-start.5 = (bf16[4,72,768]{2,1,0:T(8,128)(2,1)}, bf16[4,72,768]{2,1,0:T(8,128)(2,1)}, u32[]{:S(2)}, u32[]{:S(2)}) collective-permute-start(bf16[4,72,768]{2,1,0:T(8,128)(2,1)} %get-tuple-element.101), channel_id=1, source_target_pairs={{0,4},{2,6},{4,0},{6,2},{8,12},{10,14},{12,8},{14,10},{16,20},{18,... | collective-permute-start | bytes 1327112 | tf_op jit(solution)/shard_map/ppermute | solution.py:613
  39.2 12.5 %collective-permute-start.7 = (bf16[4,72,768]{2,1,0:T(8,128)(2,1)}, bf16[4,72,768]{2,1,0:T(8,128)(2,1)}, u32[]{:S(2)}, u32[]{:S(2)}) collective-permute-start(bf16[4,72,768]{2,1,0:T(8,128)(2,1)} %get-tuple-element.100), channel_id=1, source_target_pairs={{0,2},{2,0},{4,6},{6,4},{8,10},{10,8},{12,14},{14,12},{16,18},{18,... | collective-permute-start | bytes 1327112 | tf_op jit(solution)/shard_map/ppermute | solution.py:613
  50.4 19.3 %collective-permute-start.6 = (bf16[4,2,72,768]{3,2,0,1:T(8,128)(2,1)S(1)}, bf16[4,2,72,768]{3,2,0,1:T(8,128)(2,1)S(1)}, u32[]{:S(2)}, u32[]{:S(2)}) collective-permute-start(bf16[4,2,72,768]{3,2,0,1:T(8,128)(2,1)S(1)} %maximum_select_fusion.4), channel_id=1, source_target_pairs={{0,2},{2,0},{4,6},{6,4},{8,10},{10,8},{12,14},{14,12},{16,18},{18,... | collective-permute-start | bytes 2654216 | tf_op jit(solution)/shard_map/ppermute | solution.py:613
  53.8 19.1 %collective-permute-start.8 = (bf16[4,2,72,768]{3,2,0,1:T(8,128)(2,1)}, bf16[4,2,72,768]{3,2,0,1:T(8,128)(2,1)}, u32[]{:S(2)}, u32[]{:S(2)}) collective-permute-start(bf16[4,2,72,768]{3,2,0,1:T(8,128)(2,1)} %maximum_select_fusion.6), channel_id=1, source_target_pairs={{0,4},{2,6},{4,0},{6,2},{8,12},{10,14},{12,8},{14,10},{16,20},{18,... | collective-permute-start | bytes 2654216 | tf_op jit(solution)/shard_map/ppermute | solution.py:613
  80.3 6.3 collective-permute-start.9
  90.4 72.9 %all-to-all-start = ((bf16[16,192,512]{2,1,0:T(8,128)(2,1)}), bf16[16,192,512]{2,1,0:T(8,128)(2,1)S(1)}, u32[]{:S(2)}, u32[]{:S(2)}) async-start(bf16[16,192,512]{2,1,0:T(8,128)(2,1)} %bitcast.153), calls=%async_computation | async-start | bytes 6291456 | tf_op jit(solution)/shard_map/all_to_all | solution.py:758
  95.3 210.4 %all-gather.2.cloned.1.call-start = ((), (), s32[]{:S(2)}) async-start(), calls=%async_computation.9 | async-start | bytes 10027008 | tf_op jit(solution)/shard_map/all_gather | solution.py:762
  163.5 6.9 collective-permute-start.11
  165.0 5.5 collective-permute-start.10
  245.7 3.4 collective-permute-start.12
  250.3 62.5 %all-to-all-start.1 = ((bf16[16,64,512]{2,1,0:T(8,128)(2,1)}), bf16[16,64,512]{2,1,0:T(8,128)(2,1)S(1)}, u32[]{:S(2)}, u32[]{:S(2)}) async-start(bf16[16,64,512]{2,1,0:T(8,128)(2,1)} %pad_maximum_fusion.22), calls=%async_computation.1 | async-start | bytes 2097152 | tf_op jit(solution)/shard_map/all_to_all | solution.py:798
  308.0 3.1 collective-permute-start.13
  317.6 2.7 collective-permute-start.14
  340.4 2.7 collective-permute-start.15
  345.4 44.1 %all-to-all-start.2 = ((bf16[16,48,1024]{2,1,0:T(8,128)(2,1)}), bf16[16,48,1024]{2,1,0:T(8,128)(2,1)S(1)}, u32[]{:S(2)}, u32[]{:S(2)}) async-start(bf16[16,48,1024]{2,1,0:T(8,128)(2,1)} %bitcast.24), calls=%async_computation.2 | async-start | bytes 3145728 | tf_op jit(solution)/shard_map/all_to_all | solution.py:51
  389.5 5.4 collective-permute-start.16
  421.3 9.6 collective-permute-start.17
  422.7 40.8 %all-to-all-start.3 = ((bf16[16,48,1024]{2,1,0:T(8,128)(2,1)}), bf16[16,48,1024]{2,1,0:T(8,128)(2,1)}, u32[]{:S(2)}, u32[]{:S(2)}) async-start(bf16[16,48,1024]{2,1,0:T(8,128)(2,1)} %bitcast.169), calls=%async_computation.3 | async-start | bytes 3145728 | tf_op jit(solution)/shard_map/all_to_all | solution.py:51
  463.5 15.3 %collective-permute-start.18 = (bf16[768,1024]{1,0:T(8,128)(2,1)}, bf16[768,1024]{1,0:T(8,128)(2,1)S(1)}, u32[]{:S(2)}, u32[]{:S(2)}) collective-permute-start(bf16[768,1024]{1,0:T(8,128)(2,1)} %bitcast.31), channel_id=1, source_target_pairs={{0,1},{1,0},{2,3},{3,2},{4,5},{5,4},{6,7},{7,6},{8,9},{9,8},{10,11... | collective-permute-start | bytes 4718600 | tf_op jit(solution)/shard_map/ppermute | solution.py:576
  477.3 23.6 %collective-permute-start.21 = (bf16[768,1024]{1,0:T(8,128)(2,1)}, bf16[768,1024]{1,0:T(8,128)(2,1)}, u32[]{:S(2)}, u32[]{:S(2)}) collective-permute-start(bf16[768,1024]{1,0:T(8,128)(2,1)} %slice.452), channel_id=1, source_target_pairs={{0,1},{1,0},{2,3},{3,2},{4,5},{5,4},{6,7},{7,6},{8,9},{9,8},{10,11... | collective-permute-start | bytes 4718600 | tf_op jit(solution)/shard_map/ppermute | solution.py:576
  500.8 21.6 %collective-permute-start.19 = (bf16[1536,1024]{1,0:T(8,128)(2,1)}, bf16[1536,1024]{1,0:T(8,128)(2,1)}, u32[]{:S(2)}, u32[]{:S(2)}) collective-permute-start(bf16[1536,1024]{1,0:T(8,128)(2,1)} %fusion.21), channel_id=1, source_target_pairs={{0,1},{1,0},{2,3},{3,2},{4,5},{5,4},{6,7},{7,6},{8,9},{9,8},{10,11... | collective-permute-start | bytes 9437192 | tf_op jit(solution)/shard_map/ppermute | solution.py:576
  505.8 67.0 %all-to-all-start.4 = ((bf16[16,48,1024]{2,1,0:T(8,128)(2,1)}), bf16[16,48,1024]{2,1,0:T(8,128)(2,1)}, u32[]{:S(2)}, u32[]{:S(2)}) async-start(bf16[16,48,1024]{2,1,0:T(8,128)(2,1)} %bitcast.161), calls=%async_computation.4 | async-start | bytes 3145728 | tf_op jit(solution)/shard_map/all_to_all | solution.py:51
  553.9 14.9 %collective-permute-start.20 = (bf16[768,1024]{1,0:T(8,128)(2,1)S(1)}, bf16[768,1024]{1,0:T(8,128)(2,1)S(1)}, u32[]{:S(2)}, u32[]{:S(2)}) collective-permute-start(bf16[768,1024]{1,0:T(8,128)(2,1)S(1)} %slice.453), channel_id=1, source_target_pairs={{0,1},{1,0},{2,3},{3,2},{4,5},{5,4},{6,7},{7,6},{8,9},{9,8},{10,11... | collective-permute-start | bytes 4718600 | tf_op jit(solution)/shard_map/ppermute | solution.py:576
  572.7 42.1 %all-to-all-start.5 = ((bf16[16,48,1024]{2,1,0:T(8,128)(2,1)}), bf16[16,48,1024]{2,1,0:T(8,128)(2,1)S(1)}, u32[]{:S(2)}, u32[]{:S(2)}) async-start(bf16[16,48,1024]{2,1,0:T(8,128)(2,1)} %bitcast.35), calls=%async_computation.5 | async-start | bytes 3145728 | tf_op jit(solution)/shard_map/all_to_all | solution.py:51
  615.9 5.2 collective-permute-start.22
  637.6 2.7 collective-permute-start.23
  648.4 28.2 %all-to-all-start.6 = ((bf16[16,64,512]{2,1,0:T(8,128)(2,1)}), bf16[16,64,512]{2,1,0:T(8,128)(2,1)S(1)}, u32[]{:S(2)}, u32[]{:S(2)}) async-start(bf16[16,64,512]{2,1,0:T(8,128)(2,1)} %bitcast.174), calls=%async_computation.6 | async-start | bytes 2097152 | tf_op jit(solution)/shard_map/all_to_all | solution.py:879
  652.3 320.9 %reduce-scatter.2.cloned.1.call-start = ((), (), s32[]{:S(2)}) async-start(), calls=%async_computation.10 | async-start | bytes 10027008 | tf_op jit(solution)/shard_map/reduce_scatter | solution.py:888
  655.0 16.1 %collective-permute-start.36 = (bf16[1024,512]{1,0:T(8,128)(2,1)S(1)}, bf16[1024,512]{1,0:T(8,128)(2,1)S(1)}, u32[]{:S(2)}, u32[]{:S(2)}) collective-permute-start(bf16[1024,512]{1,0:T(8,128)(2,1)S(1)} %select_convert_fusion.1), channel_id=1, source_target_pairs={{0,1},{1,0},{2,3},{3,2},{4,5},{5,4},{6,7},{7,6},{8,9},{9,8},{10,11... | collective-permute-start | bytes 3145736 | tf_op jit(solution)/shard_map/ppermute | solution.py:576
  677.4 14.5 %collective-permute-start.24 = (bf16[4,64,512]{2,1,0:T(8,128)(2,1)}, bf16[4,64,512]{2,1,0:T(8,128)(2,1)}, u32[]{:S(2)}, u32[]{:S(2)}) collective-permute-start(bf16[4,64,512]{2,1,0:T(8,128)(2,1)} %slice.317), channel_id=1, source_target_pairs={{1,0},{3,2},{5,4},{7,6},{9,8},{11,10},{13,12},{15,14},{17,16},{19,... | collective-permute-start | bytes 786440 | tf_op jit(solution)/shard_map/ppermute | solution.py:584
  787.3 6.1 collective-permute-start.25
  790.0 4.3 collective-permute-start.26
  908.2 9.0 collective-permute-start.27
  910.1 2.7 collective-permute-start.38
  921.3 18.8 %collective-permute-start.31 = (bf16[4,2,64,768]{3,2,0,1:T(8,128)(2,1)S(1)}, bf16[4,2,64,768]{3,2,0,1:T(8,128)(2,1)S(1)}, u32[]{:S(2)}, u32[]{:S(2)}) collective-permute-start(bf16[4,2,64,768]{3,2,0,1:T(8,128)(2,1)S(1)} %select_bitcast_fusion), channel_id=1, source_target_pairs={{0,4},{2,6},{4,0},{6,2},{8,12},{10,14},{12,8},{14,10},{16,20},{18,... | collective-permute-start | bytes 2359304 | tf_op jit(solution)/shard_map/ppermute | solution.py:613
  922.2 18.7 %collective-permute-start.29 = (bf16[4,2,64,768]{3,2,0,1:T(8,128)(2,1)S(1)}, bf16[4,2,64,768]{3,2,0,1:T(8,128)(2,1)S(1)}, u32[]{:S(2)}, u32[]{:S(2)}) collective-permute-start(bf16[4,2,64,768]{3,2,0,1:T(8,128)(2,1)S(1)} %select_bitcast_fusion.1), channel_id=1, source_target_pairs={{0,2},{2,0},{4,6},{6,4},{8,10},{10,8},{12,14},{14,12},{16,18},{18,... | collective-permute-start | bytes 2359304 | tf_op jit(solution)/shard_map/ppermute | solution.py:613
  926.8 15.2 %collective-permute-start.28 = (bf16[512,1024]{1,0:T(8,128)(2,1)S(1)}, bf16[512,1024]{1,0:T(8,128)(2,1)S(1)}, u32[]{:S(2)}, u32[]{:S(2)}) collective-permute-start(bf16[512,1024]{1,0:T(8,128)(2,1)S(1)} %slice.454), channel_id=1, source_target_pairs={{0,1},{1,0},{2,3},{3,2},{4,5},{5,4},{6,7},{7,6},{8,9},{9,8},{10,11... | collective-permute-start | bytes 3145736 | tf_op jit(solution)/shard_map/ppermute | solution.py:576
  940.5 9.5 collective-permute-start.32
  941.2 9.2 collective-permute-start.30
  950.7 4.6 collective-permute-start.33
  950.7 8.2 collective-permute-start.34
  952.5 17.2 %collective-permute-start.35 = (bf16[64,1536]{1,0:T(8,128)(2,1)S(1)}, bf16[64,1536]{1,0:T(8,128)(2,1)S(1)}, u32[]{:S(2)}, u32[]{:S(2)}) collective-permute-start(bf16[64,1536]{1,0:T(8,128)(2,1)S(1)} %get-tuple-element.108), channel_id=1, source_target_pairs={{0,24},{2,26},{4,28},{6,30},{8,16},{10,18},{12,20},{14,22},{16,8},... | collective-permute-start | bytes 589832 | tf_op jit(solution)/shard_map/ppermute | solution.py:613
  975.2 4.9 collective-permute-start.37
  (98 other events, 1204.1 us)
Sparse Core Ops, SparseCore 0:
  163.5 142.1 all-gather.1
  692.0 210.4 reduce-scatter.1

commit v4 on v3

--- a/solution.py
+++ b/solution.py
@@ -2,6 +2,7 @@
 
 import jax
 import jax.numpy as jnp
+import numpy as np
 from jax import lax
 from jax.experimental import pallas as pl
 from jax.experimental.pallas import tpu as pltpu
@@ -424,42 +425,45 @@
     return lax.dot_general(left, right, (((0,), (0,)), ((), ())), preferred_element_type=F32)
 
 
-def attn_fwd_kernel(plan, own, prompts, out, log_sums, *, head, factor):
+def attn_fwd_kernel(plan, own, prompts, out, log_sums, values, *, head, factor):
     step_id = pl.program_id(0)
     block, full, first = plan[0, step_id], plan[1, step_id], plan[2, step_id]
 
+    def with_ones(value):
+        return jnp.concatenate([value.T, jnp.ones((value.shape[1], head), BF16)], 1)
+
+    @pl.when(step_id == 0)
+    def _():
+        def turn(k, carry):
+            values[k] = with_ones(prompts[k, head : 2 * head, :])
+            return carry
+
+        lax.fori_loop(0, prompts.shape[0], turn, 0)
+
     @pl.when(plan[3, step_id] > 0)
     def _():
-        query = own[block, 0:head, :]
-
-        def tile(key, value, carry, diagonal):
-            scores = dot_tt(key, query) * factor
-            if diagonal:
-                key_at = lax.broadcasted_iota(jnp.int32, scores.shape, 0)
-                query_at = lax.broadcasted_iota(jnp.int32, scores.shape, 1)
-                scores = jnp.where(key_at <= query_at, scores, -1e30)
-            top = jnp.max(scores, 0, keepdims=True)
-            if carry is None:
-                expo = jnp.exp2(scores - top)
-                return top, jnp.sum(expo, 0, keepdims=True), matmul(value, expo.astype(BF16))
-            before, total, result = carry
-            top = jnp.maximum(before, top)
-            expo = jnp.exp2(scores - top)
-            shrink = jnp.exp2(before - top)
-            return (
-                top,
-                total * shrink + jnp.sum(expo, 0, keepdims=True),
-                result * shrink + matmul(value, expo.astype(BF16)),
-            )
-
-        carry = tile(own[block, head : 2 * head, :], own[block, 2 * head : 3 * head, :], None, True)
+        query = own[block, 0:head, :].T
+        scores = matmul(query, own[block, head : 2 * head, :])
+        query_at = lax.broadcasted_iota(jnp.int32, scores.shape, 0)
+        key_at = lax.broadcasted_iota(jnp.int32, scores.shape, 1)
+        scores = jnp.where(key_at <= query_at, scores, -1e30)
+        top = jnp.max(scores, 1, keepdims=True) * factor
+        expo = jnp.exp2(scores * factor - top)
+        result = matmul(expo.astype(BF16), with_ones(own[block, 2 * head : 3 * head, :]))
 
         def step(k, carry):
-            at = first + k
-            return tile(prompts[at, 0:head, :], prompts[at, head : 2 * head, :], carry, False)
-
-        top, total, result = lax.fori_loop(0, full, step, carry)
-        out[block] = (result / total).astype(BF16)
+            before, result = carry
+            scores = matmul(query, prompts[first + k, 0:head, :])
+            top = jnp.maximum(before, jnp.max(scores, 1, keepdims=True) * factor)
+            expo = jnp.exp2(scores * factor - top)
+            result = result * jnp.exp2(before - top) + matmul(expo.astype(BF16), values[first + k])
+            return top, result
+
+        top, result = lax.fori_loop(0, full, step, (top, result))
+        result = result.T
+        total = result[head : head + 1]
+        out[block] = (result[:head] / total).astype(BF16)
+        top = jnp.broadcast_to(top, (top.shape[0], 128)).T[0:1]
         log_sums[block] = top + jnp.log2(total)
 
 
@@ -528,6 +532,7 @@
             grid=(plan.shape[1],),
             in_specs=[whole, whole],
             out_specs=[whole, whole],
+            scratch_shapes=[pltpu.VMEM((prompts.shape[0], length, 2 * head), BF16)],
         ),
         out_shape=[
             jax.ShapeDtypeStruct((blocks, head, length), BF16),
@@ -590,7 +595,7 @@
 
 def keep_rows(value):
     half = value.shape[0] // 2
-    return value[:half] + swap(value[half:].astype(BF16)).astype(F32)
+    return value[:half].astype(F32) + swap(value[half:].astype(BF16)).astype(F32)
 
 
 def pair_parts(value):
@@ -602,11 +607,57 @@
 
 def gelu_pair(preact):
     square = preact * preact
-    tanh = jnp.tanh(preact * (GELU_A + GELU_A * GELU_B * square))
-    half = 0.5 * preact
-    act = half + half * tanh
-    slope = 0.5 + 0.5 * tanh + half * (1.0 - tanh * tanh) * (GELU_A + 3.0 * GELU_A * GELU_B * square)
-    return lax.optimization_barrier((act.astype(BF16), slope.astype(BF16)))
+    gate = 0.5 + 0.5 * jnp.tanh(preact * (GELU_A + GELU_A * GELU_B * square))
+    act = preact * gate
+    slope = gate + act * (1.0 - gate) * (2.0 * GELU_A + 6.0 * GELU_A * GELU_B * square)
+    return act.astype(BF16), slope.astype(BF16)
+
+
+def mlp_kernel(*refs, terms, transposed):
+    ins, (w_in, w_out), outs = refs[:terms], refs[terms : terms + 2], refs[terms + 2 :]
+    rows = ins[0][...]
+    if terms > 1:
+        total = rows.astype(F32)
+        for term in ins[1:]:
+            total = total + term[...].astype(F32)
+        rows = total.astype(BF16)
+        outs[0][...] = rows
+    act, slope = gelu_pair(matmul(rows, w_in[...]))
+    outs[-3][...] = act
+    outs[-2][...] = slope
+    outs[-1][...] = (matmul_nt if transposed else matmul)(act, w_out[...]).astype(BF16)
+
+
+def mlp_forward(terms, w_in, w_out, hidden, length, transposed=False, columns=(0, 0)):
+    rows, width = terms[0].shape
+    steps = rows // length
+    row_block = pl.BlockSpec((length, width), lambda m: (m, 0))
+    turned = pl.BlockSpec((length, width), lambda m: ((m + steps // 2) % steps, 0))
+    hidden_block = pl.BlockSpec((length, hidden), lambda m: (m, 0))
+    once = dict(pipeline_mode=pl.Buffered(1))
+    in_block = pl.BlockSpec((width, hidden), lambda m: (0, columns[0]), **once)
+    out_block = (
+        pl.BlockSpec((width, hidden), lambda m: (0, columns[1]), **once)
+        if transposed
+        else pl.BlockSpec((hidden, width), lambda m: (0, 0), **once)
+    )
+    several = len(terms) > 1
+    return pl.pallas_call(
+        functools.partial(mlp_kernel, terms=len(terms), transposed=transposed),
+        grid=(steps,),
+        in_specs=([row_block, row_block, turned] if several else [row_block]) + [in_block, out_block],
+        out_specs=[row_block] * several + [hidden_block, hidden_block, row_block],
+        out_shape=[jax.ShapeDtypeStruct((rows, width), BF16)] * several
+        + [jax.ShapeDtypeStruct((rows, hidden), BF16)] * 2
+        + [jax.ShapeDtypeStruct((rows, width), BF16)],
+        compiler_params=pltpu.CompilerParams(vmem_limit_bytes=52 * 2**20),
+        cost_estimate=pl.CostEstimate(
+            flops=4 * rows * width * hidden,
+            bytes_accessed=4 * width * hidden + 4 * rows * hidden + 4 * rows * width,
+            transcendentals=rows * hidden,
+        ),
+        name="mlp_fwd",
+    )(*terms, w_in, w_out)
 
 
 def from_bit(value, bit):
@@ -624,18 +675,31 @@
     )
 
 
-def gather_chips(value):
+def gather_line(value):
     planes = lax.axis_size("dp") // 4
-    half = value.shape[1] // 2
-    z, y, x = chip_place()
+    z = chip_place()[0]
     blocks = jnp.stack([value] + [from_bit(value, 4 * k) for k in range(1, planes)])
-    line = jnp.stack(
+    return jnp.stack(
         [lax.dynamic_index_in_dim(blocks, z ^ k, 0, keepdims=False) for k in range(planes)]
     )
-    first, second = line[:, :, :half], line[:, :, half:]
+
+
+def gather_second(line):
+    half = line.shape[-1] // 2
+    y, x = chip_place()[1:]
+    first, second = line[..., :half], line[..., half:]
     first = ordered(y, first, from_bit(first, 2), 1)
     second = ordered(x, second, from_bit(second, 1), 1)
-    return ordered(x, first, from_bit(first, 1), 2), ordered(y, second, from_bit(second, 2), 1)
+    return first, second
+
+
+def gather_third(first, second, cuts):
+    y, x = chip_place()[1:]
+    first_other, second_other = from_bit(first, 1), from_bit(second, 2)
+    return (
+        [ordered(x, first[at], first_other[at], 2) for at in cuts],
+        [ordered(y, second[at], second_other[at], 1) for at in cuts],
+    )
 
 
 def halve(value, bit, axis, partner):
@@ -689,6 +753,7 @@
     shard = w_query.shape[0]
     half_heads = w_query.shape[1] // HEAD
     hidden = w_ffn_in.shape[1]
+    assert expert_in_a.shape[2] == hidden
     triple = 3 * HEAD
     heads = 2 * half_heads
     both = lambda lower, upper: (jnp.where(core_zero, lower, upper), jnp.where(core_zero, upper, lower))
@@ -714,11 +779,19 @@
     ).reshape(shard, half_heads * triple)
     extra = jnp.concatenate([norm1_gain, norm2_gain, counts_pair], 0)
     extra = jnp.pad(extra[None, :], ((0, 7), (0, half_heads * triple - extra.shape[0])))
-    first_all, last_all = gather_chips(jnp.concatenate([qkv_shard, extra], 0))
-    qkv_full = jnp.concatenate([first_all[..., :shard, :], last_all[..., :shard, :]], -1).reshape(
-        width, half_heads * triple
-    )
-    extra_all = first_all[..., shard, :].reshape(experts, -1)
+    line_one = gather_line(jnp.concatenate([qkv_shard, extra], 0))
+    second_all = lax.all_gather(
+        jnp.concatenate([w_ffn_in, w_ffn_out.T, w_attn_out.T], 1), "dp", axis=0, tiled=True
+    )
+    ffn_in = second_all[:, :hidden]
+    ffn_out_t = second_all[:, hidden : 2 * hidden]
+    attn_half = second_all[:, 2 * hidden :]
+    weight_rows, extra_row = np.s_[..., :shard, :], np.s_[..., shard, :]
+    (first_all, extra_all), (last_all, unused) = gather_third(
+        *gather_second(line_one), (weight_rows, extra_row)
+    )
+    qkv_full = jnp.concatenate([first_all, last_all], -1).reshape(width, half_heads * triple)
+    extra_all = extra_all.reshape(experts, -1)
     gain_one = extra_all[:, :shard].reshape(width).astype(F32)
     gain_two = extra_all[:, shard : 2 * shard].reshape(width).astype(F32)
     counts_all = extra_all[:, 2 * shard : 2 * shard + 2 * experts].reshape(experts, 2, experts)
@@ -756,16 +829,6 @@
     ).astype(BF16)
     qkv_t = jnp.concatenate(both(own_t, swap(other_t)), 0).reshape(heads, triple, rows)
     by_head = lax.all_to_all(qkv_t, "dp", split_axis=0, concat_axis=0, tiled=True)
-
-    second_shard = jnp.concatenate([w_ffn_in, w_ffn_out.T, w_attn_out.T], 1)
-    by_head, second_shard = lax.optimization_barrier((by_head, second_shard))
-    second_all = lax.all_gather(
-        second_shard, "dp", axis=0, tiled=True
-    )
-    ffn_in = second_all[:, :hidden]
-    ffn_out_t = second_all[:, hidden : 2 * hidden]
-    attn_half = second_all[:, 2 * hidden :]
-
 
     lent = experts // 4
     span = PLEN // rows
@@ -805,8 +868,10 @@
     )
     normed_two, hat_two, inv_two = norm_forward(hidden_one, gain_two)
     rows_two = with_other(normed_two.astype(BF16))
-    ffn_act, ffn_slope = gelu_pair(matmul(rows_two, ffn_in))
-    hidden_two = hidden_one + keep_rows(matmul_nt(ffn_act, ffn_out_t))
+    ffn_act, ffn_slope, ffn_sum = mlp_forward(
+        [rows_two], second_all, second_all, hidden, rows, transposed=True, columns=(0, 1)
+    )
+    hidden_two = hidden_one + keep_rows(ffn_sum)
 
     sent_rows = (
         matmul_tn(placer, hidden_two.astype(BF16)).astype(BF16).reshape(experts, slots_per, width)
@@ -817,15 +882,16 @@
     expert_rows = with_other(own_rows.reshape(-1, width))
     centre = centroids[0]
     gate_value = jax.nn.sigmoid(matmul(expert_rows, centre))
-    act_a, slope_a = gelu_pair(matmul(expert_rows, expert_in_a[0]))
-    part_a, other_a = pair_parts(matmul(act_a, expert_out_a[0]))
-    middle = (expert_rows.astype(F32) + part_a.astype(F32) + other_a.astype(F32)).astype(BF16)
-    act_b, slope_b = gelu_pair(matmul(middle, expert_in_b[0]))
-    act_b, grad_own = lax.optimization_barrier((act_b, grad_own))
+    act_a, slope_a, part_a = mlp_forward(
+        [expert_rows], expert_in_a[0], expert_out_a[0], hidden, half_rows // 2
+    )
+    from_a = swap(part_a)
+    middle, act_b, slope_b, part_b = mlp_forward(
+        [expert_rows, part_a, from_a], expert_in_b[0], expert_out_b[0], hidden, half_rows // 2
+    )
+    part_b, grad_own = lax.optimization_barrier((part_b, grad_own))
     branch_half = (
-        part_a[:half_rows].astype(F32)
-        + other_a[:half_rows].astype(F32)
-        + keep_rows(matmul(act_b, expert_out_b[0]))
+        part_a[:half_rows].astype(F32) + from_a[half_rows:].astype(F32) + keep_rows(part_b)
     )
     gate_half = gate_value[:half_rows]
     returned = (
@@ -851,16 +917,14 @@
         + other_m[:half_rows].astype(F32)
         + grad_logit_half[:, None] * centre.astype(F32)[None, :]
     )
-    grad_out_b = matmul_tn(act_b, grad_b)
-    grad_in_b = matmul_tn(middle, grad_pre_b)
+    grad_rows, came_back, act_a, grad_a, expert_rows, grad_pre_a = lax.optimization_barrier(
+        (grad_rows.astype(BF16), came_back, act_a, grad_a, expert_rows, grad_pre_a)
+    )
     grad_out_a = matmul_tn(act_a, grad_a)
     grad_in_a = matmul_tn(expert_rows, grad_pre_a)
-    grad_rows, came_back = lax.optimization_barrier((grad_rows.astype(BF16), came_back))
     output = hidden_two + matmul(placer, came_back)
     grad_back = to_experts(grad_rows.reshape(experts, slots_per, width))
-    grad_back, grad_out_b, grad_in_b, grad_out_a, grad_in_a = lax.optimization_barrier(
-        (grad_back, grad_out_b, grad_in_b, grad_out_a, grad_in_a)
-    )
+    grad_back, grad_out_a, grad_in_a = lax.optimization_barrier((grad_back, grad_out_a, grad_in_a))
     grad_back = grad_back.reshape(half_rows, width)
     grad_two = grad_out.astype(F32) + matmul(placer, grad_back)
 
@@ -885,14 +949,11 @@
     half_width = width // 2
     part_own, part_other = both(grad_attn_out[:, :half_width], grad_attn_out[:, half_width:])
     grad_attn_half = part_own + swap(part_other.astype(BF16)).astype(F32)
-    second_sum = lax.psum_scatter(
-        jnp.concatenate(
-            [grad_ffn_in.astype(BF16), grad_ffn_out_t.astype(BF16), grad_attn_half.astype(BF16)], 1
-        ),
-        "dp",
-        scatter_dimension=0,
-        tiled=True,
-    ).astype(F32)
+    second_part = jnp.concatenate(
+        [grad_ffn_in.astype(BF16), grad_ffn_out_t.astype(BF16), grad_attn_half.astype(BF16)], 1
+    )
+    grad_by_head, second_part = lax.optimization_barrier((grad_by_head, second_part))
+    second_sum = lax.psum_scatter(second_part, "dp", scatter_dimension=0, tiled=True).astype(F32)
     grad_blocks = jnp.concatenate([grad_by_head, to_core_zero(grad_by_head[:lent])], 0)
     grad_own_blocks, grad_prompts = attn_backward(
         plan, own_blocks, prompt_kv, grad_blocks, attn_blocks, log_sums
@@ -907,9 +968,14 @@
         1,
     )
     cont_part = jnp.concatenate([lent_grad, grad_own_blocks[lent:experts]], 0)
-    grad_qkv = lax.all_to_all(
-        jnp.where(core_zero, prompt_part, cont_part), "dp", split_axis=0, concat_axis=0, tiled=True
-    ).reshape(2, half_heads * triple, rows)
+    grad_head, act_b, grad_b, middle, grad_pre_b = lax.optimization_barrier(
+        (jnp.where(core_zero, prompt_part, cont_part), act_b, grad_b, middle, grad_pre_b)
+    )
+    grad_qkv = lax.all_to_all(grad_head, "dp", split_axis=0, concat_axis=0, tiled=True)
+    grad_out_b = matmul_tn(act_b, grad_b)
+    grad_in_b = matmul_tn(middle, grad_pre_b)
+    grad_qkv, grad_out_b, grad_in_b = lax.optimization_barrier((grad_qkv, grad_out_b, grad_in_b))
+    grad_qkv = grad_qkv.reshape(2, half_heads * triple, rows)
     keep_half, send_half = both(grad_qkv[0], grad_qkv[1])
     grad_qkv_t = jnp.concatenate([keep_half, swap(send_half)], 1)
     grad_qkv_w = lax.dot_general(

time: 998 us -> 1000 us (level)
  matrix products: 226 us -> 155 us
  Pallas kernels: 167 us -> 217 us
  blocking collectives: 112 us -> 133 us
    dot_general x11 -> x6, matrix products: 84.2 us -> 19.2 us  [matmul(): return jnp.dot(left, right, preferred_element_type=jnp.float32)]
    pallas_call x0 -> x3, Pallas kernels: none -> 55.8 us  [mlp_forward(): pl.pallas_call(functools.partial(mlp_kernel, terms=len(terms), transposed...]
    all_gather x1, waiting for transfers between devices: 47.8 us -> 0.01 us  [body_paired(): lax.all_gather(jnp.concatenate([w_ffn_in, w_ffn_out.T, w_attn_out.T], 1),...]
    all_to_all x1, blocking collectives: 112 us -> 133 us  [body_paired(): lax.all_to_all(qkv_t, 'dp', split_axis=0, concat_axis=0, tiled=True)]
    all_to_all x1, waiting for transfers between devices: 0.01 us -> 15.8 us  [body_paired(): lax.all_to_all(attn_own, 'dp', split_axis=0, concat_axis=0, tiled=True)]
    all_to_all x1, waiting for transfers between devices: 66 us -> 79.5 us  [body_paired(): lax.all_to_all(grad_head, 'dp', split_axis=0, concat_axis=0, tiled=True)]
    dot_general x6 -> x5, matrix products: 53.9 us -> 49.3 us  [matmul_nt(): lax.dot_general(left, right, (((1,), (1,)), ((), ())), preferred_element_...]
  transfers between devices with their start and end apart: 48 -> 48, of which waited for: 28 -> 30; matrix products, arithmetic and copies ran while one was open for 23% -> 19% of each run, Pallas kernels for 17% -> 18%
where the time goes in v4:
time: 1000 us; the launch traced here: 989 us
  waiting for transfers between devices  272 us (27%)
  Pallas kernels  217 us (22%)
  matrix products  155 us (16%)
  blocking collectives  133 us (13%)
  starting transfers between devices  89.2 us (9%)
  other arithmetic  71.2 us (7%)
  local copies, waits for them, and re-layouts  36.7 us (4%)
  between operations  15.7 us (2%)
    all_to_all x1, blocking collectives, body_paired(): lax.all_to_all(qkv_t, 'dp', split_axis=0, concat_axis=0, tiled=True)  133 us
    pallas_call x1, Pallas kernels, attn_backward(): pl.pallas_call(functools.partial(attn_bwd_kernel, head=head, factor=head...  93.7 us
    ppermute x14, waiting for transfers between devices, from_bit(): lax.ppermute(value, 'dp', [(i, i ^ bit) for i in range(lax.axis_size('dp'...  79.8 us
    all_to_all x1, waiting for transfers between devices, body_paired(): lax.all_to_all(grad_head, 'dp', split_axis=0, concat_axis=0, tiled=True)  79.5 us
    dot_general x8, matrix products, matmul_tn(): lax.dot_general(left, right, (((0,), (0,)), ((), ())), preferred_element_...  67.4 us
    pallas_call x1, Pallas kernels, attn_forward(): pl.pallas_call(functools.partial(attn_fwd_kernel, head=head, factor=head...  67.3 us
    all_to_all x4, waiting for transfers between devices, to_experts(): return lax.all_to_all(value, 'dp', split_axis=0, concat_axis=0, tiled=True)  58.5 us
    pallas_call x3, Pallas kernels, mlp_forward(): pl.pallas_call(functools.partial(mlp_kernel, terms=len(terms), transposed...  55.8 us
  transfers between devices with their start and end apart: 48, of which 30 were waited for; matrix products, arithmetic and copies ran while one was open for 19% of the time, Pallas kernels for 18%

profile of v4, /device:TPU:9, one launch (start us, length us, event | category | flops | bytes accessed | tf_op | source)
XLA Modules:
  0.0 989.0 jit_solution(9262767838735227470)
XLA Ops:
  17.8 5.9 collective-permute-done.2
  23.7 7.0 collective-permute-done.3
  30.7 5.8 collective-permute-done.4
  41.2 7.5 collective-permute-done.5
  54.1 20.4 %collective-permute-done.6 = bf16[4,2,72,768]{3,2,0,1:T(8,128)(2,1)S(1)} collective-permute-done((bf16[4,2,72,768]{3,2,0,1:T(8,128)(2,1)S(1)}, bf16[4,2,72,768]{3,2,0,1:T(8,128)(2,1)S(1)}, u32[]{:S(2)}, u32[]{:S(2)}) %collective-permute-start.6) | collective-permute-done | bytes 884768 | tf_op jit(solution)/shard_map/ppermute | solution.py:664
  89.6 132.6 %all_to_all.40 = bf16[16,192,512]{2,1,0:T(8,128)(2,1)S(1)} all-to-all(bf16[16,192,512]{2,1,0:T(8,128)(2,1)S(1)} %bitcast.138), channel_id=1, replica_groups=mesh['dp'=16,'tensor'=2] {'dp'}, dimensions={0} | all-to-all | bytes 6291456 | tf_op jit(solution)/shard_map/all_to_all | solution.py:831
  230.8 67.3 %attn_fwd.1 = (bf16[20,64,512]{2,1,0:T(8,128)(2,1)S(1)}, f32[20,1,512]{2,1,0:T(1,128)S(1)}) custom-call(s32[4,20]{1,0:T(4,128)S(1)} %add_select_fusion.2.plan, bf16[20,192,512]{2,1,0:T(8,128)(2,1)S(1)} %constant_dynamic-update-slice_fusion.own, bf16[16,128,512]{2,1,0:T(8,128)(2,1)S(1)} %broadcast_select_fusion.prompts), custom_call_target="tpu_custom_call" | custom-call | flops 26843545600 | bytes 8388608 | tf_op jit(solution)/shard_map/attn_fwd/pallas_call | solution.py:528
  304.1 5.1 all-to-all-start.1
  317.8 15.8 %all-to-all-done.1 = bf16[16,64,512]{2,1,0:T(8,128)(2,1)S(1)} async-done(((bf16[16,64,512]{2,1,0:T(8,128)(2,1)}), bf16[16,64,512]{2,1,0:T(8,128)(2,1)S(1)}, u32[]{:S(2)}, u32[]{:S(2)}) %all-to-all-start.1) | async-done | bytes 1048608 | tf_op jit(solution)/shard_map/all_to_all | solution.py:861
  333.6 4.0 fusion.75
  345.4 14.9 %mlp_fwd.3 = (bf16[1024,2048]{1,0:T(8,128)(2,1)}, bf16[1024,2048]{1,0:T(8,128)(2,1)}, bf16[1024,1024]{1,0:T(8,128)(2,1)}) custom-call(bf16[1024,1024]{1,0:T(8,128)(2,1)} %pad_maximum_fusion.7.refs_0_, bf16[1024,4608]{1,0:T(8,128)(2,1)} %all-gather.2.cloned.1.call-done.refs_1_.refs_2_, bf16[1024,4608]{1,0:T(8,128)(2,1)} %all-gather.2.cloned.1.call-done.refs_1_.refs_2_), custom_call_target="tpu_custom_call" | custom-call | flops 8589934592 | bytes 20971520 | tf_op jit(solution)/shard_map/mlp_fwd/pallas_call | solution.py:645
  368.3 4.8 all-to-all-start.2
  376.6 32.2 %all-to-all-done.2 = bf16[16,48,1024]{2,1,0:T(8,128)(2,1)} async-done(((bf16[16,48,1024]{2,1,0:T(8,128)(2,1)}), bf16[16,48,1024]{2,1,0:T(8,128)(2,1)}, u32[]{:S(2)}, u32[]{:S(2)}) %all-to-all-start.2) | async-done | bytes 1572896 | tf_op jit(solution)/shard_map/all_to_all | solution.py:52
  418.4 19.8 %mlp_fwd.4 = (bf16[1536,2048]{1,0:T(8,128)(2,1)}, bf16[1536,2048]{1,0:T(8,128)(2,1)}, bf16[1536,1024]{1,0:T(8,128)(2,1)}) custom-call(bf16[1536,1024]{1,0:T(8,128)(2,1)} %pad_maximum_fusion.3.refs_0_, bf16[1024,2048]{1,0:T(8,128)(2,1)} %bitcast.177, bf16[2048,1024]{1,0:T(8,128)(2,1)} %bitcast.176), custom_call_target="tpu_custom_call" | custom-call | flops 12884901888 | bytes 27262976 | tf_op jit(solution)/shard_map/mlp_fwd/pallas_call | solution.py:645
  438.6 4.9 all-to-all-start.3
  444.2 21.0 %mlp_fwd.5 = (bf16[1536,1024]{1,0:T(8,128)(2,1)}, bf16[1536,2048]{1,0:T(8,128)(2,1)}, bf16[1536,2048]{1,0:T(8,128)(2,1)}, bf16[1536,1024]{1,0:T(8,128)(2,1)}) custom-call(bf16[1536,1024]{1,0:T(8,128)(2,1)} %pad_maximum_fusion.3.refs_0_, bf16[1536,1024]{1,0:T(8,128)(2,1)} %get-tuple-element.55.refs_1_, bf16[1536,1024]{1,0:T(8,128)(2,1)} %collective-permute-done.17.refs_2_, ...), custom_call_target="tpu_custom_call" | custom-call | flops 12884901888 | bytes 27262976 | tf_op jit(solution)/shard_map/mlp_fwd/pallas_call | solution.py:645
  465.3 13.8 %all-to-all-done.3 = bf16[16,48,1024]{2,1,0:T(8,128)(2,1)} async-done(((bf16[16,48,1024]{2,1,0:T(8,128)(2,1)}), bf16[16,48,1024]{2,1,0:T(8,128)(2,1)}, u32[]{:S(2)}, u32[]{:S(2)}) %all-to-all-start.3) | async-done | bytes 1572896 | tf_op jit(solution)/shard_map/all_to_all | solution.py:52
  485.1 4.9 fusion
  490.1 11.9 %multiply_convert_fusion.1 = bf16[1536,2048]{1,0:T(8,128)(2,1)} fusion(bf16[1536,2048]{1,0:T(8,128)(2,1)} %get-tuple-element.59, bf16[1536,1024]{1,0:T(8,128)(2,1)S(1)} %get-tuple-element.80, bf16[1,2048,1024]{2,1,0:T(8,128)(2,1)S(1)} %copy-done.65), kind=kOutput, calls=%fused_computation.1 | convolution fusion | flops 6451888128 | bytes 19922944 | tf_op jit(solution)/shard_map/dot_general | solution.py:66
  502.0 10.3 %convolution_convert_fusion = bf16[1536,1024]{1,0:T(8,128)(2,1)} fusion(bf16[1536,2048]{1,0:T(8,128)(2,1)} %multiply_convert_fusion.1, bf16[1,1024,2048]{2,1,0:T(8,128)(2,1)S(1)} %copy-done.66), kind=kOutput, calls=%fused_computation.14 | convolution fusion | flops 6444023808 | bytes 13631488 | tf_op jit(solution)/shard_map/dot_general | solution.py:66
  514.1 6.4 collective-permute-done.21
  520.5 5.1 select_convert_fusion
  525.6 4.9 all-to-all-start.4
  533.3 7.1 add_convert_fusion
  540.4 11.8 %multiply_convert_fusion = bf16[1536,2048]{1,0:T(8,128)(2,1)} fusion(bf16[1536,2048]{1,0:T(8,128)(2,1)} %get-tuple-element.60, bf16[1536,1024]{1,0:T(8,128)(2,1)S(1)} %add_convert_fusion, bf16[1,2048,1024]{2,1,0:T(8,128)(2,1)S(1)} %copy-done.67), kind=kOutput, calls=%fused_computation | convolution fusion | flops 6451888128 | bytes 19922944 | tf_op jit(solution)/shard_map/dot_general | solution.py:66
  552.2 8.8 fusion.67
  569.2 5.3 fusion.7
  574.6 6.9 all-to-all-start.5
  581.5 12.0 %fusion.78 = f32[1024,2048]{1,0:T(8,128)} fusion(bf16[1536,1024]{1,0:T(8,128)(2,1)} %pad_maximum_fusion.3.refs_0_, bf16[1536,2048]{1,0:T(8,128)(2,1)} %multiply_convert_fusion), kind=kOutput, calls=%fused_computation.233 | convolution fusion | flops 6442450944 | bytes 17825792 | tf_op jit(solution)/shard_map/dot_general | solution.py:60
  593.5 11.2 %fusion.77 = f32[2048,1024]{1,0:T(8,128)} fusion(bf16[1536,2048]{1,0:T(8,128)(2,1)} %get-tuple-element.65, bf16[1536,1024]{1,0:T(8,128)(2,1)S(1)} %copy-done.24), kind=kOutput, calls=%fused_computation.232 | convolution fusion | flops 6442450944 | bytes 17825792 | tf_op jit(solution)/shard_map/dot_general | solution.py:60
  604.6 12.4 %all-to-all-done.5 = bf16[16,48,1024]{2,1,0:T(8,128)(2,1)} async-done(((bf16[16,48,1024]{2,1,0:T(8,128)(2,1)}), bf16[16,48,1024]{2,1,0:T(8,128)(2,1)}, u32[]{:S(2)}, u32[]{:S(2)}) %all-to-all-start.5) | async-done | bytes 1572896 | tf_op jit(solution)/shard_map/all_to_all | solution.py:52
  624.4 8.2 multiply_convert_fusion.2
  632.6 6.5 fusion.1
  639.8 6.3 convolution_convert_fusion.3
  654.8 4.6 all-to-all-start.6
  659.5 7.5 convolution_convert_fusion.2
  669.5 5.7 pad_maximum_fusion
  675.2 8.7 all-to-all-done.6
  685.6 5.0 collective-permute-start.25
  692.8 93.7 %attn_bwd.1 = (bf16[20,192,512]{2,1,0:T(8,128)(2,1)}, bf16[16,128,512]{2,1,0:T(8,128)(2,1)S(1)}) custom-call(s32[4,20]{1,0:T(4,128)S(1)} %copy-done.5, bf16[20,192,512]{2,1,0:T(8,128)(2,1)} %copy-done, bf16[16,128,512]{2,1,0:T(8,128)(2,1)} %copy-done.1, bf16[20,64,512]{2,1,0:T(8,128)(2,1)S(1)} %pad_maximum_fusion.17.grad, ...), custom_call_target="tpu_custom_call" | custom-call | flops 67108864000 | bytes 16777216 | tf_op jit(solution)/shard_map/attn_bwd/pallas_call | solution.py:555
  797.4 4.8 all-to-all-start.7
  802.2 12.0 %fusion.80 = f32[1024,2048]{1,0:T(8,128)} fusion(bf16[1536,1024]{1,0:T(8,128)(2,1)} %get-tuple-element.81, bf16[1536,2048]{1,0:T(8,128)(2,1)} %multiply_convert_fusion.1), kind=kOutput, calls=%fused_computation.235 | convolution fusion | flops 6442450944 | bytes 17825792 | tf_op jit(solution)/shard_map/dot_general | solution.py:60
  814.2 11.1 %fusion.79 = f32[2048,1024]{1,0:T(8,128)} fusion(bf16[1536,2048]{1,0:T(8,128)(2,1)} %get-tuple-element.79, bf16[1536,1024]{1,0:T(8,128)(2,1)S(1)} %copy-done.22), kind=kOutput, calls=%fused_computation.234 | convolution fusion | flops 6442450944 | bytes 17825792 | tf_op jit(solution)/shard_map/dot_general | solution.py:60
  825.3 79.5 %all-to-all-done.7 = bf16[16,192,512]{2,1,0:T(8,128)(2,1)} async-done(((bf16[16,192,512]{2,1,0:T(8,128)(2,1)}), bf16[16,192,512]{2,1,0:T(8,128)(2,1)}, u32[]{:S(2)}, u32[]{:S(2)}) %all-to-all-start.7) | async-done | bytes 3145760 | tf_op jit(solution)/shard_map/all_to_all | solution.py:974
  929.0 12.0 %collective-permute-done.32 = bf16[4,2,64,768]{3,2,0,1:T(8,128)(2,1)S(1)} collective-permute-done((bf16[4,2,64,768]{3,2,0,1:T(8,128)(2,1)S(1)}, bf16[4,2,64,768]{3,2,0,1:T(8,128)(2,1)S(1)}, u32[]{:S(2)}, u32[]{:S(2)}) %collective-permute-start.32) | collective-permute-done | bytes 786464 | tf_op jit(solution)/shard_map/ppermute | solution.py:664
  944.4 6.8 collective-permute-done.33
  956.5 4.5 collective-permute-done.35
  961.0 9.4 collective-permute-done.36
  (386 shorter events, 185.2 us)
Async XLA Ops:
  7.2 302.0 %all-gather.2.cloned.1.call-start = ((), (), s32[]{:S(2)}) async-start(), calls=%async_computation.9 | async-start | bytes 10027008 | tf_op jit(solution)/shard_map/all_gather | solution.py:783
  8.1 5.3 collective-permute-start.1
  14.2 9.4 collective-permute-start.2
  14.3 16.4 %collective-permute-start.3 = (bf16[72,1536]{1,0:T(8,128)(2,1)S(1)}, bf16[72,1536]{1,0:T(8,128)(2,1)S(1)}, u32[]{:S(2)}, u32[]{:S(2)}) collective-permute-start(bf16[72,1536]{1,0:T(8,128)(2,1)S(1)} %get-tuple-element.130), channel_id=1, source_target_pairs={{0,16},{2,18},{4,20},{6,22},{8,24},{10,26},{12,28},{14,30},{16,0},... | collective-permute-start | bytes 663560 | tf_op jit(solution)/shard_map/ppermute | solution.py:664
  16.8 19.7 %collective-permute-start.4 = (bf16[72,1536]{1,0:T(8,128)(2,1)S(1)}, bf16[72,1536]{1,0:T(8,128)(2,1)S(1)}, u32[]{:S(2)}, u32[]{:S(2)}) collective-permute-start(bf16[72,1536]{1,0:T(8,128)(2,1)S(1)} %get-tuple-element.130), channel_id=1, source_target_pairs={{0,24},{2,26},{4,28},{6,30},{8,16},{10,18},{12,20},{14,22},{16,8},... | collective-permute-start | bytes 663560 | tf_op jit(solution)/shard_map/ppermute | solution.py:664
  16.9 36.0 %collective-permute-start = (bf16[512,1024]{1,0:T(8,128)(2,1)S(1)}, bf16[512,1024]{1,0:T(8,128)(2,1)S(1)}, u32[]{:S(2)}, u32[]{:S(2)}) collective-permute-start(bf16[512,1024]{1,0:T(8,128)(2,1)S(1)} %copy-done.12), channel_id=1, source_target_pairs={{0,1},{1,0},{2,3},{3,2},{4,5},{5,4},{6,7},{7,6},{8,9},{9,8},{10,11... | collective-permute-start | bytes 3145736 | tf_op jit(solution)/shard_map/ppermute | solution.py:581
  37.9 10.9 %collective-permute-start.5 = (bf16[4,72,768]{2,1,0:T(8,128)(2,1)}, bf16[4,72,768]{2,1,0:T(8,128)(2,1)}, u32[]{:S(2)}, u32[]{:S(2)}) collective-permute-start(bf16[4,72,768]{2,1,0:T(8,128)(2,1)} %get-tuple-element.121), channel_id=1, source_target_pairs={{0,4},{2,6},{4,0},{6,2},{8,12},{10,14},{12,8},{14,10},{16,20},{18,... | collective-permute-start | bytes 1327112 | tf_op jit(solution)/shard_map/ppermute | solution.py:664
  39.1 12.3 %collective-permute-start.7 = (bf16[4,72,768]{2,1,0:T(8,128)(2,1)}, bf16[4,72,768]{2,1,0:T(8,128)(2,1)S(1)}, u32[]{:S(2)}, u32[]{:S(2)}) collective-permute-start(bf16[4,72,768]{2,1,0:T(8,128)(2,1)} %get-tuple-element.120), channel_id=1, source_target_pairs={{0,2},{2,0},{4,6},{6,4},{8,10},{10,8},{12,14},{14,12},{16,18},{18,... | collective-permute-start | bytes 1327112 | tf_op jit(solution)/shard_map/ppermute | solution.py:664
  50.1 24.3 %collective-permute-start.6 = (bf16[4,2,72,768]{3,2,0,1:T(8,128)(2,1)S(1)}, bf16[4,2,72,768]{3,2,0,1:T(8,128)(2,1)S(1)}, u32[]{:S(2)}, u32[]{:S(2)}) collective-permute-start(bf16[4,2,72,768]{3,2,0,1:T(8,128)(2,1)S(1)} %maximum_select_fusion.4), channel_id=1, source_target_pairs={{0,2},{2,0},{4,6},{6,4},{8,10},{10,8},{12,14},{14,12},{16,18},{18,... | collective-permute-start | bytes 2654216 | tf_op jit(solution)/shard_map/ppermute | solution.py:664
  51.5 24.5 %collective-permute-start.8 = (bf16[4,2,72,768]{3,2,0,1:T(8,128)(2,1)S(1)}, bf16[4,2,72,768]{3,2,0,1:T(8,128)(2,1)S(1)}, u32[]{:S(2)}, u32[]{:S(2)}) collective-permute-start(bf16[4,2,72,768]{3,2,0,1:T(8,128)(2,1)S(1)} %maximum_select_fusion.5), channel_id=1, source_target_pairs={{0,4},{2,6},{4,0},{6,2},{8,12},{10,14},{12,8},{14,10},{16,20},{18,... | collective-permute-start | bytes 2654216 | tf_op jit(solution)/shard_map/ppermute | solution.py:664
  83.0 4.5 collective-permute-start.9
  222.4 6.5 collective-permute-start.11
  223.8 5.1 collective-permute-start.10
  298.1 4.8 collective-permute-start.12
  304.1 29.6 %all-to-all-start.1 = ((bf16[16,64,512]{2,1,0:T(8,128)(2,1)}), bf16[16,64,512]{2,1,0:T(8,128)(2,1)S(1)}, u32[]{:S(2)}, u32[]{:S(2)}) async-start(bf16[16,64,512]{2,1,0:T(8,128)(2,1)} %pad_maximum_fusion.18), calls=%async_computation.1 | async-start | bytes 2097152 | tf_op jit(solution)/shard_map/all_to_all | solution.py:861
  311.5 3.3 collective-permute-start.13
  338.4 4.6 collective-permute-start.14
  361.6 2.7 collective-permute-start.15
  368.3 40.6 %all-to-all-start.2 = ((bf16[16,48,1024]{2,1,0:T(8,128)(2,1)}), bf16[16,48,1024]{2,1,0:T(8,128)(2,1)}, u32[]{:S(2)}, u32[]{:S(2)}) async-start(bf16[16,48,1024]{2,1,0:T(8,128)(2,1)} %bitcast.152), calls=%async_computation.2 | async-start | bytes 3145728 | tf_op jit(solution)/shard_map/all_to_all | solution.py:52
  408.8 5.7 collective-permute-start.16
  438.2 6.0 collective-permute-start.17
  438.6 40.5 %all-to-all-start.3 = ((bf16[16,48,1024]{2,1,0:T(8,128)(2,1)}), bf16[16,48,1024]{2,1,0:T(8,128)(2,1)}, u32[]{:S(2)}, u32[]{:S(2)}) async-start(bf16[16,48,1024]{2,1,0:T(8,128)(2,1)} %bitcast.151), calls=%async_computation.3 | async-start | bytes 3145728 | tf_op jit(solution)/shard_map/all_to_all | solution.py:52
  479.1 6.0 collective-permute-start.18
  512.3 18.2 %collective-permute-start.19 = (bf16[1536,1024]{1,0:T(8,128)(2,1)}, bf16[1536,1024]{1,0:T(8,128)(2,1)}, u32[]{:S(2)}, u32[]{:S(2)}) collective-permute-start(bf16[1536,1024]{1,0:T(8,128)(2,1)} %convolution_convert_fusion), channel_id=1, source_target_pairs={{0,1},{1,0},{2,3},{3,2},{4,5},{5,4},{6,7},{7,6},{8,9},{9,8},{10,11... | collective-permute-start | bytes 9437192 | tf_op jit(solution)/shard_map/ppermute | solution.py:581
  513.5 7.0 collective-permute-start.21
  525.6 49.0 %all-to-all-start.4 = ((bf16[16,48,1024]{2,1,0:T(8,128)(2,1)}), bf16[16,48,1024]{2,1,0:T(8,128)(2,1)}, u32[]{:S(2)}, u32[]{:S(2)}) async-start(bf16[16,48,1024]{2,1,0:T(8,128)(2,1)} %bitcast.139), calls=%async_computation.4 | async-start | bytes 3145728 | tf_op jit(solution)/shard_map/all_to_all | solution.py:52
  565.2 4.1 collective-permute-start.20
  574.6 42.5 %all-to-all-start.5 = ((bf16[16,48,1024]{2,1,0:T(8,128)(2,1)}), bf16[16,48,1024]{2,1,0:T(8,128)(2,1)}, u32[]{:S(2)}, u32[]{:S(2)}) async-start(bf16[16,48,1024]{2,1,0:T(8,128)(2,1)} %bitcast.140), calls=%async_computation.5 | async-start | bytes 3145728 | tf_op jit(solution)/shard_map/all_to_all | solution.py:52
  619.7 4.8 collective-permute-start.22
  639.3 6.8 collective-permute-start.23
  650.7 16.4 %collective-permute-start.24 = (bf16[1024,512]{1,0:T(8,128)(2,1)}, bf16[1024,512]{1,0:T(8,128)(2,1)}, u32[]{:S(2)}, u32[]{:S(2)}) collective-permute-start(bf16[1024,512]{1,0:T(8,128)(2,1)} %select_convert_fusion.1), channel_id=1, source_target_pairs={{0,1},{1,0},{2,3},{3,2},{4,5},{5,4},{6,7},{7,6},{8,9},{9,8},{10,11... | collective-permute-start | bytes 3145736 | tf_op jit(solution)/shard_map/ppermute | solution.py:581
  654.8 29.1 %all-to-all-start.6 = ((bf16[16,64,512]{2,1,0:T(8,128)(2,1)}), bf16[16,64,512]{2,1,0:T(8,128)(2,1)S(1)}, u32[]{:S(2)}, u32[]{:S(2)}) async-start(bf16[16,64,512]{2,1,0:T(8,128)(2,1)} %bitcast.156), calls=%async_computation.6 | async-start | bytes 2097152 | tf_op jit(solution)/shard_map/all_to_all | solution.py:943
  659.4 314.5 %reduce-scatter.2.cloned.1.call-start = ((), (), s32[]{:S(2)}) async-start(), calls=%async_computation.10 | async-start | bytes 10027008 | tf_op jit(solution)/shard_map/reduce_scatter | solution.py:956
  685.6 5.8 collective-permute-start.25
  786.5 7.5 collective-permute-start.26
  790.7 4.3 collective-permute-start.27
  797.4 107.4 %all-to-all-start.7 = ((bf16[16,192,512]{2,1,0:T(8,128)(2,1)}), bf16[16,192,512]{2,1,0:T(8,128)(2,1)}, u32[]{:S(2)}, u32[]{:S(2)}) async-start(bf16[16,192,512]{2,1,0:T(8,128)(2,1)} %maximum_select_fusion.1), calls=%async_computation.7 | async-start | bytes 6291456 | tf_op jit(solution)/shard_map/all_to_all | solution.py:974
  907.0 8.9 collective-permute-start.28
  910.3 1.3 collective-permute-start.38
  920.0 21.0 %collective-permute-start.32 = (bf16[4,2,64,768]{3,2,0,1:T(8,128)(2,1)S(1)}, bf16[4,2,64,768]{3,2,0,1:T(8,128)(2,1)S(1)}, u32[]{:S(2)}, u32[]{:S(2)}) collective-permute-start(bf16[4,2,64,768]{3,2,0,1:T(8,128)(2,1)S(1)} %select_bitcast_fusion), channel_id=1, source_target_pairs={{0,4},{2,6},{4,0},{6,2},{8,12},{10,14},{12,8},{14,10},{16,20},{18,... | collective-permute-start | bytes 2359304 | tf_op jit(solution)/shard_map/ppermute | solution.py:664
  923.7 18.5 %collective-permute-start.30 = (bf16[4,2,64,768]{3,2,0,1:T(8,128)(2,1)S(1)}, bf16[4,2,64,768]{3,2,0,1:T(8,128)(2,1)S(1)}, u32[]{:S(2)}, u32[]{:S(2)}) collective-permute-start(bf16[4,2,64,768]{3,2,0,1:T(8,128)(2,1)S(1)} %select_bitcast_fusion.1), channel_id=1, source_target_pairs={{0,2},{2,0},{4,6},{6,4},{8,10},{10,8},{12,14},{14,12},{16,18},{18,... | collective-permute-start | bytes 2359304 | tf_op jit(solution)/shard_map/ppermute | solution.py:664
  928.0 15.7 %collective-permute-start.29 = (bf16[512,1024]{1,0:T(8,128)(2,1)S(1)}, bf16[512,1024]{1,0:T(8,128)(2,1)S(1)}, u32[]{:S(2)}, u32[]{:S(2)}) collective-permute-start(bf16[512,1024]{1,0:T(8,128)(2,1)S(1)} %slice.451), channel_id=1, source_target_pairs={{0,1},{1,0},{2,3},{3,2},{4,5},{5,4},{6,7},{7,6},{8,9},{9,8},{10,11... | collective-permute-start | bytes 3145736 | tf_op jit(solution)/shard_map/ppermute | solution.py:581
  941.4 9.8 collective-permute-start.33
  942.6 9.2 collective-permute-start.31
  951.9 4.6 collective-permute-start.34
  952.0 9.0 collective-permute-start.35
  954.6 15.8 %collective-permute-start.36 = (bf16[64,1536]{1,0:T(8,128)(2,1)S(1)}, bf16[64,1536]{1,0:T(8,128)(2,1)S(1)}, u32[]{:S(2)}, u32[]{:S(2)}) collective-permute-start(bf16[64,1536]{1,0:T(8,128)(2,1)S(1)} %get-tuple-element.128), channel_id=1, source_target_pairs={{0,24},{2,26},{4,28},{6,30},{8,16},{10,18},{12,20},{14,22},{16,8},... | collective-permute-start | bytes 589832 | tf_op jit(solution)/shard_map/ppermute | solution.py:664
  975.9 5.5 collective-permute-start.37
  (77 other events, 1149.2 us)
Sparse Core Ops, SparseCore 0:
  41.3 177.7 all-gather.1
  690.7 215.3 reduce-scatter.1

commit v5 on v4

--- a/solution.py
+++ b/solution.py
@@ -425,6 +425,21 @@
     return lax.dot_general(left, right, (((0,), (0,)), ((), ())), preferred_element_type=F32)
 
 
+def beside(blocks, at, count, start, stop):
+    return jnp.concatenate([blocks[at + j, start:stop, :] for j in range(count)], 1)
+
+
+def in_groups(sizes, first, count, take, carry):
+    for size in sizes:
+        groups = count // size
+        step = take(size)
+        carry = lax.fori_loop(
+            0, groups, lambda k, value, at=first, n=size, f=step: f(at + k * n, value), carry
+        )
+        first, count = first + groups * size, count - groups * size
+    return carry
+
+
 def attn_fwd_kernel(plan, own, prompts, out, log_sums, values, *, head, factor):
     step_id = pl.program_id(0)
     block, full, first = plan[0, step_id], plan[1, step_id], plan[2, step_id]
@@ -451,15 +466,18 @@
         expo = jnp.exp2(scores * factor - top)
         result = matmul(expo.astype(BF16), with_ones(own[block, 2 * head : 3 * head, :]))
 
-        def step(k, carry):
-            before, result = carry
-            scores = matmul(query, prompts[first + k, 0:head, :])
-            top = jnp.maximum(before, jnp.max(scores, 1, keepdims=True) * factor)
-            expo = jnp.exp2(scores * factor - top)
-            result = result * jnp.exp2(before - top) + matmul(expo.astype(BF16), values[first + k])
-            return top, result
-
-        top, result = lax.fori_loop(0, full, step, (top, result))
+        def take(count):
+            def step(at, carry):
+                before, result = carry
+                scores = matmul(query, beside(prompts, at, count, 0, head))
+                top = jnp.maximum(before, jnp.max(scores, 1, keepdims=True) * factor)
+                expo = jnp.exp2(scores * factor - top).astype(BF16)
+                rows = jnp.concatenate([values[at + j] for j in range(count)], 0)
+                return top, result * jnp.exp2(before - top) + matmul(expo, rows)
+
+            return step
+
+        top, result = in_groups((4, 2, 1), first, full, take, (top, result))
         result = result.T
         total = result[head : head + 1]
         out[block] = (result[:head] / total).astype(BF16)
@@ -499,16 +517,22 @@
         grad_own[block, head : 2 * head, :] = (grad_k * scale).T.astype(BF16)
         grad_own[block, 2 * head : 3 * head, :] = grad_v.T.astype(BF16)
 
-        def step(k, grad_q):
-            at = first + k
-            more_k, more_v, more_q = tile(
-                prompts[at, 0:head, :], prompts[at, head : 2 * head, :], False
-            )
-            sum_k[at] += more_k
-            sum_v[at] += more_v
-            return grad_q + more_q
-
-        grad_q = lax.fori_loop(0, full, step, grad_q)
+        def take(count):
+            def step(at, grad_q):
+                more_k, more_v, more_q = tile(
+                    beside(prompts, at, count, 0, head),
+                    beside(prompts, at, count, head, 2 * head),
+                    False,
+                )
+                length = more_k.shape[0] // count
+                for j in range(count):
+                    sum_k[at + j] += more_k[j * length : (j + 1) * length]
+                    sum_v[at + j] += more_v[j * length : (j + 1) * length]
+                return grad_q + more_q
+
+            return step
+
+        grad_q = in_groups((4, 2, 1), first, full, take, grad_q)
         grad_own[block, 0:head, :] = (grad_q * scale).astype(BF16)
 
     @pl.when(step_id == pl.num_programs(0) - 1)
@@ -598,13 +622,6 @@
     return value[:half].astype(F32) + swap(value[half:].astype(BF16)).astype(F32)
 
 
-def pair_parts(value):
-    half = value.shape[0] // 2
-    low = value.astype(BF16)
-    other = swap(low)
-    return low, jnp.concatenate([other[half:], other[:half]], 0)
-
-
 def gelu_pair(preact):
     square = preact * preact
     gate = 0.5 + 0.5 * jnp.tanh(preact * (GELU_A + GELU_A * GELU_B * square))
@@ -658,6 +675,56 @@
         ),
         name="mlp_fwd",
     )(*terms, w_in, w_out)
+
+
+def mlp_back_kernel(*refs, terms, transposed):
+    ins, (w_out, w_in, slope), outs = refs[:terms], refs[terms : terms + 3], refs[terms + 3 :]
+    if terms > 1:
+        total = ins[0][...] * ins[1][...].astype(F32)
+        for term in ins[2:]:
+            total = total + term[...].astype(F32)
+        grad = total.astype(BF16)
+        outs[0][...] = grad
+    else:
+        grad = ins[0][...]
+    grad = (matmul_nt if transposed else matmul)(grad, w_out[...])
+    grad_pre = (grad * slope[...].astype(F32)).astype(BF16)
+    outs[-2][...] = grad_pre
+    outs[-1][...] = matmul_nt(grad_pre, w_in[...]).astype(BF16)
+
+
+def mlp_backward(terms, w_out, w_in, slope, length, transposed=True, columns=(0, 0)):
+    rows, width = terms[-1].shape
+    hidden = slope.shape[1]
+    steps = rows // length
+    row_block = pl.BlockSpec((length, width), lambda m: (m, 0))
+    turned = pl.BlockSpec((length, width), lambda m: ((m + steps // 2) % steps, 0))
+    hidden_block = pl.BlockSpec((length, hidden), lambda m: (m, 0))
+    factor_block = pl.BlockSpec((length, 1), lambda m: (m, 0))
+    once = dict(pipeline_mode=pl.Buffered(1))
+    out_block = (
+        pl.BlockSpec((hidden, width), lambda m: (0, 0), **once)
+        if transposed
+        else pl.BlockSpec((width, hidden), lambda m: (0, columns[1]), **once)
+    )
+    in_block = pl.BlockSpec((width, hidden), lambda m: (0, columns[0]), **once)
+    term_blocks = [row_block] if len(terms) == 1 else [factor_block, row_block, row_block, turned][: len(terms)]
+    several = len(terms) > 1
+    return pl.pallas_call(
+        functools.partial(mlp_back_kernel, terms=len(terms), transposed=transposed),
+        grid=(steps,),
+        in_specs=term_blocks + [out_block, in_block, hidden_block],
+        out_specs=[row_block] * several + [hidden_block, row_block],
+        out_shape=[jax.ShapeDtypeStruct((rows, width), BF16)] * several
+        + [jax.ShapeDtypeStruct((rows, hidden), BF16), jax.ShapeDtypeStruct((rows, width), BF16)],
+        compiler_params=pltpu.CompilerParams(vmem_limit_bytes=52 * 2**20),
+        cost_estimate=pl.CostEstimate(
+            flops=4 * rows * width * hidden,
+            bytes_accessed=4 * width * hidden + 4 * rows * hidden + 4 * rows * width,
+            transcendentals=0,
+        ),
+        name="mlp_bwd",
+    )(*terms, w_out, w_in, slope)
 
 
 def from_bit(value, bit):
@@ -780,12 +847,12 @@
     extra = jnp.concatenate([norm1_gain, norm2_gain, counts_pair], 0)
     extra = jnp.pad(extra[None, :], ((0, 7), (0, half_heads * triple - extra.shape[0])))
     line_one = gather_line(jnp.concatenate([qkv_shard, extra], 0))
-    second_all = lax.all_gather(
-        jnp.concatenate([w_ffn_in, w_ffn_out.T, w_attn_out.T], 1), "dp", axis=0, tiled=True
-    )
-    ffn_in = second_all[:, :hidden]
-    ffn_out_t = second_all[:, hidden : 2 * hidden]
-    attn_half = second_all[:, 2 * hidden :]
+    planes = experts // 4
+    second_line = lax.all_gather(
+        jnp.concatenate([w_ffn_in, w_ffn_out.T, w_attn_out.T], 1),
+        "dp",
+        axis_index_groups=[[4 * z + k for z in range(planes)] for k in range(4)],
+    )
     weight_rows, extra_row = np.s_[..., :shard, :], np.s_[..., shard, :]
     (first_all, extra_all), (last_all, unused) = gather_third(
         *gather_second(line_one), (weight_rows, extra_row)
@@ -828,9 +895,17 @@
         qkv_full, rows_one[:rows], (((0,), (1,)), ((), ())), preferred_element_type=F32
     ).astype(BF16)
     qkv_t = jnp.concatenate(both(own_t, swap(other_t)), 0).reshape(heads, triple, rows)
+    qkv_t, second_line = lax.optimization_barrier((qkv_t, second_line))
     by_head = lax.all_to_all(qkv_t, "dp", split_axis=0, concat_axis=0, tiled=True)
 
-    lent = experts // 4
+    by_head, second_line = lax.optimization_barrier((by_head, second_line))
+    second_all = lax.all_gather(
+        second_line, "dp", axis_index_groups=[[4 * z + k for k in range(4)] for z in range(planes)]
+    )
+    second_all = second_all.transpose(1, 0, 2, 3).reshape(width, -1)
+    attn_half = second_all[:, 2 * hidden :]
+
+    lent = 3 * experts // 16
     span = PLEN // rows
     own_blocks = jnp.concatenate([by_head, to_core_zero(by_head[:lent])], 0)
     prompt_kv = jnp.where(core_zero, by_head[:, HEAD:], to_core_one(by_head[:, HEAD:]))
@@ -905,16 +980,22 @@
     grad_half = grad_returned[:half_rows].astype(F32)
     grad_logit_half = jnp.sum(grad_half * branch_half, 1) * gate_half * (1.0 - gate_half)
     centre_part = matmul(grad_logit_half, expert_rows[:half_rows].astype(F32))
-    grad_branch = gate_value[:, None] * grad_returned.astype(F32)
-    grad_b = grad_branch.astype(BF16)
-    grad_pre_b = (matmul_nt(grad_b, expert_out_b[0]) * slope_b.astype(F32)).astype(BF16)
-    part_m, other_m = pair_parts(matmul_nt(grad_pre_b, expert_in_b[0]))
-    grad_a = (grad_branch + part_m.astype(F32) + other_m.astype(F32)).astype(BF16)
-    grad_pre_a = (matmul_nt(grad_a, expert_out_a[0]) * slope_a.astype(F32)).astype(BF16)
+    gate_column = gate_value[:, None]
+    grad_b, grad_pre_b, part_m = mlp_backward(
+        [gate_column, grad_returned], expert_out_b[0], expert_in_b[0], slope_b, half_rows // 2
+    )
+    from_m = swap(part_m)
+    grad_a, grad_pre_a, part_x = mlp_backward(
+        [gate_column, grad_returned, part_m, from_m],
+        expert_out_a[0],
+        expert_in_a[0],
+        slope_a,
+        half_rows // 2,
+    )
     grad_rows = (
-        keep_rows(matmul_nt(grad_pre_a, expert_in_a[0]))
+        keep_rows(part_x)
         + part_m[:half_rows].astype(F32)
-        + other_m[:half_rows].astype(F32)
+        + from_m[half_rows:].astype(F32)
         + grad_logit_half[:, None] * centre.astype(F32)[None, :]
     )
     grad_rows, came_back, act_a, grad_a, expert_rows, grad_pre_a = lax.optimization_barrier(
@@ -929,10 +1010,12 @@
     grad_two = grad_out.astype(F32) + matmul(placer, grad_back)
 
     rows_down = with_other(grad_two.astype(BF16))
-    grad_ffn_pre = (matmul(rows_down, ffn_out_t) * ffn_slope.astype(F32)).astype(BF16)
+    grad_ffn_pre, ffn_part = mlp_backward(
+        [rows_down], second_all, second_all, ffn_slope, rows, transposed=False, columns=(0, 1)
+    )
     grad_ffn_out_t = matmul_tn(rows_down, ffn_act)
     grad_ffn_in = matmul_tn(rows_two, grad_ffn_pre)
-    grad_norm_two = keep_rows(matmul_nt(grad_ffn_pre, ffn_in))
+    grad_norm_two = keep_rows(ffn_part)
     back_two = norm_backward(grad_norm_two, hat_two, inv_two, gain_two)[0]
     grad_one = grad_two + back_two
 

time: 1000 us -> 927 us (0.927)
  matrix products: 155 us -> 98 us
  blocking collectives: 133 us -> 76 us
  Pallas kernels: 217 us -> 252 us
  waiting for transfers between devices: 272 us -> 284 us
    all_to_all x1, blocking collectives: 133 us -> 76 us  [body_paired(): lax.all_to_all(qkv_t, 'dp', split_axis=0, concat_axis=0, tiled=True)]
    pallas_call x0 -> x3, Pallas kernels: none -> 54.9 us  [mlp_backward(): pl.pallas_call(functools.partial(mlp_back_kernel, terms=len(terms), trans...]
    dot_general x5 -> x0, matrix products: 49.3 us -> none  [matmul_nt(): lax.dot_general(left, right, (((1,), (1,)), ((), ())), preferred_element_...]
    all_gather x0 -> x1, waiting for transfers between devices: none -> 38 us  [body_paired(): lax.all_gather(second_line, 'dp', axis_index_groups=[[4 * z + k for k in...]
    pallas_call x1, Pallas kernels: 67.3 us -> 51.4 us  [attn_forward(): pl.pallas_call(functools.partial(attn_fwd_kernel, head=head, factor=head...]
    all_to_all x1, waiting for transfers between devices: 15.8 us -> 0.01 us  [body_paired(): lax.all_to_all(attn_own, 'dp', split_axis=0, concat_axis=0, tiled=True)]
    convert_element_type x2 -> x0, other arithmetic: 12 us -> none  [the longest x1 7.07 us: body_paired(): (grad_branch + part_m.astype(F32) + other_m.astype(F32)).astype(BF16)]
    all_to_all x1, waiting for transfers between devices: 79.5 us -> 69.2 us  [body_paired(): lax.all_to_all(grad_head, 'dp', split_axis=0, concat_axis=0, tiled=True)]
  transfers between devices with their start and end apart: 48 -> 49, of which waited for: 30 -> 31; matrix products, arithmetic and copies ran while one was open for 19% -> 18% of each run, Pallas kernels for 18% -> 20%
where the time goes in v5:
time: 927 us; the launch traced here: 917 us
  waiting for transfers between devices  284 us (31%)
  Pallas kernels  252 us (27%)
  matrix products  98 us (11%)
  starting transfers between devices  87.9 us (9%)
  blocking collectives  76 us (8%)
  other arithmetic  63.9 us (7%)
  local copies, waits for them, and re-layouts  40.3 us (4%)
  between operations  15.3 us (2%)
    pallas_call x1, Pallas kernels, attn_backward(): pl.pallas_call(functools.partial(attn_bwd_kernel, head=head, factor=head...  90.2 us
    all_to_all x1, blocking collectives, body_paired(): lax.all_to_all(qkv_t, 'dp', split_axis=0, concat_axis=0, tiled=True)  76 us
    ppermute x14, waiting for transfers between devices, from_bit(): lax.ppermute(value, 'dp', [(i, i ^ bit) for i in range(lax.axis_size('dp'...  75.6 us
    all_to_all x1, waiting for transfers between devices, body_paired(): lax.all_to_all(grad_head, 'dp', split_axis=0, concat_axis=0, tiled=True)  69.2 us
    dot_general x8, matrix products, matmul_tn(): lax.dot_general(left, right, (((0,), (0,)), ((), ())), preferred_element_...  68.1 us
    all_to_all x4, waiting for transfers between devices, to_experts(): return lax.all_to_all(value, 'dp', split_axis=0, concat_axis=0, tiled=True)  61.5 us
    pallas_call x3, Pallas kernels, mlp_forward(): pl.pallas_call(functools.partial(mlp_kernel, terms=len(terms), transposed...  55.7 us
    pallas_call x3, Pallas kernels, mlp_backward(): pl.pallas_call(functools.partial(mlp_back_kernel, terms=len(terms), trans...  54.9 us
  transfers between devices with their start and end apart: 49, of which 31 were waited for; matrix products, arithmetic and copies ran while one was open for 18% of the time, Pallas kernels for 20%

profile of v5, /device:TPU:9, one launch (start us, length us, event | category | flops | bytes accessed | tf_op | source)
XLA Modules:
  0.0 917.4 jit_solution(11170808227427568668)
XLA Ops:
  17.2 5.9 collective-permute-done.2
  23.0 7.0 collective-permute-done.3
  30.1 5.8 collective-permute-done.4
  40.7 7.4 collective-permute-done.5
  53.4 15.3 %collective-permute-done.6 = bf16[4,2,72,768]{3,2,0,1:T(8,128)(2,1)S(1)} collective-permute-done((bf16[4,2,72,768]{3,2,0,1:T(8,128)(2,1)S(1)}, bf16[4,2,72,768]{3,2,0,1:T(8,128)(2,1)S(1)}, u32[]{:S(2)}, u32[]{:S(2)}) %collective-permute-start.6) | collective-permute-done | bytes 884768 | tf_op jit(solution)/shard_map/ppermute | solution.py:731
  88.7 76.0 %all_to_all.40 = bf16[16,192,512]{2,1,0:T(8,128)(2,1)S(1)} all-to-all(bf16[16,192,512]{2,1,0:T(8,128)(2,1)} %bitcast.132), channel_id=1, replica_groups=mesh['dp'=16,'tensor'=2] {'dp'}, dimensions={0} | all-to-all | bytes 6291456 | tf_op jit(solution)/shard_map/all_to_all | solution.py:899
  166.6 4.2 collective-permute-start.10
  174.4 51.4 %attn_fwd.1 = (bf16[19,64,512]{2,1,0:T(8,128)(2,1)S(1)}, f32[19,1,512]{2,1,0:T(1,128)S(1)}) custom-call(s32[4,19]{1,0:T(4,128)S(1)} %add_select_fusion.2.plan, bf16[19,192,512]{2,1,0:T(8,128)(2,1)S(1)} %constant_dynamic-update-slice_fusion.own, bf16[16,128,512]{2,1,0:T(8,128)(2,1)S(1)} %broadcast_select_fusion.prompts), custom_call_target="tpu_custom_call" | custom-call | flops 26843545600 | bytes 8388608 | tf_op jit(solution)/shard_map/attn_fwd/pallas_call | solution.py:552
  230.4 4.0 all-to-all-start.1
  234.3 38.0 %all-gather.7.cloned.1.call-done = bf16[16,64,4608]{2,1,0:T(8,128)(2,1)} async-done(((bf16[4,64,4608]{2,1,0:T(8,128)(2,1)}), bf16[16,64,4608]{2,1,0:T(8,128)(2,1)}) %all-gather.7.cloned.1.call-update) | async-done | bytes 9437200 | tf_op jit(solution)/shard_map/all_gather | solution.py:902
  272.4 8.2 copy.127
  288.0 4.0 fusion.52
  297.9 14.9 %mlp_fwd.3 = (bf16[1024,2048]{1,0:T(8,128)(2,1)}, bf16[1024,2048]{1,0:T(8,128)(2,1)}, bf16[1024,1024]{1,0:T(8,128)(2,1)}) custom-call(bf16[1024,1024]{1,0:T(8,128)(2,1)} %pad_maximum_fusion.7.refs_0_, bf16[1024,4608]{1,0:T(8,128)(2,1)} %bitcast.128, bf16[1024,4608]{1,0:T(8,128)(2,1)} %bitcast.129), custom_call_target="tpu_custom_call" | custom-call | flops 8589934592 | bytes 20971520 | tf_op jit(solution)/shard_map/mlp_fwd/pallas_call | solution.py:662
  319.4 6.0 all-to-all-start.2
  328.9 32.1 %all-to-all-done.2 = bf16[16,48,1024]{2,1,0:T(8,128)(2,1)} async-done(((bf16[16,48,1024]{2,1,0:T(8,128)(2,1)}), bf16[16,48,1024]{2,1,0:T(8,128)(2,1)}, u32[]{:S(2)}, u32[]{:S(2)}) %all-to-all-start.2) | async-done | bytes 1572896 | tf_op jit(solution)/shard_map/all_to_all | solution.py:52
  366.6 3.9 pad_maximum_fusion.3.refs_0_
  370.6 19.8 %mlp_fwd.4 = (bf16[1536,2048]{1,0:T(8,128)(2,1)}, bf16[1536,2048]{1,0:T(8,128)(2,1)}, bf16[1536,1024]{1,0:T(8,128)(2,1)}) custom-call(bf16[1536,1024]{1,0:T(8,128)(2,1)} %pad_maximum_fusion.3.refs_0_, bf16[1024,2048]{1,0:T(8,128)(2,1)} %bitcast.174, bf16[2048,1024]{1,0:T(8,128)(2,1)} %bitcast.176), custom_call_target="tpu_custom_call" | custom-call | flops 12884901888 | bytes 27262976 | tf_op jit(solution)/shard_map/mlp_fwd/pallas_call | solution.py:662
  390.8 4.6 all-to-all-start.3
  396.4 21.0 %mlp_fwd.5 = (bf16[1536,1024]{1,0:T(8,128)(2,1)}, bf16[1536,2048]{1,0:T(8,128)(2,1)}, bf16[1536,2048]{1,0:T(8,128)(2,1)}, bf16[1536,1024]{1,0:T(8,128)(2,1)}) custom-call(bf16[1536,1024]{1,0:T(8,128)(2,1)} %pad_maximum_fusion.3.refs_0_, bf16[1536,1024]{1,0:T(8,128)(2,1)} %get-tuple-element.71.refs_1_, bf16[1536,1024]{1,0:T(8,128)(2,1)} %collective-permute-done.17.refs_2_, ...), custom_call_target="tpu_custom_call" | custom-call | flops 12884901888 | bytes 27262976 | tf_op jit(solution)/shard_map/mlp_fwd/pallas_call | solution.py:662
  417.3 13.8 %all-to-all-done.3 = bf16[16,48,1024]{2,1,0:T(8,128)(2,1)} async-done(((bf16[16,48,1024]{2,1,0:T(8,128)(2,1)}), bf16[16,48,1024]{2,1,0:T(8,128)(2,1)}, u32[]{:S(2)}, u32[]{:S(2)}) %all-to-all-start.3) | async-done | bytes 1572896 | tf_op jit(solution)/shard_map/all_to_all | solution.py:52
  437.4 4.5 maximum_select_fusion.refs_1_
  442.0 19.5 %mlp_bwd.3 = (bf16[1536,1024]{1,0:T(8,128)(2,1)}, bf16[1536,2048]{1,0:T(8,128)(2,1)}, bf16[1536,1024]{1,0:T(8,128)(2,1)}) custom-call(f32[1536,1]{1,0:T(8,128)S(1)} %broadcast_in_dim.125.refs_0_, bf16[1536,1024]{1,0:T(8,128)(2,1)} %maximum_select_fusion.refs_1_, bf16[2048,1024]{1,0:T(8,128)(2,1)} %bitcast.173, bf16[1024,2048]{1,0:T(8,128)(2,1)} %bitcast.171, ...), custom_call_target="tpu_custom_call" | custom-call | flops 12884901888 | bytes 27262976 | tf_op jit(solution)/shard_map/mlp_bwd/pallas_call | solution.py:713
  463.3 6.4 collective-permute-done.21
  469.7 4.9 select_convert_fusion
  474.6 5.2 all-to-all-start.4
  479.8 21.0 %mlp_bwd.4 = (bf16[1536,1024]{1,0:T(8,128)(2,1)}, bf16[1536,2048]{1,0:T(8,128)(2,1)}, bf16[1536,1024]{1,0:T(8,128)(2,1)}) custom-call(f32[1536,1]{1,0:T(8,128)S(1)} %broadcast_in_dim.125.refs_0_, bf16[1536,1024]{1,0:T(8,128)(2,1)} %maximum_select_fusion.refs_1_, bf16[1536,1024]{1,0:T(8,128)(2,1)} %get-tuple-element.76.refs_2_, ...), custom_call_target="tpu_custom_call" | custom-call | flops 12884901888 | bytes 27262976 | tf_op jit(solution)/shard_map/mlp_bwd/pallas_call | solution.py:713
  507.5 4.9 add_convert_fusion.1
  515.4 5.8 all-to-all-start.5
  521.2 12.0 %fusion.55 = f32[1024,2048]{1,0:T(8,128)} fusion(bf16[1536,1024]{1,0:T(8,128)(2,1)} %pad_maximum_fusion.3.refs_0_, bf16[1536,2048]{1,0:T(8,128)(2,1)} %get-tuple-element.88), kind=kOutput, calls=%fused_computation.206 | convolution fusion | flops 6442450944 | bytes 17825792 | tf_op jit(solution)/shard_map/dot_general | solution.py:60
  533.1 11.1 %fusion.54 = f32[2048,1024]{1,0:T(8,128)} fusion(bf16[1536,2048]{1,0:T(8,128)(2,1)} %get-tuple-element.85, bf16[1536,1024]{1,0:T(8,128)(2,1)S(1)} %copy-done.62), kind=kOutput, calls=%fused_computation.205 | convolution fusion | flops 6442450944 | bytes 17825792 | tf_op jit(solution)/shard_map/dot_general | solution.py:60
  544.2 12.7 %all-to-all-done.5 = bf16[16,48,1024]{2,1,0:T(8,128)(2,1)} async-done(((bf16[16,48,1024]{2,1,0:T(8,128)(2,1)}), bf16[16,48,1024]{2,1,0:T(8,128)(2,1)}, u32[]{:S(2)}, u32[]{:S(2)}) %all-to-all-start.5) | async-done | bytes 1572896 | tf_op jit(solution)/shard_map/all_to_all | solution.py:52
  566.5 14.4 %mlp_bwd.5 = (bf16[1024,2048]{1,0:T(8,128)(2,1)}, bf16[1024,1024]{1,0:T(8,128)(2,1)}) custom-call(bf16[1024,1024]{1,0:T(8,128)(2,1)} %pad_maximum_fusion.8.refs_0_, bf16[1024,4608]{1,0:T(8,128)(2,1)} %bitcast.130, bf16[1024,4608]{1,0:T(8,128)(2,1)} %bitcast.131, bf16[1024,2048]{1,0:T(8,128)(2,1)} %get-tuple-element.90.refs_3_), custom_call_target="tpu_custom_call" | custom-call | flops 8589934592 | bytes 20971520 | tf_op jit(solution)/shard_map/mlp_bwd/pallas_call | solution.py:713
  582.8 8.6 convolution_convert_fusion.2
  600.2 3.9 all-to-all-start.6
  604.5 7.5 convolution_convert_fusion.1
  614.6 5.3 pad_maximum_fusion
  619.9 8.5 all-to-all-done.6
  629.0 4.3 collective-permute-start.25
  634.7 90.2 %attn_bwd.1 = (bf16[19,192,512]{2,1,0:T(8,128)(2,1)}, bf16[16,128,512]{2,1,0:T(8,128)(2,1)S(1)}) custom-call(s32[4,19]{1,0:T(4,128)S(1)} %copy-done.5, bf16[19,192,512]{2,1,0:T(8,128)(2,1)} %copy-done, bf16[16,128,512]{2,1,0:T(8,128)(2,1)} %copy-done.1, bf16[19,64,512]{2,1,0:T(8,128)(2,1)S(1)} %pad_maximum_fusion.15.grad, ...), custom_call_target="tpu_custom_call" | custom-call | flops 67108864000 | bytes 16777216 | tf_op jit(solution)/shard_map/attn_bwd/pallas_call | solution.py:579
  734.5 4.6 all-to-all-start.7
  739.1 12.0 %fusion.57 = f32[1024,2048]{1,0:T(8,128)} fusion(bf16[1536,1024]{1,0:T(8,128)(2,1)} %get-tuple-element.105, bf16[1536,2048]{1,0:T(8,128)(2,1)} %get-tuple-element.106), kind=kOutput, calls=%fused_computation.208 | convolution fusion | flops 6442450944 | bytes 17825792 | tf_op jit(solution)/shard_map/dot_general | solution.py:60
  751.1 11.1 %fusion.56 = f32[2048,1024]{1,0:T(8,128)} fusion(bf16[1536,2048]{1,0:T(8,128)(2,1)} %get-tuple-element.103, bf16[1536,1024]{1,0:T(8,128)(2,1)S(1)} %copy-done.63), kind=kOutput, calls=%fused_computation.207 | convolution fusion | flops 6442450944 | bytes 17825792 | tf_op jit(solution)/shard_map/dot_general | solution.py:60
  762.2 69.2 %all-to-all-done.7 = bf16[16,192,512]{2,1,0:T(8,128)(2,1)} async-done(((bf16[16,192,512]{2,1,0:T(8,128)(2,1)}), bf16[16,192,512]{2,1,0:T(8,128)(2,1)}, u32[]{:S(2)}, u32[]{:S(2)}) %all-to-all-start.7) | async-done | bytes 3145760 | tf_op jit(solution)/shard_map/all_to_all | solution.py:1057
  840.0 3.7 add_convert_fusion.4
  843.7 4.0 convolution_convert_fusion
  857.4 11.5 %collective-permute-done.32 = bf16[4,2,64,768]{3,2,0,1:T(8,128)(2,1)S(1)} collective-permute-done((bf16[4,2,64,768]{3,2,0,1:T(8,128)(2,1)S(1)}, bf16[4,2,64,768]{3,2,0,1:T(8,128)(2,1)S(1)}, u32[]{:S(2)}, u32[]{:S(2)}) %collective-permute-start.32) | collective-permute-done | bytes 786464 | tf_op jit(solution)/shard_map/ppermute | solution.py:731
  872.7 6.3 collective-permute-done.33
  888.2 12.0 %collective-permute-done.36 = bf16[64,1536]{1,0:T(8,128)(2,1)S(1)} collective-permute-done((bf16[64,1536]{1,0:T(8,128)(2,1)S(1)}, bf16[64,1536]{1,0:T(8,128)(2,1)S(1)}, u32[]{:S(2)}, u32[]{:S(2)}) %collective-permute-start.36) | collective-permute-done | bytes 196640 | tf_op jit(solution)/shard_map/ppermute | solution.py:731
  (363 shorter events, 173.8 us)
Async XLA Ops:
  7.2 81.5 %all-gather.5.cloned.1.call-start = ((), (), s32[]{:S(2)}) async-start(), calls=%async_computation.10 | async-start | bytes 2949120 | tf_op jit(solution)/shard_map/all_gather | solution.py:851
  8.1 5.3 collective-permute-start.1
  13.6 9.4 %collective-permute-start.2 = (bf16[72,1536]{1,0:T(8,128)(2,1)S(1)}, bf16[72,1536]{1,0:T(8,128)(2,1)S(1)}, u32[]{:S(2)}, u32[]{:S(2)}) collective-permute-start(bf16[72,1536]{1,0:T(8,128)(2,1)S(1)} %get-tuple-element.150), channel_id=1, source_target_pairs={{0,8},{2,10},{4,12},{6,14},{8,0},{10,2},{12,4},{14,6},{16,24},{18,... | collective-permute-start | bytes 663560 | tf_op jit(solution)/shard_map/ppermute | solution.py:731
  13.7 16.4 %collective-permute-start.3 = (bf16[72,1536]{1,0:T(8,128)(2,1)S(1)}, bf16[72,1536]{1,0:T(8,128)(2,1)S(1)}, u32[]{:S(2)}, u32[]{:S(2)}) collective-permute-start(bf16[72,1536]{1,0:T(8,128)(2,1)S(1)} %get-tuple-element.150), channel_id=1, source_target_pairs={{0,16},{2,18},{4,20},{6,22},{8,24},{10,26},{12,28},{14,30},{16,0},... | collective-permute-start | bytes 663560 | tf_op jit(solution)/shard_map/ppermute | solution.py:731
  16.1 19.7 %collective-permute-start.4 = (bf16[72,1536]{1,0:T(8,128)(2,1)S(1)}, bf16[72,1536]{1,0:T(8,128)(2,1)S(1)}, u32[]{:S(2)}, u32[]{:S(2)}) collective-permute-start(bf16[72,1536]{1,0:T(8,128)(2,1)S(1)} %get-tuple-element.150), channel_id=1, source_target_pairs={{0,24},{2,26},{4,28},{6,30},{8,16},{10,18},{12,20},{14,22},{16,8},... | collective-permute-start | bytes 663560 | tf_op jit(solution)/shard_map/ppermute | solution.py:731
  16.3 36.0 %collective-permute-start = (bf16[512,1024]{1,0:T(8,128)(2,1)S(1)}, bf16[512,1024]{1,0:T(8,128)(2,1)S(1)}, u32[]{:S(2)}, u32[]{:S(2)}) collective-permute-start(bf16[512,1024]{1,0:T(8,128)(2,1)S(1)} %copy-done.11), channel_id=1, source_target_pairs={{0,1},{1,0},{2,3},{3,2},{4,5},{5,4},{6,7},{7,6},{8,9},{9,8},{10,11... | collective-permute-start | bytes 3145736 | tf_op jit(solution)/shard_map/ppermute | solution.py:605
  37.3 10.9 %collective-permute-start.5 = (bf16[4,72,768]{2,1,0:T(8,128)(2,1)}, bf16[4,72,768]{2,1,0:T(8,128)(2,1)}, u32[]{:S(2)}, u32[]{:S(2)}) collective-permute-start(bf16[4,72,768]{2,1,0:T(8,128)(2,1)} %get-tuple-element.141), channel_id=1, source_target_pairs={{0,4},{2,6},{4,0},{6,2},{8,12},{10,14},{12,8},{14,10},{16,20},{18,... | collective-permute-start | bytes 1327112 | tf_op jit(solution)/shard_map/ppermute | solution.py:731
  38.5 12.2 %collective-permute-start.7 = (bf16[4,72,768]{2,1,0:T(8,128)(2,1)}, bf16[4,72,768]{2,1,0:T(8,128)(2,1)S(1)}, u32[]{:S(2)}, u32[]{:S(2)}) collective-permute-start(bf16[4,72,768]{2,1,0:T(8,128)(2,1)} %get-tuple-element.140), channel_id=1, source_target_pairs={{0,2},{2,0},{4,6},{6,4},{8,10},{10,8},{12,14},{14,12},{16,18},{18,... | collective-permute-start | bytes 1327112 | tf_op jit(solution)/shard_map/ppermute | solution.py:731
  40.6 231.8 %all-gather.7.cloned.1.call-start = ((), (), s32[]{:S(2)}) async-start(), calls=%async_computation.11 | async-start | bytes 11796480 | tf_op jit(solution)/shard_map/all_gather | solution.py:902
  49.4 19.3 %collective-permute-start.6 = (bf16[4,2,72,768]{3,2,0,1:T(8,128)(2,1)S(1)}, bf16[4,2,72,768]{3,2,0,1:T(8,128)(2,1)S(1)}, u32[]{:S(2)}, u32[]{:S(2)}) collective-permute-start(bf16[4,2,72,768]{3,2,0,1:T(8,128)(2,1)S(1)} %maximum_select_fusion.4), channel_id=1, source_target_pairs={{0,2},{2,0},{4,6},{6,4},{8,10},{10,8},{12,14},{14,12},{16,18},{18,... | collective-permute-start | bytes 2654216 | tf_op jit(solution)/shard_map/ppermute | solution.py:731
  50.9 19.5 %collective-permute-start.8 = (bf16[4,2,72,768]{3,2,0,1:T(8,128)(2,1)S(1)}, bf16[4,2,72,768]{3,2,0,1:T(8,128)(2,1)S(1)}, u32[]{:S(2)}, u32[]{:S(2)}) collective-permute-start(bf16[4,2,72,768]{3,2,0,1:T(8,128)(2,1)S(1)} %maximum_select_fusion.5), channel_id=1, source_target_pairs={{0,4},{2,6},{4,0},{6,2},{8,12},{10,14},{12,8},{14,10},{16,20},{18,... | collective-permute-start | bytes 2654216 | tf_op jit(solution)/shard_map/ppermute | solution.py:731
  77.3 5.9 collective-permute-start.9
  164.9 7.5 collective-permute-start.11
  166.6 5.7 collective-permute-start.10
  225.9 3.4 collective-permute-start.12
  230.4 57.6 %all-to-all-start.1 = ((bf16[16,64,512]{2,1,0:T(8,128)(2,1)}), bf16[16,64,512]{2,1,0:T(8,128)(2,1)S(1)}, u32[]{:S(2)}, u32[]{:S(2)}) async-start(bf16[16,64,512]{2,1,0:T(8,128)(2,1)} %pad_maximum_fusion.16), calls=%async_computation.1 | async-start | bytes 2097152 | tf_op jit(solution)/shard_map/all_to_all | solution.py:936
  282.0 3.3 collective-permute-start.13
  292.7 2.7 collective-permute-start.14
  314.3 2.7 collective-permute-start.15
  319.4 41.6 %all-to-all-start.2 = ((bf16[16,48,1024]{2,1,0:T(8,128)(2,1)}), bf16[16,48,1024]{2,1,0:T(8,128)(2,1)}, u32[]{:S(2)}, u32[]{:S(2)}) async-start(bf16[16,48,1024]{2,1,0:T(8,128)(2,1)} %bitcast.148), calls=%async_computation.2 | async-start | bytes 3145728 | tf_op jit(solution)/shard_map/all_to_all | solution.py:52
  361.0 5.6 collective-permute-start.16
  390.4 6.0 collective-permute-start.17
  390.8 40.4 %all-to-all-start.3 = ((bf16[16,48,1024]{2,1,0:T(8,128)(2,1)}), bf16[16,48,1024]{2,1,0:T(8,128)(2,1)}, u32[]{:S(2)}, u32[]{:S(2)}) async-start(bf16[16,48,1024]{2,1,0:T(8,128)(2,1)} %bitcast.147), calls=%async_computation.3 | async-start | bytes 3145728 | tf_op jit(solution)/shard_map/all_to_all | solution.py:52
  431.2 6.3 collective-permute-start.18
  461.5 18.4 %collective-permute-start.19 = (bf16[1536,1024]{1,0:T(8,128)(2,1)}, bf16[1536,1024]{1,0:T(8,128)(2,1)}, u32[]{:S(2)}, u32[]{:S(2)}) collective-permute-start(bf16[1536,1024]{1,0:T(8,128)(2,1)} %get-tuple-element.76.refs_2_), channel_id=1, source_target_pairs={{0,1},{1,0},{2,3},{3,2},{4,5},{5,4},{6,7},{7,6},{8,9},{9,8},{10,11... | collective-permute-start | bytes 9437192 | tf_op jit(solution)/shard_map/ppermute | solution.py:605
  462.7 7.0 collective-permute-start.21
  474.6 40.8 %all-to-all-start.4 = ((bf16[16,48,1024]{2,1,0:T(8,128)(2,1)}), bf16[16,48,1024]{2,1,0:T(8,128)(2,1)}, u32[]{:S(2)}, u32[]{:S(2)}) async-start(bf16[16,48,1024]{2,1,0:T(8,128)(2,1)} %bitcast.135), calls=%async_computation.4 | async-start | bytes 3145728 | tf_op jit(solution)/shard_map/all_to_all | solution.py:52
  503.4 4.1 collective-permute-start.20
  515.4 41.5 %all-to-all-start.5 = ((bf16[16,48,1024]{2,1,0:T(8,128)(2,1)}), bf16[16,48,1024]{2,1,0:T(8,128)(2,1)}, u32[]{:S(2)}, u32[]{:S(2)}) async-start(bf16[16,48,1024]{2,1,0:T(8,128)(2,1)} %bitcast.134), calls=%async_computation.5 | async-start | bytes 3145728 | tf_op jit(solution)/shard_map/all_to_all | solution.py:52
  559.7 5.2 collective-permute-start.22
  582.3 9.1 collective-permute-start.23
  596.0 16.1 %collective-permute-start.24 = (bf16[1024,512]{1,0:T(8,128)(2,1)}, bf16[1024,512]{1,0:T(8,128)(2,1)}, u32[]{:S(2)}, u32[]{:S(2)}) collective-permute-start(bf16[1024,512]{1,0:T(8,128)(2,1)} %select_convert_fusion.1), channel_id=1, source_target_pairs={{0,1},{1,0},{2,3},{3,2},{4,5},{5,4},{6,7},{7,6},{8,9},{9,8},{10,11... | collective-permute-start | bytes 3145736 | tf_op jit(solution)/shard_map/ppermute | solution.py:605
  600.2 28.2 %all-to-all-start.6 = ((bf16[16,64,512]{2,1,0:T(8,128)(2,1)}), bf16[16,64,512]{2,1,0:T(8,128)(2,1)S(1)}, u32[]{:S(2)}, u32[]{:S(2)}) async-start(bf16[16,64,512]{2,1,0:T(8,128)(2,1)} %bitcast.152), calls=%async_computation.6 | async-start | bytes 2097152 | tf_op jit(solution)/shard_map/all_to_all | solution.py:1026
  604.1 299.7 %reduce-scatter.2.cloned.1.call-start = ((), (), s32[]{:S(2)}) async-start(), calls=%async_computation.9 | async-start | bytes 10027008 | tf_op jit(solution)/shard_map/reduce_scatter | solution.py:1039
  629.0 5.5 collective-permute-start.25
  724.9 6.3 collective-permute-start.26
  727.4 4.7 collective-permute-start.27
  734.5 96.8 %all-to-all-start.7 = ((bf16[16,192,512]{2,1,0:T(8,128)(2,1)}), bf16[16,192,512]{2,1,0:T(8,128)(2,1)}, u32[]{:S(2)}, u32[]{:S(2)}) async-start(bf16[16,192,512]{2,1,0:T(8,128)(2,1)} %maximum_select_fusion.1), calls=%async_computation.7 | async-start | bytes 6291456 | tf_op jit(solution)/shard_map/all_to_all | solution.py:1057
  833.6 10.1 %collective-permute-start.28 = (bf16[1536,512]{1,0:T(8,128)(2,1)S(1)}, bf16[1536,512]{1,0:T(8,128)(2,1)S(1)}, u32[]{:S(2)}, u32[]{:S(2)}) collective-permute-start(bf16[1536,512]{1,0:T(8,128)(2,1)S(1)} %bitcast.151), channel_id=1, source_target_pairs={{0,1},{1,0},{2,3},{3,2},{4,5},{5,4},{6,7},{7,6},{8,9},{9,8},{10,11... | collective-permute-start | bytes 4718600 | tf_op jit(solution)/shard_map/ppermute | solution.py:605
  847.9 21.0 %collective-permute-start.32 = (bf16[4,2,64,768]{3,2,0,1:T(8,128)(2,1)S(1)}, bf16[4,2,64,768]{3,2,0,1:T(8,128)(2,1)S(1)}, u32[]{:S(2)}, u32[]{:S(2)}) collective-permute-start(bf16[4,2,64,768]{3,2,0,1:T(8,128)(2,1)S(1)} %select_bitcast_fusion), channel_id=1, source_target_pairs={{0,4},{2,6},{4,0},{6,2},{8,12},{10,14},{12,8},{14,10},{16,20},{18,... | collective-permute-start | bytes 2359304 | tf_op jit(solution)/shard_map/ppermute | solution.py:731
  851.5 19.1 %collective-permute-start.30 = (bf16[4,2,64,768]{3,2,0,1:T(8,128)(2,1)S(1)}, bf16[4,2,64,768]{3,2,0,1:T(8,128)(2,1)S(1)}, u32[]{:S(2)}, u32[]{:S(2)}) collective-permute-start(bf16[4,2,64,768]{3,2,0,1:T(8,128)(2,1)S(1)} %select_bitcast_fusion.1), channel_id=1, source_target_pairs={{0,2},{2,0},{4,6},{6,4},{8,10},{10,8},{12,14},{14,12},{16,18},{18,... | collective-permute-start | bytes 2359304 | tf_op jit(solution)/shard_map/ppermute | solution.py:731
  856.4 15.7 %collective-permute-start.29 = (bf16[512,1024]{1,0:T(8,128)(2,1)S(1)}, bf16[512,1024]{1,0:T(8,128)(2,1)S(1)}, u32[]{:S(2)}, u32[]{:S(2)}) collective-permute-start(bf16[512,1024]{1,0:T(8,128)(2,1)S(1)} %slice.406), channel_id=1, source_target_pairs={{0,1},{1,0},{2,3},{3,2},{4,5},{5,4},{6,7},{7,6},{8,9},{9,8},{10,11... | collective-permute-start | bytes 3145736 | tf_op jit(solution)/shard_map/ppermute | solution.py:605
  869.3 9.8 %collective-permute-start.33 = (bf16[4,64,768]{2,1,0:T(8,128)(2,1)S(1)}, bf16[4,64,768]{2,1,0:T(8,128)(2,1)S(1)}, u32[]{:S(2)}, u32[]{:S(2)}) collective-permute-start(bf16[4,64,768]{2,1,0:T(8,128)(2,1)S(1)} %select_bitcast_fusion.2), channel_id=1, source_target_pairs={{0,2},{2,0},{4,6},{6,4},{8,10},{10,8},{12,14},{14,12},{16,18},{18,... | collective-permute-start | bytes 1179656 | tf_op jit(solution)/shard_map/ppermute | solution.py:731
  870.9 9.5 %collective-permute-start.31 = (bf16[4,64,768]{2,1,0:T(8,128)(2,1)S(1)}, bf16[4,64,768]{2,1,0:T(8,128)(2,1)S(1)}, u32[]{:S(2)}, u32[]{:S(2)}) collective-permute-start(bf16[4,64,768]{2,1,0:T(8,128)(2,1)S(1)} %select_bitcast_fusion.3), channel_id=1, source_target_pairs={{0,4},{2,6},{4,0},{6,2},{8,12},{10,14},{12,8},{14,10},{16,20},{18,... | collective-permute-start | bytes 1179656 | tf_op jit(solution)/shard_map/ppermute | solution.py:731
  880.6 4.6 collective-permute-start.34
  880.7 7.5 collective-permute-start.35
  881.7 18.4 %collective-permute-start.36 = (bf16[64,1536]{1,0:T(8,128)(2,1)S(1)}, bf16[64,1536]{1,0:T(8,128)(2,1)S(1)}, u32[]{:S(2)}, u32[]{:S(2)}) collective-permute-start(bf16[64,1536]{1,0:T(8,128)(2,1)S(1)} %get-tuple-element.148), channel_id=1, source_target_pairs={{0,24},{2,26},{4,28},{6,30},{8,16},{10,18},{12,20},{14,22},{16,8},... | collective-permute-start | bytes 589832 | tf_op jit(solution)/shard_map/ppermute | solution.py:731
  905.7 4.4 collective-permute-start.37
  (66 other events, 571.0 us)
Sparse Core Ops, SparseCore 0:
  40.7 47.9 all-gather.4
  164.8 107.4 all-gather.6
  633.5 215.9 reduce-scatter.1

commit v6 on v5

--- a/solution.py
+++ b/solution.py
@@ -630,26 +630,85 @@
     return act.astype(BF16), slope.astype(BF16)
 
 
-def mlp_kernel(*refs, terms, transposed):
-    ins, (w_in, w_out), outs = refs[:terms], refs[terms : terms + 2], refs[terms + 2 :]
-    rows = ins[0][...]
-    if terms > 1:
+def take_terms(refs, kinds):
+    early = pl.program_id(0) < pl.num_programs(0) // 2
+    values, at = [], 0
+    for paired in kinds:
+        if paired:
+            values.append(jnp.where(early, refs[at][...], refs[at + 1][...]))
+        else:
+            values.append(refs[at][...])
+        at += 1 + paired
+    return values, refs[at:]
+
+
+def give_halves(refs, value):
+    early = pl.program_id(0) < pl.num_programs(0) // 2
+
+    @pl.when(early)
+    def _():
+        refs[0][...] = value
+
+    @pl.when(jnp.logical_not(early))
+    def _():
+        refs[1][...] = value
+
+
+def mlp_kernel(*refs, kinds, transposed, gated):
+    terms, refs = take_terms(refs, kinds)
+    rows = terms[0]
+    if len(terms) > 1:
         total = rows.astype(F32)
-        for term in ins[1:]:
-            total = total + term[...].astype(F32)
+        for term in terms[1:]:
+            total = total + term.astype(F32)
         rows = total.astype(BF16)
-        outs[0][...] = rows
+    if gated:
+        centre, refs = refs[0], refs[1:]
+        logit = jnp.sum(rows.astype(F32) * centre[...].astype(F32), 1, keepdims=True)
+        refs[-1][...] = 1.0 / (1.0 + jnp.exp(-logit))
+    w_in, w_out, kept_rows, kept_act, kept_slope, first, second = refs[:7]
+    kept_rows[...] = rows
     act, slope = gelu_pair(matmul(rows, w_in[...]))
-    outs[-3][...] = act
-    outs[-2][...] = slope
-    outs[-1][...] = (matmul_nt if transposed else matmul)(act, w_out[...]).astype(BF16)
-
-
-def mlp_forward(terms, w_in, w_out, hidden, length, transposed=False, columns=(0, 0)):
-    rows, width = terms[0].shape
-    steps = rows // length
-    row_block = pl.BlockSpec((length, width), lambda m: (m, 0))
-    turned = pl.BlockSpec((length, width), lambda m: ((m + steps // 2) % steps, 0))
+    kept_act[...] = act
+    kept_slope[...] = slope
+    result = (matmul_nt if transposed else matmul)(act, w_out[...])
+    give_halves((first, second), result.astype(BF16))
+
+
+def mlp_back_kernel(*refs, kinds, transposed, scaled):
+    factor, refs = (refs[0], refs[1:]) if scaled else (None, refs)
+    terms, refs = take_terms(refs, kinds)
+    grad = terms[0]
+    if scaled:
+        total = factor[...] * grad.astype(F32)
+        for term in terms[1:]:
+            total = total + term.astype(F32)
+        grad = total.astype(BF16)
+    w_out, w_in, slope, kept_grad, kept_pre, first, second = refs
+    kept_grad[...] = grad
+    grad = (matmul_nt if transposed else matmul)(grad, w_out[...])
+    grad_pre = (grad * slope[...].astype(F32)).astype(BF16)
+    kept_pre[...] = grad_pre
+    give_halves((first, second), matmul_nt(grad_pre, w_in[...]).astype(BF16))
+
+
+def mlp_blocks(terms, length):
+    paired = [isinstance(term, tuple) for term in terms]
+    arrays = [part for term in terms for part in (term if isinstance(term, tuple) else (term,))]
+    half = max(part.shape[0] // length // (1 + (not pair)) for term, pair in zip(terms, paired) for part in (term if pair else (term,)))
+    width = arrays[0].shape[1]
+    block = pl.BlockSpec((length, width), lambda m: (m, 0))
+    halves = [
+        pl.BlockSpec((length, width), lambda m: (jnp.minimum(m, half - 1), 0)),
+        pl.BlockSpec((length, width), lambda m: (jnp.maximum(m - half, 0), 0)),
+    ]
+    specs = [spec for pair in paired for spec in (halves if pair else [block])]
+    return tuple(paired), arrays, specs, block, halves, 2 * half
+
+
+def mlp_forward(terms, w_in, w_out, hidden, length, transposed=False, columns=(0, 0), centre=None):
+    kinds, arrays, specs, block, halves, steps = mlp_blocks(terms, length)
+    rows, width = steps * length, arrays[0].shape[1]
     hidden_block = pl.BlockSpec((length, hidden), lambda m: (m, 0))
     once = dict(pipeline_mode=pl.Buffered(1))
     in_block = pl.BlockSpec((width, hidden), lambda m: (0, columns[0]), **once)
@@ -658,49 +717,33 @@
         if transposed
         else pl.BlockSpec((hidden, width), lambda m: (0, 0), **once)
     )
-    several = len(terms) > 1
+    gated = centre is not None
     return pl.pallas_call(
-        functools.partial(mlp_kernel, terms=len(terms), transposed=transposed),
+        functools.partial(mlp_kernel, kinds=kinds, transposed=transposed, gated=gated),
         grid=(steps,),
-        in_specs=([row_block, row_block, turned] if several else [row_block]) + [in_block, out_block],
-        out_specs=[row_block] * several + [hidden_block, hidden_block, row_block],
-        out_shape=[jax.ShapeDtypeStruct((rows, width), BF16)] * several
+        in_specs=specs + [pl.BlockSpec((1, width), lambda m: (0, 0))] * gated + [in_block, out_block],
+        out_specs=[block, hidden_block, hidden_block]
+        + halves
+        + [pl.BlockSpec((length, 1), lambda m: (m, 0))] * gated,
+        out_shape=[jax.ShapeDtypeStruct((rows, width), BF16)]
         + [jax.ShapeDtypeStruct((rows, hidden), BF16)] * 2
-        + [jax.ShapeDtypeStruct((rows, width), BF16)],
-        compiler_params=pltpu.CompilerParams(vmem_limit_bytes=52 * 2**20),
+        + [jax.ShapeDtypeStruct((rows // 2, width), BF16)] * 2
+        + [jax.ShapeDtypeStruct((rows, 1), F32)] * gated,
+        compiler_params=pltpu.CompilerParams(vmem_limit_bytes=54 * 2**20),
         cost_estimate=pl.CostEstimate(
             flops=4 * rows * width * hidden,
             bytes_accessed=4 * width * hidden + 4 * rows * hidden + 4 * rows * width,
             transcendentals=rows * hidden,
         ),
         name="mlp_fwd",
-    )(*terms, w_in, w_out)
-
-
-def mlp_back_kernel(*refs, terms, transposed):
-    ins, (w_out, w_in, slope), outs = refs[:terms], refs[terms : terms + 3], refs[terms + 3 :]
-    if terms > 1:
-        total = ins[0][...] * ins[1][...].astype(F32)
-        for term in ins[2:]:
-            total = total + term[...].astype(F32)
-        grad = total.astype(BF16)
-        outs[0][...] = grad
-    else:
-        grad = ins[0][...]
-    grad = (matmul_nt if transposed else matmul)(grad, w_out[...])
-    grad_pre = (grad * slope[...].astype(F32)).astype(BF16)
-    outs[-2][...] = grad_pre
-    outs[-1][...] = matmul_nt(grad_pre, w_in[...]).astype(BF16)
-
-
-def mlp_backward(terms, w_out, w_in, slope, length, transposed=True, columns=(0, 0)):
-    rows, width = terms[-1].shape
+    )(*arrays, *([centre] * gated), w_in, w_out)
+
+
+def mlp_backward(terms, w_out, w_in, slope, length, transposed=True, columns=(0, 0), factor=None):
+    kinds, arrays, specs, block, halves, steps = mlp_blocks(terms, length)
+    rows, width = steps * length, arrays[0].shape[1]
     hidden = slope.shape[1]
-    steps = rows // length
-    row_block = pl.BlockSpec((length, width), lambda m: (m, 0))
-    turned = pl.BlockSpec((length, width), lambda m: ((m + steps // 2) % steps, 0))
     hidden_block = pl.BlockSpec((length, hidden), lambda m: (m, 0))
-    factor_block = pl.BlockSpec((length, 1), lambda m: (m, 0))
     once = dict(pipeline_mode=pl.Buffered(1))
     out_block = (
         pl.BlockSpec((hidden, width), lambda m: (0, 0), **once)
@@ -708,23 +751,27 @@
         else pl.BlockSpec((width, hidden), lambda m: (0, columns[1]), **once)
     )
     in_block = pl.BlockSpec((width, hidden), lambda m: (0, columns[0]), **once)
-    term_blocks = [row_block] if len(terms) == 1 else [factor_block, row_block, row_block, turned][: len(terms)]
-    several = len(terms) > 1
+    scaled = factor is not None
     return pl.pallas_call(
-        functools.partial(mlp_back_kernel, terms=len(terms), transposed=transposed),
+        functools.partial(mlp_back_kernel, kinds=kinds, transposed=transposed, scaled=scaled),
         grid=(steps,),
-        in_specs=term_blocks + [out_block, in_block, hidden_block],
-        out_specs=[row_block] * several + [hidden_block, row_block],
-        out_shape=[jax.ShapeDtypeStruct((rows, width), BF16)] * several
-        + [jax.ShapeDtypeStruct((rows, hidden), BF16), jax.ShapeDtypeStruct((rows, width), BF16)],
-        compiler_params=pltpu.CompilerParams(vmem_limit_bytes=52 * 2**20),
+        in_specs=[pl.BlockSpec((length, 1), lambda m: (m, 0))] * scaled
+        + specs
+        + [out_block, in_block, hidden_block],
+        out_specs=[block, hidden_block] + halves,
+        out_shape=[
+            jax.ShapeDtypeStruct((rows, width), BF16),
+            jax.ShapeDtypeStruct((rows, hidden), BF16),
+        ]
+        + [jax.ShapeDtypeStruct((rows // 2, width), BF16)] * 2,
+        compiler_params=pltpu.CompilerParams(vmem_limit_bytes=54 * 2**20),
         cost_estimate=pl.CostEstimate(
             flops=4 * rows * width * hidden,
             bytes_accessed=4 * width * hidden + 4 * rows * hidden + 4 * rows * width,
             transcendentals=0,
         ),
         name="mlp_bwd",
-    )(*terms, w_out, w_in, slope)
+    )(*([factor] * scaled), *arrays, w_out, w_in, slope)
 
 
 def from_bit(value, bit):
@@ -846,13 +893,19 @@
     ).reshape(shard, half_heads * triple)
     extra = jnp.concatenate([norm1_gain, norm2_gain, counts_pair], 0)
     extra = jnp.pad(extra[None, :], ((0, 7), (0, half_heads * triple - extra.shape[0])))
-    line_one = gather_line(jnp.concatenate([qkv_shard, extra], 0))
     planes = experts // 4
+    first_shard, second_shard = lax.optimization_barrier(
+        (
+            jnp.concatenate([qkv_shard, extra], 0),
+            jnp.concatenate([w_ffn_in, w_ffn_out.T, w_attn_out.T], 1),
+        )
+    )
     second_line = lax.all_gather(
-        jnp.concatenate([w_ffn_in, w_ffn_out.T, w_attn_out.T], 1),
+        second_shard,
         "dp",
         axis_index_groups=[[4 * z + k for z in range(planes)] for k in range(4)],
     )
+    line_one = gather_line(first_shard)
     weight_rows, extra_row = np.s_[..., :shard, :], np.s_[..., shard, :]
     (first_all, extra_all), (last_all, unused) = gather_third(
         *gather_second(line_one), (weight_rows, extra_row)
@@ -905,7 +958,7 @@
     second_all = second_all.transpose(1, 0, 2, 3).reshape(width, -1)
     attn_half = second_all[:, 2 * hidden :]
 
-    lent = 3 * experts // 16
+    lent = experts // 4
     span = PLEN // rows
     own_blocks = jnp.concatenate([by_head, to_core_zero(by_head[:lent])], 0)
     prompt_kv = jnp.where(core_zero, by_head[:, HEAD:], to_core_one(by_head[:, HEAD:]))
@@ -937,37 +990,57 @@
         width, rows
     )
 
-    attn_out_t = jnp.concatenate(both(attn_half, swap(attn_half)), 1)
-    hidden_one = inputs + lax.dot_general(
-        attn_t, attn_out_t, (((0,), (1,)), ((), ())), preferred_element_type=F32
+    sent_grad = matmul_tn(placer, grad_out).astype(BF16).reshape(experts, slots_per, width)
+    attn_t, sent_grad = lax.optimization_barrier((attn_t, sent_grad))
+    grad_own = to_experts(sent_grad).reshape(-1, width)
+    half_width = width // 2
+    own_heads, other_heads = both(attn_t[:half_width], attn_t[half_width:])
+    attn_other = swap(attn_half)
+    hidden_one = (
+        inputs
+        + lax.dot_general(
+            own_heads, attn_half, (((0,), (1,)), ((), ())), preferred_element_type=F32
+        )
+        + lax.dot_general(
+            other_heads, attn_other, (((0,), (1,)), ((), ())), preferred_element_type=F32
+        )
     )
     normed_two, hat_two, inv_two = norm_forward(hidden_one, gain_two)
-    rows_two = with_other(normed_two.astype(BF16))
-    ffn_act, ffn_slope, ffn_sum = mlp_forward(
-        [rows_two], second_all, second_all, hidden, rows, transposed=True, columns=(0, 1)
-    )
-    hidden_two = hidden_one + keep_rows(ffn_sum)
+    normed_two = normed_two.astype(BF16)
+    rows_two, ffn_act, ffn_slope, ffn_own, ffn_other = mlp_forward(
+        [(normed_two, swap(normed_two))],
+        second_all,
+        second_all,
+        hidden,
+        rows,
+        transposed=True,
+        columns=(0, 1),
+    )
+    hidden_two = hidden_one + ffn_own.astype(F32) + swap(ffn_other).astype(F32)
 
     sent_rows = (
         matmul_tn(placer, hidden_two.astype(BF16)).astype(BF16).reshape(experts, slots_per, width)
     )
-    sent_grad = matmul_tn(placer, grad_out).astype(BF16).reshape(experts, slots_per, width)
-    own_rows, sent_grad = lax.optimization_barrier((to_experts(sent_rows), sent_grad))
-    grad_own = to_experts(sent_grad)
-    expert_rows = with_other(own_rows.reshape(-1, width))
+    sent_rows, grad_own = lax.optimization_barrier((sent_rows, grad_own))
+    own_rows = to_experts(sent_rows).reshape(half_rows, width)
     centre = centroids[0]
-    gate_value = jax.nn.sigmoid(matmul(expert_rows, centre))
-    act_a, slope_a, part_a = mlp_forward(
-        [expert_rows], expert_in_a[0], expert_out_a[0], hidden, half_rows // 2
-    )
-    from_a = swap(part_a)
-    middle, act_b, slope_b, part_b = mlp_forward(
-        [expert_rows, part_a, from_a], expert_in_b[0], expert_out_b[0], hidden, half_rows // 2
-    )
-    part_b, grad_own = lax.optimization_barrier((part_b, grad_own))
+    length = half_rows // 2
+    expert_rows, act_a, slope_a, own_a, other_a, gate_column = mlp_forward(
+        [(own_rows, swap(own_rows))],
+        expert_in_a[0],
+        expert_out_a[0],
+        hidden,
+        length,
+        centre=centroids,
+    )
+    from_a = (swap(other_a), swap(own_a))
+    middle, act_b, slope_b, own_b, other_b = mlp_forward(
+        [expert_rows, (own_a, other_a), from_a], expert_in_b[0], expert_out_b[0], hidden, length
+    )
     branch_half = (
-        part_a[:half_rows].astype(F32) + from_a[half_rows:].astype(F32) + keep_rows(part_b)
-    )
+        own_a.astype(F32) + from_a[0].astype(F32) + own_b.astype(F32) + swap(other_b).astype(F32)
+    )
+    gate_value = gate_column[:, 0]
     gate_half = gate_value[:half_rows]
     returned = (
         jnp.where(kept[:half_rows], gate_half[:, None] * branch_half, 0.0)
@@ -976,26 +1049,32 @@
     )
     came_back = to_experts(returned).reshape(half_rows, width)
 
-    grad_returned = jnp.where(kept, with_other(grad_own.reshape(-1, width)), 0.0).astype(BF16)
-    grad_half = grad_returned[:half_rows].astype(F32)
-    grad_logit_half = jnp.sum(grad_half * branch_half, 1) * gate_half * (1.0 - gate_half)
-    centre_part = matmul(grad_logit_half, expert_rows[:half_rows].astype(F32))
-    gate_column = gate_value[:, None]
-    grad_b, grad_pre_b, part_m = mlp_backward(
-        [gate_column, grad_returned], expert_out_b[0], expert_in_b[0], slope_b, half_rows // 2
-    )
-    from_m = swap(part_m)
-    grad_a, grad_pre_a, part_x = mlp_backward(
-        [gate_column, grad_returned, part_m, from_m],
+    kept_half = kept[:half_rows, 0]
+    grad_logit_half = jnp.where(
+        kept_half,
+        jnp.sum(grad_own.astype(F32) * branch_half, 1) * gate_half * (1.0 - gate_half),
+        0.0,
+    )
+    centre_part = matmul(grad_logit_half, own_rows.astype(F32))
+    kept_gate = jnp.where(kept, gate_column, 0.0)
+    grad_pair = (grad_own, swap(grad_own))
+    grad_b, grad_pre_b, own_m, other_m = mlp_backward(
+        [grad_pair], expert_out_b[0], expert_in_b[0], slope_b, length, factor=kept_gate
+    )
+    from_m = (swap(other_m), swap(own_m))
+    grad_a, grad_pre_a, own_x, other_x = mlp_backward(
+        [grad_pair, (own_m, other_m), from_m],
         expert_out_a[0],
         expert_in_a[0],
         slope_a,
-        half_rows // 2,
+        length,
+        factor=kept_gate,
     )
     grad_rows = (
-        keep_rows(part_x)
-        + part_m[:half_rows].astype(F32)
-        + from_m[half_rows:].astype(F32)
+        own_x.astype(F32)
+        + swap(other_x).astype(F32)
+        + own_m.astype(F32)
+        + from_m[0].astype(F32)
         + grad_logit_half[:, None] * centre.astype(F32)[None, :]
     )
     grad_rows, came_back, act_a, grad_a, expert_rows, grad_pre_a = lax.optimization_barrier(
@@ -1009,28 +1088,47 @@
     grad_back = grad_back.reshape(half_rows, width)
     grad_two = grad_out.astype(F32) + matmul(placer, grad_back)
 
-    rows_down = with_other(grad_two.astype(BF16))
-    grad_ffn_pre, ffn_part = mlp_backward(
-        [rows_down], second_all, second_all, ffn_slope, rows, transposed=False, columns=(0, 1)
-    )
+    grad_down = grad_two.astype(BF16)
+    rows_down, grad_ffn_pre, down_own, down_other = mlp_backward(
+        [(grad_down, swap(grad_down))],
+        second_all,
+        second_all,
+        ffn_slope,
+        rows,
+        transposed=False,
+        columns=(0, 1),
+    )
+    grad_norm_two = down_own.astype(F32) + swap(down_other).astype(F32)
+    back_two = norm_backward(grad_norm_two, hat_two, inv_two, gain_two)[0]
+    grad_one = grad_two + back_two
+
+    grad_branch_one = grad_one.astype(BF16)
+    grad_halves = both(
+        *(
+            lax.dot_general(
+                part, grad_branch_one, (((0,), (1,)), ((), ())), preferred_element_type=F32
+            ).astype(BF16)
+            for part in (attn_half, attn_other)
+        )
+    )
+    grad_attn, rows_down, ffn_act, rows_two, grad_ffn_pre = lax.optimization_barrier(
+        (
+            jnp.concatenate(grad_halves, 0).reshape(heads, HEAD, rows),
+            rows_down,
+            ffn_act,
+            rows_two,
+            grad_ffn_pre,
+        )
+    )
+    grad_by_head = lax.all_to_all(grad_attn, "dp", split_axis=0, concat_axis=0, tiled=True)
     grad_ffn_out_t = matmul_tn(rows_down, ffn_act)
     grad_ffn_in = matmul_tn(rows_two, grad_ffn_pre)
-    grad_norm_two = keep_rows(ffn_part)
-    back_two = norm_backward(grad_norm_two, hat_two, inv_two, gain_two)[0]
-    grad_one = grad_two + back_two
-
-    grad_branch_one = grad_one.astype(BF16)
-    grad_attn_t = lax.dot_general(
-        attn_out_t, grad_branch_one, (((0,), (1,)), ((), ())), preferred_element_type=F32
-    ).astype(BF16)
-    grad_by_head = lax.all_to_all(
-        grad_attn_t.reshape(heads, HEAD, rows), "dp", split_axis=0, concat_axis=0, tiled=True
-    )
-    grad_attn_out = lax.dot_general(
-        grad_branch_one, attn_t, (((0,), (1,)), ((), ())), preferred_element_type=F32
-    )
-    half_width = width // 2
-    part_own, part_other = both(grad_attn_out[:, :half_width], grad_attn_out[:, half_width:])
+    part_own, part_other = (
+        lax.dot_general(
+            grad_branch_one, part, (((0,), (1,)), ((), ())), preferred_element_type=F32
+        )
+        for part in (own_heads, other_heads)
+    )
     grad_attn_half = part_own + swap(part_other.astype(BF16)).astype(F32)
     second_part = jnp.concatenate(
         [grad_ffn_in.astype(BF16), grad_ffn_out_t.astype(BF16), grad_attn_half.astype(BF16)], 1

time: 927 us -> 926 us (level)
  waiting for transfers between devices: 284 us -> 240 us
  blocking collectives: 76 us -> 118 us
    all_to_all x0 -> x1, blocking collectives: none -> 41.5 us  [to_experts(): return lax.all_to_all(value, 'dp', split_axis=0, concat_axis=0, tiled=True)]
    all_to_all x4 -> x3, waiting for transfers between devices: 61.5 us -> 27.2 us  [to_experts(): return lax.all_to_all(value, 'dp', split_axis=0, concat_axis=0, tiled=True)]
    pallas_call x6, Pallas kernels: 111 us -> 126 us  [the longest x3 63.6 us: mlp_forward(): pl.pallas_call(functools.partial(mlp_kernel, kinds=kinds, transposed=tran...]
    ppermute x19 -> x21, waiting for transfers between devices: 24.9 us -> 18.5 us  [swap(): return lax.ppermute(value, 'tensor', [(0, 1), (1, 0)])]
    all_to_all x4 -> x3, starting transfers between devices: 21.6 us -> 16.4 us  [to_experts(): return lax.all_to_all(value, 'dp', split_axis=0, concat_axis=0, tiled=True)]
    ppermute x19 -> x21, starting transfers between devices: 21.3 us -> 21.2 us  [swap(): return lax.ppermute(value, 'tensor', [(0, 1), (1, 0)])]
  transfers between devices with their start and end apart: 49 -> 50, of which waited for: 31 -> 29; matrix products, arithmetic and copies ran while one was open for 18% -> 18% of each run, Pallas kernels for 20% -> 24%
where the time goes in v6:
time: 926 us; the launch traced here: 916 us
  Pallas kernels  258 us (28%)
  waiting for transfers between devices  240 us (26%)
  blocking collectives  118 us (13%)
  matrix products  101 us (11%)
  starting transfers between devices  86.6 us (9%)
  other arithmetic  59.9 us (6%)
  local copies, waits for them, and re-layouts  37.9 us (4%)
  between operations  15.4 us (2%)
    pallas_call x1, Pallas kernels, attn_backward(): pl.pallas_call(functools.partial(attn_bwd_kernel, head=head, factor=head...  84.1 us
    all_to_all x1, blocking collectives, body_paired(): lax.all_to_all(qkv_t, 'dp', split_axis=0, concat_axis=0, tiled=True)  76 us
    ppermute x14, waiting for transfers between devices, from_bit(): lax.ppermute(value, 'dp', [(i, i ^ bit) for i in range(lax.axis_size('dp'...  75.1 us
    all_to_all x1, waiting for transfers between devices, body_paired(): lax.all_to_all(grad_head, 'dp', split_axis=0, concat_axis=0, tiled=True)  69 us
    dot_general x8, matrix products, matmul_tn(): lax.dot_general(left, right, (((0,), (0,)), ((), ())), preferred_element_...  64.7 us
    pallas_call x3, Pallas kernels, mlp_forward(): pl.pallas_call(functools.partial(mlp_kernel, kinds=kinds, transposed=tran...  63.6 us
    pallas_call x3, Pallas kernels, mlp_backward(): pl.pallas_call(functools.partial(mlp_back_kernel, kinds=kinds, transposed...  62.5 us
    pallas_call x1, Pallas kernels, attn_forward(): pl.pallas_call(functools.partial(attn_fwd_kernel, head=head, factor=head...  47.6 us
  transfers between devices with their start and end apart: 50, of which 29 were waited for; matrix products, arithmetic and copies ran while one was open for 18% of the time, Pallas kernels for 24%

profile of v6, /device:TPU:9, one launch (start us, length us, event | category | flops | bytes accessed | tf_op | source)
XLA Modules:
  0.0 916.0 jit_solution(3055992675032000162)
XLA Ops:
  17.2 6.7 collective-permute-done.2
  23.9 7.0 collective-permute-done.3
  30.9 5.8 collective-permute-done.4
  42.3 6.7 collective-permute-done.7
  54.3 15.4 %collective-permute-done.8 = bf16[4,2,72,768]{3,2,0,1:T(8,128)(2,1)S(1)} collective-permute-done((bf16[4,2,72,768]{3,2,0,1:T(8,128)(2,1)S(1)}, bf16[4,2,72,768]{3,2,0,1:T(8,128)(2,1)S(1)}, u32[]{:S(2)}, u32[]{:S(2)}) %collective-permute-start.8) | collective-permute-done | bytes 884768 | tf_op jit(solution)/shard_map/ppermute | solution.py:778
  88.8 76.0 %all_to_all.40 = bf16[16,192,512]{2,1,0:T(8,128)(2,1)S(1)} all-to-all(bf16[16,192,512]{2,1,0:T(8,128)(2,1)} %bitcast.132), channel_id=1, replica_groups=mesh['dp'=16,'tensor'=2] {'dp'}, dimensions={0} | all-to-all | bytes 6291456 | tf_op jit(solution)/shard_map/all_to_all | solution.py:952
  166.5 4.3 collective-permute-start.10
  174.8 47.6 %attn_fwd.1 = (bf16[20,64,512]{2,1,0:T(8,128)(2,1)S(1)}, f32[20,1,512]{2,1,0:T(1,128)S(1)}) custom-call(s32[4,20]{1,0:T(4,128)S(1)} %add_select_fusion.2.plan, bf16[20,192,512]{2,1,0:T(8,128)(2,1)S(1)} %constant_dynamic-update-slice_fusion.own, bf16[16,128,512]{2,1,0:T(8,128)(2,1)S(1)} %broadcast_select_fusion.prompts), custom_call_target="tpu_custom_call" | custom-call | flops 26843545600 | bytes 8388608 | tf_op jit(solution)/shard_map/attn_fwd/pallas_call | solution.py:552
  223.9 9.7 %collective-permute-done.12 = bf16[4,64,512]{2,1,0:T(8,128)(2,1)S(1)} collective-permute-done((bf16[4,64,512]{2,1,0:T(8,128)(2,1)S(1)}, bf16[4,64,512]{2,1,0:T(8,128)(2,1)S(1)}, u32[]{:S(2)}, u32[]{:S(2)}) %collective-permute-start.12) | collective-permute-done | bytes 262176 | tf_op jit(solution)/shard_map/ppermute | solution.py:609
  234.7 4.1 all-to-all-start.1
  239.0 33.5 %all-gather.7.cloned.1.call-done = bf16[16,64,4608]{2,1,0:T(8,128)(2,1)} async-done(((bf16[4,64,4608]{2,1,0:T(8,128)(2,1)}), bf16[16,64,4608]{2,1,0:T(8,128)(2,1)}) %all-gather.7.cloned.1.call-update) | async-done | bytes 9437200 | tf_op jit(solution)/shard_map/all_gather | solution.py:955
  272.5 8.2 copy.128
  295.0 5.5 all-to-all-start.2
  300.5 17.3 %mlp_fwd.3 = (bf16[1024,1024]{1,0:T(8,128)(2,1)}, bf16[1024,2048]{1,0:T(8,128)(2,1)}, bf16[1024,2048]{1,0:T(8,128)(2,1)}, bf16[512,1024]{1,0:T(8,128)(2,1)}, bf16[512,1024]{1,0:T(8,128)(2,1)}) custom-call(bf16[512,1024]{1,0:T(8,128)(2,1)} %multiply_convert_fusion.1.refs_0_, bf16[512,1024]{1,0:T(8,128)(2,1)} %collective-permute-done.14.refs_1_, ...), custom_call_target="tpu_custom_call" | custom-call | flops 8589934592 | bytes 20971520 | tf_op jit(solution)/shard_map/mlp_fwd/pallas_call | solution.py:721
  325.8 10.4 %all-to-all-done.2 = bf16[16,48,1024]{2,1,0:T(8,128)(2,1)} async-done(((bf16[16,48,1024]{2,1,0:T(8,128)(2,1)}), bf16[16,48,1024]{2,1,0:T(8,128)(2,1)}, u32[]{:S(2)}, u32[]{:S(2)}) %all-to-all-start.2) | async-done | bytes 1572896 | tf_op jit(solution)/shard_map/all_to_all | solution.py:52
  336.2 41.5 %all_to_all.41 = bf16[16,48,1024]{2,1,0:T(8,128)(2,1)} all-to-all(bf16[16,48,1024]{2,1,0:T(8,128)(2,1)} %bitcast.158), channel_id=1, replica_groups=mesh['dp'=16,'tensor'=2] {'dp'}, dimensions={0} | all-to-all | bytes 3145728 | tf_op jit(solution)/shard_map/all_to_all | solution.py:52
  383.5 22.2 %mlp_fwd.4 = (bf16[1536,1024]{1,0:T(8,128)(2,1)}, bf16[1536,2048]{1,0:T(8,128)(2,1)}, bf16[1536,2048]{1,0:T(8,128)(2,1)}, bf16[768,1024]{1,0:T(8,128)(2,1)}, bf1...) custom-call(bf16[768,1024]{1,0:T(8,128)(2,1)} %bitcast.31.refs_0_, bf16[768,1024]{1,0:T(8,128)(2,1)} %collective-permute-done.16.refs_1_, ...), custom_call_target="tpu_custom_call" | custom-call | flops 12884901888 | bytes 27262976 | tf_op jit(solution)/shard_map/mlp_fwd/pallas_call | solution.py:721
  411.9 24.1 %mlp_fwd.5 = (bf16[1536,1024]{1,0:T(8,128)(2,1)}, bf16[1536,2048]{1,0:T(8,128)(2,1)}, bf16[1536,2048]{1,0:T(8,128)(2,1)}, bf16[768,1024]{1,0:T(8,128)(2,1)}, bf16[768,1024]{1,0:T(8,128)(2,1)}) custom-call(bf16[1536,1024]{1,0:T(8,128)(2,1)} %get-tuple-element.113.refs_0_, bf16[768,1024]{1,0:T(8,128)(2,1)} %get-tuple-element.96.refs_1_, ...), custom_call_target="tpu_custom_call" | custom-call | flops 12884901888 | bytes 27262976 | tf_op jit(solution)/shard_map/mlp_fwd/pallas_call | solution.py:721
  437.6 21.9 %mlp_bwd.3 = (bf16[1536,1024]{1,0:T(8,128)(2,1)}, bf16[1536,2048]{1,0:T(8,128)(2,1)}, bf16[768,1024]{1,0:T(8,128)(2,1)}, bf16[768,1024]{1,0:T(8,128)(2,1)}) custom-call(f32[1536,1]{1,0:T(8,128)} %broadcast_select_fusion.9.refs_0_, bf16[768,1024]{1,0:T(8,128)(2,1)} %bitcast.30.refs_1_, bf16[768,1024]{1,0:T(8,128)(2,1)} %copy-done.63, ...), custom_call_target="tpu_custom_call" | custom-call | flops 12884901888 | bytes 27262976 | tf_op jit(solution)/shard_map/mlp_bwd/pallas_call | solution.py:755
  462.4 4.5 multiply_reduce_fusion.1
  467.9 4.1 select_convert_fusion
  472.0 4.6 all-to-all-start.4
  476.7 24.0 %mlp_bwd.4 = (bf16[1536,1024]{1,0:T(8,128)(2,1)}, bf16[1536,2048]{1,0:T(8,128)(2,1)}, bf16[768,1024]{1,0:T(8,128)(2,1)}, bf16[768,1024]{1,0:T(8,128)(2,1)}) custom-call(f32[1536,1]{1,0:T(8,128)} %broadcast_select_fusion.9.refs_0_, bf16[768,1024]{1,0:T(8,128)(2,1)} %bitcast.30.refs_1_, bf16[768,1024]{1,0:T(8,128)(2,1)} %copy-done.63, ...), custom_call_target="tpu_custom_call" | custom-call | flops 12884901888 | bytes 27262976 | tf_op jit(solution)/shard_map/mlp_bwd/pallas_call | solution.py:755
  504.4 4.0 add_convert_fusion.1
  508.4 4.4 all-to-all-done.4
  512.8 6.2 all-to-all-start.5
  519.0 12.0 %fusion.57 = f32[1024,2048]{1,0:T(8,128)} fusion(bf16[1536,1024]{1,0:T(8,128)(2,1)} %get-tuple-element.113.refs_0_, bf16[1536,2048]{1,0:T(8,128)(2,1)} %get-tuple-element.114), kind=kOutput, calls=%fused_computation.208 | convolution fusion | flops 6442450944 | bytes 17825792 | tf_op jit(solution)/shard_map/dot_general | solution.py:60
  531.0 11.1 %fusion.56 = f32[2048,1024]{1,0:T(8,128)} fusion(bf16[1536,2048]{1,0:T(8,128)(2,1)} %get-tuple-element.111, bf16[1536,1024]{1,0:T(8,128)(2,1)S(1)} %copy-done.72), kind=kOutput, calls=%fused_computation.207 | convolution fusion | flops 6442450944 | bytes 17825792 | tf_op jit(solution)/shard_map/dot_general | solution.py:60
  542.0 12.4 %all-to-all-done.5 = bf16[16,48,1024]{2,1,0:T(8,128)(2,1)} async-done(((bf16[16,48,1024]{2,1,0:T(8,128)(2,1)}), bf16[16,48,1024]{2,1,0:T(8,128)(2,1)}, u32[]{:S(2)}, u32[]{:S(2)}) %all-to-all-start.5) | async-done | bytes 1572896 | tf_op jit(solution)/shard_map/all_to_all | solution.py:52
  563.4 16.6 %mlp_bwd.5 = (bf16[1024,1024]{1,0:T(8,128)(2,1)}, bf16[1024,2048]{1,0:T(8,128)(2,1)}, bf16[512,1024]{1,0:T(8,128)(2,1)}, bf16[512,1024]{1,0:T(8,128)(2,1)}) custom-call(bf16[512,1024]{1,0:T(8,128)(2,1)} %copy-done.67, bf16[512,1024]{1,0:T(8,128)(2,1)} %copy-done.68, bf16[1024,4608]{1,0:T(8,128)(2,1)} %bitcast.137, bf16[1024,4608]{1,0:T(8,128)(2,1)} %bitcast.138, ...), custom_call_target="tpu_custom_call" | custom-call | flops 8589934592 | bytes 20971520 | tf_op jit(solution)/shard_map/mlp_bwd/pallas_call | solution.py:755
  594.5 4.2 all-to-all-start.6
  598.8 7.5 convolution_convert_fusion.2
  606.4 5.3 convolution_convert_fusion.1
  613.7 5.3 pad_maximum_fusion
  619.0 4.0 all-to-all-done.6
  624.7 4.9 collective-permute-start.27
  631.8 84.1 %attn_bwd.1 = (bf16[20,192,512]{2,1,0:T(8,128)(2,1)}, bf16[16,128,512]{2,1,0:T(8,128)(2,1)S(1)}) custom-call(s32[4,20]{1,0:T(4,128)S(1)} %copy-done.3, bf16[20,192,512]{2,1,0:T(8,128)(2,1)} %copy-done, bf16[16,128,512]{2,1,0:T(8,128)(2,1)} %copy-done.1, bf16[20,64,512]{2,1,0:T(8,128)(2,1)S(1)} %pad_maximum_fusion.7.grad, ...), custom_call_target="tpu_custom_call" | custom-call | flops 67108864000 | bytes 16777216 | tf_op jit(solution)/shard_map/attn_bwd/pallas_call | solution.py:579
  715.9 5.1 collective-permute-start.28
  729.0 5.2 all-to-all-start.7
  734.3 12.0 %fusion.59 = f32[1024,2048]{1,0:T(8,128)} fusion(bf16[1536,1024]{1,0:T(8,128)(2,1)} %get-tuple-element.139, bf16[1536,2048]{1,0:T(8,128)(2,1)} %get-tuple-element.140), kind=kOutput, calls=%fused_computation.210 | convolution fusion | flops 6442450944 | bytes 17825792 | tf_op jit(solution)/shard_map/dot_general | solution.py:60
  746.3 11.1 %fusion.58 = f32[2048,1024]{1,0:T(8,128)} fusion(bf16[1536,2048]{1,0:T(8,128)(2,1)} %get-tuple-element.137, bf16[1536,1024]{1,0:T(8,128)(2,1)S(1)} %copy-done.73), kind=kOutput, calls=%fused_computation.209 | convolution fusion | flops 6442450944 | bytes 17825792 | tf_op jit(solution)/shard_map/dot_general | solution.py:60
  757.4 69.0 %all-to-all-done.7 = bf16[16,192,512]{2,1,0:T(8,128)(2,1)} async-done(((bf16[16,192,512]{2,1,0:T(8,128)(2,1)}), bf16[16,192,512]{2,1,0:T(8,128)(2,1)}, u32[]{:S(2)}, u32[]{:S(2)}) %all-to-all-start.7) | async-done | bytes 3145760 | tf_op jit(solution)/shard_map/all_to_all | solution.py:1155
  836.9 3.9 add_convert_fusion.4
  840.8 5.4 convolution_convert_fusion
  850.9 4.9 fusion.2
  856.8 10.6 %collective-permute-done.34 = bf16[4,2,64,768]{3,2,0,1:T(8,128)(2,1)S(1)} collective-permute-done((bf16[4,2,64,768]{3,2,0,1:T(8,128)(2,1)S(1)}, bf16[4,2,64,768]{3,2,0,1:T(8,128)(2,1)S(1)}, u32[]{:S(2)}, u32[]{:S(2)}) %collective-permute-start.34) | collective-permute-done | bytes 786464 | tf_op jit(solution)/shard_map/ppermute | solution.py:778
  871.1 6.7 collective-permute-done.35
  886.9 11.7 %collective-permute-done.38 = bf16[64,1536]{1,0:T(8,128)(2,1)S(1)} collective-permute-done((bf16[64,1536]{1,0:T(8,128)(2,1)S(1)}, bf16[64,1536]{1,0:T(8,128)(2,1)S(1)}, u32[]{:S(2)}, u32[]{:S(2)}) %collective-permute-start.38) | collective-permute-done | bytes 196640 | tf_op jit(solution)/shard_map/ppermute | solution.py:778
  (380 shorter events, 167.6 us)
Async XLA Ops:
  7.2 81.6 %all-gather.5.cloned.1.call-start = ((), (), s32[]{:S(2)}) async-start(), calls=%async_computation.10 | async-start | bytes 2949120 | tf_op jit(solution)/shard_map/all_gather | solution.py:903
  8.1 6.2 collective-permute-start.1
  14.5 9.4 %collective-permute-start.2 = (bf16[72,1536]{1,0:T(8,128)(2,1)S(1)}, bf16[72,1536]{1,0:T(8,128)(2,1)S(1)}, u32[]{:S(2)}, u32[]{:S(2)}) collective-permute-start(bf16[72,1536]{1,0:T(8,128)(2,1)S(1)} %fusion.23), channel_id=1, source_target_pairs={{0,8},{2,10},{4,12},{6,14},{8,0},{10,2},{12,4},{14,6},{16,24},{18,... | collective-permute-start | bytes 663560 | tf_op jit(solution)/shard_map/ppermute | solution.py:778
  14.5 16.4 %collective-permute-start.3 = (bf16[72,1536]{1,0:T(8,128)(2,1)S(1)}, bf16[72,1536]{1,0:T(8,128)(2,1)S(1)}, u32[]{:S(2)}, u32[]{:S(2)}) collective-permute-start(bf16[72,1536]{1,0:T(8,128)(2,1)S(1)} %fusion.23), channel_id=1, source_target_pairs={{0,16},{2,18},{4,20},{6,22},{8,24},{10,26},{12,28},{14,30},{16,0},... | collective-permute-start | bytes 663560 | tf_op jit(solution)/shard_map/ppermute | solution.py:778
  17.0 19.7 %collective-permute-start.4 = (bf16[72,1536]{1,0:T(8,128)(2,1)S(1)}, bf16[72,1536]{1,0:T(8,128)(2,1)S(1)}, u32[]{:S(2)}, u32[]{:S(2)}) collective-permute-start(bf16[72,1536]{1,0:T(8,128)(2,1)S(1)} %fusion.23), channel_id=1, source_target_pairs={{0,24},{2,26},{4,28},{6,30},{8,16},{10,18},{12,20},{14,22},{16,8},... | collective-permute-start | bytes 663560 | tf_op jit(solution)/shard_map/ppermute | solution.py:778
  38.1 10.9 %collective-permute-start.7 = (bf16[4,72,768]{2,1,0:T(8,128)(2,1)}, bf16[4,72,768]{2,1,0:T(8,128)(2,1)}, u32[]{:S(2)}, u32[]{:S(2)}) collective-permute-start(bf16[4,72,768]{2,1,0:T(8,128)(2,1)} %get-tuple-element.176), channel_id=1, source_target_pairs={{0,2},{2,0},{4,6},{6,4},{8,10},{10,8},{12,14},{14,12},{16,18},{18,... | collective-permute-start | bytes 1327112 | tf_op jit(solution)/shard_map/ppermute | solution.py:778
  39.3 12.3 %collective-permute-start.5 = (bf16[4,72,768]{2,1,0:T(8,128)(2,1)}, bf16[4,72,768]{2,1,0:T(8,128)(2,1)S(1)}, u32[]{:S(2)}, u32[]{:S(2)}) collective-permute-start(bf16[4,72,768]{2,1,0:T(8,128)(2,1)} %get-tuple-element.177), channel_id=1, source_target_pairs={{0,4},{2,6},{4,0},{6,2},{8,12},{10,14},{12,8},{14,10},{16,20},{18,... | collective-permute-start | bytes 1327112 | tf_op jit(solution)/shard_map/ppermute | solution.py:778
  40.5 12.7 %collective-permute-start = (bf16[512,1024]{1,0:T(8,128)(2,1)S(1)}, bf16[512,1024]{1,0:T(8,128)(2,1)S(1)}, u32[]{:S(2)}, u32[]{:S(2)}) collective-permute-start(bf16[512,1024]{1,0:T(8,128)(2,1)S(1)} %copy-done.5), channel_id=1, source_target_pairs={{0,1},{1,0},{2,3},{3,2},{4,5},{5,4},{6,7},{7,6},{8,9},{9,8},{10,11... | collective-permute-start | bytes 3145736 | tf_op jit(solution)/shard_map/ppermute | solution.py:605
  42.2 230.3 %all-gather.7.cloned.1.call-start = ((), (), s32[]{:S(2)}) async-start(), calls=%async_computation.11 | async-start | bytes 11796480 | tf_op jit(solution)/shard_map/all_gather | solution.py:955
  50.3 19.4 %collective-permute-start.8 = (bf16[4,2,72,768]{3,2,0,1:T(8,128)(2,1)S(1)}, bf16[4,2,72,768]{3,2,0,1:T(8,128)(2,1)S(1)}, u32[]{:S(2)}, u32[]{:S(2)}) collective-permute-start(bf16[4,2,72,768]{3,2,0,1:T(8,128)(2,1)S(1)} %maximum_select_fusion.4), channel_id=1, source_target_pairs={{0,4},{2,6},{4,0},{6,2},{8,12},{10,14},{12,8},{14,10},{16,20},{18,... | collective-permute-start | bytes 2654216 | tf_op jit(solution)/shard_map/ppermute | solution.py:778
  51.8 19.5 %collective-permute-start.6 = (bf16[4,2,72,768]{3,2,0,1:T(8,128)(2,1)S(1)}, bf16[4,2,72,768]{3,2,0,1:T(8,128)(2,1)S(1)}, u32[]{:S(2)}, u32[]{:S(2)}) collective-permute-start(bf16[4,2,72,768]{3,2,0,1:T(8,128)(2,1)S(1)} %maximum_select_fusion.3), channel_id=1, source_target_pairs={{0,2},{2,0},{4,6},{6,4},{8,10},{10,8},{12,14},{14,12},{16,18},{18,... | collective-permute-start | bytes 2654216 | tf_op jit(solution)/shard_map/ppermute | solution.py:778
  78.2 5.9 collective-permute-start.9
  165.1 7.7 collective-permute-start.11
  166.5 6.2 collective-permute-start.10
  222.5 11.0 %collective-permute-start.12 = (bf16[4,64,512]{2,1,0:T(8,128)(2,1)S(1)}, bf16[4,64,512]{2,1,0:T(8,128)(2,1)S(1)}, u32[]{:S(2)}, u32[]{:S(2)}) collective-permute-start(bf16[4,64,512]{2,1,0:T(8,128)(2,1)S(1)} %slice.194), channel_id=1, source_target_pairs={{0,1},{2,3},{4,5},{6,7},{8,9},{10,11},{12,13},{14,15},{16,17},{18,... | collective-permute-start | bytes 786440 | tf_op jit(solution)/shard_map/ppermute | solution.py:609
  234.7 53.0 %all-to-all-start.1 = ((bf16[16,64,512]{2,1,0:T(8,128)(2,1)}), bf16[16,64,512]{2,1,0:T(8,128)(2,1)S(1)}, u32[]{:S(2)}, u32[]{:S(2)}) async-start(bf16[16,64,512]{2,1,0:T(8,128)(2,1)} %pad_maximum_fusion.8), calls=%async_computation.1 | async-start | bytes 2097152 | tf_op jit(solution)/shard_map/all_to_all | solution.py:989
  282.1 7.9 collective-permute-start.13
  294.9 5.6 collective-permute-start.14
  295.0 41.3 %all-to-all-start.2 = ((bf16[16,48,1024]{2,1,0:T(8,128)(2,1)}), bf16[16,48,1024]{2,1,0:T(8,128)(2,1)}, u32[]{:S(2)}, u32[]{:S(2)}) async-start(bf16[16,48,1024]{2,1,0:T(8,128)(2,1)} %bitcast.157), calls=%async_computation.2 | async-start | bytes 3145728 | tf_op jit(solution)/shard_map/all_to_all | solution.py:52
  317.8 3.5 collective-permute-start.15
  377.8 5.8 collective-permute-start.16
  405.8 5.6 collective-permute-start.18
  406.3 5.6 collective-permute-start.19
  408.8 27.7 %collective-permute-start.17 = (bf16[768,1024]{1,0:T(8,128)(2,1)}, bf16[768,1024]{1,0:T(8,128)(2,1)S(1)}, u32[]{:S(2)}, u32[]{:S(2)}) collective-permute-start(bf16[768,1024]{1,0:T(8,128)(2,1)} %bitcast.30.refs_1_), channel_id=1, source_target_pairs={{0,1},{1,0},{2,3},{3,2},{4,5},{5,4},{6,7},{7,6},{8,9},{9,8},{10,11... | collective-permute-start | bytes 4718600 | tf_op jit(solution)/shard_map/ppermute | solution.py:605
  436.0 26.4 %collective-permute-start.23 = (bf16[768,1024]{1,0:T(8,128)(2,1)}, bf16[768,1024]{1,0:T(8,128)(2,1)}, u32[]{:S(2)}, u32[]{:S(2)}) collective-permute-start(bf16[768,1024]{1,0:T(8,128)(2,1)} %get-tuple-element.105), channel_id=1, source_target_pairs={{0,1},{1,0},{2,3},{3,2},{4,5},{5,4},{6,7},{7,6},{8,9},{9,8},{10,11... | collective-permute-start | bytes 4718600 | tf_op jit(solution)/shard_map/ppermute | solution.py:605
  459.5 17.1 %collective-permute-start.20 = (bf16[768,1024]{1,0:T(8,128)(2,1)}, bf16[768,1024]{1,0:T(8,128)(2,1)}, u32[]{:S(2)}, u32[]{:S(2)}) collective-permute-start(bf16[768,1024]{1,0:T(8,128)(2,1)} %get-tuple-element.100.refs_4_), channel_id=1, source_target_pairs={{0,1},{1,0},{2,3},{3,2},{4,5},{5,4},{6,7},{7,6},{8,9},{9,8},{10,11... | collective-permute-start | bytes 4718600 | tf_op jit(solution)/shard_map/ppermute | solution.py:605
  459.7 16.9 %collective-permute-start.21 = (bf16[768,1024]{1,0:T(8,128)(2,1)}, bf16[768,1024]{1,0:T(8,128)(2,1)}, u32[]{:S(2)}, u32[]{:S(2)}) collective-permute-start(bf16[768,1024]{1,0:T(8,128)(2,1)} %get-tuple-element.99.refs_3_), channel_id=1, source_target_pairs={{0,1},{1,0},{2,3},{3,2},{4,5},{5,4},{6,7},{7,6},{8,9},{9,8},{10,11... | collective-permute-start | bytes 4718600 | tf_op jit(solution)/shard_map/ppermute | solution.py:605
  472.0 40.8 %all-to-all-start.4 = ((bf16[16,48,1024]{2,1,0:T(8,128)(2,1)}), bf16[16,48,1024]{2,1,0:T(8,128)(2,1)}, u32[]{:S(2)}, u32[]{:S(2)}) async-start(bf16[16,48,1024]{2,1,0:T(8,128)(2,1)} %bitcast.142), calls=%async_computation.4 | async-start | bytes 3145728 | tf_op jit(solution)/shard_map/all_to_all | solution.py:52
  500.7 3.7 collective-permute-start.22
  512.8 41.7 %all-to-all-start.5 = ((bf16[16,48,1024]{2,1,0:T(8,128)(2,1)}), bf16[16,48,1024]{2,1,0:T(8,128)(2,1)}, u32[]{:S(2)}, u32[]{:S(2)}) async-start(bf16[16,48,1024]{2,1,0:T(8,128)(2,1)} %bitcast.141), calls=%async_computation.5 | async-start | bytes 3145728 | tf_op jit(solution)/shard_map/all_to_all | solution.py:52
  557.2 5.2 collective-permute-start.24
  594.1 17.6 %collective-permute-start.26 = (bf16[1024,512]{1,0:T(8,128)(2,1)}, bf16[1024,512]{1,0:T(8,128)(2,1)}, u32[]{:S(2)}, u32[]{:S(2)}) collective-permute-start(bf16[1024,512]{1,0:T(8,128)(2,1)} %convolution_convert_fusion.7), channel_id=1, source_target_pairs={{0,1},{1,0},{2,3},{3,2},{4,5},{5,4},{6,7},{7,6},{8,9},{9,8},{10,11... | collective-permute-start | bytes 3145736 | tf_op jit(solution)/shard_map/ppermute | solution.py:605
  594.5 28.6 %all-to-all-start.6 = ((bf16[16,64,512]{2,1,0:T(8,128)(2,1)}), bf16[16,64,512]{2,1,0:T(8,128)(2,1)}, u32[]{:S(2)}, u32[]{:S(2)}) async-start(bf16[16,64,512]{2,1,0:T(8,128)(2,1)} %bitcast.143), calls=%async_computation.6 | async-start | bytes 2097152 | tf_op jit(solution)/shard_map/all_to_all | solution.py:1123
  598.7 303.6 %reduce-scatter.2.cloned.1.call-start = ((), (), s32[]{:S(2)}) async-start(), calls=%async_computation.9 | async-start | bytes 10027008 | tf_op jit(solution)/shard_map/reduce_scatter | solution.py:1137
  624.7 5.7 collective-permute-start.27
  715.9 9.9 %collective-permute-start.28 = (bf16[16,128,512]{2,1,0:T(8,128)(2,1)S(1)}, bf16[16,128,512]{2,1,0:T(8,128)(2,1)S(1)}, u32[]{:S(2)}, u32[]{:S(2)}) collective-permute-start(bf16[16,128,512]{2,1,0:T(8,128)(2,1)S(1)} %get-tuple-element.131), channel_id=1, source_target_pairs={{1,0},{3,2},{5,4},{7,6},{9,8},{11,10},{13,12},{15,14},{17,16},{19,... | collective-permute-start | bytes 6291464 | tf_op jit(solution)/shard_map/ppermute | solution.py:613
  722.2 4.5 collective-permute-start.29
  729.0 97.3 %all-to-all-start.7 = ((bf16[16,192,512]{2,1,0:T(8,128)(2,1)}), bf16[16,192,512]{2,1,0:T(8,128)(2,1)}, u32[]{:S(2)}, u32[]{:S(2)}) async-start(bf16[16,192,512]{2,1,0:T(8,128)(2,1)} %maximum_select_fusion), calls=%async_computation.7 | async-start | bytes 6291456 | tf_op jit(solution)/shard_map/all_to_all | solution.py:1155
  830.1 10.7 %collective-permute-start.30 = (bf16[1536,512]{1,0:T(8,128)(2,1)}, bf16[1536,512]{1,0:T(8,128)(2,1)}, u32[]{:S(2)}, u32[]{:S(2)}) collective-permute-start(bf16[1536,512]{1,0:T(8,128)(2,1)} %bitcast.43), channel_id=1, source_target_pairs={{0,1},{1,0},{2,3},{3,2},{4,5},{5,4},{6,7},{7,6},{8,9},{9,8},{10,11... | collective-permute-start | bytes 4718600 | tf_op jit(solution)/shard_map/ppermute | solution.py:605
  846.5 20.9 %collective-permute-start.34 = (bf16[4,2,64,768]{3,2,0,1:T(8,128)(2,1)S(1)}, bf16[4,2,64,768]{3,2,0,1:T(8,128)(2,1)S(1)}, u32[]{:S(2)}, u32[]{:S(2)}) collective-permute-start(bf16[4,2,64,768]{3,2,0,1:T(8,128)(2,1)S(1)} %select_bitcast_fusion), channel_id=1, source_target_pairs={{0,4},{2,6},{4,0},{6,2},{8,12},{10,14},{12,8},{14,10},{16,20},{18,... | collective-permute-start | bytes 2359304 | tf_op jit(solution)/shard_map/ppermute | solution.py:778
  849.8 19.1 %collective-permute-start.32 = (bf16[4,2,64,768]{3,2,0,1:T(8,128)(2,1)S(1)}, bf16[4,2,64,768]{3,2,0,1:T(8,128)(2,1)S(1)}, u32[]{:S(2)}, u32[]{:S(2)}) collective-permute-start(bf16[4,2,64,768]{3,2,0,1:T(8,128)(2,1)S(1)} %select_bitcast_fusion.1), channel_id=1, source_target_pairs={{0,2},{2,0},{4,6},{6,4},{8,10},{10,8},{12,14},{14,12},{16,18},{18,... | collective-permute-start | bytes 2359304 | tf_op jit(solution)/shard_map/ppermute | solution.py:778
  855.9 14.5 %collective-permute-start.31 = (bf16[512,1024]{1,0:T(8,128)(2,1)S(1)}, bf16[512,1024]{1,0:T(8,128)(2,1)S(1)}, u32[]{:S(2)}, u32[]{:S(2)}) collective-permute-start(bf16[512,1024]{1,0:T(8,128)(2,1)S(1)} %slice.345), channel_id=1, source_target_pairs={{0,1},{1,0},{2,3},{3,2},{4,5},{5,4},{6,7},{7,6},{8,9},{9,8},{10,11... | collective-permute-start | bytes 3145736 | tf_op jit(solution)/shard_map/ppermute | solution.py:605
  867.8 10.0 %collective-permute-start.35 = (bf16[4,64,768]{2,1,0:T(8,128)(2,1)S(1)}, bf16[4,64,768]{2,1,0:T(8,128)(2,1)S(1)}, u32[]{:S(2)}, u32[]{:S(2)}) collective-permute-start(bf16[4,64,768]{2,1,0:T(8,128)(2,1)S(1)} %select_bitcast_fusion.2), channel_id=1, source_target_pairs={{0,2},{2,0},{4,6},{6,4},{8,10},{10,8},{12,14},{14,12},{16,18},{18,... | collective-permute-start | bytes 1179656 | tf_op jit(solution)/shard_map/ppermute | solution.py:778
  869.2 9.7 %collective-permute-start.33 = (bf16[4,64,768]{2,1,0:T(8,128)(2,1)S(1)}, bf16[4,64,768]{2,1,0:T(8,128)(2,1)S(1)}, u32[]{:S(2)}, u32[]{:S(2)}) collective-permute-start(bf16[4,64,768]{2,1,0:T(8,128)(2,1)S(1)} %select_bitcast_fusion.3), channel_id=1, source_target_pairs={{0,4},{2,6},{4,0},{6,2},{8,12},{10,14},{12,8},{14,10},{16,20},{18,... | collective-permute-start | bytes 1179656 | tf_op jit(solution)/shard_map/ppermute | solution.py:778
  879.1 4.6 collective-permute-start.36
  879.2 7.7 collective-permute-start.37
  880.3 18.4 %collective-permute-start.38 = (bf16[64,1536]{1,0:T(8,128)(2,1)S(1)}, bf16[64,1536]{1,0:T(8,128)(2,1)S(1)}, u32[]{:S(2)}, u32[]{:S(2)}) collective-permute-start(bf16[64,1536]{1,0:T(8,128)(2,1)S(1)} %get-tuple-element.184), channel_id=1, source_target_pairs={{0,24},{2,26},{4,28},{6,30},{8,16},{10,18},{12,20},{14,22},{16,8},... | collective-permute-start | bytes 589832 | tf_op jit(solution)/shard_map/ppermute | solution.py:778
  904.2 4.4 collective-permute-start.39
  (77 other events, 976.4 us)
Sparse Core Ops, SparseCore 0:
  42.4 46.3 all-gather.4
  165.0 107.4 all-gather.6
  629.7 215.3 reduce-scatter.1

commit v7 on v6

--- a/solution.py
+++ b/solution.py
@@ -654,7 +654,20 @@
         refs[1][...] = value
 
 
-def mlp_kernel(*refs, kinds, transposed, gated):
+def copy_in(source, target, semaphore, at):
+    if at is not None:
+        source = source.at[:, at : at + target.shape[1]]
+    return pltpu.make_async_copy(source, target, semaphore)
+
+
+def mlp_kernel(*refs, kinds, transposed, gated, at):
+    *refs, held, semaphore = refs
+    w_out = refs[sum(kinds) + len(kinds) + gated + 1]
+
+    @pl.when(pl.program_id(0) == 0)
+    def _():
+        copy_in(w_out, held, semaphore, at).start()
+
     terms, refs = take_terms(refs, kinds)
     rows = terms[0]
     if len(terms) > 1:
@@ -671,11 +684,23 @@
     act, slope = gelu_pair(matmul(rows, w_in[...]))
     kept_act[...] = act
     kept_slope[...] = slope
-    result = (matmul_nt if transposed else matmul)(act, w_out[...])
+
+    @pl.when(pl.program_id(0) == 0)
+    def _():
+        copy_in(w_out, held, semaphore, at).wait()
+
+    result = (matmul_nt if transposed else matmul)(act, held[...])
     give_halves((first, second), result.astype(BF16))
 
 
-def mlp_back_kernel(*refs, kinds, transposed, scaled):
+def mlp_back_kernel(*refs, kinds, transposed, scaled, at):
+    *refs, held, semaphore = refs
+    w_in = refs[scaled + sum(kinds) + len(kinds) + 1]
+
+    @pl.when(pl.program_id(0) == 0)
+    def _():
+        copy_in(w_in, held, semaphore, at).start()
+
     factor, refs = (refs[0], refs[1:]) if scaled else (None, refs)
     terms, refs = take_terms(refs, kinds)
     grad = terms[0]
@@ -689,7 +714,12 @@
     grad = (matmul_nt if transposed else matmul)(grad, w_out[...])
     grad_pre = (grad * slope[...].astype(F32)).astype(BF16)
     kept_pre[...] = grad_pre
-    give_halves((first, second), matmul_nt(grad_pre, w_in[...]).astype(BF16))
+
+    @pl.when(pl.program_id(0) == 0)
+    def _():
+        copy_in(w_in, held, semaphore, at).wait()
+
+    give_halves((first, second), matmul_nt(grad_pre, held[...]).astype(BF16))
 
 
 def mlp_blocks(terms, length):
@@ -712,16 +742,18 @@
     hidden_block = pl.BlockSpec((length, hidden), lambda m: (m, 0))
     once = dict(pipeline_mode=pl.Buffered(1))
     in_block = pl.BlockSpec((width, hidden), lambda m: (0, columns[0]), **once)
-    out_block = (
-        pl.BlockSpec((width, hidden), lambda m: (0, columns[1]), **once)
-        if transposed
-        else pl.BlockSpec((hidden, width), lambda m: (0, 0), **once)
-    )
+    out_shape = (width, hidden) if transposed else (hidden, width)
     gated = centre is not None
     return pl.pallas_call(
-        functools.partial(mlp_kernel, kinds=kinds, transposed=transposed, gated=gated),
+        functools.partial(
+            mlp_kernel,
+            kinds=kinds,
+            transposed=transposed,
+            gated=gated,
+            at=columns[1] * hidden if transposed else None,
+        ),
         grid=(steps,),
-        in_specs=specs + [pl.BlockSpec((1, width), lambda m: (0, 0))] * gated + [in_block, out_block],
+        in_specs=specs + [pl.BlockSpec((1, width), lambda m: (0, 0))] * gated + [in_block, pl.BlockSpec(memory_space=pl.ANY)],
         out_specs=[block, hidden_block, hidden_block]
         + halves
         + [pl.BlockSpec((length, 1), lambda m: (m, 0))] * gated,
@@ -729,11 +761,12 @@
         + [jax.ShapeDtypeStruct((rows, hidden), BF16)] * 2
         + [jax.ShapeDtypeStruct((rows // 2, width), BF16)] * 2
         + [jax.ShapeDtypeStruct((rows, 1), F32)] * gated,
+        scratch_shapes=[pltpu.VMEM(out_shape, BF16), pltpu.SemaphoreType.DMA],
         compiler_params=pltpu.CompilerParams(vmem_limit_bytes=54 * 2**20),
         cost_estimate=pl.CostEstimate(
-            flops=4 * rows * width * hidden,
-            bytes_accessed=4 * width * hidden + 4 * rows * hidden + 4 * rows * width,
-            transcendentals=rows * hidden,
+            flops=rows * width * hidden,
+            bytes_accessed=width * hidden + rows * hidden + rows * width,
+            transcendentals=0,
         ),
         name="mlp_fwd",
     )(*arrays, *([centre] * gated), w_in, w_out)
@@ -750,20 +783,26 @@
         if transposed
         else pl.BlockSpec((width, hidden), lambda m: (0, columns[1]), **once)
     )
-    in_block = pl.BlockSpec((width, hidden), lambda m: (0, columns[0]), **once)
     scaled = factor is not None
     return pl.pallas_call(
-        functools.partial(mlp_back_kernel, kinds=kinds, transposed=transposed, scaled=scaled),
+        functools.partial(
+            mlp_back_kernel,
+            kinds=kinds,
+            transposed=transposed,
+            scaled=scaled,
+            at=None if transposed else columns[0] * hidden,
+        ),
         grid=(steps,),
         in_specs=[pl.BlockSpec((length, 1), lambda m: (m, 0))] * scaled
         + specs
-        + [out_block, in_block, hidden_block],
+        + [out_block, pl.BlockSpec(memory_space=pl.ANY), hidden_block],
         out_specs=[block, hidden_block] + halves,
         out_shape=[
             jax.ShapeDtypeStruct((rows, width), BF16),
             jax.ShapeDtypeStruct((rows, hidden), BF16),
         ]
         + [jax.ShapeDtypeStruct((rows // 2, width), BF16)] * 2,
+        scratch_shapes=[pltpu.VMEM((width, hidden), BF16), pltpu.SemaphoreType.DMA],
         compiler_params=pltpu.CompilerParams(vmem_limit_bytes=54 * 2**20),
         cost_estimate=pl.CostEstimate(
             flops=4 * rows * width * hidden,
@@ -948,10 +987,11 @@
         qkv_full, rows_one[:rows], (((0,), (1,)), ((), ())), preferred_element_type=F32
     ).astype(BF16)
     qkv_t = jnp.concatenate(both(own_t, swap(other_t)), 0).reshape(heads, triple, rows)
-    qkv_t, second_line = lax.optimization_barrier((qkv_t, second_line))
+    qkv_t, second_line, late_grad = lax.optimization_barrier((qkv_t, second_line, grad_out))
+    sent_grad = matmul_tn(placer, late_grad).astype(BF16).reshape(experts, slots_per, width)
     by_head = lax.all_to_all(qkv_t, "dp", split_axis=0, concat_axis=0, tiled=True)
 
-    by_head, second_line = lax.optimization_barrier((by_head, second_line))
+    by_head, second_line, sent_grad = lax.optimization_barrier((by_head, second_line, sent_grad))
     second_all = lax.all_gather(
         second_line, "dp", axis_index_groups=[[4 * z + k for k in range(4)] for z in range(planes)]
     )
@@ -990,9 +1030,6 @@
         width, rows
     )
 
-    sent_grad = matmul_tn(placer, grad_out).astype(BF16).reshape(experts, slots_per, width)
-    attn_t, sent_grad = lax.optimization_barrier((attn_t, sent_grad))
-    grad_own = to_experts(sent_grad).reshape(-1, width)
     half_width = width // 2
     own_heads, other_heads = both(attn_t[:half_width], attn_t[half_width:])
     attn_other = swap(attn_half)
@@ -1021,8 +1058,9 @@
     sent_rows = (
         matmul_tn(placer, hidden_two.astype(BF16)).astype(BF16).reshape(experts, slots_per, width)
     )
-    sent_rows, grad_own = lax.optimization_barrier((sent_rows, grad_own))
-    own_rows = to_experts(sent_rows).reshape(half_rows, width)
+    own_rows, sent_grad = lax.optimization_barrier((to_experts(sent_rows), sent_grad))
+    own_rows = own_rows.reshape(half_rows, width)
+    grad_own = to_experts(sent_grad).reshape(half_rows, width)
     centre = centroids[0]
     length = half_rows // 2
     expert_rows, act_a, slope_a, own_a, other_a, gate_column = mlp_forward(
@@ -1037,6 +1075,7 @@
     middle, act_b, slope_b, own_b, other_b = mlp_forward(
         [expert_rows, (own_a, other_a), from_a], expert_in_b[0], expert_out_b[0], hidden, length
     )
+    own_b, grad_own = lax.optimization_barrier((own_b, grad_own))
     branch_half = (
         own_a.astype(F32) + from_a[0].astype(F32) + own_b.astype(F32) + swap(other_b).astype(F32)
     )

time: 926 us -> 921 us (level)
  blocking collectives: 118 us -> 41.6 us
  waiting for transfers between devices: 240 us -> 298 us
  starting transfers between devices: 86.6 us -> 96.2 us
    all_to_all x1 -> x0, blocking collectives: 76 us -> none  [body_paired(): lax.all_to_all(qkv_t, 'dp', split_axis=0, concat_axis=0, tiled=True)]
    all_to_all x0 -> x1, waiting for transfers between devices: none -> 63.7 us  [body_paired(): lax.all_to_all(qkv_t, 'dp', split_axis=0, concat_axis=0, tiled=True)]
    all_to_all x3, waiting for transfers between devices: 27.2 us -> 16.3 us  [to_experts(): return lax.all_to_all(value, 'dp', split_axis=0, concat_axis=0, tiled=True)]
  transfers between devices with their start and end apart: 50 -> 51, of which waited for: 29 -> 30; matrix products, arithmetic and copies ran while one was open for 18% -> 18% of each run, Pallas kernels for 24% -> 25%
where the time goes in v7:
time: 921 us; the launch traced here: 912 us
  waiting for transfers between devices  298 us (32%)
  Pallas kernels  264 us (29%)
  matrix products  98.8 us (11%)
  starting transfers between devices  96.2 us (10%)
  other arithmetic  59 us (6%)
  blocking collectives  41.6 us (5%)
  local copies, waits for them, and re-layouts  38.5 us (4%)
  between operations  15.7 us (2%)
    pallas_call x1, Pallas kernels, attn_backward(): pl.pallas_call(functools.partial(attn_bwd_kernel, head=head, factor=head...  84.1 us
    ppermute x14, waiting for transfers between devices, from_bit(): lax.ppermute(value, 'dp', [(i, i ^ bit) for i in range(lax.axis_size('dp'...  75.1 us
    pallas_call x3, Pallas kernels, mlp_forward(): pl.pallas_call(functools.partial(mlp_kernel, kinds=kinds, transposed=tran...  70.4 us
    all_to_all x1, waiting for transfers between devices, body_paired(): lax.all_to_all(grad_head, 'dp', split_axis=0, concat_axis=0, tiled=True)  69 us
    dot_general x8, matrix products, matmul_tn(): lax.dot_general(left, right, (((0,), (0,)), ((), ())), preferred_element_...  64.9 us
    all_to_all x1, waiting for transfers between devices, body_paired(): lax.all_to_all(qkv_t, 'dp', split_axis=0, concat_axis=0, tiled=True)  63.7 us
    pallas_call x3, Pallas kernels, mlp_backward(): pl.pallas_call(functools.partial(mlp_back_kernel, kinds=kinds, transposed...  61.7 us
    pallas_call x1, Pallas kernels, attn_forward(): pl.pallas_call(functools.partial(attn_fwd_kernel, head=head, factor=head...  47.8 us
  transfers between devices with their start and end apart: 51, of which 30 were waited for; matrix products, arithmetic and copies ran while one was open for 18% of the time, Pallas kernels for 25%

profile of v7, /device:TPU:9, one launch (start us, length us, event | category | flops | bytes accessed | tf_op | source)
XLA Modules:
  0.0 911.7 jit_solution(9479156732811833439)
XLA Ops:
  17.2 6.7 collective-permute-done.2
  23.9 7.0 collective-permute-done.3
  30.9 5.8 collective-permute-done.4
  42.2 6.7 collective-permute-done.7
  54.3 15.4 %collective-permute-done.8 = bf16[4,2,72,768]{3,2,0,1:T(8,128)(2,1)S(1)} collective-permute-done((bf16[4,2,72,768]{3,2,0,1:T(8,128)(2,1)S(1)}, bf16[4,2,72,768]{3,2,0,1:T(8,128)(2,1)S(1)}, u32[]{:S(2)}, u32[]{:S(2)}) %collective-permute-start.8) | collective-permute-done | bytes 884768 | tf_op jit(solution)/shard_map/ppermute | solution.py:817
  88.8 6.4 all-to-all-start
  99.2 63.7 %all-to-all-done = bf16[16,192,512]{2,1,0:T(8,128)(2,1)S(1)} async-done(((bf16[16,192,512]{2,1,0:T(8,128)(2,1)}), bf16[16,192,512]{2,1,0:T(8,128)(2,1)S(1)}, u32[]{:S(2)}, u32[]{:S(2)}) %all-to-all-start) | async-done | bytes 3145760 | tf_op jit(solution)/shard_map/all_to_all | solution.py:992
  164.5 3.8 collective-permute-start.10
  172.1 47.8 %attn_fwd.1 = (bf16[20,64,512]{2,1,0:T(8,128)(2,1)S(1)}, f32[20,1,512]{2,1,0:T(1,128)S(1)}) custom-call(s32[4,20]{1,0:T(4,128)S(1)} %add_select_fusion.2.plan, bf16[20,192,512]{2,1,0:T(8,128)(2,1)S(1)} %constant_dynamic-update-slice_fusion.own, bf16[16,128,512]{2,1,0:T(8,128)(2,1)S(1)} %broadcast_select_fusion.prompts), custom_call_target="tpu_custom_call" | custom-call | flops 26843545600 | bytes 8388608 | tf_op jit(solution)/shard_map/attn_fwd/pallas_call | solution.py:552
  221.4 9.5 %collective-permute-done.12 = bf16[4,64,512]{2,1,0:T(8,128)(2,1)S(1)} collective-permute-done((bf16[4,64,512]{2,1,0:T(8,128)(2,1)S(1)}, bf16[4,64,512]{2,1,0:T(8,128)(2,1)S(1)}, u32[]{:S(2)}, u32[]{:S(2)}) %collective-permute-start.12) | collective-permute-done | bytes 262176 | tf_op jit(solution)/shard_map/ppermute | solution.py:609
  232.0 7.8 all-to-all-start.1
  239.8 33.7 %all-gather.7.cloned.1.call-done = bf16[16,64,4608]{2,1,0:T(8,128)(2,1)} async-done(((bf16[4,64,4608]{2,1,0:T(8,128)(2,1)}), bf16[16,64,4608]{2,1,0:T(8,128)(2,1)}) %all-gather.7.cloned.1.call-update) | async-done | bytes 9437200 | tf_op jit(solution)/shard_map/all_gather | solution.py:995
  273.6 8.2 copy.128
  297.4 18.8 %mlp_fwd.3 = (bf16[1024,1024]{1,0:T(8,128)(2,1)}, bf16[1024,2048]{1,0:T(8,128)(2,1)}, bf16[1024,2048]{1,0:T(8,128)(2,1)}, bf16[512,1024]{1,0:T(8,128)(2,1)}, bf16[512,1024]{1,0:T(8,128)(2,1)}) custom-call(bf16[512,1024]{1,0:T(8,128)(2,1)} %copy-done.13, bf16[512,1024]{1,0:T(8,128)(2,1)} %copy-done.31, bf16[1024,4608]{1,0:T(8,128)(2,1)} %bitcast.139, ...), custom_call_target="tpu_custom_call" | custom-call | flops 2147483648 | bytes 5242880 | tf_op jit(solution)/shard_map/mlp_fwd/pallas_call | solution.py:747
  321.9 41.6 %all_to_all.40 = bf16[16,48,1024]{2,1,0:T(8,128)(2,1)} all-to-all(bf16[16,48,1024]{2,1,0:T(8,128)(2,1)S(1)} %bitcast.167), channel_id=1, replica_groups=mesh['dp'=16,'tensor'=2] {'dp'}, dimensions={0} | all-to-all | bytes 3145728 | tf_op jit(solution)/shard_map/all_to_all | solution.py:52
  365.5 5.0 all-to-all-start.3
  370.5 25.0 %mlp_fwd.4 = (bf16[1536,1024]{1,0:T(8,128)(2,1)}, bf16[1536,2048]{1,0:T(8,128)(2,1)}, bf16[1536,2048]{1,0:T(8,128)(2,1)}, bf16[768,1024]{1,0:T(8,128)(2,1)}, bf1...) custom-call(bf16[768,1024]{1,0:T(8,128)(2,1)} %bitcast.31.refs_0_, bf16[768,1024]{1,0:T(8,128)(2,1)} %collective-permute-done.16.refs_1_, ...), custom_call_target="tpu_custom_call" | custom-call | flops 3221225472 | bytes 6815744 | tf_op jit(solution)/shard_map/mlp_fwd/pallas_call | solution.py:747
  401.6 26.6 %mlp_fwd.5 = (bf16[1536,1024]{1,0:T(8,128)(2,1)}, bf16[1536,2048]{1,0:T(8,128)(2,1)}, bf16[1536,2048]{1,0:T(8,128)(2,1)}, bf16[768,1024]{1,0:T(8,128)(2,1)}, bf16[768,1024]{1,0:T(8,128)(2,1)}) custom-call(bf16[1536,1024]{1,0:T(8,128)(2,1)} %get-tuple-element.117.refs_0_, bf16[768,1024]{1,0:T(8,128)(2,1)} %get-tuple-element.97.refs_1_, ...), custom_call_target="tpu_custom_call" | custom-call | flops 3221225472 | bytes 6815744 | tf_op jit(solution)/shard_map/mlp_fwd/pallas_call | solution.py:747
  433.5 21.6 %mlp_bwd.3 = (bf16[1536,1024]{1,0:T(8,128)(2,1)}, bf16[1536,2048]{1,0:T(8,128)(2,1)}, bf16[768,1024]{1,0:T(8,128)(2,1)}, bf16[768,1024]{1,0:T(8,128)(2,1)}) custom-call(f32[1536,1]{1,0:T(8,128)} %broadcast_select_fusion.9.refs_0_, bf16[768,1024]{1,0:T(8,128)(2,1)} %bitcast.36.refs_1_, bf16[768,1024]{1,0:T(8,128)(2,1)} %collective-permute-done.19.refs_2_, ...), custom_call_target="tpu_custom_call" | custom-call | flops 12884901888 | bytes 27262976 | tf_op jit(solution)/shard_map/mlp_bwd/pallas_call | solution.py:787
  458.0 4.5 multiply_reduce_fusion.1
  463.5 4.1 select_convert_fusion
  467.6 6.4 all-to-all-start.4
  474.1 23.7 %mlp_bwd.4 = (bf16[1536,1024]{1,0:T(8,128)(2,1)}, bf16[1536,2048]{1,0:T(8,128)(2,1)}, bf16[768,1024]{1,0:T(8,128)(2,1)}, bf16[768,1024]{1,0:T(8,128)(2,1)}) custom-call(f32[1536,1]{1,0:T(8,128)} %broadcast_select_fusion.9.refs_0_, bf16[768,1024]{1,0:T(8,128)(2,1)} %bitcast.36.refs_1_, bf16[768,1024]{1,0:T(8,128)(2,1)} %collective-permute-done.19.refs_2_, ...), custom_call_target="tpu_custom_call" | custom-call | flops 12884901888 | bytes 27262976 | tf_op jit(solution)/shard_map/mlp_bwd/pallas_call | solution.py:787
  501.9 4.0 add_convert_fusion.1
  505.9 3.8 all-to-all-done.4
  509.8 5.9 all-to-all-start.5
  515.7 12.0 %fusion.56 = f32[1024,2048]{1,0:T(8,128)} fusion(bf16[1536,1024]{1,0:T(8,128)(2,1)} %get-tuple-element.117.refs_0_, bf16[1536,2048]{1,0:T(8,128)(2,1)} %get-tuple-element.118), kind=kOutput, calls=%fused_computation.206 | convolution fusion | flops 6442450944 | bytes 17825792 | tf_op jit(solution)/shard_map/dot_general | solution.py:60
  527.6 11.1 %fusion.55 = f32[2048,1024]{1,0:T(8,128)} fusion(bf16[1536,2048]{1,0:T(8,128)(2,1)} %get-tuple-element.115, bf16[1536,1024]{1,0:T(8,128)(2,1)S(1)} %copy-done.76), kind=kOutput, calls=%fused_computation.205 | convolution fusion | flops 6442450944 | bytes 17825792 | tf_op jit(solution)/shard_map/dot_general | solution.py:60
  538.7 12.5 %all-to-all-done.5 = bf16[16,48,1024]{2,1,0:T(8,128)(2,1)} async-done(((bf16[16,48,1024]{2,1,0:T(8,128)(2,1)}), bf16[16,48,1024]{2,1,0:T(8,128)(2,1)}, u32[]{:S(2)}, u32[]{:S(2)}) %all-to-all-start.5) | async-done | bytes 1572896 | tf_op jit(solution)/shard_map/all_to_all | solution.py:52
  560.1 16.4 %mlp_bwd.5 = (bf16[1024,1024]{1,0:T(8,128)(2,1)}, bf16[1024,2048]{1,0:T(8,128)(2,1)}, bf16[512,1024]{1,0:T(8,128)(2,1)}, bf16[512,1024]{1,0:T(8,128)(2,1)}) custom-call(bf16[512,1024]{1,0:T(8,128)(2,1)} %copy-done.72, bf16[512,1024]{1,0:T(8,128)(2,1)} %copy-done.73, bf16[1024,4608]{1,0:T(8,128)(2,1)} %bitcast.141, bf16[1024,4608]{1,0:T(8,128)(2,1)} %bitcast.142, ...), custom_call_target="tpu_custom_call" | custom-call | flops 8589934592 | bytes 20971520 | tf_op jit(solution)/shard_map/mlp_bwd/pallas_call | solution.py:787
  589.8 4.2 all-to-all-start.6
  594.1 7.5 convolution_convert_fusion.2
  601.7 5.1 convolution_convert_fusion.1
  608.8 5.3 pad_maximum_fusion
  614.1 4.1 all-to-all-done.6
  619.9 4.9 collective-permute-start.27
  627.0 84.1 %attn_bwd.1 = (bf16[20,192,512]{2,1,0:T(8,128)(2,1)}, bf16[16,128,512]{2,1,0:T(8,128)(2,1)S(1)}) custom-call(s32[4,20]{1,0:T(4,128)S(1)} %add_select_fusion.2.plan, bf16[20,192,512]{2,1,0:T(8,128)(2,1)} %copy-done, bf16[16,128,512]{2,1,0:T(8,128)(2,1)} %copy-done.1, bf16[20,64,512]{2,1,0:T(8,128)(2,1)S(1)} %pad_maximum_fusion.7.grad, ...), custom_call_target="tpu_custom_call" | custom-call | flops 67108864000 | bytes 16777216 | tf_op jit(solution)/shard_map/attn_bwd/pallas_call | solution.py:579
  711.1 5.1 collective-permute-start.28
  724.2 5.4 all-to-all-start.7
  729.7 12.0 %fusion.58 = f32[1024,2048]{1,0:T(8,128)} fusion(bf16[1536,1024]{1,0:T(8,128)(2,1)} %get-tuple-element.143, bf16[1536,2048]{1,0:T(8,128)(2,1)} %get-tuple-element.144), kind=kOutput, calls=%fused_computation.208 | convolution fusion | flops 6442450944 | bytes 17825792 | tf_op jit(solution)/shard_map/dot_general | solution.py:60
  741.7 11.1 %fusion.57 = f32[2048,1024]{1,0:T(8,128)} fusion(bf16[1536,2048]{1,0:T(8,128)(2,1)} %get-tuple-element.141, bf16[1536,1024]{1,0:T(8,128)(2,1)S(1)} %copy-done.77), kind=kOutput, calls=%fused_computation.207 | convolution fusion | flops 6442450944 | bytes 17825792 | tf_op jit(solution)/shard_map/dot_general | solution.py:60
  752.7 69.0 %all-to-all-done.7 = bf16[16,192,512]{2,1,0:T(8,128)(2,1)} async-done(((bf16[16,192,512]{2,1,0:T(8,128)(2,1)}), bf16[16,192,512]{2,1,0:T(8,128)(2,1)}, u32[]{:S(2)}, u32[]{:S(2)}) %all-to-all-start.7) | async-done | bytes 3145760 | tf_op jit(solution)/shard_map/all_to_all | solution.py:1194
  832.2 4.0 add_convert_fusion.4
  836.3 5.5 convolution_convert_fusion
  846.4 4.9 fusion.2
  852.2 10.6 %collective-permute-done.34 = bf16[4,2,64,768]{3,2,0,1:T(8,128)(2,1)S(1)} collective-permute-done((bf16[4,2,64,768]{3,2,0,1:T(8,128)(2,1)S(1)}, bf16[4,2,64,768]{3,2,0,1:T(8,128)(2,1)S(1)}, u32[]{:S(2)}, u32[]{:S(2)}) %collective-permute-start.34) | collective-permute-done | bytes 786464 | tf_op jit(solution)/shard_map/ppermute | solution.py:817
  866.6 6.8 collective-permute-done.35
  882.4 11.7 %collective-permute-done.38 = bf16[64,1536]{1,0:T(8,128)(2,1)S(1)} collective-permute-done((bf16[64,1536]{1,0:T(8,128)(2,1)S(1)}, bf16[64,1536]{1,0:T(8,128)(2,1)S(1)}, u32[]{:S(2)}, u32[]{:S(2)}) %collective-permute-start.38) | collective-permute-done | bytes 196640 | tf_op jit(solution)/shard_map/ppermute | solution.py:817
  (390 shorter events, 169.0 us)
Async XLA Ops:
  7.2 81.6 %all-gather.5.cloned.1.call-start = ((), (), s32[]{:S(2)}) async-start(), calls=%async_computation.10 | async-start | bytes 2949120 | tf_op jit(solution)/shard_map/all_gather | solution.py:942
  8.1 6.2 collective-permute-start.1
  14.5 9.4 %collective-permute-start.2 = (bf16[72,1536]{1,0:T(8,128)(2,1)S(1)}, bf16[72,1536]{1,0:T(8,128)(2,1)S(1)}, u32[]{:S(2)}, u32[]{:S(2)}) collective-permute-start(bf16[72,1536]{1,0:T(8,128)(2,1)S(1)} %fusion.23), channel_id=1, source_target_pairs={{0,8},{2,10},{4,12},{6,14},{8,0},{10,2},{12,4},{14,6},{16,24},{18,... | collective-permute-start | bytes 663560 | tf_op jit(solution)/shard_map/ppermute | solution.py:817
  14.5 16.4 %collective-permute-start.3 = (bf16[72,1536]{1,0:T(8,128)(2,1)S(1)}, bf16[72,1536]{1,0:T(8,128)(2,1)S(1)}, u32[]{:S(2)}, u32[]{:S(2)}) collective-permute-start(bf16[72,1536]{1,0:T(8,128)(2,1)S(1)} %fusion.23), channel_id=1, source_target_pairs={{0,16},{2,18},{4,20},{6,22},{8,24},{10,26},{12,28},{14,30},{16,0},... | collective-permute-start | bytes 663560 | tf_op jit(solution)/shard_map/ppermute | solution.py:817
  17.0 19.7 %collective-permute-start.4 = (bf16[72,1536]{1,0:T(8,128)(2,1)S(1)}, bf16[72,1536]{1,0:T(8,128)(2,1)S(1)}, u32[]{:S(2)}, u32[]{:S(2)}) collective-permute-start(bf16[72,1536]{1,0:T(8,128)(2,1)S(1)} %fusion.23), channel_id=1, source_target_pairs={{0,24},{2,26},{4,28},{6,30},{8,16},{10,18},{12,20},{14,22},{16,8},... | collective-permute-start | bytes 663560 | tf_op jit(solution)/shard_map/ppermute | solution.py:817
  38.1 10.9 %collective-permute-start.7 = (bf16[4,72,768]{2,1,0:T(8,128)(2,1)}, bf16[4,72,768]{2,1,0:T(8,128)(2,1)}, u32[]{:S(2)}, u32[]{:S(2)}) collective-permute-start(bf16[4,72,768]{2,1,0:T(8,128)(2,1)} %get-tuple-element.184), channel_id=1, source_target_pairs={{0,2},{2,0},{4,6},{6,4},{8,10},{10,8},{12,14},{14,12},{16,18},{18,... | collective-permute-start | bytes 1327112 | tf_op jit(solution)/shard_map/ppermute | solution.py:817
  39.3 12.3 %collective-permute-start.5 = (bf16[4,72,768]{2,1,0:T(8,128)(2,1)}, bf16[4,72,768]{2,1,0:T(8,128)(2,1)S(1)}, u32[]{:S(2)}, u32[]{:S(2)}) collective-permute-start(bf16[4,72,768]{2,1,0:T(8,128)(2,1)} %get-tuple-element.185), channel_id=1, source_target_pairs={{0,4},{2,6},{4,0},{6,2},{8,12},{10,14},{12,8},{14,10},{16,20},{18,... | collective-permute-start | bytes 1327112 | tf_op jit(solution)/shard_map/ppermute | solution.py:817
  40.5 12.7 %collective-permute-start = (bf16[512,1024]{1,0:T(8,128)(2,1)S(1)}, bf16[512,1024]{1,0:T(8,128)(2,1)S(1)}, u32[]{:S(2)}, u32[]{:S(2)}) collective-permute-start(bf16[512,1024]{1,0:T(8,128)(2,1)S(1)} %copy-done.3), channel_id=1, source_target_pairs={{0,1},{1,0},{2,3},{3,2},{4,5},{5,4},{6,7},{7,6},{8,9},{9,8},{10,11... | collective-permute-start | bytes 3145736 | tf_op jit(solution)/shard_map/ppermute | solution.py:605
  50.3 19.3 %collective-permute-start.8 = (bf16[4,2,72,768]{3,2,0,1:T(8,128)(2,1)S(1)}, bf16[4,2,72,768]{3,2,0,1:T(8,128)(2,1)S(1)}, u32[]{:S(2)}, u32[]{:S(2)}) collective-permute-start(bf16[4,2,72,768]{3,2,0,1:T(8,128)(2,1)S(1)} %maximum_select_fusion.4), channel_id=1, source_target_pairs={{0,4},{2,6},{4,0},{6,2},{8,12},{10,14},{12,8},{14,10},{16,20},{18,... | collective-permute-start | bytes 2654216 | tf_op jit(solution)/shard_map/ppermute | solution.py:817
  51.8 19.5 %collective-permute-start.6 = (bf16[4,2,72,768]{3,2,0,1:T(8,128)(2,1)S(1)}, bf16[4,2,72,768]{3,2,0,1:T(8,128)(2,1)S(1)}, u32[]{:S(2)}, u32[]{:S(2)}) collective-permute-start(bf16[4,2,72,768]{3,2,0,1:T(8,128)(2,1)S(1)} %maximum_select_fusion.3), channel_id=1, source_target_pairs={{0,2},{2,0},{4,6},{6,4},{8,10},{10,8},{12,14},{14,12},{16,18},{18,... | collective-permute-start | bytes 2654216 | tf_op jit(solution)/shard_map/ppermute | solution.py:817
  78.2 5.9 collective-permute-start.9
  88.8 74.1 %all-to-all-start = ((bf16[16,192,512]{2,1,0:T(8,128)(2,1)}), bf16[16,192,512]{2,1,0:T(8,128)(2,1)S(1)}, u32[]{:S(2)}, u32[]{:S(2)}) async-start(bf16[16,192,512]{2,1,0:T(8,128)(2,1)} %bitcast.144), calls=%async_computation | async-start | bytes 6291456 | tf_op jit(solution)/shard_map/all_to_all | solution.py:992
  95.2 178.4 %all-gather.7.cloned.1.call-start = ((), (), s32[]{:S(2)}) async-start(), calls=%async_computation.11 | async-start | bytes 11796480 | tf_op jit(solution)/shard_map/all_gather | solution.py:995
  163.1 7.2 collective-permute-start.11
  164.5 5.7 collective-permute-start.10
  220.0 10.9 %collective-permute-start.12 = (bf16[4,64,512]{2,1,0:T(8,128)(2,1)S(1)}, bf16[4,64,512]{2,1,0:T(8,128)(2,1)S(1)}, u32[]{:S(2)}, u32[]{:S(2)}) collective-permute-start(bf16[4,64,512]{2,1,0:T(8,128)(2,1)S(1)} %slice.196), channel_id=1, source_target_pairs={{0,1},{2,3},{4,5},{6,7},{8,9},{10,11},{12,13},{14,15},{16,17},{18,... | collective-permute-start | bytes 786440 | tf_op jit(solution)/shard_map/ppermute | solution.py:609
  232.0 55.4 %all-to-all-start.1 = ((bf16[16,64,512]{2,1,0:T(8,128)(2,1)}), bf16[16,64,512]{2,1,0:T(8,128)(2,1)S(1)}, u32[]{:S(2)}, u32[]{:S(2)}) async-start(bf16[16,64,512]{2,1,0:T(8,128)(2,1)} %pad_maximum_fusion.8), calls=%async_computation.1 | async-start | bytes 2097152 | tf_op jit(solution)/shard_map/all_to_all | solution.py:1029
  284.2 5.7 collective-permute-start.13
  316.2 2.9 collective-permute-start.15
  363.6 7.0 collective-permute-start.16
  365.5 62.8 %all-to-all-start.3 = ((bf16[16,48,1024]{2,1,0:T(8,128)(2,1)}), bf16[16,48,1024]{2,1,0:T(8,128)(2,1)}, u32[]{:S(2)}, u32[]{:S(2)}) async-start(bf16[16,48,1024]{2,1,0:T(8,128)(2,1)} %bitcast.166), calls=%async_computation.3 | async-start | bytes 3145728 | tf_op jit(solution)/shard_map/all_to_all | solution.py:52
  395.6 3.8 collective-permute-start.17
  395.9 5.7 collective-permute-start.18
  428.3 5.2 collective-permute-start.19
  433.2 24.7 %collective-permute-start.23 = (bf16[768,1024]{1,0:T(8,128)(2,1)}, bf16[768,1024]{1,0:T(8,128)(2,1)}, u32[]{:S(2)}, u32[]{:S(2)}) collective-permute-start(bf16[768,1024]{1,0:T(8,128)(2,1)} %get-tuple-element.109), channel_id=1, source_target_pairs={{0,1},{1,0},{2,3},{3,2},{4,5},{5,4},{6,7},{7,6},{8,9},{9,8},{10,11... | collective-permute-start | bytes 4718600 | tf_op jit(solution)/shard_map/ppermute | solution.py:605
  455.1 18.9 %collective-permute-start.20 = (bf16[768,1024]{1,0:T(8,128)(2,1)}, bf16[768,1024]{1,0:T(8,128)(2,1)}, u32[]{:S(2)}, u32[]{:S(2)}) collective-permute-start(bf16[768,1024]{1,0:T(8,128)(2,1)} %get-tuple-element.104.refs_4_), channel_id=1, source_target_pairs={{0,1},{1,0},{2,3},{3,2},{4,5},{5,4},{6,7},{7,6},{8,9},{9,8},{10,11... | collective-permute-start | bytes 4718600 | tf_op jit(solution)/shard_map/ppermute | solution.py:605
  455.4 18.6 %collective-permute-start.21 = (bf16[768,1024]{1,0:T(8,128)(2,1)}, bf16[768,1024]{1,0:T(8,128)(2,1)}, u32[]{:S(2)}, u32[]{:S(2)}) collective-permute-start(bf16[768,1024]{1,0:T(8,128)(2,1)} %get-tuple-element.103.refs_3_), channel_id=1, source_target_pairs={{0,1},{1,0},{2,3},{3,2},{4,5},{5,4},{6,7},{7,6},{8,9},{9,8},{10,11... | collective-permute-start | bytes 4718600 | tf_op jit(solution)/shard_map/ppermute | solution.py:605
  467.6 42.2 %all-to-all-start.4 = ((bf16[16,48,1024]{2,1,0:T(8,128)(2,1)}), bf16[16,48,1024]{2,1,0:T(8,128)(2,1)}, u32[]{:S(2)}, u32[]{:S(2)}) async-start(bf16[16,48,1024]{2,1,0:T(8,128)(2,1)} %bitcast.147), calls=%async_computation.4 | async-start | bytes 3145728 | tf_op jit(solution)/shard_map/all_to_all | solution.py:52
  497.8 4.2 collective-permute-start.22
  509.8 41.5 %all-to-all-start.5 = ((bf16[16,48,1024]{2,1,0:T(8,128)(2,1)}), bf16[16,48,1024]{2,1,0:T(8,128)(2,1)}, u32[]{:S(2)}, u32[]{:S(2)}) async-start(bf16[16,48,1024]{2,1,0:T(8,128)(2,1)} %bitcast.146), calls=%async_computation.5 | async-start | bytes 3145728 | tf_op jit(solution)/shard_map/all_to_all | solution.py:52
  554.0 5.2 collective-permute-start.24
  589.4 17.4 %collective-permute-start.26 = (bf16[1024,512]{1,0:T(8,128)(2,1)}, bf16[1024,512]{1,0:T(8,128)(2,1)}, u32[]{:S(2)}, u32[]{:S(2)}) collective-permute-start(bf16[1024,512]{1,0:T(8,128)(2,1)} %convolution_convert_fusion.7), channel_id=1, source_target_pairs={{0,1},{1,0},{2,3},{3,2},{4,5},{5,4},{6,7},{7,6},{8,9},{9,8},{10,11... | collective-permute-start | bytes 3145736 | tf_op jit(solution)/shard_map/ppermute | solution.py:605
  589.8 28.4 %all-to-all-start.6 = ((bf16[16,64,512]{2,1,0:T(8,128)(2,1)}), bf16[16,64,512]{2,1,0:T(8,128)(2,1)}, u32[]{:S(2)}, u32[]{:S(2)}) async-start(bf16[16,64,512]{2,1,0:T(8,128)(2,1)} %bitcast.152), calls=%async_computation.6 | async-start | bytes 2097152 | tf_op jit(solution)/shard_map/all_to_all | solution.py:1162
  594.1 303.7 %reduce-scatter.2.cloned.1.call-start = ((), (), s32[]{:S(2)}) async-start(), calls=%async_computation.9 | async-start | bytes 10027008 | tf_op jit(solution)/shard_map/reduce_scatter | solution.py:1176
  619.9 5.7 collective-permute-start.27
  711.1 9.9 %collective-permute-start.28 = (bf16[16,128,512]{2,1,0:T(8,128)(2,1)S(1)}, bf16[16,128,512]{2,1,0:T(8,128)(2,1)S(1)}, u32[]{:S(2)}, u32[]{:S(2)}) collective-permute-start(bf16[16,128,512]{2,1,0:T(8,128)(2,1)S(1)} %get-tuple-element.135), channel_id=1, source_target_pairs={{1,0},{3,2},{5,4},{7,6},{9,8},{11,10},{13,12},{15,14},{17,16},{19,... | collective-permute-start | bytes 6291464 | tf_op jit(solution)/shard_map/ppermute | solution.py:613
  717.4 4.5 collective-permute-start.29
  724.2 97.5 %all-to-all-start.7 = ((bf16[16,192,512]{2,1,0:T(8,128)(2,1)}), bf16[16,192,512]{2,1,0:T(8,128)(2,1)}, u32[]{:S(2)}, u32[]{:S(2)}) async-start(bf16[16,192,512]{2,1,0:T(8,128)(2,1)} %maximum_select_fusion), calls=%async_computation.7 | async-start | bytes 6291456 | tf_op jit(solution)/shard_map/all_to_all | solution.py:1194
  825.5 10.7 %collective-permute-start.30 = (bf16[1536,512]{1,0:T(8,128)(2,1)}, bf16[1536,512]{1,0:T(8,128)(2,1)}, u32[]{:S(2)}, u32[]{:S(2)}) collective-permute-start(bf16[1536,512]{1,0:T(8,128)(2,1)} %bitcast.44), channel_id=1, source_target_pairs={{0,1},{1,0},{2,3},{3,2},{4,5},{5,4},{6,7},{7,6},{8,9},{9,8},{10,11... | collective-permute-start | bytes 4718600 | tf_op jit(solution)/shard_map/ppermute | solution.py:605
  842.0 20.9 %collective-permute-start.34 = (bf16[4,2,64,768]{3,2,0,1:T(8,128)(2,1)S(1)}, bf16[4,2,64,768]{3,2,0,1:T(8,128)(2,1)S(1)}, u32[]{:S(2)}, u32[]{:S(2)}) collective-permute-start(bf16[4,2,64,768]{3,2,0,1:T(8,128)(2,1)S(1)} %select_bitcast_fusion), channel_id=1, source_target_pairs={{0,4},{2,6},{4,0},{6,2},{8,12},{10,14},{12,8},{14,10},{16,20},{18,... | collective-permute-start | bytes 2359304 | tf_op jit(solution)/shard_map/ppermute | solution.py:817
  845.3 19.1 %collective-permute-start.32 = (bf16[4,2,64,768]{3,2,0,1:T(8,128)(2,1)S(1)}, bf16[4,2,64,768]{3,2,0,1:T(8,128)(2,1)S(1)}, u32[]{:S(2)}, u32[]{:S(2)}) collective-permute-start(bf16[4,2,64,768]{3,2,0,1:T(8,128)(2,1)S(1)} %select_bitcast_fusion.1), channel_id=1, source_target_pairs={{0,2},{2,0},{4,6},{6,4},{8,10},{10,8},{12,14},{14,12},{16,18},{18,... | collective-permute-start | bytes 2359304 | tf_op jit(solution)/shard_map/ppermute | solution.py:817
  851.4 14.5 %collective-permute-start.31 = (bf16[512,1024]{1,0:T(8,128)(2,1)S(1)}, bf16[512,1024]{1,0:T(8,128)(2,1)S(1)}, u32[]{:S(2)}, u32[]{:S(2)}) collective-permute-start(bf16[512,1024]{1,0:T(8,128)(2,1)S(1)} %slice.333), channel_id=1, source_target_pairs={{0,1},{1,0},{2,3},{3,2},{4,5},{5,4},{6,7},{7,6},{8,9},{9,8},{10,11... | collective-permute-start | bytes 3145736 | tf_op jit(solution)/shard_map/ppermute | solution.py:605
  863.3 10.0 %collective-permute-start.35 = (bf16[4,64,768]{2,1,0:T(8,128)(2,1)S(1)}, bf16[4,64,768]{2,1,0:T(8,128)(2,1)S(1)}, u32[]{:S(2)}, u32[]{:S(2)}) collective-permute-start(bf16[4,64,768]{2,1,0:T(8,128)(2,1)S(1)} %select_bitcast_fusion.2), channel_id=1, source_target_pairs={{0,2},{2,0},{4,6},{6,4},{8,10},{10,8},{12,14},{14,12},{16,18},{18,... | collective-permute-start | bytes 1179656 | tf_op jit(solution)/shard_map/ppermute | solution.py:817
  864.7 9.7 %collective-permute-start.33 = (bf16[4,64,768]{2,1,0:T(8,128)(2,1)S(1)}, bf16[4,64,768]{2,1,0:T(8,128)(2,1)S(1)}, u32[]{:S(2)}, u32[]{:S(2)}) collective-permute-start(bf16[4,64,768]{2,1,0:T(8,128)(2,1)S(1)} %select_bitcast_fusion.3), channel_id=1, source_target_pairs={{0,4},{2,6},{4,0},{6,2},{8,12},{10,14},{12,8},{14,10},{16,20},{18,... | collective-permute-start | bytes 1179656 | tf_op jit(solution)/shard_map/ppermute | solution.py:817
  874.6 4.6 collective-permute-start.36
  874.7 7.7 collective-permute-start.37
  875.8 18.4 %collective-permute-start.38 = (bf16[64,1536]{1,0:T(8,128)(2,1)S(1)}, bf16[64,1536]{1,0:T(8,128)(2,1)S(1)}, u32[]{:S(2)}, u32[]{:S(2)}) collective-permute-start(bf16[64,1536]{1,0:T(8,128)(2,1)S(1)} %get-tuple-element.192), channel_id=1, source_target_pairs={{0,24},{2,26},{4,28},{6,30},{8,16},{10,18},{12,20},{14,22},{16,8},... | collective-permute-start | bytes 589832 | tf_op jit(solution)/shard_map/ppermute | solution.py:817
  899.7 4.4 collective-permute-start.39
  (82 other events, 1217.5 us)
Sparse Core Ops, SparseCore 0:
  42.4 46.3 all-gather.4
  163.1 110.4 all-gather.6
  624.9 215.5 reduce-scatter.1

commit v8 on v6

--- a/solution.py
+++ b/solution.py
@@ -630,66 +630,62 @@
     return act.astype(BF16), slope.astype(BF16)
 
 
-def take_terms(refs, kinds):
+def by_halves(run):
     early = pl.program_id(0) < pl.num_programs(0) // 2
+    pl.when(early)(functools.partial(run, 0))
+    pl.when(jnp.logical_not(early))(functools.partial(run, 1))
+
+
+def take_terms(refs, kinds, half):
     values, at = [], 0
     for paired in kinds:
-        if paired:
-            values.append(jnp.where(early, refs[at][...], refs[at + 1][...]))
-        else:
-            values.append(refs[at][...])
+        values.append(refs[at + half * paired][...])
         at += 1 + paired
     return values, refs[at:]
 
 
-def give_halves(refs, value):
-    early = pl.program_id(0) < pl.num_programs(0) // 2
-
-    @pl.when(early)
-    def _():
-        refs[0][...] = value
-
-    @pl.when(jnp.logical_not(early))
-    def _():
-        refs[1][...] = value
-
-
 def mlp_kernel(*refs, kinds, transposed, gated):
-    terms, refs = take_terms(refs, kinds)
-    rows = terms[0]
-    if len(terms) > 1:
-        total = rows.astype(F32)
-        for term in terms[1:]:
-            total = total + term.astype(F32)
-        rows = total.astype(BF16)
-    if gated:
-        centre, refs = refs[0], refs[1:]
-        logit = jnp.sum(rows.astype(F32) * centre[...].astype(F32), 1, keepdims=True)
-        refs[-1][...] = 1.0 / (1.0 + jnp.exp(-logit))
-    w_in, w_out, kept_rows, kept_act, kept_slope, first, second = refs[:7]
-    kept_rows[...] = rows
-    act, slope = gelu_pair(matmul(rows, w_in[...]))
-    kept_act[...] = act
-    kept_slope[...] = slope
-    result = (matmul_nt if transposed else matmul)(act, w_out[...])
-    give_halves((first, second), result.astype(BF16))
+    def run(half):
+        terms, rest = take_terms(refs, kinds, half)
+        rows = terms[0]
+        if len(terms) > 1:
+            total = rows.astype(F32)
+            for term in terms[1:]:
+                total = total + term.astype(F32)
+            rows = total.astype(BF16)
+        if gated:
+            centre, rest = rest[0], rest[1:]
+            logit = jnp.sum(rows.astype(F32) * centre[...].astype(F32), 1, keepdims=True)
+            rest[-1][...] = 1.0 / (1.0 + jnp.exp(-logit))
+        w_in, w_out, kept_rows, kept_act, kept_slope, *results = rest[:7]
+        kept_rows[...] = rows
+        act, slope = gelu_pair(matmul(rows, w_in[...]))
+        kept_act[...] = act
+        kept_slope[...] = slope
+        product = matmul_nt if transposed else matmul
+        results[half][...] = product(act, w_out[...]).astype(BF16)
+
+    by_halves(run)
 
 
 def mlp_back_kernel(*refs, kinds, transposed, scaled):
-    factor, refs = (refs[0], refs[1:]) if scaled else (None, refs)
-    terms, refs = take_terms(refs, kinds)
-    grad = terms[0]
-    if scaled:
-        total = factor[...] * grad.astype(F32)
-        for term in terms[1:]:
-            total = total + term.astype(F32)
-        grad = total.astype(BF16)
-    w_out, w_in, slope, kept_grad, kept_pre, first, second = refs
-    kept_grad[...] = grad
-    grad = (matmul_nt if transposed else matmul)(grad, w_out[...])
-    grad_pre = (grad * slope[...].astype(F32)).astype(BF16)
-    kept_pre[...] = grad_pre
-    give_halves((first, second), matmul_nt(grad_pre, w_in[...]).astype(BF16))
+    def run(half):
+        factor, rest = (refs[0], refs[1:]) if scaled else (None, refs)
+        terms, rest = take_terms(rest, kinds, half)
+        grad = terms[0]
+        if scaled:
+            total = factor[...] * grad.astype(F32)
+            for term in terms[1:]:
+                total = total + term.astype(F32)
+            grad = total.astype(BF16)
+        w_out, w_in, slope, kept_grad, kept_pre, *results = rest
+        kept_grad[...] = grad
+        grad = (matmul_nt if transposed else matmul)(grad, w_out[...])
+        grad_pre = (grad * slope[...].astype(F32)).astype(BF16)
+        kept_pre[...] = grad_pre
+        results[half][...] = matmul_nt(grad_pre, w_in[...]).astype(BF16)
+
+    by_halves(run)
 
 
 def mlp_blocks(terms, length):
@@ -731,9 +727,9 @@
         + [jax.ShapeDtypeStruct((rows, 1), F32)] * gated,
         compiler_params=pltpu.CompilerParams(vmem_limit_bytes=54 * 2**20),
         cost_estimate=pl.CostEstimate(
-            flops=4 * rows * width * hidden,
-            bytes_accessed=4 * width * hidden + 4 * rows * hidden + 4 * rows * width,
-            transcendentals=rows * hidden,
+            flops=rows * width * hidden,
+            bytes_accessed=width * hidden + rows * hidden + rows * width,
+            transcendentals=0,
         ),
         name="mlp_fwd",
     )(*arrays, *([centre] * gated), w_in, w_out)
@@ -883,7 +879,8 @@
     earlier = matmul(below.astype(BF16), onehot_low)
     local_rank = jnp.sum(jnp.where(onehot, earlier, 0.0), 1).astype(jnp.int32)
     target = route * slots_per + local_rank
-    columns = lax.broadcasted_iota(jnp.int32, (1, experts * slots_per), 1)
+    half_rows = experts * slots_per
+    columns = lax.broadcasted_iota(jnp.int32, (1, half_rows), 1)
     placer = (columns == target[:, None]).astype(BF16)
     counts = jnp.sum(onehot_low.astype(F32), 0).astype(BF16)
     counts_pair = jnp.concatenate(both(counts, swap(counts)), 0)
@@ -915,27 +912,6 @@
     gain_one = extra_all[:, :shard].reshape(width).astype(F32)
     gain_two = extra_all[:, shard : 2 * shard].reshape(width).astype(F32)
     counts_all = extra_all[:, 2 * shard : 2 * shard + 2 * experts].reshape(experts, 2, experts)
-
-    mine = jnp.sum(
-        jnp.where(lax.broadcasted_iota(jnp.int32, (1, 1, experts), 2) == dp_index, counts_all.astype(F32), 0.0),
-        2,
-    )
-    per_chip = jnp.sum(mine, 1)
-    chip_before = jnp.sum(
-        jnp.where(
-            lax.broadcasted_iota(jnp.int32, (experts, experts), 1)
-            < lax.broadcasted_iota(jnp.int32, (experts, experts), 0),
-            per_chip[None, :],
-            0.0,
-        ),
-        1,
-    )
-    starts = both(chip_before, chip_before + mine[:, 0])
-    slot_at = lax.broadcasted_iota(jnp.int32, (1, slots_per), 1).astype(F32)
-    kept = jnp.concatenate(
-        [(start[:, None] + slot_at < capacity).reshape(-1, 1) for start in starts], 0
-    )
-    half_rows = experts * slots_per
 
     pair_tokens = with_other(tokens).astype(F32)
     normed_one, hat_pair, inv_pair = norm_forward(pair_tokens, gain_one)
@@ -948,10 +924,11 @@
         qkv_full, rows_one[:rows], (((0,), (1,)), ((), ())), preferred_element_type=F32
     ).astype(BF16)
     qkv_t = jnp.concatenate(both(own_t, swap(other_t)), 0).reshape(heads, triple, rows)
-    qkv_t, second_line = lax.optimization_barrier((qkv_t, second_line))
+    qkv_t, second_line, late_grad = lax.optimization_barrier((qkv_t, second_line, grad_out))
+    sent_grad = matmul_tn(placer, late_grad).astype(BF16).reshape(experts, slots_per, width)
     by_head = lax.all_to_all(qkv_t, "dp", split_axis=0, concat_axis=0, tiled=True)
 
-    by_head, second_line = lax.optimization_barrier((by_head, second_line))
+    by_head, second_line, sent_grad = lax.optimization_barrier((by_head, second_line, sent_grad))
     second_all = lax.all_gather(
         second_line, "dp", axis_index_groups=[[4 * z + k for k in range(4)] for z in range(planes)]
     )
@@ -990,9 +967,6 @@
         width, rows
     )
 
-    sent_grad = matmul_tn(placer, grad_out).astype(BF16).reshape(experts, slots_per, width)
-    attn_t, sent_grad = lax.optimization_barrier((attn_t, sent_grad))
-    grad_own = to_experts(sent_grad).reshape(-1, width)
     half_width = width // 2
     own_heads, other_heads = both(attn_t[:half_width], attn_t[half_width:])
     attn_other = swap(attn_half)
@@ -1021,8 +995,29 @@
     sent_rows = (
         matmul_tn(placer, hidden_two.astype(BF16)).astype(BF16).reshape(experts, slots_per, width)
     )
-    sent_rows, grad_own = lax.optimization_barrier((sent_rows, grad_own))
-    own_rows = to_experts(sent_rows).reshape(half_rows, width)
+    sent_rows, counts_all = lax.optimization_barrier((sent_rows, counts_all))
+    mine = jnp.sum(
+        jnp.where(lax.broadcasted_iota(jnp.int32, (1, 1, experts), 2) == dp_index, counts_all.astype(F32), 0.0),
+        2,
+    )
+    per_chip = jnp.sum(mine, 1)
+    chip_before = jnp.sum(
+        jnp.where(
+            lax.broadcasted_iota(jnp.int32, (experts, experts), 1)
+            < lax.broadcasted_iota(jnp.int32, (experts, experts), 0),
+            per_chip[None, :],
+            0.0,
+        ),
+        1,
+    )
+    starts = both(chip_before, chip_before + mine[:, 0])
+    slot_at = lax.broadcasted_iota(jnp.int32, (1, slots_per), 1).astype(F32)
+    kept = jnp.concatenate(
+        [(start[:, None] + slot_at < capacity).reshape(-1, 1) for start in starts], 0
+    )
+    own_rows, sent_grad, kept = lax.optimization_barrier((to_experts(sent_rows), sent_grad, kept))
+    own_rows = own_rows.reshape(half_rows, width)
+    grad_own = to_experts(sent_grad).reshape(half_rows, width)
     centre = centroids[0]
     length = half_rows // 2
     expert_rows, act_a, slope_a, own_a, other_a, gate_column = mlp_forward(
@@ -1037,6 +1032,7 @@
     middle, act_b, slope_b, own_b, other_b = mlp_forward(
         [expert_rows, (own_a, other_a), from_a], expert_in_b[0], expert_out_b[0], hidden, length
     )
+    own_b, grad_own = lax.optimization_barrier((own_b, grad_own))
     branch_half = (
         own_a.astype(F32) + from_a[0].astype(F32) + own_b.astype(F32) + swap(other_b).astype(F32)
     )

time: 926 us -> 906 us (0.978)
  blocking collectives: 118 us -> 0 us
  waiting for transfers between devices: 240 us -> 333 us
  starting transfers between devices: 86.6 us -> 103 us
    all_to_all x2 -> x0, blocking collectives: 118 us -> none  [the longest x1 76 us: body_paired(): lax.all_to_all(qkv_t, 'dp', split_axis=0, concat_axis=0, tiled=True)]
    all_to_all x0 -> x1, waiting for transfers between devices: none -> 63.3 us  [body_paired(): lax.all_to_all(qkv_t, 'dp', split_axis=0, concat_axis=0, tiled=True)]
    all_to_all x3 -> x4, waiting for transfers between devices: 27.2 us -> 51.2 us  [to_experts(): return lax.all_to_all(value, 'dp', split_axis=0, concat_axis=0, tiled=True)]
    all_to_all x3 -> x4, starting transfers between devices: 16.4 us -> 22.8 us  [to_experts(): return lax.all_to_all(value, 'dp', split_axis=0, concat_axis=0, tiled=True)]
  transfers between devices with their start and end apart: 50 -> 52, of which waited for: 29 -> 31; matrix products, arithmetic and copies ran while one was open for 18% -> 17% of each run, Pallas kernels for 24% -> 25%
where the time goes in v8:
time: 906 us; the launch traced here: 896 us
  waiting for transfers between devices  333 us (37%)
  Pallas kernels  256 us (28%)
  starting transfers between devices  103 us (11%)
  matrix products  98 us (11%)
  other arithmetic  54.1 us (6%)
  local copies, waits for them, and re-layouts  35.8 us (4%)
  between operations  15.4 us (2%)
    pallas_call x1, Pallas kernels, attn_backward(): pl.pallas_call(functools.partial(attn_bwd_kernel, head=head, factor=head...  84.1 us
    ppermute x14, waiting for transfers between devices, from_bit(): lax.ppermute(value, 'dp', [(i, i ^ bit) for i in range(lax.axis_size('dp'...  76.1 us
    all_to_all x1, waiting for transfers between devices, body_paired(): lax.all_to_all(grad_head, 'dp', split_axis=0, concat_axis=0, tiled=True)  69 us
    dot_general x8, matrix products, matmul_tn(): lax.dot_general(left, right, (((0,), (0,)), ((), ())), preferred_element_...  65.9 us
    all_to_all x1, waiting for transfers between devices, body_paired(): lax.all_to_all(qkv_t, 'dp', split_axis=0, concat_axis=0, tiled=True)  63.3 us
    pallas_call x3, Pallas kernels, mlp_forward(): pl.pallas_call(functools.partial(mlp_kernel, kinds=kinds, transposed=tran...  62.8 us
    pallas_call x3, Pallas kernels, mlp_backward(): pl.pallas_call(functools.partial(mlp_back_kernel, kinds=kinds, transposed...  61.5 us
    all_to_all x4, waiting for transfers between devices, to_experts(): return lax.all_to_all(value, 'dp', split_axis=0, concat_axis=0, tiled=True)  51.2 us
  transfers between devices with their start and end apart: 52, of which 31 were waited for; matrix products, arithmetic and copies ran while one was open for 17% of the time, Pallas kernels for 25%

profile of v8, /device:TPU:9, one launch (start us, length us, event | category | flops | bytes accessed | tf_op | source)
XLA Modules:
  0.0 895.9 jit_solution(5356506405731454256)
XLA Ops:
  17.2 6.7 collective-permute-done.2
  23.9 7.0 collective-permute-done.3
  30.9 5.8 collective-permute-done.4
  42.2 6.7 collective-permute-done.5
  54.3 15.3 %collective-permute-done.6 = bf16[4,2,72,768]{3,2,0,1:T(8,128)(2,1)S(1)} collective-permute-done((bf16[4,2,72,768]{3,2,0,1:T(8,128)(2,1)S(1)}, bf16[4,2,72,768]{3,2,0,1:T(8,128)(2,1)S(1)}, u32[]{:S(2)}, u32[]{:S(2)}) %collective-permute-start.6) | collective-permute-done | bytes 884768 | tf_op jit(solution)/shard_map/ppermute | solution.py:774
  88.8 6.4 all-to-all-start
  96.0 3.5 convolution_convert_fusion.6
  99.5 63.3 %all-to-all-done = bf16[16,192,512]{2,1,0:T(8,128)(2,1)S(1)} async-done(((bf16[16,192,512]{2,1,0:T(8,128)(2,1)}), bf16[16,192,512]{2,1,0:T(8,128)(2,1)S(1)}, u32[]{:S(2)}, u32[]{:S(2)}) %all-to-all-start) | async-done | bytes 3145760 | tf_op jit(solution)/shard_map/all_to_all | solution.py:929
  164.4 3.9 collective-permute-start.10
  172.1 47.7 %attn_fwd.1 = (bf16[20,64,512]{2,1,0:T(8,128)(2,1)S(1)}, f32[20,1,512]{2,1,0:T(1,128)S(1)}) custom-call(s32[4,20]{1,0:T(4,128)S(1)} %add_select_fusion.2.plan, bf16[20,192,512]{2,1,0:T(8,128)(2,1)S(1)} %constant_dynamic-update-slice_fusion.own, bf16[16,128,512]{2,1,0:T(8,128)(2,1)S(1)} %broadcast_select_fusion.prompts), custom_call_target="tpu_custom_call" | custom-call | flops 26843545600 | bytes 8388608 | tf_op jit(solution)/shard_map/attn_fwd/pallas_call | solution.py:552
  221.2 9.6 %collective-permute-done.12 = bf16[4,64,512]{2,1,0:T(8,128)(2,1)S(1)} collective-permute-done((bf16[4,64,512]{2,1,0:T(8,128)(2,1)S(1)}, bf16[4,64,512]{2,1,0:T(8,128)(2,1)S(1)}, u32[]{:S(2)}, u32[]{:S(2)}) %collective-permute-start.12) | collective-permute-done | bytes 262176 | tf_op jit(solution)/shard_map/ppermute | solution.py:609
  231.9 7.9 all-to-all-start.1
  239.8 33.7 %all-gather.7.cloned.1.call-done = bf16[16,64,4608]{2,1,0:T(8,128)(2,1)} async-done(((bf16[4,64,4608]{2,1,0:T(8,128)(2,1)}), bf16[16,64,4608]{2,1,0:T(8,128)(2,1)}) %all-gather.7.cloned.1.call-update) | async-done | bytes 9437200 | tf_op jit(solution)/shard_map/all_gather | solution.py:932
  273.5 8.2 copy.126
  297.8 17.3 %mlp_fwd.3 = (bf16[1024,1024]{1,0:T(8,128)(2,1)}, bf16[1024,2048]{1,0:T(8,128)(2,1)}, bf16[1024,2048]{1,0:T(8,128)(2,1)}, bf16[512,1024]{1,0:T(8,128)(2,1)}, bf16[512,1024]{1,0:T(8,128)(2,1)}) custom-call(bf16[512,1024]{1,0:T(8,128)(2,1)} %copy-done.15, bf16[512,1024]{1,0:T(8,128)(2,1)} %copy-done.32, bf16[1024,4608]{1,0:T(8,128)(2,1)} %bitcast.136, ...), custom_call_target="tpu_custom_call" | custom-call | flops 2147483648 | bytes 5242880 | tf_op jit(solution)/shard_map/mlp_fwd/pallas_call | solution.py:717
  318.2 3.8 convolution_convert_fusion.5
  322.0 5.5 all-to-all-start.2
  328.3 34.9 %all-to-all-done.2 = bf16[16,48,1024]{2,1,0:T(8,128)(2,1)} async-done(((bf16[16,48,1024]{2,1,0:T(8,128)(2,1)}), bf16[16,48,1024]{2,1,0:T(8,128)(2,1)}, u32[]{:S(2)}, u32[]{:S(2)}) %all-to-all-start.2) | async-done | bytes 1572896 | tf_op jit(solution)/shard_map/all_to_all | solution.py:52
  365.4 4.9 all-to-all-start.3
  370.2 22.0 %mlp_fwd.4 = (bf16[1536,1024]{1,0:T(8,128)(2,1)}, bf16[1536,2048]{1,0:T(8,128)(2,1)}, bf16[1536,2048]{1,0:T(8,128)(2,1)}, bf16[768,1024]{1,0:T(8,128)(2,1)}, bf1...) custom-call(bf16[768,1024]{1,0:T(8,128)(2,1)} %bitcast.31.refs_0_, bf16[768,1024]{1,0:T(8,128)(2,1)} %collective-permute-done.16.refs_1_, ...), custom_call_target="tpu_custom_call" | custom-call | flops 3221225472 | bytes 6815744 | tf_op jit(solution)/shard_map/mlp_fwd/pallas_call | solution.py:717
  399.5 23.5 %mlp_fwd.5 = (bf16[1536,1024]{1,0:T(8,128)(2,1)}, bf16[1536,2048]{1,0:T(8,128)(2,1)}, bf16[1536,2048]{1,0:T(8,128)(2,1)}, bf16[768,1024]{1,0:T(8,128)(2,1)}, bf16[768,1024]{1,0:T(8,128)(2,1)}) custom-call(bf16[1536,1024]{1,0:T(8,128)(2,1)} %get-tuple-element.123.refs_0_, bf16[768,1024]{1,0:T(8,128)(2,1)} %get-tuple-element.103.refs_1_, ...), custom_call_target="tpu_custom_call" | custom-call | flops 3221225472 | bytes 6815744 | tf_op jit(solution)/shard_map/mlp_fwd/pallas_call | solution.py:717
  426.9 21.5 %mlp_bwd.3 = (bf16[1536,1024]{1,0:T(8,128)(2,1)}, bf16[1536,2048]{1,0:T(8,128)(2,1)}, bf16[768,1024]{1,0:T(8,128)(2,1)}, bf16[768,1024]{1,0:T(8,128)(2,1)}) custom-call(f32[1536,1]{1,0:T(8,128)} %broadcast_select_fusion.9.refs_0_, bf16[768,1024]{1,0:T(8,128)(2,1)} %bitcast.36.refs_1_, bf16[768,1024]{1,0:T(8,128)(2,1)} %collective-permute-done.19.refs_2_, ...), custom_call_target="tpu_custom_call" | custom-call | flops 12884901888 | bytes 27262976 | tf_op jit(solution)/shard_map/mlp_bwd/pallas_call | solution.py:751
  454.2 6.7 all-to-all-start.4
  460.9 23.5 %mlp_bwd.4 = (bf16[1536,1024]{1,0:T(8,128)(2,1)}, bf16[1536,2048]{1,0:T(8,128)(2,1)}, bf16[768,1024]{1,0:T(8,128)(2,1)}, bf16[768,1024]{1,0:T(8,128)(2,1)}) custom-call(f32[1536,1]{1,0:T(8,128)} %broadcast_select_fusion.9.refs_0_, bf16[768,1024]{1,0:T(8,128)(2,1)} %bitcast.36.refs_1_, bf16[768,1024]{1,0:T(8,128)(2,1)} %collective-permute-done.19.refs_2_, ...), custom_call_target="tpu_custom_call" | custom-call | flops 12884901888 | bytes 27262976 | tf_op jit(solution)/shard_map/mlp_bwd/pallas_call | solution.py:751
  488.6 4.0 add_convert_fusion.1
  492.6 3.8 all-to-all-done.4
  496.5 5.7 all-to-all-start.5
  502.2 12.0 %fusion.58 = f32[1024,2048]{1,0:T(8,128)} fusion(bf16[1536,1024]{1,0:T(8,128)(2,1)} %get-tuple-element.123.refs_0_, bf16[1536,2048]{1,0:T(8,128)(2,1)} %get-tuple-element.124), kind=kOutput, calls=%fused_computation.206 | convolution fusion | flops 6442450944 | bytes 17825792 | tf_op jit(solution)/shard_map/dot_general | solution.py:60
  514.2 11.1 %fusion.57 = f32[2048,1024]{1,0:T(8,128)} fusion(bf16[1536,2048]{1,0:T(8,128)(2,1)} %get-tuple-element.121, bf16[1536,1024]{1,0:T(8,128)(2,1)S(1)} %copy-done.60), kind=kOutput, calls=%fused_computation.205 | convolution fusion | flops 6442450944 | bytes 17825792 | tf_op jit(solution)/shard_map/dot_general | solution.py:60
  525.2 12.5 %all-to-all-done.5 = bf16[16,48,1024]{2,1,0:T(8,128)(2,1)} async-done(((bf16[16,48,1024]{2,1,0:T(8,128)(2,1)}), bf16[16,48,1024]{2,1,0:T(8,128)(2,1)}, u32[]{:S(2)}, u32[]{:S(2)}) %all-to-all-start.5) | async-done | bytes 1572896 | tf_op jit(solution)/shard_map/all_to_all | solution.py:52
  546.6 16.6 %mlp_bwd.5 = (bf16[1024,1024]{1,0:T(8,128)(2,1)}, bf16[1024,2048]{1,0:T(8,128)(2,1)}, bf16[512,1024]{1,0:T(8,128)(2,1)}, bf16[512,1024]{1,0:T(8,128)(2,1)}) custom-call(bf16[512,1024]{1,0:T(8,128)(2,1)} %copy-done.56, bf16[512,1024]{1,0:T(8,128)(2,1)} %copy-done.57, bf16[1024,4608]{1,0:T(8,128)(2,1)} %bitcast.138, bf16[1024,4608]{1,0:T(8,128)(2,1)} %bitcast.139, ...), custom_call_target="tpu_custom_call" | custom-call | flops 8589934592 | bytes 20971520 | tf_op jit(solution)/shard_map/mlp_bwd/pallas_call | solution.py:751
  577.7 4.2 all-to-all-start.6
  582.2 7.5 convolution_convert_fusion.2
  589.8 4.9 convolution_convert_fusion.1
  596.7 5.3 pad_maximum_fusion
  602.0 4.0 all-to-all-done.6
  607.8 5.0 collective-permute-start.27
  614.8 84.1 %attn_bwd.1 = (bf16[20,192,512]{2,1,0:T(8,128)(2,1)}, bf16[16,128,512]{2,1,0:T(8,128)(2,1)S(1)}) custom-call(s32[4,20]{1,0:T(4,128)S(1)} %add_select_fusion.2.plan, bf16[20,192,512]{2,1,0:T(8,128)(2,1)} %copy-done, bf16[16,128,512]{2,1,0:T(8,128)(2,1)} %copy-done.1, bf16[20,64,512]{2,1,0:T(8,128)(2,1)S(1)} %pad_maximum_fusion.7.grad, ...), custom_call_target="tpu_custom_call" | custom-call | flops 67108864000 | bytes 16777216 | tf_op jit(solution)/shard_map/attn_bwd/pallas_call | solution.py:579
  698.9 5.1 collective-permute-start.28
  712.1 5.7 all-to-all-start.7
  717.8 12.0 %fusion.60 = f32[1024,2048]{1,0:T(8,128)} fusion(bf16[1536,1024]{1,0:T(8,128)(2,1)} %get-tuple-element.149, bf16[1536,2048]{1,0:T(8,128)(2,1)} %get-tuple-element.150), kind=kOutput, calls=%fused_computation.208 | convolution fusion | flops 6442450944 | bytes 17825792 | tf_op jit(solution)/shard_map/dot_general | solution.py:60
  729.7 11.1 %fusion.59 = f32[2048,1024]{1,0:T(8,128)} fusion(bf16[1536,2048]{1,0:T(8,128)(2,1)} %get-tuple-element.147, bf16[1536,1024]{1,0:T(8,128)(2,1)S(1)} %copy-done.61), kind=kOutput, calls=%fused_computation.207 | convolution fusion | flops 6442450944 | bytes 17825792 | tf_op jit(solution)/shard_map/dot_general | solution.py:60
  740.8 69.0 %all-to-all-done.7 = bf16[16,192,512]{2,1,0:T(8,128)(2,1)} async-done(((bf16[16,192,512]{2,1,0:T(8,128)(2,1)}), bf16[16,192,512]{2,1,0:T(8,128)(2,1)}, u32[]{:S(2)}, u32[]{:S(2)}) %all-to-all-start.7) | async-done | bytes 3145760 | tf_op jit(solution)/shard_map/all_to_all | solution.py:1151
  818.5 4.0 add_convert_fusion.4
  822.5 3.9 convolution_convert_fusion
  835.8 11.8 %collective-permute-done.34 = bf16[4,2,64,768]{3,2,0,1:T(8,128)(2,1)S(1)} collective-permute-done((bf16[4,2,64,768]{3,2,0,1:T(8,128)(2,1)S(1)}, bf16[4,2,64,768]{3,2,0,1:T(8,128)(2,1)S(1)}, u32[]{:S(2)}, u32[]{:S(2)}) %collective-permute-start.34) | collective-permute-done | bytes 786464 | tf_op jit(solution)/shard_map/ppermute | solution.py:774
  851.2 6.6 collective-permute-done.35
  866.7 12.0 %collective-permute-done.38 = bf16[64,1536]{1,0:T(8,128)(2,1)S(1)} collective-permute-done((bf16[64,1536]{1,0:T(8,128)(2,1)S(1)}, bf16[64,1536]{1,0:T(8,128)(2,1)S(1)}, u32[]{:S(2)}, u32[]{:S(2)}) %collective-permute-start.38) | collective-permute-done | bytes 196640 | tf_op jit(solution)/shard_map/ppermute | solution.py:774
  (353 shorter events, 169.2 us)
Async XLA Ops:
  7.2 81.6 %all-gather.5.cloned.1.call-start = ((), (), s32[]{:S(2)}) async-start(), calls=%async_computation.10 | async-start | bytes 2949120 | tf_op jit(solution)/shard_map/all_gather | solution.py:900
  8.1 6.2 collective-permute-start.1
  14.5 9.4 %collective-permute-start.2 = (bf16[72,1536]{1,0:T(8,128)(2,1)S(1)}, bf16[72,1536]{1,0:T(8,128)(2,1)S(1)}, u32[]{:S(2)}, u32[]{:S(2)}) collective-permute-start(bf16[72,1536]{1,0:T(8,128)(2,1)S(1)} %fusion.23), channel_id=1, source_target_pairs={{0,8},{2,10},{4,12},{6,14},{8,0},{10,2},{12,4},{14,6},{16,24},{18,... | collective-permute-start | bytes 663560 | tf_op jit(solution)/shard_map/ppermute | solution.py:774
  14.5 16.4 %collective-permute-start.3 = (bf16[72,1536]{1,0:T(8,128)(2,1)S(1)}, bf16[72,1536]{1,0:T(8,128)(2,1)S(1)}, u32[]{:S(2)}, u32[]{:S(2)}) collective-permute-start(bf16[72,1536]{1,0:T(8,128)(2,1)S(1)} %fusion.23), channel_id=1, source_target_pairs={{0,16},{2,18},{4,20},{6,22},{8,24},{10,26},{12,28},{14,30},{16,0},... | collective-permute-start | bytes 663560 | tf_op jit(solution)/shard_map/ppermute | solution.py:774
  17.0 19.7 %collective-permute-start.4 = (bf16[72,1536]{1,0:T(8,128)(2,1)S(1)}, bf16[72,1536]{1,0:T(8,128)(2,1)S(1)}, u32[]{:S(2)}, u32[]{:S(2)}) collective-permute-start(bf16[72,1536]{1,0:T(8,128)(2,1)S(1)} %fusion.23), channel_id=1, source_target_pairs={{0,24},{2,26},{4,28},{6,30},{8,16},{10,18},{12,20},{14,22},{16,8},... | collective-permute-start | bytes 663560 | tf_op jit(solution)/shard_map/ppermute | solution.py:774
  38.1 10.9 %collective-permute-start.5 = (bf16[4,72,768]{2,1,0:T(8,128)(2,1)}, bf16[4,72,768]{2,1,0:T(8,128)(2,1)}, u32[]{:S(2)}, u32[]{:S(2)}) collective-permute-start(bf16[4,72,768]{2,1,0:T(8,128)(2,1)} %get-tuple-element.193), channel_id=1, source_target_pairs={{0,4},{2,6},{4,0},{6,2},{8,12},{10,14},{12,8},{14,10},{16,20},{18,... | collective-permute-start | bytes 1327112 | tf_op jit(solution)/shard_map/ppermute | solution.py:774
  39.3 12.3 %collective-permute-start.7 = (bf16[4,72,768]{2,1,0:T(8,128)(2,1)}, bf16[4,72,768]{2,1,0:T(8,128)(2,1)S(1)}, u32[]{:S(2)}, u32[]{:S(2)}) collective-permute-start(bf16[4,72,768]{2,1,0:T(8,128)(2,1)} %get-tuple-element.192), channel_id=1, source_target_pairs={{0,2},{2,0},{4,6},{6,4},{8,10},{10,8},{12,14},{14,12},{16,18},{18,... | collective-permute-start | bytes 1327112 | tf_op jit(solution)/shard_map/ppermute | solution.py:774
  40.5 12.7 %collective-permute-start = (bf16[512,1024]{1,0:T(8,128)(2,1)S(1)}, bf16[512,1024]{1,0:T(8,128)(2,1)S(1)}, u32[]{:S(2)}, u32[]{:S(2)}) collective-permute-start(bf16[512,1024]{1,0:T(8,128)(2,1)S(1)} %copy-done.3), channel_id=1, source_target_pairs={{0,1},{1,0},{2,3},{3,2},{4,5},{5,4},{6,7},{7,6},{8,9},{9,8},{10,11... | collective-permute-start | bytes 3145736 | tf_op jit(solution)/shard_map/ppermute | solution.py:605
  50.3 19.3 %collective-permute-start.6 = (bf16[4,2,72,768]{3,2,0,1:T(8,128)(2,1)S(1)}, bf16[4,2,72,768]{3,2,0,1:T(8,128)(2,1)S(1)}, u32[]{:S(2)}, u32[]{:S(2)}) collective-permute-start(bf16[4,2,72,768]{3,2,0,1:T(8,128)(2,1)S(1)} %maximum_select_fusion.3), channel_id=1, source_target_pairs={{0,2},{2,0},{4,6},{6,4},{8,10},{10,8},{12,14},{14,12},{16,18},{18,... | collective-permute-start | bytes 2654216 | tf_op jit(solution)/shard_map/ppermute | solution.py:774
  51.7 19.5 %collective-permute-start.8 = (bf16[4,2,72,768]{3,2,0,1:T(8,128)(2,1)S(1)}, bf16[4,2,72,768]{3,2,0,1:T(8,128)(2,1)S(1)}, u32[]{:S(2)}, u32[]{:S(2)}) collective-permute-start(bf16[4,2,72,768]{3,2,0,1:T(8,128)(2,1)S(1)} %maximum_select_fusion.4), channel_id=1, source_target_pairs={{0,4},{2,6},{4,0},{6,2},{8,12},{10,14},{12,8},{14,10},{16,20},{18,... | collective-permute-start | bytes 2654216 | tf_op jit(solution)/shard_map/ppermute | solution.py:774
  78.2 5.9 collective-permute-start.9
  88.8 74.0 %all-to-all-start = ((bf16[16,192,512]{2,1,0:T(8,128)(2,1)}), bf16[16,192,512]{2,1,0:T(8,128)(2,1)S(1)}, u32[]{:S(2)}, u32[]{:S(2)}) async-start(bf16[16,192,512]{2,1,0:T(8,128)(2,1)} %bitcast.141), calls=%async_computation | async-start | bytes 6291456 | tf_op jit(solution)/shard_map/all_to_all | solution.py:929
  95.2 178.4 %all-gather.7.cloned.1.call-start = ((), (), s32[]{:S(2)}) async-start(), calls=%async_computation.11 | async-start | bytes 11796480 | tf_op jit(solution)/shard_map/all_gather | solution.py:932
  163.0 7.2 collective-permute-start.11
  164.4 5.7 collective-permute-start.10
  219.8 11.0 %collective-permute-start.12 = (bf16[4,64,512]{2,1,0:T(8,128)(2,1)S(1)}, bf16[4,64,512]{2,1,0:T(8,128)(2,1)S(1)}, u32[]{:S(2)}, u32[]{:S(2)}) collective-permute-start(bf16[4,64,512]{2,1,0:T(8,128)(2,1)S(1)} %slice.198), channel_id=1, source_target_pairs={{0,1},{2,3},{4,5},{6,7},{8,9},{10,11},{12,13},{14,15},{16,17},{18,... | collective-permute-start | bytes 786440 | tf_op jit(solution)/shard_map/ppermute | solution.py:609
  231.9 55.4 %all-to-all-start.1 = ((bf16[16,64,512]{2,1,0:T(8,128)(2,1)}), bf16[16,64,512]{2,1,0:T(8,128)(2,1)}, u32[]{:S(2)}, u32[]{:S(2)}) async-start(bf16[16,64,512]{2,1,0:T(8,128)(2,1)} %pad_maximum_fusion.8), calls=%async_computation.1 | async-start | bytes 2097152 | tf_op jit(solution)/shard_map/all_to_all | solution.py:966
  284.2 7.1 collective-permute-start.13
  322.0 41.2 %all-to-all-start.2 = ((bf16[16,48,1024]{2,1,0:T(8,128)(2,1)}), bf16[16,48,1024]{2,1,0:T(8,128)(2,1)}, u32[]{:S(2)}, u32[]{:S(2)}) async-start(bf16[16,48,1024]{2,1,0:T(8,128)(2,1)} %bitcast.164), calls=%async_computation.2 | async-start | bytes 3145728 | tf_op jit(solution)/shard_map/all_to_all | solution.py:52
  363.2 7.0 collective-permute-start.16
  365.4 57.7 %all-to-all-start.3 = ((bf16[16,48,1024]{2,1,0:T(8,128)(2,1)}), bf16[16,48,1024]{2,1,0:T(8,128)(2,1)}, u32[]{:S(2)}, u32[]{:S(2)}) async-start(bf16[16,48,1024]{2,1,0:T(8,128)(2,1)} %bitcast.163), calls=%async_computation.3 | async-start | bytes 3145728 | tf_op jit(solution)/shard_map/all_to_all | solution.py:52
  392.3 3.9 collective-permute-start.17
  392.9 5.5 collective-permute-start.18
  423.0 3.8 collective-permute-start.19
  426.7 22.4 %collective-permute-start.23 = (bf16[768,1024]{1,0:T(8,128)(2,1)}, bf16[768,1024]{1,0:T(8,128)(2,1)S(1)}, u32[]{:S(2)}, u32[]{:S(2)}) collective-permute-start(bf16[768,1024]{1,0:T(8,128)(2,1)} %get-tuple-element.115), channel_id=1, source_target_pairs={{0,1},{1,0},{2,3},{3,2},{4,5},{5,4},{6,7},{7,6},{8,9},{9,8},{10,11... | collective-permute-start | bytes 4718600 | tf_op jit(solution)/shard_map/ppermute | solution.py:605
  448.3 12.6 %collective-permute-start.20 = (bf16[768,1024]{1,0:T(8,128)(2,1)}, bf16[768,1024]{1,0:T(8,128)(2,1)}, u32[]{:S(2)}, u32[]{:S(2)}) collective-permute-start(bf16[768,1024]{1,0:T(8,128)(2,1)} %get-tuple-element.110.refs_4_), channel_id=1, source_target_pairs={{0,1},{1,0},{2,3},{3,2},{4,5},{5,4},{6,7},{7,6},{8,9},{9,8},{10,11... | collective-permute-start | bytes 4718600 | tf_op jit(solution)/shard_map/ppermute | solution.py:605
  448.7 12.2 %collective-permute-start.21 = (bf16[768,1024]{1,0:T(8,128)(2,1)}, bf16[768,1024]{1,0:T(8,128)(2,1)}, u32[]{:S(2)}, u32[]{:S(2)}) collective-permute-start(bf16[768,1024]{1,0:T(8,128)(2,1)} %get-tuple-element.109.refs_3_), channel_id=1, source_target_pairs={{0,1},{1,0},{2,3},{3,2},{4,5},{5,4},{6,7},{7,6},{8,9},{9,8},{10,11... | collective-permute-start | bytes 4718600 | tf_op jit(solution)/shard_map/ppermute | solution.py:605
  454.2 42.3 %all-to-all-start.4 = ((bf16[16,48,1024]{2,1,0:T(8,128)(2,1)}), bf16[16,48,1024]{2,1,0:T(8,128)(2,1)}, u32[]{:S(2)}, u32[]{:S(2)}) async-start(bf16[16,48,1024]{2,1,0:T(8,128)(2,1)} %bitcast.144), calls=%async_computation.4 | async-start | bytes 3145728 | tf_op jit(solution)/shard_map/all_to_all | solution.py:52
  484.4 4.2 collective-permute-start.22
  496.5 41.3 %all-to-all-start.5 = ((bf16[16,48,1024]{2,1,0:T(8,128)(2,1)}), bf16[16,48,1024]{2,1,0:T(8,128)(2,1)}, u32[]{:S(2)}, u32[]{:S(2)}) async-start(bf16[16,48,1024]{2,1,0:T(8,128)(2,1)} %bitcast.143), calls=%async_computation.5 | async-start | bytes 3145728 | tf_op jit(solution)/shard_map/all_to_all | solution.py:52
  540.5 5.2 collective-permute-start.24
  577.3 17.4 %collective-permute-start.26 = (bf16[1024,512]{1,0:T(8,128)(2,1)}, bf16[1024,512]{1,0:T(8,128)(2,1)}, u32[]{:S(2)}, u32[]{:S(2)}) collective-permute-start(bf16[1024,512]{1,0:T(8,128)(2,1)} %convolution_convert_fusion.7), channel_id=1, source_target_pairs={{0,1},{1,0},{2,3},{3,2},{4,5},{5,4},{6,7},{7,6},{8,9},{9,8},{10,11... | collective-permute-start | bytes 3145736 | tf_op jit(solution)/shard_map/ppermute | solution.py:605
  577.7 28.4 %all-to-all-start.6 = ((bf16[16,64,512]{2,1,0:T(8,128)(2,1)}), bf16[16,64,512]{2,1,0:T(8,128)(2,1)}, u32[]{:S(2)}, u32[]{:S(2)}) async-start(bf16[16,64,512]{2,1,0:T(8,128)(2,1)} %bitcast.149), calls=%async_computation.6 | async-start | bytes 2097152 | tf_op jit(solution)/shard_map/all_to_all | solution.py:1119
  582.0 300.3 %reduce-scatter.2.cloned.1.call-start = ((), (), s32[]{:S(2)}) async-start(), calls=%async_computation.9 | async-start | bytes 10027008 | tf_op jit(solution)/shard_map/reduce_scatter | solution.py:1133
  607.8 5.7 collective-permute-start.27
  698.9 9.9 %collective-permute-start.28 = (bf16[16,128,512]{2,1,0:T(8,128)(2,1)S(1)}, bf16[16,128,512]{2,1,0:T(8,128)(2,1)S(1)}, u32[]{:S(2)}, u32[]{:S(2)}) collective-permute-start(bf16[16,128,512]{2,1,0:T(8,128)(2,1)S(1)} %get-tuple-element.141), channel_id=1, source_target_pairs={{1,0},{3,2},{5,4},{7,6},{9,8},{11,10},{13,12},{15,14},{17,16},{19,... | collective-permute-start | bytes 6291464 | tf_op jit(solution)/shard_map/ppermute | solution.py:613
  705.2 4.5 collective-permute-start.29
  712.1 97.8 %all-to-all-start.7 = ((bf16[16,192,512]{2,1,0:T(8,128)(2,1)}), bf16[16,192,512]{2,1,0:T(8,128)(2,1)}, u32[]{:S(2)}, u32[]{:S(2)}) async-start(bf16[16,192,512]{2,1,0:T(8,128)(2,1)} %maximum_select_fusion), calls=%async_computation.7 | async-start | bytes 6291456 | tf_op jit(solution)/shard_map/all_to_all | solution.py:1151
  811.9 10.6 %collective-permute-start.30 = (bf16[1536,512]{1,0:T(8,128)(2,1)S(1)}, bf16[1536,512]{1,0:T(8,128)(2,1)S(1)}, u32[]{:S(2)}, u32[]{:S(2)}) collective-permute-start(bf16[1536,512]{1,0:T(8,128)(2,1)S(1)} %bitcast.167), channel_id=1, source_target_pairs={{0,1},{1,0},{2,3},{3,2},{4,5},{5,4},{6,7},{7,6},{8,9},{9,8},{10,11... | collective-permute-start | bytes 4718600 | tf_op jit(solution)/shard_map/ppermute | solution.py:605
  826.7 20.9 %collective-permute-start.34 = (bf16[4,2,64,768]{3,2,0,1:T(8,128)(2,1)S(1)}, bf16[4,2,64,768]{3,2,0,1:T(8,128)(2,1)S(1)}, u32[]{:S(2)}, u32[]{:S(2)}) collective-permute-start(bf16[4,2,64,768]{3,2,0,1:T(8,128)(2,1)S(1)} %select_bitcast_fusion), channel_id=1, source_target_pairs={{0,4},{2,6},{4,0},{6,2},{8,12},{10,14},{12,8},{14,10},{16,20},{18,... | collective-permute-start | bytes 2359304 | tf_op jit(solution)/shard_map/ppermute | solution.py:774
  830.1 18.9 %collective-permute-start.32 = (bf16[4,2,64,768]{3,2,0,1:T(8,128)(2,1)S(1)}, bf16[4,2,64,768]{3,2,0,1:T(8,128)(2,1)S(1)}, u32[]{:S(2)}, u32[]{:S(2)}) collective-permute-start(bf16[4,2,64,768]{3,2,0,1:T(8,128)(2,1)S(1)} %select_bitcast_fusion.1), channel_id=1, source_target_pairs={{0,2},{2,0},{4,6},{6,4},{8,10},{10,8},{12,14},{14,12},{16,18},{18,... | collective-permute-start | bytes 2359304 | tf_op jit(solution)/shard_map/ppermute | solution.py:774
  834.8 15.8 %collective-permute-start.31 = (bf16[512,1024]{1,0:T(8,128)(2,1)S(1)}, bf16[512,1024]{1,0:T(8,128)(2,1)S(1)}, u32[]{:S(2)}, u32[]{:S(2)}) collective-permute-start(bf16[512,1024]{1,0:T(8,128)(2,1)S(1)} %slice.335), channel_id=1, source_target_pairs={{0,1},{1,0},{2,3},{3,2},{4,5},{5,4},{6,7},{7,6},{8,9},{9,8},{10,11... | collective-permute-start | bytes 3145736 | tf_op jit(solution)/shard_map/ppermute | solution.py:605
  848.0 9.9 %collective-permute-start.35 = (bf16[4,64,768]{2,1,0:T(8,128)(2,1)S(1)}, bf16[4,64,768]{2,1,0:T(8,128)(2,1)S(1)}, u32[]{:S(2)}, u32[]{:S(2)}) collective-permute-start(bf16[4,64,768]{2,1,0:T(8,128)(2,1)S(1)} %select_bitcast_fusion.2), channel_id=1, source_target_pairs={{0,2},{2,0},{4,6},{6,4},{8,10},{10,8},{12,14},{14,12},{16,18},{18,... | collective-permute-start | bytes 1179656 | tf_op jit(solution)/shard_map/ppermute | solution.py:774
  849.4 9.5 %collective-permute-start.33 = (bf16[4,64,768]{2,1,0:T(8,128)(2,1)S(1)}, bf16[4,64,768]{2,1,0:T(8,128)(2,1)S(1)}, u32[]{:S(2)}, u32[]{:S(2)}) collective-permute-start(bf16[4,64,768]{2,1,0:T(8,128)(2,1)S(1)} %select_bitcast_fusion.3), channel_id=1, source_target_pairs={{0,4},{2,6},{4,0},{6,2},{8,12},{10,14},{12,8},{14,10},{16,20},{18,... | collective-permute-start | bytes 1179656 | tf_op jit(solution)/shard_map/ppermute | solution.py:774
  859.1 4.6 collective-permute-start.36
  859.2 7.5 collective-permute-start.37
  860.2 18.4 %collective-permute-start.38 = (bf16[64,1536]{1,0:T(8,128)(2,1)S(1)}, bf16[64,1536]{1,0:T(8,128)(2,1)S(1)}, u32[]{:S(2)}, u32[]{:S(2)}) collective-permute-start(bf16[64,1536]{1,0:T(8,128)(2,1)S(1)} %get-tuple-element.200), channel_id=1, source_target_pairs={{0,24},{2,26},{4,28},{6,30},{8,16},{10,18},{12,20},{14,22},{16,8},... | collective-permute-start | bytes 589832 | tf_op jit(solution)/shard_map/ppermute | solution.py:774
  884.2 4.4 collective-permute-start.39
  (67 other events, 658.8 us)
Sparse Core Ops, SparseCore 0:
  42.4 46.3 all-gather.4
  163.0 110.5 all-gather.6
  613.0 215.7 reduce-scatter.1

commit v9 on v8

--- a/solution.py
+++ b/solution.py
@@ -928,7 +928,7 @@
     sent_grad = matmul_tn(placer, late_grad).astype(BF16).reshape(experts, slots_per, width)
     by_head = lax.all_to_all(qkv_t, "dp", split_axis=0, concat_axis=0, tiled=True)
 
-    by_head, second_line, sent_grad = lax.optimization_barrier((by_head, second_line, sent_grad))
+    by_head, sent_grad = lax.optimization_barrier((by_head, sent_grad))
     second_all = lax.all_gather(
         second_line, "dp", axis_index_groups=[[4 * z + k for k in range(4)] for z in range(planes)]
     )

time: 906 us -> 884 us (0.976)
  waiting for transfers between devices: 333 us -> 310 us
    all_gather x1, waiting for transfers between devices: 33.7 us -> 0.02 us  [body_paired(): lax.all_gather(second_line, 'dp', axis_index_groups=[[4 * z + k for k in...]
    all_to_all x1, waiting for transfers between devices: 0.01 us -> 10.5 us  [body_paired(): lax.all_to_all(attn_own, 'dp', split_axis=0, concat_axis=0, tiled=True)]
  transfers between devices with their start and end apart: 52 -> 52, of which waited for: 31 -> 31; matrix products, arithmetic and copies ran while one was open for 17% -> 18% of each run, Pallas kernels for 25% -> 25%
where the time goes in v9:
time: 884 us; the launch traced here: 874 us
  waiting for transfers between devices  310 us (35%)
  Pallas kernels  256 us (29%)
  starting transfers between devices  105 us (12%)
  matrix products  98 us (11%)
  other arithmetic  54.1 us (6%)
  local copies, waits for them, and re-layouts  35.8 us (4%)
  between operations  15.4 us (2%)
    pallas_call x1, Pallas kernels, attn_backward(): pl.pallas_call(functools.partial(attn_bwd_kernel, head=head, factor=head...  84.1 us
    ppermute x14, waiting for transfers between devices, from_bit(): lax.ppermute(value, 'dp', [(i, i ^ bit) for i in range(lax.axis_size('dp'...  76.1 us
    all_to_all x1, waiting for transfers between devices, body_paired(): lax.all_to_all(grad_head, 'dp', split_axis=0, concat_axis=0, tiled=True)  69 us
    dot_general x8, matrix products, matmul_tn(): lax.dot_general(left, right, (((0,), (0,)), ((), ())), preferred_element_...  65.9 us
    all_to_all x1, waiting for transfers between devices, body_paired(): lax.all_to_all(qkv_t, 'dp', split_axis=0, concat_axis=0, tiled=True)  63.8 us
    pallas_call x3, Pallas kernels, mlp_forward(): pl.pallas_call(functools.partial(mlp_kernel, kinds=kinds, transposed=tran...  62.8 us
    pallas_call x3, Pallas kernels, mlp_backward(): pl.pallas_call(functools.partial(mlp_back_kernel, kinds=kinds, transposed...  61.5 us
    all_to_all x4, waiting for transfers between devices, to_experts(): return lax.all_to_all(value, 'dp', split_axis=0, concat_axis=0, tiled=True)  51.2 us
  transfers between devices with their start and end apart: 52, of which 31 were waited for; matrix products, arithmetic and copies ran while one was open for 18% of the time, Pallas kernels for 25%

profile of v9, /device:TPU:9, one launch (start us, length us, event | category | flops | bytes accessed | tf_op | source)
XLA Modules:
  0.0 874.3 jit_solution(5854264234714720544)
XLA Ops:
  17.2 6.7 collective-permute-done.2
  23.9 7.0 collective-permute-done.3
  30.9 5.8 collective-permute-done.4
  42.3 6.7 collective-permute-done.5
  54.3 15.3 %collective-permute-done.6 = bf16[4,2,72,768]{3,2,0,1:T(8,128)(2,1)S(1)} collective-permute-done((bf16[4,2,72,768]{3,2,0,1:T(8,128)(2,1)S(1)}, bf16[4,2,72,768]{3,2,0,1:T(8,128)(2,1)S(1)}, u32[]{:S(2)}, u32[]{:S(2)}) %collective-permute-start.6) | collective-permute-done | bytes 884768 | tf_op jit(solution)/shard_map/ppermute | solution.py:774
  88.8 6.8 all-to-all-start
  96.0 3.5 convolution_convert_fusion.6
  99.5 63.8 %all-to-all-done = bf16[16,192,512]{2,1,0:T(8,128)(2,1)S(1)} async-done(((bf16[16,192,512]{2,1,0:T(8,128)(2,1)}), bf16[16,192,512]{2,1,0:T(8,128)(2,1)S(1)}, u32[]{:S(2)}, u32[]{:S(2)}) %all-to-all-start) | async-done | bytes 3145760 | tf_op jit(solution)/shard_map/all_to_all | solution.py:929
  164.8 3.9 collective-permute-start.10
  172.5 47.7 %attn_fwd.1 = (bf16[20,64,512]{2,1,0:T(8,128)(2,1)S(1)}, f32[20,1,512]{2,1,0:T(1,128)S(1)}) custom-call(s32[4,20]{1,0:T(4,128)S(1)} %add_select_fusion.2.plan, bf16[20,192,512]{2,1,0:T(8,128)(2,1)S(1)} %constant_dynamic-update-slice_fusion.own, bf16[16,128,512]{2,1,0:T(8,128)(2,1)S(1)} %broadcast_select_fusion.prompts), custom_call_target="tpu_custom_call" | custom-call | flops 26843545600 | bytes 8388608 | tf_op jit(solution)/shard_map/attn_fwd/pallas_call | solution.py:552
  221.6 9.6 %collective-permute-done.12 = bf16[4,64,512]{2,1,0:T(8,128)(2,1)S(1)} collective-permute-done((bf16[4,64,512]{2,1,0:T(8,128)(2,1)S(1)}, bf16[4,64,512]{2,1,0:T(8,128)(2,1)S(1)}, u32[]{:S(2)}, u32[]{:S(2)}) %collective-permute-start.12) | collective-permute-done | bytes 262176 | tf_op jit(solution)/shard_map/ppermute | solution.py:609
  232.3 7.7 all-to-all-start.1
  240.1 8.2 copy.126
  254.0 10.5 %all-to-all-done.1 = bf16[16,64,512]{2,1,0:T(8,128)(2,1)} async-done(((bf16[16,64,512]{2,1,0:T(8,128)(2,1)}), bf16[16,64,512]{2,1,0:T(8,128)(2,1)}, u32[]{:S(2)}, u32[]{:S(2)}) %all-to-all-start.1) | async-done | bytes 1048608 | tf_op jit(solution)/shard_map/all_to_all | solution.py:966
  276.8 17.3 %mlp_fwd.3 = (bf16[1024,1024]{1,0:T(8,128)(2,1)}, bf16[1024,2048]{1,0:T(8,128)(2,1)}, bf16[1024,2048]{1,0:T(8,128)(2,1)}, bf16[512,1024]{1,0:T(8,128)(2,1)}, bf16[512,1024]{1,0:T(8,128)(2,1)}) custom-call(bf16[512,1024]{1,0:T(8,128)(2,1)} %copy-done.15, bf16[512,1024]{1,0:T(8,128)(2,1)} %copy-done.32, bf16[1024,4608]{1,0:T(8,128)(2,1)} %bitcast.136, ...), custom_call_target="tpu_custom_call" | custom-call | flops 2147483648 | bytes 5242880 | tf_op jit(solution)/shard_map/mlp_fwd/pallas_call | solution.py:717
  297.2 3.8 convolution_convert_fusion.5
  301.0 4.8 all-to-all-start.2
  306.7 34.9 %all-to-all-done.2 = bf16[16,48,1024]{2,1,0:T(8,128)(2,1)} async-done(((bf16[16,48,1024]{2,1,0:T(8,128)(2,1)}), bf16[16,48,1024]{2,1,0:T(8,128)(2,1)}, u32[]{:S(2)}, u32[]{:S(2)}) %all-to-all-start.2) | async-done | bytes 1572896 | tf_op jit(solution)/shard_map/all_to_all | solution.py:52
  344.0 4.6 all-to-all-start.3
  348.6 22.0 %mlp_fwd.4 = (bf16[1536,1024]{1,0:T(8,128)(2,1)}, bf16[1536,2048]{1,0:T(8,128)(2,1)}, bf16[1536,2048]{1,0:T(8,128)(2,1)}, bf16[768,1024]{1,0:T(8,128)(2,1)}, bf1...) custom-call(bf16[768,1024]{1,0:T(8,128)(2,1)} %bitcast.31.refs_0_, bf16[768,1024]{1,0:T(8,128)(2,1)} %collective-permute-done.16.refs_1_, ...), custom_call_target="tpu_custom_call" | custom-call | flops 3221225472 | bytes 6815744 | tf_op jit(solution)/shard_map/mlp_fwd/pallas_call | solution.py:717
  377.9 23.5 %mlp_fwd.5 = (bf16[1536,1024]{1,0:T(8,128)(2,1)}, bf16[1536,2048]{1,0:T(8,128)(2,1)}, bf16[1536,2048]{1,0:T(8,128)(2,1)}, bf16[768,1024]{1,0:T(8,128)(2,1)}, bf16[768,1024]{1,0:T(8,128)(2,1)}) custom-call(bf16[1536,1024]{1,0:T(8,128)(2,1)} %get-tuple-element.121.refs_0_, bf16[768,1024]{1,0:T(8,128)(2,1)} %get-tuple-element.101.refs_1_, ...), custom_call_target="tpu_custom_call" | custom-call | flops 3221225472 | bytes 6815744 | tf_op jit(solution)/shard_map/mlp_fwd/pallas_call | solution.py:717
  405.3 21.5 %mlp_bwd.3 = (bf16[1536,1024]{1,0:T(8,128)(2,1)}, bf16[1536,2048]{1,0:T(8,128)(2,1)}, bf16[768,1024]{1,0:T(8,128)(2,1)}, bf16[768,1024]{1,0:T(8,128)(2,1)}) custom-call(f32[1536,1]{1,0:T(8,128)} %broadcast_select_fusion.9.refs_0_, bf16[768,1024]{1,0:T(8,128)(2,1)} %bitcast.36.refs_1_, bf16[768,1024]{1,0:T(8,128)(2,1)} %collective-permute-done.19.refs_2_, ...), custom_call_target="tpu_custom_call" | custom-call | flops 12884901888 | bytes 27262976 | tf_op jit(solution)/shard_map/mlp_bwd/pallas_call | solution.py:751
  432.6 6.7 all-to-all-start.4
  439.4 23.5 %mlp_bwd.4 = (bf16[1536,1024]{1,0:T(8,128)(2,1)}, bf16[1536,2048]{1,0:T(8,128)(2,1)}, bf16[768,1024]{1,0:T(8,128)(2,1)}, bf16[768,1024]{1,0:T(8,128)(2,1)}) custom-call(f32[1536,1]{1,0:T(8,128)} %broadcast_select_fusion.9.refs_0_, bf16[768,1024]{1,0:T(8,128)(2,1)} %bitcast.36.refs_1_, bf16[768,1024]{1,0:T(8,128)(2,1)} %collective-permute-done.19.refs_2_, ...), custom_call_target="tpu_custom_call" | custom-call | flops 12884901888 | bytes 27262976 | tf_op jit(solution)/shard_map/mlp_bwd/pallas_call | solution.py:751
  467.1 4.0 add_convert_fusion.1
  471.1 3.8 all-to-all-done.4
  474.9 5.7 all-to-all-start.5
  480.6 12.0 %fusion.58 = f32[1024,2048]{1,0:T(8,128)} fusion(bf16[1536,1024]{1,0:T(8,128)(2,1)} %get-tuple-element.121.refs_0_, bf16[1536,2048]{1,0:T(8,128)(2,1)} %get-tuple-element.122), kind=kOutput, calls=%fused_computation.206 | convolution fusion | flops 6442450944 | bytes 17825792 | tf_op jit(solution)/shard_map/dot_general | solution.py:60
  492.6 11.1 %fusion.57 = f32[2048,1024]{1,0:T(8,128)} fusion(bf16[1536,2048]{1,0:T(8,128)(2,1)} %get-tuple-element.119, bf16[1536,1024]{1,0:T(8,128)(2,1)S(1)} %copy-done.60), kind=kOutput, calls=%fused_computation.205 | convolution fusion | flops 6442450944 | bytes 17825792 | tf_op jit(solution)/shard_map/dot_general | solution.py:60
  503.7 12.5 %all-to-all-done.5 = bf16[16,48,1024]{2,1,0:T(8,128)(2,1)} async-done(((bf16[16,48,1024]{2,1,0:T(8,128)(2,1)}), bf16[16,48,1024]{2,1,0:T(8,128)(2,1)}, u32[]{:S(2)}, u32[]{:S(2)}) %all-to-all-start.5) | async-done | bytes 1572896 | tf_op jit(solution)/shard_map/all_to_all | solution.py:52
  525.1 16.6 %mlp_bwd.5 = (bf16[1024,1024]{1,0:T(8,128)(2,1)}, bf16[1024,2048]{1,0:T(8,128)(2,1)}, bf16[512,1024]{1,0:T(8,128)(2,1)}, bf16[512,1024]{1,0:T(8,128)(2,1)}) custom-call(bf16[512,1024]{1,0:T(8,128)(2,1)} %copy-done.56, bf16[512,1024]{1,0:T(8,128)(2,1)} %copy-done.57, bf16[1024,4608]{1,0:T(8,128)(2,1)} %bitcast.138, bf16[1024,4608]{1,0:T(8,128)(2,1)} %bitcast.139, ...), custom_call_target="tpu_custom_call" | custom-call | flops 8589934592 | bytes 20971520 | tf_op jit(solution)/shard_map/mlp_bwd/pallas_call | solution.py:751
  556.1 4.2 all-to-all-start.6
  560.6 7.5 convolution_convert_fusion.2
  568.2 4.9 convolution_convert_fusion.1
  575.2 5.3 pad_maximum_fusion
  580.5 4.0 all-to-all-done.6
  586.2 5.0 collective-permute-start.27
  593.3 84.1 %attn_bwd.1 = (bf16[20,192,512]{2,1,0:T(8,128)(2,1)}, bf16[16,128,512]{2,1,0:T(8,128)(2,1)S(1)}) custom-call(s32[4,20]{1,0:T(4,128)S(1)} %add_select_fusion.2.plan, bf16[20,192,512]{2,1,0:T(8,128)(2,1)} %copy-done, bf16[16,128,512]{2,1,0:T(8,128)(2,1)} %copy-done.1, bf16[20,64,512]{2,1,0:T(8,128)(2,1)S(1)} %pad_maximum_fusion.7.grad, ...), custom_call_target="tpu_custom_call" | custom-call | flops 67108864000 | bytes 16777216 | tf_op jit(solution)/shard_map/attn_bwd/pallas_call | solution.py:579
  677.3 5.1 collective-permute-start.28
  690.5 5.7 all-to-all-start.7
  696.2 12.0 %fusion.60 = f32[1024,2048]{1,0:T(8,128)} fusion(bf16[1536,1024]{1,0:T(8,128)(2,1)} %get-tuple-element.147, bf16[1536,2048]{1,0:T(8,128)(2,1)} %get-tuple-element.148), kind=kOutput, calls=%fused_computation.208 | convolution fusion | flops 6442450944 | bytes 17825792 | tf_op jit(solution)/shard_map/dot_general | solution.py:60
  708.2 11.1 %fusion.59 = f32[2048,1024]{1,0:T(8,128)} fusion(bf16[1536,2048]{1,0:T(8,128)(2,1)} %get-tuple-element.145, bf16[1536,1024]{1,0:T(8,128)(2,1)S(1)} %copy-done.61), kind=kOutput, calls=%fused_computation.207 | convolution fusion | flops 6442450944 | bytes 17825792 | tf_op jit(solution)/shard_map/dot_general | solution.py:60
  719.2 69.0 %all-to-all-done.7 = bf16[16,192,512]{2,1,0:T(8,128)(2,1)} async-done(((bf16[16,192,512]{2,1,0:T(8,128)(2,1)}), bf16[16,192,512]{2,1,0:T(8,128)(2,1)}, u32[]{:S(2)}, u32[]{:S(2)}) %all-to-all-start.7) | async-done | bytes 3145760 | tf_op jit(solution)/shard_map/all_to_all | solution.py:1151
  796.9 4.0 add_convert_fusion.4
  801.0 3.9 convolution_convert_fusion
  814.2 11.8 %collective-permute-done.34 = bf16[4,2,64,768]{3,2,0,1:T(8,128)(2,1)S(1)} collective-permute-done((bf16[4,2,64,768]{3,2,0,1:T(8,128)(2,1)S(1)}, bf16[4,2,64,768]{3,2,0,1:T(8,128)(2,1)S(1)}, u32[]{:S(2)}, u32[]{:S(2)}) %collective-permute-start.34) | collective-permute-done | bytes 786464 | tf_op jit(solution)/shard_map/ppermute | solution.py:774
  829.6 6.6 collective-permute-done.35
  845.1 12.0 %collective-permute-done.38 = bf16[64,1536]{1,0:T(8,128)(2,1)S(1)} collective-permute-done((bf16[64,1536]{1,0:T(8,128)(2,1)S(1)}, bf16[64,1536]{1,0:T(8,128)(2,1)S(1)}, u32[]{:S(2)}, u32[]{:S(2)}) %collective-permute-start.38) | collective-permute-done | bytes 196640 | tf_op jit(solution)/shard_map/ppermute | solution.py:774
  (353 shorter events, 171.0 us)
Async XLA Ops:
  7.2 81.6 %all-gather.5.cloned.1.call-start = ((), (), s32[]{:S(2)}) async-start(), calls=%async_computation.10 | async-start | bytes 2949120 | tf_op jit(solution)/shard_map/all_gather | solution.py:900
  8.1 6.2 collective-permute-start.1
  14.5 9.4 %collective-permute-start.2 = (bf16[72,1536]{1,0:T(8,128)(2,1)S(1)}, bf16[72,1536]{1,0:T(8,128)(2,1)S(1)}, u32[]{:S(2)}, u32[]{:S(2)}) collective-permute-start(bf16[72,1536]{1,0:T(8,128)(2,1)S(1)} %fusion.23), channel_id=1, source_target_pairs={{0,8},{2,10},{4,12},{6,14},{8,0},{10,2},{12,4},{14,6},{16,24},{18,... | collective-permute-start | bytes 663560 | tf_op jit(solution)/shard_map/ppermute | solution.py:774
  14.5 16.4 %collective-permute-start.3 = (bf16[72,1536]{1,0:T(8,128)(2,1)S(1)}, bf16[72,1536]{1,0:T(8,128)(2,1)S(1)}, u32[]{:S(2)}, u32[]{:S(2)}) collective-permute-start(bf16[72,1536]{1,0:T(8,128)(2,1)S(1)} %fusion.23), channel_id=1, source_target_pairs={{0,16},{2,18},{4,20},{6,22},{8,24},{10,26},{12,28},{14,30},{16,0},... | collective-permute-start | bytes 663560 | tf_op jit(solution)/shard_map/ppermute | solution.py:774
  17.0 19.7 %collective-permute-start.4 = (bf16[72,1536]{1,0:T(8,128)(2,1)S(1)}, bf16[72,1536]{1,0:T(8,128)(2,1)S(1)}, u32[]{:S(2)}, u32[]{:S(2)}) collective-permute-start(bf16[72,1536]{1,0:T(8,128)(2,1)S(1)} %fusion.23), channel_id=1, source_target_pairs={{0,24},{2,26},{4,28},{6,30},{8,16},{10,18},{12,20},{14,22},{16,8},... | collective-permute-start | bytes 663560 | tf_op jit(solution)/shard_map/ppermute | solution.py:774
  38.1 10.9 %collective-permute-start.5 = (bf16[4,72,768]{2,1,0:T(8,128)(2,1)}, bf16[4,72,768]{2,1,0:T(8,128)(2,1)}, u32[]{:S(2)}, u32[]{:S(2)}) collective-permute-start(bf16[4,72,768]{2,1,0:T(8,128)(2,1)} %get-tuple-element.191), channel_id=1, source_target_pairs={{0,4},{2,6},{4,0},{6,2},{8,12},{10,14},{12,8},{14,10},{16,20},{18,... | collective-permute-start | bytes 1327112 | tf_op jit(solution)/shard_map/ppermute | solution.py:774
  39.3 12.3 %collective-permute-start.7 = (bf16[4,72,768]{2,1,0:T(8,128)(2,1)}, bf16[4,72,768]{2,1,0:T(8,128)(2,1)S(1)}, u32[]{:S(2)}, u32[]{:S(2)}) collective-permute-start(bf16[4,72,768]{2,1,0:T(8,128)(2,1)} %get-tuple-element.190), channel_id=1, source_target_pairs={{0,2},{2,0},{4,6},{6,4},{8,10},{10,8},{12,14},{14,12},{16,18},{18,... | collective-permute-start | bytes 1327112 | tf_op jit(solution)/shard_map/ppermute | solution.py:774
  40.5 12.7 %collective-permute-start = (bf16[512,1024]{1,0:T(8,128)(2,1)S(1)}, bf16[512,1024]{1,0:T(8,128)(2,1)S(1)}, u32[]{:S(2)}, u32[]{:S(2)}) collective-permute-start(bf16[512,1024]{1,0:T(8,128)(2,1)S(1)} %copy-done.3), channel_id=1, source_target_pairs={{0,1},{1,0},{2,3},{3,2},{4,5},{5,4},{6,7},{7,6},{8,9},{9,8},{10,11... | collective-permute-start | bytes 3145736 | tf_op jit(solution)/shard_map/ppermute | solution.py:605
  42.2 197.9 %all-gather.7.cloned.1.call-start = ((), (), s32[]{:S(2)}) async-start(), calls=%async_computation.11 | async-start | bytes 11796480 | tf_op jit(solution)/shard_map/all_gather | solution.py:932
  50.3 19.3 %collective-permute-start.6 = (bf16[4,2,72,768]{3,2,0,1:T(8,128)(2,1)S(1)}, bf16[4,2,72,768]{3,2,0,1:T(8,128)(2,1)S(1)}, u32[]{:S(2)}, u32[]{:S(2)}) collective-permute-start(bf16[4,2,72,768]{3,2,0,1:T(8,128)(2,1)S(1)} %maximum_select_fusion.3), channel_id=1, source_target_pairs={{0,2},{2,0},{4,6},{6,4},{8,10},{10,8},{12,14},{14,12},{16,18},{18,... | collective-permute-start | bytes 2654216 | tf_op jit(solution)/shard_map/ppermute | solution.py:774
  51.7 19.5 %collective-permute-start.8 = (bf16[4,2,72,768]{3,2,0,1:T(8,128)(2,1)S(1)}, bf16[4,2,72,768]{3,2,0,1:T(8,128)(2,1)S(1)}, u32[]{:S(2)}, u32[]{:S(2)}) collective-permute-start(bf16[4,2,72,768]{3,2,0,1:T(8,128)(2,1)S(1)} %maximum_select_fusion.4), channel_id=1, source_target_pairs={{0,4},{2,6},{4,0},{6,2},{8,12},{10,14},{12,8},{14,10},{16,20},{18,... | collective-permute-start | bytes 2654216 | tf_op jit(solution)/shard_map/ppermute | solution.py:774
  78.2 5.9 collective-permute-start.9
  88.8 74.5 %all-to-all-start = ((bf16[16,192,512]{2,1,0:T(8,128)(2,1)}), bf16[16,192,512]{2,1,0:T(8,128)(2,1)S(1)}, u32[]{:S(2)}, u32[]{:S(2)}) async-start(bf16[16,192,512]{2,1,0:T(8,128)(2,1)} %bitcast.141), calls=%async_computation | async-start | bytes 6291456 | tf_op jit(solution)/shard_map/all_to_all | solution.py:929
  163.4 7.2 collective-permute-start.11
  164.8 5.7 collective-permute-start.10
  220.3 11.0 %collective-permute-start.12 = (bf16[4,64,512]{2,1,0:T(8,128)(2,1)S(1)}, bf16[4,64,512]{2,1,0:T(8,128)(2,1)S(1)}, u32[]{:S(2)}, u32[]{:S(2)}) collective-permute-start(bf16[4,64,512]{2,1,0:T(8,128)(2,1)S(1)} %slice.198), channel_id=1, source_target_pairs={{0,1},{2,3},{4,5},{6,7},{8,9},{10,11},{12,13},{14,15},{16,17},{18,... | collective-permute-start | bytes 786440 | tf_op jit(solution)/shard_map/ppermute | solution.py:609
  232.3 32.1 %all-to-all-start.1 = ((bf16[16,64,512]{2,1,0:T(8,128)(2,1)}), bf16[16,64,512]{2,1,0:T(8,128)(2,1)}, u32[]{:S(2)}, u32[]{:S(2)}) async-start(bf16[16,64,512]{2,1,0:T(8,128)(2,1)} %pad_maximum_fusion.8), calls=%async_computation.1 | async-start | bytes 2097152 | tf_op jit(solution)/shard_map/all_to_all | solution.py:966
  250.7 17.7 %collective-permute-start.13 = (bf16[1024,512]{1,0:T(8,128)(2,1)}, bf16[1024,512]{1,0:T(8,128)(2,1)}, u32[]{:S(2)}, u32[]{:S(2)}) collective-permute-start(bf16[1024,512]{1,0:T(8,128)(2,1)} %slice.249), channel_id=1, source_target_pairs={{0,1},{1,0},{2,3},{3,2},{4,5},{5,4},{6,7},{7,6},{8,9},{9,8},{10,11... | collective-permute-start | bytes 3145736 | tf_op jit(solution)/shard_map/ppermute | solution.py:605
  271.2 4.6 collective-permute-start.14
  301.0 40.6 %all-to-all-start.2 = ((bf16[16,48,1024]{2,1,0:T(8,128)(2,1)}), bf16[16,48,1024]{2,1,0:T(8,128)(2,1)}, u32[]{:S(2)}, u32[]{:S(2)}) async-start(bf16[16,48,1024]{2,1,0:T(8,128)(2,1)} %bitcast.164), calls=%async_computation.2 | async-start | bytes 3145728 | tf_op jit(solution)/shard_map/all_to_all | solution.py:52
  341.6 7.0 collective-permute-start.16
  344.0 57.4 %all-to-all-start.3 = ((bf16[16,48,1024]{2,1,0:T(8,128)(2,1)}), bf16[16,48,1024]{2,1,0:T(8,128)(2,1)}, u32[]{:S(2)}, u32[]{:S(2)}) async-start(bf16[16,48,1024]{2,1,0:T(8,128)(2,1)} %bitcast.163), calls=%async_computation.3 | async-start | bytes 3145728 | tf_op jit(solution)/shard_map/all_to_all | solution.py:52
  370.7 3.9 collective-permute-start.17
  371.3 5.5 collective-permute-start.18
  405.1 22.4 %collective-permute-start.23 = (bf16[768,1024]{1,0:T(8,128)(2,1)}, bf16[768,1024]{1,0:T(8,128)(2,1)S(1)}, u32[]{:S(2)}, u32[]{:S(2)}) collective-permute-start(bf16[768,1024]{1,0:T(8,128)(2,1)} %get-tuple-element.113), channel_id=1, source_target_pairs={{0,1},{1,0},{2,3},{3,2},{4,5},{5,4},{6,7},{7,6},{8,9},{9,8},{10,11... | collective-permute-start | bytes 4718600 | tf_op jit(solution)/shard_map/ppermute | solution.py:605
  426.7 12.6 %collective-permute-start.20 = (bf16[768,1024]{1,0:T(8,128)(2,1)}, bf16[768,1024]{1,0:T(8,128)(2,1)}, u32[]{:S(2)}, u32[]{:S(2)}) collective-permute-start(bf16[768,1024]{1,0:T(8,128)(2,1)} %get-tuple-element.108.refs_4_), channel_id=1, source_target_pairs={{0,1},{1,0},{2,3},{3,2},{4,5},{5,4},{6,7},{7,6},{8,9},{9,8},{10,11... | collective-permute-start | bytes 4718600 | tf_op jit(solution)/shard_map/ppermute | solution.py:605
  427.1 12.2 %collective-permute-start.21 = (bf16[768,1024]{1,0:T(8,128)(2,1)}, bf16[768,1024]{1,0:T(8,128)(2,1)}, u32[]{:S(2)}, u32[]{:S(2)}) collective-permute-start(bf16[768,1024]{1,0:T(8,128)(2,1)} %get-tuple-element.107.refs_3_), channel_id=1, source_target_pairs={{0,1},{1,0},{2,3},{3,2},{4,5},{5,4},{6,7},{7,6},{8,9},{9,8},{10,11... | collective-permute-start | bytes 4718600 | tf_op jit(solution)/shard_map/ppermute | solution.py:605
  432.6 42.3 %all-to-all-start.4 = ((bf16[16,48,1024]{2,1,0:T(8,128)(2,1)}), bf16[16,48,1024]{2,1,0:T(8,128)(2,1)}, u32[]{:S(2)}, u32[]{:S(2)}) async-start(bf16[16,48,1024]{2,1,0:T(8,128)(2,1)} %bitcast.144), calls=%async_computation.4 | async-start | bytes 3145728 | tf_op jit(solution)/shard_map/all_to_all | solution.py:52
  462.8 4.2 collective-permute-start.22
  474.9 41.3 %all-to-all-start.5 = ((bf16[16,48,1024]{2,1,0:T(8,128)(2,1)}), bf16[16,48,1024]{2,1,0:T(8,128)(2,1)}, u32[]{:S(2)}, u32[]{:S(2)}) async-start(bf16[16,48,1024]{2,1,0:T(8,128)(2,1)} %bitcast.143), calls=%async_computation.5 | async-start | bytes 3145728 | tf_op jit(solution)/shard_map/all_to_all | solution.py:52
  518.9 5.2 collective-permute-start.24
  555.8 17.4 %collective-permute-start.26 = (bf16[1024,512]{1,0:T(8,128)(2,1)}, bf16[1024,512]{1,0:T(8,128)(2,1)}, u32[]{:S(2)}, u32[]{:S(2)}) collective-permute-start(bf16[1024,512]{1,0:T(8,128)(2,1)} %convolution_convert_fusion.7), channel_id=1, source_target_pairs={{0,1},{1,0},{2,3},{3,2},{4,5},{5,4},{6,7},{7,6},{8,9},{9,8},{10,11... | collective-permute-start | bytes 3145736 | tf_op jit(solution)/shard_map/ppermute | solution.py:605
  556.1 28.4 %all-to-all-start.6 = ((bf16[16,64,512]{2,1,0:T(8,128)(2,1)}), bf16[16,64,512]{2,1,0:T(8,128)(2,1)}, u32[]{:S(2)}, u32[]{:S(2)}) async-start(bf16[16,64,512]{2,1,0:T(8,128)(2,1)} %bitcast.149), calls=%async_computation.6 | async-start | bytes 2097152 | tf_op jit(solution)/shard_map/all_to_all | solution.py:1119
  560.4 300.3 %reduce-scatter.2.cloned.1.call-start = ((), (), s32[]{:S(2)}) async-start(), calls=%async_computation.9 | async-start | bytes 10027008 | tf_op jit(solution)/shard_map/reduce_scatter | solution.py:1133
  586.2 5.7 collective-permute-start.27
  677.3 9.9 %collective-permute-start.28 = (bf16[16,128,512]{2,1,0:T(8,128)(2,1)S(1)}, bf16[16,128,512]{2,1,0:T(8,128)(2,1)S(1)}, u32[]{:S(2)}, u32[]{:S(2)}) collective-permute-start(bf16[16,128,512]{2,1,0:T(8,128)(2,1)S(1)} %get-tuple-element.139), channel_id=1, source_target_pairs={{1,0},{3,2},{5,4},{7,6},{9,8},{11,10},{13,12},{15,14},{17,16},{19,... | collective-permute-start | bytes 6291464 | tf_op jit(solution)/shard_map/ppermute | solution.py:613
  683.6 4.5 collective-permute-start.29
  690.5 97.8 %all-to-all-start.7 = ((bf16[16,192,512]{2,1,0:T(8,128)(2,1)}), bf16[16,192,512]{2,1,0:T(8,128)(2,1)}, u32[]{:S(2)}, u32[]{:S(2)}) async-start(bf16[16,192,512]{2,1,0:T(8,128)(2,1)} %maximum_select_fusion), calls=%async_computation.7 | async-start | bytes 6291456 | tf_op jit(solution)/shard_map/all_to_all | solution.py:1151
  790.4 10.6 %collective-permute-start.30 = (bf16[1536,512]{1,0:T(8,128)(2,1)S(1)}, bf16[1536,512]{1,0:T(8,128)(2,1)S(1)}, u32[]{:S(2)}, u32[]{:S(2)}) collective-permute-start(bf16[1536,512]{1,0:T(8,128)(2,1)S(1)} %bitcast.167), channel_id=1, source_target_pairs={{0,1},{1,0},{2,3},{3,2},{4,5},{5,4},{6,7},{7,6},{8,9},{9,8},{10,11... | collective-permute-start | bytes 4718600 | tf_op jit(solution)/shard_map/ppermute | solution.py:605
  805.1 20.9 %collective-permute-start.34 = (bf16[4,2,64,768]{3,2,0,1:T(8,128)(2,1)S(1)}, bf16[4,2,64,768]{3,2,0,1:T(8,128)(2,1)S(1)}, u32[]{:S(2)}, u32[]{:S(2)}) collective-permute-start(bf16[4,2,64,768]{3,2,0,1:T(8,128)(2,1)S(1)} %select_bitcast_fusion), channel_id=1, source_target_pairs={{0,4},{2,6},{4,0},{6,2},{8,12},{10,14},{12,8},{14,10},{16,20},{18,... | collective-permute-start | bytes 2359304 | tf_op jit(solution)/shard_map/ppermute | solution.py:774
  808.5 18.9 %collective-permute-start.32 = (bf16[4,2,64,768]{3,2,0,1:T(8,128)(2,1)S(1)}, bf16[4,2,64,768]{3,2,0,1:T(8,128)(2,1)S(1)}, u32[]{:S(2)}, u32[]{:S(2)}) collective-permute-start(bf16[4,2,64,768]{3,2,0,1:T(8,128)(2,1)S(1)} %select_bitcast_fusion.1), channel_id=1, source_target_pairs={{0,2},{2,0},{4,6},{6,4},{8,10},{10,8},{12,14},{14,12},{16,18},{18,... | collective-permute-start | bytes 2359304 | tf_op jit(solution)/shard_map/ppermute | solution.py:774
  813.2 15.8 %collective-permute-start.31 = (bf16[512,1024]{1,0:T(8,128)(2,1)S(1)}, bf16[512,1024]{1,0:T(8,128)(2,1)S(1)}, u32[]{:S(2)}, u32[]{:S(2)}) collective-permute-start(bf16[512,1024]{1,0:T(8,128)(2,1)S(1)} %slice.335), channel_id=1, source_target_pairs={{0,1},{1,0},{2,3},{3,2},{4,5},{5,4},{6,7},{7,6},{8,9},{9,8},{10,11... | collective-permute-start | bytes 3145736 | tf_op jit(solution)/shard_map/ppermute | solution.py:605
  826.4 9.9 %collective-permute-start.35 = (bf16[4,64,768]{2,1,0:T(8,128)(2,1)S(1)}, bf16[4,64,768]{2,1,0:T(8,128)(2,1)S(1)}, u32[]{:S(2)}, u32[]{:S(2)}) collective-permute-start(bf16[4,64,768]{2,1,0:T(8,128)(2,1)S(1)} %select_bitcast_fusion.2), channel_id=1, source_target_pairs={{0,2},{2,0},{4,6},{6,4},{8,10},{10,8},{12,14},{14,12},{16,18},{18,... | collective-permute-start | bytes 1179656 | tf_op jit(solution)/shard_map/ppermute | solution.py:774
  827.8 9.5 %collective-permute-start.33 = (bf16[4,64,768]{2,1,0:T(8,128)(2,1)S(1)}, bf16[4,64,768]{2,1,0:T(8,128)(2,1)S(1)}, u32[]{:S(2)}, u32[]{:S(2)}) collective-permute-start(bf16[4,64,768]{2,1,0:T(8,128)(2,1)S(1)} %select_bitcast_fusion.3), channel_id=1, source_target_pairs={{0,4},{2,6},{4,0},{6,2},{8,12},{10,14},{12,8},{14,10},{16,20},{18,... | collective-permute-start | bytes 1179656 | tf_op jit(solution)/shard_map/ppermute | solution.py:774
  837.6 4.6 collective-permute-start.36
  837.6 7.5 collective-permute-start.37
  838.6 18.4 %collective-permute-start.38 = (bf16[64,1536]{1,0:T(8,128)(2,1)S(1)}, bf16[64,1536]{1,0:T(8,128)(2,1)S(1)}, u32[]{:S(2)}, u32[]{:S(2)}) collective-permute-start(bf16[64,1536]{1,0:T(8,128)(2,1)S(1)} %get-tuple-element.198), channel_id=1, source_target_pairs={{0,24},{2,26},{4,28},{6,30},{8,16},{10,18},{12,20},{14,22},{16,8},... | collective-permute-start | bytes 589832 | tf_op jit(solution)/shard_map/ppermute | solution.py:774
  862.7 4.4 collective-permute-start.39
  (67 other events, 661.9 us)
Sparse Core Ops, SparseCore 0:
  42.4 46.3 all-gather.4
  90.6 126.8 all-gather.6
  591.4 215.7 reduce-scatter.1

commit v10 on v9

--- a/solution.py
+++ b/solution.py
@@ -1129,8 +1129,22 @@
     second_part = jnp.concatenate(
         [grad_ffn_in.astype(BF16), grad_ffn_out_t.astype(BF16), grad_attn_half.astype(BF16)], 1
     )
+    second_part = second_part.reshape(planes, 4, shard, -1).transpose(1, 0, 2, 3).reshape(width, -1)
     grad_by_head, second_part = lax.optimization_barrier((grad_by_head, second_part))
-    second_sum = lax.psum_scatter(second_part, "dp", scatter_dimension=0, tiled=True).astype(F32)
+    second_plane = lax.psum_scatter(
+        second_part,
+        "dp",
+        scatter_dimension=0,
+        axis_index_groups=[[4 * z + k for k in range(4)] for z in range(planes)],
+        tiled=True,
+    )
+    second_sum = lax.psum_scatter(
+        second_plane,
+        "dp",
+        scatter_dimension=0,
+        axis_index_groups=[[4 * z + k for z in range(planes)] for k in range(4)],
+        tiled=True,
+    ).astype(F32)
     grad_blocks = jnp.concatenate([grad_by_head, to_core_zero(grad_by_head[:lent])], 0)
     grad_own_blocks, grad_prompts = attn_backward(
         plan, own_blocks, prompt_kv, grad_blocks, attn_blocks, log_sums

time: 884 us -> 874 us (0.989)
  waiting for transfers between devices: 310 us -> 288 us
  local copies, waits for them, and re-layouts: 35.8 us -> 44.8 us
    all_to_all x1, waiting for transfers between devices: 69 us -> 43.5 us  [body_paired(): lax.all_to_all(grad_head, 'dp', split_axis=0, concat_axis=0, tiled=True)]
  transfers between devices with their start and end apart: 52 -> 53, of which waited for: 31 -> 30; matrix products, arithmetic and copies ran while one was open for 18% -> 20% of each run, Pallas kernels for 25% -> 26%
where the time goes in v10:
time: 874 us; the launch traced here: 865 us
  waiting for transfers between devices  288 us (33%)
  Pallas kernels  256 us (29%)
  starting transfers between devices  104 us (12%)
  matrix products  99.5 us (11%)
  other arithmetic  56.8 us (6%)
  local copies, waits for them, and re-layouts  44.8 us (5%)
  between operations  15.4 us (2%)
    ppermute x14, waiting for transfers between devices, from_bit(): lax.ppermute(value, 'dp', [(i, i ^ bit) for i in range(lax.axis_size('dp'...  84.2 us
    pallas_call x1, Pallas kernels, attn_backward(): pl.pallas_call(functools.partial(attn_bwd_kernel, head=head, factor=head...  84.1 us
    dot_general x8, matrix products, matmul_tn(): lax.dot_general(left, right, (((0,), (0,)), ((), ())), preferred_element_...  65.9 us
    all_to_all x1, waiting for transfers between devices, body_paired(): lax.all_to_all(qkv_t, 'dp', split_axis=0, concat_axis=0, tiled=True)  63.9 us
    pallas_call x3, Pallas kernels, mlp_forward(): pl.pallas_call(functools.partial(mlp_kernel, kinds=kinds, transposed=tran...  62.8 us
    pallas_call x3, Pallas kernels, mlp_backward(): pl.pallas_call(functools.partial(mlp_back_kernel, kinds=kinds, transposed...  61.6 us
    all_to_all x4, waiting for transfers between devices, to_experts(): return lax.all_to_all(value, 'dp', split_axis=0, concat_axis=0, tiled=True)  51.3 us
    pallas_call x1, Pallas kernels, attn_forward(): pl.pallas_call(functools.partial(attn_fwd_kernel, head=head, factor=head...  47.8 us
  transfers between devices with their start and end apart: 53, of which 30 were waited for; matrix products, arithmetic and copies ran while one was open for 20% of the time, Pallas kernels for 26%

profile of v10, /device:TPU:9, one launch (start us, length us, event | category | flops | bytes accessed | tf_op | source)
XLA Modules:
  0.0 864.6 jit_solution(11823113426396908004)
XLA Ops:
  17.2 6.7 collective-permute-done.2
  23.9 7.0 collective-permute-done.3
  30.9 5.8 collective-permute-done.4
  42.3 6.7 collective-permute-done.5
  54.3 15.4 %collective-permute-done.6 = bf16[4,2,72,768]{3,2,0,1:T(8,128)(2,1)S(1)} collective-permute-done((bf16[4,2,72,768]{3,2,0,1:T(8,128)(2,1)S(1)}, bf16[4,2,72,768]{3,2,0,1:T(8,128)(2,1)S(1)}, u32[]{:S(2)}, u32[]{:S(2)}) %collective-permute-start.6) | collective-permute-done | bytes 884768 | tf_op jit(solution)/shard_map/ppermute | solution.py:774
  88.8 6.8 all-to-all-start
  99.5 63.9 %all-to-all-done = bf16[16,192,512]{2,1,0:T(8,128)(2,1)S(1)} async-done(((bf16[16,192,512]{2,1,0:T(8,128)(2,1)}), bf16[16,192,512]{2,1,0:T(8,128)(2,1)S(1)}, u32[]{:S(2)}, u32[]{:S(2)}) %all-to-all-start) | async-done | bytes 3145760 | tf_op jit(solution)/shard_map/all_to_all | solution.py:929
  164.9 3.8 collective-permute-start.10
  172.5 47.8 %attn_fwd.1 = (bf16[20,64,512]{2,1,0:T(8,128)(2,1)S(1)}, f32[20,1,512]{2,1,0:T(1,128)S(1)}) custom-call(s32[4,20]{1,0:T(4,128)S(1)} %add_select_fusion.2.plan, bf16[20,192,512]{2,1,0:T(8,128)(2,1)S(1)} %constant_dynamic-update-slice_fusion.own, bf16[16,128,512]{2,1,0:T(8,128)(2,1)S(1)} %broadcast_select_fusion.prompts), custom_call_target="tpu_custom_call" | custom-call | flops 26843545600 | bytes 8388608 | tf_op jit(solution)/shard_map/attn_fwd/pallas_call | solution.py:552
  221.8 9.6 %collective-permute-done.12 = bf16[4,64,512]{2,1,0:T(8,128)(2,1)S(1)} collective-permute-done((bf16[4,64,512]{2,1,0:T(8,128)(2,1)S(1)}, bf16[4,64,512]{2,1,0:T(8,128)(2,1)S(1)}, u32[]{:S(2)}, u32[]{:S(2)}) %collective-permute-start.12) | collective-permute-done | bytes 262176 | tf_op jit(solution)/shard_map/ppermute | solution.py:609
  232.4 7.7 all-to-all-start.1
  240.1 8.1 copy.131
  253.9 10.5 %all-to-all-done.1 = bf16[16,64,512]{2,1,0:T(8,128)(2,1)S(1)} async-done(((bf16[16,64,512]{2,1,0:T(8,128)(2,1)}), bf16[16,64,512]{2,1,0:T(8,128)(2,1)S(1)}, u32[]{:S(2)}, u32[]{:S(2)}) %all-to-all-start.1) | async-done | bytes 1048608 | tf_op jit(solution)/shard_map/all_to_all | solution.py:966
  276.3 17.3 %mlp_fwd.3 = (bf16[1024,1024]{1,0:T(8,128)(2,1)}, bf16[1024,2048]{1,0:T(8,128)(2,1)}, bf16[1024,2048]{1,0:T(8,128)(2,1)}, bf16[512,1024]{1,0:T(8,128)(2,1)}, bf16[512,1024]{1,0:T(8,128)(2,1)}) custom-call(bf16[512,1024]{1,0:T(8,128)(2,1)} %copy-done.15, bf16[512,1024]{1,0:T(8,128)(2,1)} %copy-done.33, bf16[1024,4608]{1,0:T(8,128)(2,1)} %bitcast.140, ...), custom_call_target="tpu_custom_call" | custom-call | flops 2147483648 | bytes 5242880 | tf_op jit(solution)/shard_map/mlp_fwd/pallas_call | solution.py:717
  296.7 3.8 convolution_convert_fusion.5
  300.5 4.8 all-to-all-start.2
  306.2 34.9 %all-to-all-done.2 = bf16[16,48,1024]{2,1,0:T(8,128)(2,1)} async-done(((bf16[16,48,1024]{2,1,0:T(8,128)(2,1)}), bf16[16,48,1024]{2,1,0:T(8,128)(2,1)}, u32[]{:S(2)}, u32[]{:S(2)}) %all-to-all-start.2) | async-done | bytes 1572896 | tf_op jit(solution)/shard_map/all_to_all | solution.py:52
  343.5 4.6 all-to-all-start.3
  348.1 22.0 %mlp_fwd.4 = (bf16[1536,1024]{1,0:T(8,128)(2,1)}, bf16[1536,2048]{1,0:T(8,128)(2,1)}, bf16[1536,2048]{1,0:T(8,128)(2,1)}, bf16[768,1024]{1,0:T(8,128)(2,1)}, bf1...) custom-call(bf16[768,1024]{1,0:T(8,128)(2,1)} %bitcast.31.refs_0_, bf16[768,1024]{1,0:T(8,128)(2,1)} %collective-permute-done.16.refs_1_, ...), custom_call_target="tpu_custom_call" | custom-call | flops 3221225472 | bytes 6815744 | tf_op jit(solution)/shard_map/mlp_fwd/pallas_call | solution.py:717
  377.4 23.5 %mlp_fwd.5 = (bf16[1536,1024]{1,0:T(8,128)(2,1)}, bf16[1536,2048]{1,0:T(8,128)(2,1)}, bf16[1536,2048]{1,0:T(8,128)(2,1)}, bf16[768,1024]{1,0:T(8,128)(2,1)}, bf16[768,1024]{1,0:T(8,128)(2,1)}) custom-call(bf16[1536,1024]{1,0:T(8,128)(2,1)} %get-tuple-element.121.refs_0_, bf16[768,1024]{1,0:T(8,128)(2,1)} %get-tuple-element.101.refs_1_, ...), custom_call_target="tpu_custom_call" | custom-call | flops 3221225472 | bytes 6815744 | tf_op jit(solution)/shard_map/mlp_fwd/pallas_call | solution.py:717
  404.8 21.5 %mlp_bwd.3 = (bf16[1536,1024]{1,0:T(8,128)(2,1)}, bf16[1536,2048]{1,0:T(8,128)(2,1)}, bf16[768,1024]{1,0:T(8,128)(2,1)}, bf16[768,1024]{1,0:T(8,128)(2,1)}) custom-call(f32[1536,1]{1,0:T(8,128)} %broadcast_select_fusion.9.refs_0_, bf16[768,1024]{1,0:T(8,128)(2,1)} %bitcast.36.refs_1_, bf16[768,1024]{1,0:T(8,128)(2,1)} %collective-permute-done.19.refs_2_, ...), custom_call_target="tpu_custom_call" | custom-call | flops 12884901888 | bytes 27262976 | tf_op jit(solution)/shard_map/mlp_bwd/pallas_call | solution.py:751
  432.2 6.7 all-to-all-start.4
  438.9 23.4 %mlp_bwd.4 = (bf16[1536,1024]{1,0:T(8,128)(2,1)}, bf16[1536,2048]{1,0:T(8,128)(2,1)}, bf16[768,1024]{1,0:T(8,128)(2,1)}, bf16[768,1024]{1,0:T(8,128)(2,1)}) custom-call(f32[1536,1]{1,0:T(8,128)} %broadcast_select_fusion.9.refs_0_, bf16[768,1024]{1,0:T(8,128)(2,1)} %bitcast.36.refs_1_, bf16[768,1024]{1,0:T(8,128)(2,1)} %collective-permute-done.19.refs_2_, ...), custom_call_target="tpu_custom_call" | custom-call | flops 12884901888 | bytes 27262976 | tf_op jit(solution)/shard_map/mlp_bwd/pallas_call | solution.py:751
  466.6 4.0 add_convert_fusion.1
  470.6 3.8 all-to-all-done.4
  474.4 5.7 all-to-all-start.5
  480.2 12.0 %fusion.58 = f32[1024,2048]{1,0:T(8,128)} fusion(bf16[1536,1024]{1,0:T(8,128)(2,1)} %get-tuple-element.121.refs_0_, bf16[1536,2048]{1,0:T(8,128)(2,1)} %get-tuple-element.122), kind=kOutput, calls=%fused_computation.206 | convolution fusion | flops 6442450944 | bytes 17825792 | tf_op jit(solution)/shard_map/dot_general | solution.py:60
  492.2 11.1 %fusion.57 = f32[2048,1024]{1,0:T(8,128)} fusion(bf16[1536,2048]{1,0:T(8,128)(2,1)} %get-tuple-element.119, bf16[1536,1024]{1,0:T(8,128)(2,1)S(1)} %copy-done.62), kind=kOutput, calls=%fused_computation.205 | convolution fusion | flops 6442450944 | bytes 17825792 | tf_op jit(solution)/shard_map/dot_general | solution.py:60
  503.2 12.5 %all-to-all-done.5 = bf16[16,48,1024]{2,1,0:T(8,128)(2,1)} async-done(((bf16[16,48,1024]{2,1,0:T(8,128)(2,1)}), bf16[16,48,1024]{2,1,0:T(8,128)(2,1)}, u32[]{:S(2)}, u32[]{:S(2)}) %all-to-all-start.5) | async-done | bytes 1572896 | tf_op jit(solution)/shard_map/all_to_all | solution.py:52
  524.6 16.6 %mlp_bwd.5 = (bf16[1024,1024]{1,0:T(8,128)(2,1)}, bf16[1024,2048]{1,0:T(8,128)(2,1)}, bf16[512,1024]{1,0:T(8,128)(2,1)}, bf16[512,1024]{1,0:T(8,128)(2,1)}) custom-call(bf16[512,1024]{1,0:T(8,128)(2,1)} %copy-done.58, bf16[512,1024]{1,0:T(8,128)(2,1)} %copy-done.59, bf16[1024,4608]{1,0:T(8,128)(2,1)} %bitcast.142, bf16[1024,4608]{1,0:T(8,128)(2,1)} %bitcast.143, ...), custom_call_target="tpu_custom_call" | custom-call | flops 8589934592 | bytes 20971520 | tf_op jit(solution)/shard_map/mlp_bwd/pallas_call | solution.py:751
  554.5 4.3 all-to-all-start.6
  559.0 7.5 convolution_convert_fusion.2
  566.6 4.9 convolution_convert_fusion.1
  573.6 5.2 pad_maximum_fusion
  578.8 8.0 copy.139
  593.6 84.1 %attn_bwd.1 = (bf16[20,192,512]{2,1,0:T(8,128)(2,1)}, bf16[16,128,512]{2,1,0:T(8,128)(2,1)S(1)}) custom-call(s32[4,20]{1,0:T(4,128)S(1)} %add_select_fusion.2.plan, bf16[20,192,512]{2,1,0:T(8,128)(2,1)} %copy-done, bf16[16,128,512]{2,1,0:T(8,128)(2,1)} %copy-done.1, bf16[20,64,512]{2,1,0:T(8,128)(2,1)S(1)} %pad_maximum_fusion.7.grad, ...), custom_call_target="tpu_custom_call" | custom-call | flops 67108864000 | bytes 16777216 | tf_op jit(solution)/shard_map/attn_bwd/pallas_call | solution.py:579
  677.6 5.1 collective-permute-start.28
  690.8 6.4 all-to-all-start.7
  697.6 12.0 %fusion.60 = f32[1024,2048]{1,0:T(8,128)} fusion(bf16[1536,1024]{1,0:T(8,128)(2,1)} %get-tuple-element.147, bf16[1536,2048]{1,0:T(8,128)(2,1)} %get-tuple-element.148), kind=kOutput, calls=%fused_computation.208 | convolution fusion | flops 6442450944 | bytes 17825792 | tf_op jit(solution)/shard_map/dot_general | solution.py:60
  709.6 11.1 %fusion.59 = f32[2048,1024]{1,0:T(8,128)} fusion(bf16[1536,2048]{1,0:T(8,128)(2,1)} %get-tuple-element.145, bf16[1536,1024]{1,0:T(8,128)(2,1)S(1)} %copy-done.63), kind=kOutput, calls=%fused_computation.207 | convolution fusion | flops 6442450944 | bytes 17825792 | tf_op jit(solution)/shard_map/dot_general | solution.py:60
  720.7 43.5 %all-to-all-done.7 = bf16[16,192,512]{2,1,0:T(8,128)(2,1)} async-done(((bf16[16,192,512]{2,1,0:T(8,128)(2,1)}), bf16[16,192,512]{2,1,0:T(8,128)(2,1)}, u32[]{:S(2)}, u32[]{:S(2)}) %all-to-all-start.7) | async-done | bytes 3145760 | tf_op jit(solution)/shard_map/all_to_all | solution.py:1165
  772.5 4.0 add_convert_fusion.4
  776.5 3.9 convolution_convert_fusion
  787.3 6.3 fusion.2
  794.7 8.2 collective-permute-done.34
  809.0 5.3 collective-permute-done.35
  821.3 11.7 %collective-permute-done.36 = bf16[64,1536]{1,0:T(8,128)(2,1)S(1)} collective-permute-done((bf16[64,1536]{1,0:T(8,128)(2,1)S(1)}, bf16[64,1536]{1,0:T(8,128)(2,1)S(1)}, u32[]{:S(2)}, u32[]{:S(2)}) %collective-permute-start.36) | collective-permute-done | bytes 196640 | tf_op jit(solution)/shard_map/ppermute | solution.py:774
  836.6 11.5 %collective-permute-done.38 = bf16[64,1536]{1,0:T(8,128)(2,1)S(1)} collective-permute-done((bf16[64,1536]{1,0:T(8,128)(2,1)S(1)}, bf16[64,1536]{1,0:T(8,128)(2,1)S(1)}, u32[]{:S(2)}, u32[]{:S(2)}) %collective-permute-start.38) | collective-permute-done | bytes 196640 | tf_op jit(solution)/shard_map/ppermute | solution.py:774
  (361 shorter events, 178.2 us)
Async XLA Ops:
  7.2 81.6 %all-gather.5.cloned.1.call-start = ((), (), s32[]{:S(2)}) async-start(), calls=%async_computation.12 | async-start | bytes 2949120 | tf_op jit(solution)/shard_map/all_gather | solution.py:900
  8.1 6.2 collective-permute-start.1
  14.5 9.4 %collective-permute-start.2 = (bf16[72,1536]{1,0:T(8,128)(2,1)S(1)}, bf16[72,1536]{1,0:T(8,128)(2,1)S(1)}, u32[]{:S(2)}, u32[]{:S(2)}) collective-permute-start(bf16[72,1536]{1,0:T(8,128)(2,1)S(1)} %fusion.23), channel_id=1, source_target_pairs={{0,8},{2,10},{4,12},{6,14},{8,0},{10,2},{12,4},{14,6},{16,24},{18,... | collective-permute-start | bytes 663560 | tf_op jit(solution)/shard_map/ppermute | solution.py:774
  14.5 16.4 %collective-permute-start.3 = (bf16[72,1536]{1,0:T(8,128)(2,1)S(1)}, bf16[72,1536]{1,0:T(8,128)(2,1)S(1)}, u32[]{:S(2)}, u32[]{:S(2)}) collective-permute-start(bf16[72,1536]{1,0:T(8,128)(2,1)S(1)} %fusion.23), channel_id=1, source_target_pairs={{0,16},{2,18},{4,20},{6,22},{8,24},{10,26},{12,28},{14,30},{16,0},... | collective-permute-start | bytes 663560 | tf_op jit(solution)/shard_map/ppermute | solution.py:774
  17.0 19.7 %collective-permute-start.4 = (bf16[72,1536]{1,0:T(8,128)(2,1)S(1)}, bf16[72,1536]{1,0:T(8,128)(2,1)S(1)}, u32[]{:S(2)}, u32[]{:S(2)}) collective-permute-start(bf16[72,1536]{1,0:T(8,128)(2,1)S(1)} %fusion.23), channel_id=1, source_target_pairs={{0,24},{2,26},{4,28},{6,30},{8,16},{10,18},{12,20},{14,22},{16,8},... | collective-permute-start | bytes 663560 | tf_op jit(solution)/shard_map/ppermute | solution.py:774
  38.1 10.9 %collective-permute-start.5 = (bf16[4,72,768]{2,1,0:T(8,128)(2,1)}, bf16[4,72,768]{2,1,0:T(8,128)(2,1)}, u32[]{:S(2)}, u32[]{:S(2)}) collective-permute-start(bf16[4,72,768]{2,1,0:T(8,128)(2,1)} %get-tuple-element.191), channel_id=1, source_target_pairs={{0,4},{2,6},{4,0},{6,2},{8,12},{10,14},{12,8},{14,10},{16,20},{18,... | collective-permute-start | bytes 1327112 | tf_op jit(solution)/shard_map/ppermute | solution.py:774
  39.3 12.3 %collective-permute-start.7 = (bf16[4,72,768]{2,1,0:T(8,128)(2,1)}, bf16[4,72,768]{2,1,0:T(8,128)(2,1)S(1)}, u32[]{:S(2)}, u32[]{:S(2)}) collective-permute-start(bf16[4,72,768]{2,1,0:T(8,128)(2,1)} %get-tuple-element.190), channel_id=1, source_target_pairs={{0,2},{2,0},{4,6},{6,4},{8,10},{10,8},{12,14},{14,12},{16,18},{18,... | collective-permute-start | bytes 1327112 | tf_op jit(solution)/shard_map/ppermute | solution.py:774
  40.5 12.7 %collective-permute-start = (bf16[512,1024]{1,0:T(8,128)(2,1)S(1)}, bf16[512,1024]{1,0:T(8,128)(2,1)S(1)}, u32[]{:S(2)}, u32[]{:S(2)}) collective-permute-start(bf16[512,1024]{1,0:T(8,128)(2,1)S(1)} %copy-done.3), channel_id=1, source_target_pairs={{0,1},{1,0},{2,3},{3,2},{4,5},{5,4},{6,7},{7,6},{8,9},{9,8},{10,11... | collective-permute-start | bytes 3145736 | tf_op jit(solution)/shard_map/ppermute | solution.py:605
  42.2 197.9 %all-gather.7.cloned.1.call-start = ((), (), s32[]{:S(2)}) async-start(), calls=%async_computation.13 | async-start | bytes 11796480 | tf_op jit(solution)/shard_map/all_gather | solution.py:932
  50.3 19.4 %collective-permute-start.6 = (bf16[4,2,72,768]{3,2,0,1:T(8,128)(2,1)S(1)}, bf16[4,2,72,768]{3,2,0,1:T(8,128)(2,1)S(1)}, u32[]{:S(2)}, u32[]{:S(2)}) collective-permute-start(bf16[4,2,72,768]{3,2,0,1:T(8,128)(2,1)S(1)} %maximum_select_fusion.3), channel_id=1, source_target_pairs={{0,2},{2,0},{4,6},{6,4},{8,10},{10,8},{12,14},{14,12},{16,18},{18,... | collective-permute-start | bytes 2654216 | tf_op jit(solution)/shard_map/ppermute | solution.py:774
  51.7 19.6 %collective-permute-start.8 = (bf16[4,2,72,768]{3,2,0,1:T(8,128)(2,1)S(1)}, bf16[4,2,72,768]{3,2,0,1:T(8,128)(2,1)S(1)}, u32[]{:S(2)}, u32[]{:S(2)}) collective-permute-start(bf16[4,2,72,768]{3,2,0,1:T(8,128)(2,1)S(1)} %maximum_select_fusion.4), channel_id=1, source_target_pairs={{0,4},{2,6},{4,0},{6,2},{8,12},{10,14},{12,8},{14,10},{16,20},{18,... | collective-permute-start | bytes 2654216 | tf_op jit(solution)/shard_map/ppermute | solution.py:774
  78.3 5.9 collective-permute-start.9
  88.8 74.5 %all-to-all-start = ((bf16[16,192,512]{2,1,0:T(8,128)(2,1)}), bf16[16,192,512]{2,1,0:T(8,128)(2,1)S(1)}, u32[]{:S(2)}, u32[]{:S(2)}) async-start(bf16[16,192,512]{2,1,0:T(8,128)(2,1)} %bitcast.147), calls=%async_computation | async-start | bytes 6291456 | tf_op jit(solution)/shard_map/all_to_all | solution.py:929
  163.5 7.2 collective-permute-start.11
  164.9 5.7 collective-permute-start.10
  220.4 10.9 %collective-permute-start.12 = (bf16[4,64,512]{2,1,0:T(8,128)(2,1)S(1)}, bf16[4,64,512]{2,1,0:T(8,128)(2,1)S(1)}, u32[]{:S(2)}, u32[]{:S(2)}) collective-permute-start(bf16[4,64,512]{2,1,0:T(8,128)(2,1)S(1)} %slice.198), channel_id=1, source_target_pairs={{0,1},{2,3},{4,5},{6,7},{8,9},{10,11},{12,13},{14,15},{16,17},{18,... | collective-permute-start | bytes 786440 | tf_op jit(solution)/shard_map/ppermute | solution.py:609
  232.4 32.0 %all-to-all-start.1 = ((bf16[16,64,512]{2,1,0:T(8,128)(2,1)}), bf16[16,64,512]{2,1,0:T(8,128)(2,1)S(1)}, u32[]{:S(2)}, u32[]{:S(2)}) async-start(bf16[16,64,512]{2,1,0:T(8,128)(2,1)} %pad_maximum_fusion.8), calls=%async_computation.1 | async-start | bytes 2097152 | tf_op jit(solution)/shard_map/all_to_all | solution.py:966
  250.6 16.3 %collective-permute-start.13 = (bf16[1024,512]{1,0:T(8,128)(2,1)}, bf16[1024,512]{1,0:T(8,128)(2,1)S(1)}, u32[]{:S(2)}, u32[]{:S(2)}) collective-permute-start(bf16[1024,512]{1,0:T(8,128)(2,1)} %slice.249), channel_id=1, source_target_pairs={{0,1},{1,0},{2,3},{3,2},{4,5},{5,4},{6,7},{7,6},{8,9},{9,8},{10,11... | collective-permute-start | bytes 3145736 | tf_op jit(solution)/shard_map/ppermute | solution.py:605
  270.7 4.6 collective-permute-start.14
  300.5 40.6 %all-to-all-start.2 = ((bf16[16,48,1024]{2,1,0:T(8,128)(2,1)}), bf16[16,48,1024]{2,1,0:T(8,128)(2,1)}, u32[]{:S(2)}, u32[]{:S(2)}) async-start(bf16[16,48,1024]{2,1,0:T(8,128)(2,1)} %bitcast.170), calls=%async_computation.2 | async-start | bytes 3145728 | tf_op jit(solution)/shard_map/all_to_all | solution.py:52
  341.1 7.0 collective-permute-start.16
  343.5 57.4 %all-to-all-start.3 = ((bf16[16,48,1024]{2,1,0:T(8,128)(2,1)}), bf16[16,48,1024]{2,1,0:T(8,128)(2,1)}, u32[]{:S(2)}, u32[]{:S(2)}) async-start(bf16[16,48,1024]{2,1,0:T(8,128)(2,1)} %bitcast.169), calls=%async_computation.3 | async-start | bytes 3145728 | tf_op jit(solution)/shard_map/all_to_all | solution.py:52
  370.2 3.9 collective-permute-start.17
  370.8 5.5 collective-permute-start.18
  400.9 3.8 collective-permute-start.19
  404.6 22.4 %collective-permute-start.23 = (bf16[768,1024]{1,0:T(8,128)(2,1)}, bf16[768,1024]{1,0:T(8,128)(2,1)S(1)}, u32[]{:S(2)}, u32[]{:S(2)}) collective-permute-start(bf16[768,1024]{1,0:T(8,128)(2,1)} %get-tuple-element.113), channel_id=1, source_target_pairs={{0,1},{1,0},{2,3},{3,2},{4,5},{5,4},{6,7},{7,6},{8,9},{9,8},{10,11... | collective-permute-start | bytes 4718600 | tf_op jit(solution)/shard_map/ppermute | solution.py:605
  426.3 12.6 %collective-permute-start.20 = (bf16[768,1024]{1,0:T(8,128)(2,1)}, bf16[768,1024]{1,0:T(8,128)(2,1)}, u32[]{:S(2)}, u32[]{:S(2)}) collective-permute-start(bf16[768,1024]{1,0:T(8,128)(2,1)} %get-tuple-element.108.refs_4_), channel_id=1, source_target_pairs={{0,1},{1,0},{2,3},{3,2},{4,5},{5,4},{6,7},{7,6},{8,9},{9,8},{10,11... | collective-permute-start | bytes 4718600 | tf_op jit(solution)/shard_map/ppermute | solution.py:605
  426.7 12.2 %collective-permute-start.21 = (bf16[768,1024]{1,0:T(8,128)(2,1)}, bf16[768,1024]{1,0:T(8,128)(2,1)}, u32[]{:S(2)}, u32[]{:S(2)}) collective-permute-start(bf16[768,1024]{1,0:T(8,128)(2,1)} %get-tuple-element.107.refs_3_), channel_id=1, source_target_pairs={{0,1},{1,0},{2,3},{3,2},{4,5},{5,4},{6,7},{7,6},{8,9},{9,8},{10,11... | collective-permute-start | bytes 4718600 | tf_op jit(solution)/shard_map/ppermute | solution.py:605
  432.2 42.3 %all-to-all-start.4 = ((bf16[16,48,1024]{2,1,0:T(8,128)(2,1)}), bf16[16,48,1024]{2,1,0:T(8,128)(2,1)}, u32[]{:S(2)}, u32[]{:S(2)}) async-start(bf16[16,48,1024]{2,1,0:T(8,128)(2,1)} %bitcast.150), calls=%async_computation.4 | async-start | bytes 3145728 | tf_op jit(solution)/shard_map/all_to_all | solution.py:52
  462.4 4.2 collective-permute-start.22
  474.4 41.3 %all-to-all-start.5 = ((bf16[16,48,1024]{2,1,0:T(8,128)(2,1)}), bf16[16,48,1024]{2,1,0:T(8,128)(2,1)}, u32[]{:S(2)}, u32[]{:S(2)}) async-start(bf16[16,48,1024]{2,1,0:T(8,128)(2,1)} %bitcast.149), calls=%async_computation.5 | async-start | bytes 3145728 | tf_op jit(solution)/shard_map/all_to_all | solution.py:52
  518.5 5.2 collective-permute-start.24
  554.1 17.4 %collective-permute-start.26 = (bf16[1024,512]{1,0:T(8,128)(2,1)}, bf16[1024,512]{1,0:T(8,128)(2,1)}, u32[]{:S(2)}, u32[]{:S(2)}) collective-permute-start(bf16[1024,512]{1,0:T(8,128)(2,1)} %convolution_convert_fusion.7), channel_id=1, source_target_pairs={{0,1},{1,0},{2,3},{3,2},{4,5},{5,4},{6,7},{7,6},{8,9},{9,8},{10,11... | collective-permute-start | bytes 3145736 | tf_op jit(solution)/shard_map/ppermute | solution.py:605
  554.5 32.3 %all-to-all-start.6 = ((bf16[16,64,512]{2,1,0:T(8,128)(2,1)}), bf16[16,64,512]{2,1,0:T(8,128)(2,1)}, u32[]{:S(2)}, u32[]{:S(2)}) async-start(bf16[16,64,512]{2,1,0:T(8,128)(2,1)} %bitcast.155), calls=%async_computation.6 | async-start | bytes 2097152 | tf_op jit(solution)/shard_map/all_to_all | solution.py:1119
  558.8 228.5 %reduce-scatter.3.cloned.1.call-start = ((), (), s32[]{:S(2)}) async-start(), calls=%async_computation.10 | async-start | bytes 11796480 | tf_op jit(solution)/shard_map/reduce_scatter | solution.py:1134
  677.6 9.9 %collective-permute-start.28 = (bf16[16,128,512]{2,1,0:T(8,128)(2,1)S(1)}, bf16[16,128,512]{2,1,0:T(8,128)(2,1)S(1)}, u32[]{:S(2)}, u32[]{:S(2)}) collective-permute-start(bf16[16,128,512]{2,1,0:T(8,128)(2,1)S(1)} %get-tuple-element.139), channel_id=1, source_target_pairs={{1,0},{3,2},{5,4},{7,6},{9,8},{11,10},{13,12},{15,14},{17,16},{19,... | collective-permute-start | bytes 6291464 | tf_op jit(solution)/shard_map/ppermute | solution.py:613
  684.0 4.5 collective-permute-start.29
  690.8 73.4 %all-to-all-start.7 = ((bf16[16,192,512]{2,1,0:T(8,128)(2,1)}), bf16[16,192,512]{2,1,0:T(8,128)(2,1)}, u32[]{:S(2)}, u32[]{:S(2)}) async-start(bf16[16,192,512]{2,1,0:T(8,128)(2,1)} %maximum_select_fusion), calls=%async_computation.7 | async-start | bytes 6291456 | tf_op jit(solution)/shard_map/all_to_all | solution.py:1165
  697.2 154.6 %reduce-scatter.5.cloned.1.call-start = ((), (), s32[]{:S(2)}) async-start(), calls=%async_computation.11 | async-start | bytes 2949120 | tf_op jit(solution)/shard_map/reduce_scatter | solution.py:1141
  766.3 10.2 %collective-permute-start.30 = (bf16[1536,512]{1,0:T(8,128)(2,1)S(1)}, bf16[1536,512]{1,0:T(8,128)(2,1)S(1)}, u32[]{:S(2)}, u32[]{:S(2)}) collective-permute-start(bf16[1536,512]{1,0:T(8,128)(2,1)S(1)} %bitcast.173), channel_id=1, source_target_pairs={{0,1},{1,0},{2,3},{3,2},{4,5},{5,4},{6,7},{7,6},{8,9},{9,8},{10,11... | collective-permute-start | bytes 4718600 | tf_op jit(solution)/shard_map/ppermute | solution.py:605
  781.5 21.4 %collective-permute-start.34 = (bf16[4,2,64,768]{3,2,0,1:T(8,128)(2,1)}, bf16[4,2,64,768]{3,2,0,1:T(8,128)(2,1)}, u32[]{:S(2)}, u32[]{:S(2)}) collective-permute-start(bf16[4,2,64,768]{3,2,0,1:T(8,128)(2,1)} %select_bitcast_fusion), channel_id=1, source_target_pairs={{0,4},{2,6},{4,0},{6,2},{8,12},{10,14},{12,8},{14,10},{16,20},{18,... | collective-permute-start | bytes 2359304 | tf_op jit(solution)/shard_map/ppermute | solution.py:774
  786.1 19.6 %collective-permute-start.32 = (bf16[4,2,64,768]{3,2,0,1:T(8,128)(2,1)}, bf16[4,2,64,768]{3,2,0,1:T(8,128)(2,1)}, u32[]{:S(2)}, u32[]{:S(2)}) collective-permute-start(bf16[4,2,64,768]{3,2,0,1:T(8,128)(2,1)} %select_bitcast_fusion.1), channel_id=1, source_target_pairs={{0,2},{2,0},{4,6},{6,4},{8,10},{10,8},{12,14},{14,12},{16,18},{18,... | collective-permute-start | bytes 2359304 | tf_op jit(solution)/shard_map/ppermute | solution.py:774
  793.7 14.6 %collective-permute-start.31 = (bf16[512,1024]{1,0:T(8,128)(2,1)S(1)}, bf16[512,1024]{1,0:T(8,128)(2,1)S(1)}, u32[]{:S(2)}, u32[]{:S(2)}) collective-permute-start(bf16[512,1024]{1,0:T(8,128)(2,1)S(1)} %slice.335), channel_id=1, source_target_pairs={{0,1},{1,0},{2,3},{3,2},{4,5},{5,4},{6,7},{7,6},{8,9},{9,8},{10,11... | collective-permute-start | bytes 3145736 | tf_op jit(solution)/shard_map/ppermute | solution.py:605
  804.4 9.9 %collective-permute-start.35 = (bf16[4,64,768]{2,1,0:T(8,128)(2,1)S(1)}, bf16[4,64,768]{2,1,0:T(8,128)(2,1)S(1)}, u32[]{:S(2)}, u32[]{:S(2)}) collective-permute-start(bf16[4,64,768]{2,1,0:T(8,128)(2,1)S(1)} %select_bitcast_fusion.2), channel_id=1, source_target_pairs={{0,2},{2,0},{4,6},{6,4},{8,10},{10,8},{12,14},{14,12},{16,18},{18,... | collective-permute-start | bytes 1179656 | tf_op jit(solution)/shard_map/ppermute | solution.py:774
  807.1 9.6 %collective-permute-start.33 = (bf16[4,64,768]{2,1,0:T(8,128)(2,1)S(1)}, bf16[4,64,768]{2,1,0:T(8,128)(2,1)S(1)}, u32[]{:S(2)}, u32[]{:S(2)}) collective-permute-start(bf16[4,64,768]{2,1,0:T(8,128)(2,1)S(1)} %select_bitcast_fusion.3), channel_id=1, source_target_pairs={{0,4},{2,6},{4,0},{6,2},{8,12},{10,14},{12,8},{14,10},{16,20},{18,... | collective-permute-start | bytes 1179656 | tf_op jit(solution)/shard_map/ppermute | solution.py:774
  817.0 16.0 %collective-permute-start.36 = (bf16[64,1536]{1,0:T(8,128)(2,1)S(1)}, bf16[64,1536]{1,0:T(8,128)(2,1)S(1)}, u32[]{:S(2)}, u32[]{:S(2)}) collective-permute-start(bf16[64,1536]{1,0:T(8,128)(2,1)S(1)} %get-tuple-element.196), channel_id=1, source_target_pairs={{0,8},{2,10},{4,12},{6,14},{8,0},{10,2},{12,4},{14,6},{16,24},{18,... | collective-permute-start | bytes 589832 | tf_op jit(solution)/shard_map/ppermute | solution.py:774
  817.1 19.5 %collective-permute-start.37 = (bf16[64,1536]{1,0:T(8,128)(2,1)S(1)}, bf16[64,1536]{1,0:T(8,128)(2,1)S(1)}, u32[]{:S(2)}, u32[]{:S(2)}) collective-permute-start(bf16[64,1536]{1,0:T(8,128)(2,1)S(1)} %get-tuple-element.197), channel_id=1, source_target_pairs={{0,16},{2,18},{4,20},{6,22},{8,24},{10,26},{12,28},{14,30},{16,0},... | collective-permute-start | bytes 589832 | tf_op jit(solution)/shard_map/ppermute | solution.py:774
  819.1 28.9 %collective-permute-start.38 = (bf16[64,1536]{1,0:T(8,128)(2,1)S(1)}, bf16[64,1536]{1,0:T(8,128)(2,1)S(1)}, u32[]{:S(2)}, u32[]{:S(2)}) collective-permute-start(bf16[64,1536]{1,0:T(8,128)(2,1)S(1)} %get-tuple-element.198), channel_id=1, source_target_pairs={{0,24},{2,26},{4,28},{6,30},{8,16},{10,18},{12,20},{14,22},{16,8},... | collective-permute-start | bytes 589832 | tf_op jit(solution)/shard_map/ppermute | solution.py:774
  (70 other events, 621.9 us)
Sparse Core Ops, SparseCore 0:
  42.4 46.3 all-gather.4
  90.6 126.8 all-gather.6
  591.7 95.3 reduce-scatter.2
  787.4 51.9 reduce-scatter.4

commit v11 on v10

--- a/solution.py
+++ b/solution.py
@@ -819,17 +819,28 @@
     return keep.astype(F32) + from_bit(send, partner).astype(F32)
 
 
-def scatter_chips(first, second):
-    planes = first.shape[0]
+def line_parts(line):
+    z = chip_place()[0]
+    return [
+        from_bit(lax.dynamic_index_in_dim(line, z ^ k, 0, keepdims=False), 4 * k)
+        for k in range(1, line.shape[0])
+    ]
+
+
+def line_sum(line, parts):
+    total = lax.dynamic_index_in_dim(line, chip_place()[0], 0, keepdims=False).astype(F32)
+    for part in parts:
+        total = total + part.astype(F32)
+    return total
+
+
+def scatter_chips(first, second, before):
     z, y, x = chip_place()
     first = halve(first, x, 2, 1).astype(BF16)
     second = halve(second, y, 1, 2).astype(BF16)
     line = jnp.concatenate([halve(first, y, 1, 2), halve(second, x, 1, 1)], -1).astype(BF16)
-    total = lax.dynamic_index_in_dim(line, z, 0, keepdims=False).astype(F32)
-    for k in range(1, planes):
-        part = lax.dynamic_index_in_dim(line, z ^ k, 0, keepdims=False)
-        total = total + from_bit(part, 4 * k).astype(F32)
-    return total
+    line, before = lax.optimization_barrier((line, before))
+    return line_sum(line, line_parts(line)), before
 
 
 def fits_paired(mesh):
@@ -1138,13 +1149,6 @@
         axis_index_groups=[[4 * z + k for k in range(4)] for z in range(planes)],
         tiled=True,
     )
-    second_sum = lax.psum_scatter(
-        second_plane,
-        "dp",
-        scatter_dimension=0,
-        axis_index_groups=[[4 * z + k for z in range(planes)] for k in range(4)],
-        tiled=True,
-    ).astype(F32)
     grad_blocks = jnp.concatenate([grad_by_head, to_core_zero(grad_by_head[:lent])], 0)
     grad_own_blocks, grad_prompts = attn_backward(
         plan, own_blocks, prompt_kv, grad_blocks, attn_blocks, log_sums
@@ -1165,7 +1169,10 @@
     grad_qkv = lax.all_to_all(grad_head, "dp", split_axis=0, concat_axis=0, tiled=True)
     grad_out_b = matmul_tn(act_b, grad_b)
     grad_in_b = matmul_tn(middle, grad_pre_b)
-    grad_qkv, grad_out_b, grad_in_b = lax.optimization_barrier((grad_qkv, grad_out_b, grad_in_b))
+    grad_qkv, grad_out_b, grad_in_b, second_plane = lax.optimization_barrier(
+        (grad_qkv, grad_out_b, grad_in_b, second_plane.reshape(planes, shard, -1))
+    )
+    second_parts = line_parts(second_plane)
     grad_qkv = grad_qkv.reshape(2, half_heads * triple, rows)
     keep_half, send_half = both(grad_qkv[0], grad_qkv[1])
     grad_qkv_t = jnp.concatenate([keep_half, swap(send_half)], 1)
@@ -1174,7 +1181,10 @@
     ).astype(BF16)
     by_chip = grad_qkv_w.reshape(experts // 4, 2, 2, shard, half_heads * triple)
     half_columns = half_heads * triple // 2
-    qkv_sum = scatter_chips(by_chip[..., :half_columns], by_chip[..., half_columns:])
+    qkv_sum, second_parts = scatter_chips(
+        by_chip[..., :half_columns], by_chip[..., half_columns:], second_parts
+    )
+    second_sum = line_sum(second_plane, second_parts)
     grad_norm_one = keep_rows(
         lax.dot_general(
             grad_qkv_t, qkv_full, (((0,), (1,)), ((), ())), preferred_element_type=F32

time: 874 us -> 875 us (level)
    transpose x2 -> x0, local copies, waits for them, and re-layouts: 8.86 us -> none  [the longest x1 8.03 us: body_paired(): second_part.reshape(planes, 4, shard, -1).transpose(1, 0, 2, 3)]
    ppermute x14 -> x17, starting transfers between devices: 17.5 us -> 21.3 us  [from_bit(): lax.ppermute(value, 'dp', [(i, i ^ bit) for i in range(lax.axis_size('dp'...]
    ppermute x14 -> x17, waiting for transfers between devices: 84.2 us -> 86 us  [from_bit(): lax.ppermute(value, 'dp', [(i, i ^ bit) for i in range(lax.axis_size('dp'...]
  transfers between devices with their start and end apart: 53 -> 55, of which waited for: 30 -> 33; matrix products, arithmetic and copies ran while one was open for 20% -> 18% of each run, Pallas kernels for 26% -> 26%
where the time goes in v11:
time: 875 us; the launch traced here: 865 us
  waiting for transfers between devices  291 us (33%)
  Pallas kernels  257 us (29%)
  starting transfers between devices  109 us (12%)
  matrix products  96.6 us (11%)
  other arithmetic  51.1 us (6%)
  local copies, waits for them, and re-layouts  44.7 us (5%)
  between operations  15.4 us (2%)
    ppermute x17, waiting for transfers between devices, from_bit(): lax.ppermute(value, 'dp', [(i, i ^ bit) for i in range(lax.axis_size('dp'...  86 us
    pallas_call x1, Pallas kernels, attn_backward(): pl.pallas_call(functools.partial(attn_bwd_kernel, head=head, factor=head...  84.8 us
    dot_general x8, matrix products, matmul_tn(): lax.dot_general(left, right, (((0,), (0,)), ((), ())), preferred_element_...  65.9 us
    all_to_all x1, waiting for transfers between devices, body_paired(): lax.all_to_all(qkv_t, 'dp', split_axis=0, concat_axis=0, tiled=True)  63.9 us
    pallas_call x3, Pallas kernels, mlp_forward(): pl.pallas_call(functools.partial(mlp_kernel, kinds=kinds, transposed=tran...  62.8 us
    pallas_call x3, Pallas kernels, mlp_backward(): pl.pallas_call(functools.partial(mlp_back_kernel, kinds=kinds, transposed...  61.5 us
    all_to_all x4, waiting for transfers between devices, to_experts(): return lax.all_to_all(value, 'dp', split_axis=0, concat_axis=0, tiled=True)  51.2 us
    pallas_call x1, Pallas kernels, attn_forward(): pl.pallas_call(functools.partial(attn_fwd_kernel, head=head, factor=head...  47.8 us
  transfers between devices with their start and end apart: 55, of which 33 were waited for; matrix products, arithmetic and copies ran while one was open for 18% of the time, Pallas kernels for 26%

profile of v11, /device:TPU:9, one launch (start us, length us, event | category | flops | bytes accessed | tf_op | source)
XLA Modules:
  0.0 864.6 jit_solution(9747081665479822431)
XLA Ops:
  17.2 6.7 collective-permute-done.2
  23.9 7.0 collective-permute-done.3
  30.9 5.8 collective-permute-done.4
  42.3 6.7 collective-permute-done.5
  54.3 15.4 %collective-permute-done.6 = bf16[4,2,72,768]{3,2,0,1:T(8,128)(2,1)S(1)} collective-permute-done((bf16[4,2,72,768]{3,2,0,1:T(8,128)(2,1)S(1)}, bf16[4,2,72,768]{3,2,0,1:T(8,128)(2,1)S(1)}, u32[]{:S(2)}, u32[]{:S(2)}) %collective-permute-start.6) | collective-permute-done | bytes 884768 | tf_op jit(solution)/shard_map/ppermute | solution.py:774
  88.8 6.8 all-to-all-start
  99.4 63.9 %all-to-all-done = bf16[16,192,512]{2,1,0:T(8,128)(2,1)S(1)} async-done(((bf16[16,192,512]{2,1,0:T(8,128)(2,1)}), bf16[16,192,512]{2,1,0:T(8,128)(2,1)S(1)}, u32[]{:S(2)}, u32[]{:S(2)}) %all-to-all-start) | async-done | bytes 3145760 | tf_op jit(solution)/shard_map/all_to_all | solution.py:940
  164.9 3.8 collective-permute-start.10
  172.5 47.8 %attn_fwd.1 = (bf16[20,64,512]{2,1,0:T(8,128)(2,1)S(1)}, f32[20,1,512]{2,1,0:T(1,128)S(1)}) custom-call(s32[4,20]{1,0:T(4,128)S(1)} %add_select_fusion.2.plan, bf16[20,192,512]{2,1,0:T(8,128)(2,1)S(1)} %constant_dynamic-update-slice_fusion.own, bf16[16,128,512]{2,1,0:T(8,128)(2,1)S(1)} %broadcast_select_fusion.prompts), custom_call_target="tpu_custom_call" | custom-call | flops 26843545600 | bytes 8388608 | tf_op jit(solution)/shard_map/attn_fwd/pallas_call | solution.py:552
  221.7 9.6 %collective-permute-done.12 = bf16[4,64,512]{2,1,0:T(8,128)(2,1)S(1)} collective-permute-done((bf16[4,64,512]{2,1,0:T(8,128)(2,1)S(1)}, bf16[4,64,512]{2,1,0:T(8,128)(2,1)S(1)}, u32[]{:S(2)}, u32[]{:S(2)}) %collective-permute-start.12) | collective-permute-done | bytes 262176 | tf_op jit(solution)/shard_map/ppermute | solution.py:609
  232.4 7.7 all-to-all-start.1
  240.1 8.2 copy.130
  254.0 10.4 %all-to-all-done.1 = bf16[16,64,512]{2,1,0:T(8,128)(2,1)S(1)} async-done(((bf16[16,64,512]{2,1,0:T(8,128)(2,1)}), bf16[16,64,512]{2,1,0:T(8,128)(2,1)S(1)}, u32[]{:S(2)}, u32[]{:S(2)}) %all-to-all-start.1) | async-done | bytes 1048608 | tf_op jit(solution)/shard_map/all_to_all | solution.py:977
  276.3 17.3 %mlp_fwd.3 = (bf16[1024,1024]{1,0:T(8,128)(2,1)}, bf16[1024,2048]{1,0:T(8,128)(2,1)}, bf16[1024,2048]{1,0:T(8,128)(2,1)}, bf16[512,1024]{1,0:T(8,128)(2,1)}, bf16[512,1024]{1,0:T(8,128)(2,1)}) custom-call(bf16[512,1024]{1,0:T(8,128)(2,1)} %copy-done.15, bf16[512,1024]{1,0:T(8,128)(2,1)} %copy-done.35, bf16[1024,4608]{1,0:T(8,128)(2,1)} %bitcast.148, ...), custom_call_target="tpu_custom_call" | custom-call | flops 2147483648 | bytes 5242880 | tf_op jit(solution)/shard_map/mlp_fwd/pallas_call | solution.py:717
  296.7 3.8 convolution_convert_fusion.5
  300.5 4.8 all-to-all-start.2
  306.2 34.9 %all-to-all-done.2 = bf16[16,48,1024]{2,1,0:T(8,128)(2,1)} async-done(((bf16[16,48,1024]{2,1,0:T(8,128)(2,1)}), bf16[16,48,1024]{2,1,0:T(8,128)(2,1)}, u32[]{:S(2)}, u32[]{:S(2)}) %all-to-all-start.2) | async-done | bytes 1572896 | tf_op jit(solution)/shard_map/all_to_all | solution.py:52
  343.5 4.6 all-to-all-start.3
  348.1 22.0 %mlp_fwd.4 = (bf16[1536,1024]{1,0:T(8,128)(2,1)}, bf16[1536,2048]{1,0:T(8,128)(2,1)}, bf16[1536,2048]{1,0:T(8,128)(2,1)}, bf16[768,1024]{1,0:T(8,128)(2,1)}, bf1...) custom-call(bf16[768,1024]{1,0:T(8,128)(2,1)} %bitcast.31.refs_0_, bf16[768,1024]{1,0:T(8,128)(2,1)} %collective-permute-done.16.refs_1_, ...), custom_call_target="tpu_custom_call" | custom-call | flops 3221225472 | bytes 6815744 | tf_op jit(solution)/shard_map/mlp_fwd/pallas_call | solution.py:717
  377.5 23.5 %mlp_fwd.5 = (bf16[1536,1024]{1,0:T(8,128)(2,1)}, bf16[1536,2048]{1,0:T(8,128)(2,1)}, bf16[1536,2048]{1,0:T(8,128)(2,1)}, bf16[768,1024]{1,0:T(8,128)(2,1)}, bf16[768,1024]{1,0:T(8,128)(2,1)}) custom-call(bf16[1536,1024]{1,0:T(8,128)(2,1)} %get-tuple-element.126.refs_0_, bf16[768,1024]{1,0:T(8,128)(2,1)} %get-tuple-element.106.refs_1_, ...), custom_call_target="tpu_custom_call" | custom-call | flops 3221225472 | bytes 6815744 | tf_op jit(solution)/shard_map/mlp_fwd/pallas_call | solution.py:717
  404.8 21.4 %mlp_bwd.3 = (bf16[1536,1024]{1,0:T(8,128)(2,1)}, bf16[1536,2048]{1,0:T(8,128)(2,1)}, bf16[768,1024]{1,0:T(8,128)(2,1)}, bf16[768,1024]{1,0:T(8,128)(2,1)}) custom-call(f32[1536,1]{1,0:T(8,128)} %broadcast_select_fusion.9.refs_0_, bf16[768,1024]{1,0:T(8,128)(2,1)} %bitcast.36.refs_1_, bf16[768,1024]{1,0:T(8,128)(2,1)} %collective-permute-done.19.refs_2_, ...), custom_call_target="tpu_custom_call" | custom-call | flops 12884901888 | bytes 27262976 | tf_op jit(solution)/shard_map/mlp_bwd/pallas_call | solution.py:751
  432.1 6.7 all-to-all-start.4
  438.9 23.5 %mlp_bwd.4 = (bf16[1536,1024]{1,0:T(8,128)(2,1)}, bf16[1536,2048]{1,0:T(8,128)(2,1)}, bf16[768,1024]{1,0:T(8,128)(2,1)}, bf16[768,1024]{1,0:T(8,128)(2,1)}) custom-call(f32[1536,1]{1,0:T(8,128)} %broadcast_select_fusion.9.refs_0_, bf16[768,1024]{1,0:T(8,128)(2,1)} %bitcast.36.refs_1_, bf16[768,1024]{1,0:T(8,128)(2,1)} %collective-permute-done.19.refs_2_, ...), custom_call_target="tpu_custom_call" | custom-call | flops 12884901888 | bytes 27262976 | tf_op jit(solution)/shard_map/mlp_bwd/pallas_call | solution.py:751
  466.6 4.0 add_convert_fusion.1
  470.6 3.8 all-to-all-done.4
  474.4 5.7 all-to-all-start.5
  480.1 12.0 %fusion.52 = f32[1024,2048]{1,0:T(8,128)} fusion(bf16[1536,1024]{1,0:T(8,128)(2,1)} %get-tuple-element.126.refs_0_, bf16[1536,2048]{1,0:T(8,128)(2,1)} %get-tuple-element.127), kind=kOutput, calls=%fused_computation.200 | convolution fusion | flops 6442450944 | bytes 17825792 | tf_op jit(solution)/shard_map/dot_general | solution.py:60
  492.1 11.1 %fusion.51 = f32[2048,1024]{1,0:T(8,128)} fusion(bf16[1536,2048]{1,0:T(8,128)(2,1)} %get-tuple-element.124, bf16[1536,1024]{1,0:T(8,128)(2,1)S(1)} %copy-done.63), kind=kOutput, calls=%fused_computation.199 | convolution fusion | flops 6442450944 | bytes 17825792 | tf_op jit(solution)/shard_map/dot_general | solution.py:60
  503.2 12.5 %all-to-all-done.5 = bf16[16,48,1024]{2,1,0:T(8,128)(2,1)} async-done(((bf16[16,48,1024]{2,1,0:T(8,128)(2,1)}), bf16[16,48,1024]{2,1,0:T(8,128)(2,1)}, u32[]{:S(2)}, u32[]{:S(2)}) %all-to-all-start.5) | async-done | bytes 1572896 | tf_op jit(solution)/shard_map/all_to_all | solution.py:52
  524.6 16.6 %mlp_bwd.5 = (bf16[1024,1024]{1,0:T(8,128)(2,1)}, bf16[1024,2048]{1,0:T(8,128)(2,1)}, bf16[512,1024]{1,0:T(8,128)(2,1)}, bf16[512,1024]{1,0:T(8,128)(2,1)}) custom-call(bf16[512,1024]{1,0:T(8,128)(2,1)} %copy-done.59, bf16[512,1024]{1,0:T(8,128)(2,1)} %copy-done.60, bf16[1024,4608]{1,0:T(8,128)(2,1)} %bitcast.150, bf16[1024,4608]{1,0:T(8,128)(2,1)} %bitcast.151, ...), custom_call_target="tpu_custom_call" | custom-call | flops 8589934592 | bytes 20971520 | tf_op jit(solution)/shard_map/mlp_bwd/pallas_call | solution.py:751
  554.4 4.2 all-to-all-start.6
  558.9 7.5 convolution_convert_fusion.2
  566.5 4.9 convolution_convert_fusion.1
  573.5 5.3 pad_maximum_fusion
  578.8 8.2 copy.138
  592.7 84.8 %attn_bwd.1 = (bf16[20,192,512]{2,1,0:T(8,128)(2,1)}, bf16[16,128,512]{2,1,0:T(8,128)(2,1)S(1)}) custom-call(s32[4,20]{1,0:T(4,128)S(1)} %add_select_fusion.2.plan, bf16[20,192,512]{2,1,0:T(8,128)(2,1)} %copy-done, bf16[16,128,512]{2,1,0:T(8,128)(2,1)} %copy-done.1, bf16[20,64,512]{2,1,0:T(8,128)(2,1)S(1)} %pad_maximum_fusion.7.grad, ...), custom_call_target="tpu_custom_call" | custom-call | flops 67108864000 | bytes 16777216 | tf_op jit(solution)/shard_map/attn_bwd/pallas_call | solution.py:579
  677.5 5.1 collective-permute-start.28
  690.7 6.9 all-to-all-start.7
  697.6 12.0 %fusion.54 = f32[1024,2048]{1,0:T(8,128)} fusion(bf16[1536,1024]{1,0:T(8,128)(2,1)} %get-tuple-element.152, bf16[1536,2048]{1,0:T(8,128)(2,1)} %get-tuple-element.153), kind=kOutput, calls=%fused_computation.202 | convolution fusion | flops 6442450944 | bytes 17825792 | tf_op jit(solution)/shard_map/dot_general | solution.py:60
  709.6 11.1 %fusion.53 = f32[2048,1024]{1,0:T(8,128)} fusion(bf16[1536,2048]{1,0:T(8,128)(2,1)} %get-tuple-element.150, bf16[1536,1024]{1,0:T(8,128)(2,1)S(1)} %copy-done.64), kind=kOutput, calls=%fused_computation.201 | convolution fusion | flops 6442450944 | bytes 17825792 | tf_op jit(solution)/shard_map/dot_general | solution.py:60
  720.6 43.8 %all-to-all-done.7 = bf16[16,192,512]{2,1,0:T(8,128)(2,1)} async-done(((bf16[16,192,512]{2,1,0:T(8,128)(2,1)}), bf16[16,192,512]{2,1,0:T(8,128)(2,1)}, u32[]{:S(2)}, u32[]{:S(2)}) %all-to-all-start.7) | async-done | bytes 3145760 | tf_op jit(solution)/shard_map/all_to_all | solution.py:1169
  772.9 4.0 add_convert_fusion.4
  777.1 4.3 collective-permute-start.37
  781.3 3.9 convolution_convert_fusion
  792.4 11.5 %collective-permute-done.32 = bf16[4,2,64,768]{3,2,0,1:T(8,128)(2,1)S(1)} collective-permute-done((bf16[4,2,64,768]{3,2,0,1:T(8,128)(2,1)S(1)}, bf16[4,2,64,768]{3,2,0,1:T(8,128)(2,1)S(1)}, u32[]{:S(2)}, u32[]{:S(2)}) %collective-permute-start.32) | collective-permute-done | bytes 786464 | tf_op jit(solution)/shard_map/ppermute | solution.py:774
  818.7 12.8 %collective-permute-done.38 = bf16[64,4608]{1,0:T(8,128)(2,1)S(1)} collective-permute-done((bf16[64,4608]{1,0:T(8,128)(2,1)S(1)}, bf16[64,4608]{1,0:T(8,128)(2,1)S(1)}, u32[]{:S(2)}, u32[]{:S(2)}) %collective-permute-start.38) | collective-permute-done | bytes 589856 | tf_op jit(solution)/shard_map/ppermute | solution.py:774
  836.8 9.7 %collective-permute-done.40 = bf16[64,1536]{1,0:T(8,128)(2,1)S(1)} collective-permute-done((bf16[64,1536]{1,0:T(8,128)(2,1)S(1)}, bf16[64,1536]{1,0:T(8,128)(2,1)S(1)}, u32[]{:S(2)}, u32[]{:S(2)}) %collective-permute-start.40) | collective-permute-done | bytes 196640 | tf_op jit(solution)/shard_map/ppermute | solution.py:774
  846.5 4.4 collective-permute-done.41
  (367 shorter events, 176.6 us)
Async XLA Ops:
  7.2 81.6 %all-gather.5.cloned.1.call-start = ((), (), s32[]{:S(2)}) async-start(), calls=%async_computation.10 | async-start | bytes 2949120 | tf_op jit(solution)/shard_map/all_gather | solution.py:911
  8.1 6.2 collective-permute-start.1
  14.5 9.4 %collective-permute-start.2 = (bf16[72,1536]{1,0:T(8,128)(2,1)S(1)}, bf16[72,1536]{1,0:T(8,128)(2,1)S(1)}, u32[]{:S(2)}, u32[]{:S(2)}) collective-permute-start(bf16[72,1536]{1,0:T(8,128)(2,1)S(1)} %fusion.25), channel_id=1, source_target_pairs={{0,8},{2,10},{4,12},{6,14},{8,0},{10,2},{12,4},{14,6},{16,24},{18,... | collective-permute-start | bytes 663560 | tf_op jit(solution)/shard_map/ppermute | solution.py:774
  14.5 16.4 %collective-permute-start.3 = (bf16[72,1536]{1,0:T(8,128)(2,1)S(1)}, bf16[72,1536]{1,0:T(8,128)(2,1)S(1)}, u32[]{:S(2)}, u32[]{:S(2)}) collective-permute-start(bf16[72,1536]{1,0:T(8,128)(2,1)S(1)} %fusion.25), channel_id=1, source_target_pairs={{0,16},{2,18},{4,20},{6,22},{8,24},{10,26},{12,28},{14,30},{16,0},... | collective-permute-start | bytes 663560 | tf_op jit(solution)/shard_map/ppermute | solution.py:774
  17.0 19.7 %collective-permute-start.4 = (bf16[72,1536]{1,0:T(8,128)(2,1)S(1)}, bf16[72,1536]{1,0:T(8,128)(2,1)S(1)}, u32[]{:S(2)}, u32[]{:S(2)}) collective-permute-start(bf16[72,1536]{1,0:T(8,128)(2,1)S(1)} %fusion.25), channel_id=1, source_target_pairs={{0,24},{2,26},{4,28},{6,30},{8,16},{10,18},{12,20},{14,22},{16,8},... | collective-permute-start | bytes 663560 | tf_op jit(solution)/shard_map/ppermute | solution.py:774
  38.1 10.9 %collective-permute-start.5 = (bf16[4,72,768]{2,1,0:T(8,128)(2,1)}, bf16[4,72,768]{2,1,0:T(8,128)(2,1)}, u32[]{:S(2)}, u32[]{:S(2)}) collective-permute-start(bf16[4,72,768]{2,1,0:T(8,128)(2,1)} %get-tuple-element.205), channel_id=1, source_target_pairs={{0,4},{2,6},{4,0},{6,2},{8,12},{10,14},{12,8},{14,10},{16,20},{18,... | collective-permute-start | bytes 1327112 | tf_op jit(solution)/shard_map/ppermute | solution.py:774
  39.3 12.3 %collective-permute-start.7 = (bf16[4,72,768]{2,1,0:T(8,128)(2,1)}, bf16[4,72,768]{2,1,0:T(8,128)(2,1)S(1)}, u32[]{:S(2)}, u32[]{:S(2)}) collective-permute-start(bf16[4,72,768]{2,1,0:T(8,128)(2,1)} %get-tuple-element.204), channel_id=1, source_target_pairs={{0,2},{2,0},{4,6},{6,4},{8,10},{10,8},{12,14},{14,12},{16,18},{18,... | collective-permute-start | bytes 1327112 | tf_op jit(solution)/shard_map/ppermute | solution.py:774
  40.5 12.7 %collective-permute-start = (bf16[512,1024]{1,0:T(8,128)(2,1)S(1)}, bf16[512,1024]{1,0:T(8,128)(2,1)S(1)}, u32[]{:S(2)}, u32[]{:S(2)}) collective-permute-start(bf16[512,1024]{1,0:T(8,128)(2,1)S(1)} %copy-done.3), channel_id=1, source_target_pairs={{0,1},{1,0},{2,3},{3,2},{4,5},{5,4},{6,7},{7,6},{8,9},{9,8},{10,11... | collective-permute-start | bytes 3145736 | tf_op jit(solution)/shard_map/ppermute | solution.py:605
  42.2 197.9 %all-gather.7.cloned.1.call-start = ((), (), s32[]{:S(2)}) async-start(), calls=%async_computation.11 | async-start | bytes 11796480 | tf_op jit(solution)/shard_map/all_gather | solution.py:943
  50.3 19.3 %collective-permute-start.6 = (bf16[4,2,72,768]{3,2,0,1:T(8,128)(2,1)S(1)}, bf16[4,2,72,768]{3,2,0,1:T(8,128)(2,1)S(1)}, u32[]{:S(2)}, u32[]{:S(2)}) collective-permute-start(bf16[4,2,72,768]{3,2,0,1:T(8,128)(2,1)S(1)} %maximum_select_fusion.3), channel_id=1, source_target_pairs={{0,2},{2,0},{4,6},{6,4},{8,10},{10,8},{12,14},{14,12},{16,18},{18,... | collective-permute-start | bytes 2654216 | tf_op jit(solution)/shard_map/ppermute | solution.py:774
  51.7 19.5 %collective-permute-start.8 = (bf16[4,2,72,768]{3,2,0,1:T(8,128)(2,1)S(1)}, bf16[4,2,72,768]{3,2,0,1:T(8,128)(2,1)S(1)}, u32[]{:S(2)}, u32[]{:S(2)}) collective-permute-start(bf16[4,2,72,768]{3,2,0,1:T(8,128)(2,1)S(1)} %maximum_select_fusion.4), channel_id=1, source_target_pairs={{0,4},{2,6},{4,0},{6,2},{8,12},{10,14},{12,8},{14,10},{16,20},{18,... | collective-permute-start | bytes 2654216 | tf_op jit(solution)/shard_map/ppermute | solution.py:774
  78.2 5.9 collective-permute-start.9
  88.8 74.5 %all-to-all-start = ((bf16[16,192,512]{2,1,0:T(8,128)(2,1)}), bf16[16,192,512]{2,1,0:T(8,128)(2,1)S(1)}, u32[]{:S(2)}, u32[]{:S(2)}) async-start(bf16[16,192,512]{2,1,0:T(8,128)(2,1)} %bitcast.155), calls=%async_computation | async-start | bytes 6291456 | tf_op jit(solution)/shard_map/all_to_all | solution.py:940
  163.5 7.2 collective-permute-start.11
  164.9 5.7 collective-permute-start.10
  220.4 10.9 %collective-permute-start.12 = (bf16[4,64,512]{2,1,0:T(8,128)(2,1)S(1)}, bf16[4,64,512]{2,1,0:T(8,128)(2,1)S(1)}, u32[]{:S(2)}, u32[]{:S(2)}) collective-permute-start(bf16[4,64,512]{2,1,0:T(8,128)(2,1)S(1)} %slice.198), channel_id=1, source_target_pairs={{0,1},{2,3},{4,5},{6,7},{8,9},{10,11},{12,13},{14,15},{16,17},{18,... | collective-permute-start | bytes 786440 | tf_op jit(solution)/shard_map/ppermute | solution.py:609
  232.4 32.0 %all-to-all-start.1 = ((bf16[16,64,512]{2,1,0:T(8,128)(2,1)}), bf16[16,64,512]{2,1,0:T(8,128)(2,1)S(1)}, u32[]{:S(2)}, u32[]{:S(2)}) async-start(bf16[16,64,512]{2,1,0:T(8,128)(2,1)} %pad_maximum_fusion.8), calls=%async_computation.1 | async-start | bytes 2097152 | tf_op jit(solution)/shard_map/all_to_all | solution.py:977
  250.8 16.2 %collective-permute-start.13 = (bf16[1024,512]{1,0:T(8,128)(2,1)}, bf16[1024,512]{1,0:T(8,128)(2,1)S(1)}, u32[]{:S(2)}, u32[]{:S(2)}) collective-permute-start(bf16[1024,512]{1,0:T(8,128)(2,1)} %slice.249), channel_id=1, source_target_pairs={{0,1},{1,0},{2,3},{3,2},{4,5},{5,4},{6,7},{7,6},{8,9},{9,8},{10,11... | collective-permute-start | bytes 3145736 | tf_op jit(solution)/shard_map/ppermute | solution.py:605
  270.7 4.6 collective-permute-start.14
  300.5 40.6 %all-to-all-start.2 = ((bf16[16,48,1024]{2,1,0:T(8,128)(2,1)}), bf16[16,48,1024]{2,1,0:T(8,128)(2,1)}, u32[]{:S(2)}, u32[]{:S(2)}) async-start(bf16[16,48,1024]{2,1,0:T(8,128)(2,1)} %bitcast.180), calls=%async_computation.2 | async-start | bytes 3145728 | tf_op jit(solution)/shard_map/all_to_all | solution.py:52
  341.1 7.0 collective-permute-start.16
  343.5 57.4 %all-to-all-start.3 = ((bf16[16,48,1024]{2,1,0:T(8,128)(2,1)}), bf16[16,48,1024]{2,1,0:T(8,128)(2,1)}, u32[]{:S(2)}, u32[]{:S(2)}) async-start(bf16[16,48,1024]{2,1,0:T(8,128)(2,1)} %bitcast.179), calls=%async_computation.3 | async-start | bytes 3145728 | tf_op jit(solution)/shard_map/all_to_all | solution.py:52
  370.8 5.5 collective-permute-start.18
  404.6 22.3 %collective-permute-start.23 = (bf16[768,1024]{1,0:T(8,128)(2,1)}, bf16[768,1024]{1,0:T(8,128)(2,1)S(1)}, u32[]{:S(2)}, u32[]{:S(2)}) collective-permute-start(bf16[768,1024]{1,0:T(8,128)(2,1)} %get-tuple-element.118), channel_id=1, source_target_pairs={{0,1},{1,0},{2,3},{3,2},{4,5},{5,4},{6,7},{7,6},{8,9},{9,8},{10,11... | collective-permute-start | bytes 4718600 | tf_op jit(solution)/shard_map/ppermute | solution.py:605
  426.2 12.6 %collective-permute-start.20 = (bf16[768,1024]{1,0:T(8,128)(2,1)}, bf16[768,1024]{1,0:T(8,128)(2,1)}, u32[]{:S(2)}, u32[]{:S(2)}) collective-permute-start(bf16[768,1024]{1,0:T(8,128)(2,1)} %get-tuple-element.113.refs_4_), channel_id=1, source_target_pairs={{0,1},{1,0},{2,3},{3,2},{4,5},{5,4},{6,7},{7,6},{8,9},{9,8},{10,11... | collective-permute-start | bytes 4718600 | tf_op jit(solution)/shard_map/ppermute | solution.py:605
  426.6 12.2 %collective-permute-start.21 = (bf16[768,1024]{1,0:T(8,128)(2,1)}, bf16[768,1024]{1,0:T(8,128)(2,1)}, u32[]{:S(2)}, u32[]{:S(2)}) collective-permute-start(bf16[768,1024]{1,0:T(8,128)(2,1)} %get-tuple-element.112.refs_3_), channel_id=1, source_target_pairs={{0,1},{1,0},{2,3},{3,2},{4,5},{5,4},{6,7},{7,6},{8,9},{9,8},{10,11... | collective-permute-start | bytes 4718600 | tf_op jit(solution)/shard_map/ppermute | solution.py:605
  432.1 42.3 %all-to-all-start.4 = ((bf16[16,48,1024]{2,1,0:T(8,128)(2,1)}), bf16[16,48,1024]{2,1,0:T(8,128)(2,1)}, u32[]{:S(2)}, u32[]{:S(2)}) async-start(bf16[16,48,1024]{2,1,0:T(8,128)(2,1)} %bitcast.158), calls=%async_computation.4 | async-start | bytes 3145728 | tf_op jit(solution)/shard_map/all_to_all | solution.py:52
  462.3 4.2 collective-permute-start.22
  474.4 41.3 %all-to-all-start.5 = ((bf16[16,48,1024]{2,1,0:T(8,128)(2,1)}), bf16[16,48,1024]{2,1,0:T(8,128)(2,1)}, u32[]{:S(2)}, u32[]{:S(2)}) async-start(bf16[16,48,1024]{2,1,0:T(8,128)(2,1)} %bitcast.157), calls=%async_computation.5 | async-start | bytes 3145728 | tf_op jit(solution)/shard_map/all_to_all | solution.py:52
  518.4 5.2 collective-permute-start.24
  554.1 17.4 %collective-permute-start.26 = (bf16[1024,512]{1,0:T(8,128)(2,1)}, bf16[1024,512]{1,0:T(8,128)(2,1)}, u32[]{:S(2)}, u32[]{:S(2)}) collective-permute-start(bf16[1024,512]{1,0:T(8,128)(2,1)} %convolution_convert_fusion.7), channel_id=1, source_target_pairs={{0,1},{1,0},{2,3},{3,2},{4,5},{5,4},{6,7},{7,6},{8,9},{9,8},{10,11... | collective-permute-start | bytes 3145736 | tf_op jit(solution)/shard_map/ppermute | solution.py:605
  554.4 32.5 %all-to-all-start.6 = ((bf16[16,64,512]{2,1,0:T(8,128)(2,1)}), bf16[16,64,512]{2,1,0:T(8,128)(2,1)}, u32[]{:S(2)}, u32[]{:S(2)}) async-start(bf16[16,64,512]{2,1,0:T(8,128)(2,1)} %bitcast.163), calls=%async_computation.6 | async-start | bytes 2097152 | tf_op jit(solution)/shard_map/all_to_all | solution.py:1130
  558.7 205.8 %reduce-scatter.2.cloned.1.call-start = ((), (), s32[]{:S(2)}) async-start(), calls=%async_computation.9 | async-start | bytes 11796480 | tf_op jit(solution)/shard_map/reduce_scatter | solution.py:1145
  677.5 9.8 %collective-permute-start.28 = (bf16[16,128,512]{2,1,0:T(8,128)(2,1)S(1)}, bf16[16,128,512]{2,1,0:T(8,128)(2,1)S(1)}, u32[]{:S(2)}, u32[]{:S(2)}) collective-permute-start(bf16[16,128,512]{2,1,0:T(8,128)(2,1)S(1)} %get-tuple-element.144), channel_id=1, source_target_pairs={{1,0},{3,2},{5,4},{7,6},{9,8},{11,10},{13,12},{15,14},{17,16},{19,... | collective-permute-start | bytes 6291464 | tf_op jit(solution)/shard_map/ppermute | solution.py:613
  683.8 4.5 collective-permute-start.29
  690.7 73.8 %all-to-all-start.7 = ((bf16[16,192,512]{2,1,0:T(8,128)(2,1)}), bf16[16,192,512]{2,1,0:T(8,128)(2,1)}, u32[]{:S(2)}, u32[]{:S(2)}) async-start(bf16[16,192,512]{2,1,0:T(8,128)(2,1)} %maximum_select_fusion), calls=%async_computation.7 | async-start | bytes 6291456 | tf_op jit(solution)/shard_map/all_to_all | solution.py:1169
  766.6 14.7 %collective-permute-start.30 = (bf16[1536,512]{1,0:T(8,128)(2,1)S(1)}, bf16[1536,512]{1,0:T(8,128)(2,1)S(1)}, u32[]{:S(2)}, u32[]{:S(2)}) collective-permute-start(bf16[1536,512]{1,0:T(8,128)(2,1)S(1)} %bitcast.183), channel_id=1, source_target_pairs={{0,1},{1,0},{2,3},{3,2},{4,5},{5,4},{6,7},{7,6},{8,9},{9,8},{10,11... | collective-permute-start | bytes 4718600 | tf_op jit(solution)/shard_map/ppermute | solution.py:605
  777.0 41.2 %collective-permute-start.36 = (bf16[64,4608]{1,0:T(8,128)(2,1)S(1)}, bf16[64,4608]{1,0:T(8,128)(2,1)S(1)}, u32[]{:S(2)}, u32[]{:S(2)}) collective-permute-start(bf16[64,4608]{1,0:T(8,128)(2,1)S(1)} %get-tuple-element.194), channel_id=1, source_target_pairs={{0,8},{2,10},{4,12},{6,14},{8,0},{10,2},{12,4},{14,6},{16,24},{18,... | collective-permute-start | bytes 1769480 | tf_op jit(solution)/shard_map/ppermute | solution.py:774
  777.1 41.7 %collective-permute-start.37 = (bf16[64,4608]{1,0:T(8,128)(2,1)S(1)}, bf16[64,4608]{1,0:T(8,128)(2,1)S(1)}, u32[]{:S(2)}, u32[]{:S(2)}) collective-permute-start(bf16[64,4608]{1,0:T(8,128)(2,1)S(1)} %get-tuple-element.193), channel_id=1, source_target_pairs={{0,16},{2,18},{4,20},{6,22},{8,24},{10,26},{12,28},{14,30},{16,0},... | collective-permute-start | bytes 1769480 | tf_op jit(solution)/shard_map/ppermute | solution.py:774
  781.3 50.2 %collective-permute-start.38 = (bf16[64,4608]{1,0:T(8,128)(2,1)S(1)}, bf16[64,4608]{1,0:T(8,128)(2,1)S(1)}, u32[]{:S(2)}, u32[]{:S(2)}) collective-permute-start(bf16[64,4608]{1,0:T(8,128)(2,1)S(1)} %get-tuple-element.192), channel_id=1, source_target_pairs={{0,24},{2,26},{4,28},{6,30},{8,16},{10,18},{12,20},{14,22},{16,8},... | collective-permute-start | bytes 1769480 | tf_op jit(solution)/shard_map/ppermute | solution.py:774
  785.6 18.2 %collective-permute-start.32 = (bf16[4,2,64,768]{3,2,0,1:T(8,128)(2,1)S(1)}, bf16[4,2,64,768]{3,2,0,1:T(8,128)(2,1)S(1)}, u32[]{:S(2)}, u32[]{:S(2)}) collective-permute-start(bf16[4,2,64,768]{3,2,0,1:T(8,128)(2,1)S(1)} %select_bitcast_fusion.1), channel_id=1, source_target_pairs={{0,2},{2,0},{4,6},{6,4},{8,10},{10,8},{12,14},{14,12},{16,18},{18,... | collective-permute-start | bytes 2359304 | tf_op jit(solution)/shard_map/ppermute | solution.py:774
  786.7 19.4 %collective-permute-start.34 = (bf16[4,2,64,768]{3,2,0,1:T(8,128)(2,1)S(1)}, bf16[4,2,64,768]{3,2,0,1:T(8,128)(2,1)S(1)}, u32[]{:S(2)}, u32[]{:S(2)}) collective-permute-start(bf16[4,2,64,768]{3,2,0,1:T(8,128)(2,1)S(1)} %select_bitcast_fusion), channel_id=1, source_target_pairs={{0,4},{2,6},{4,0},{6,2},{8,12},{10,14},{12,8},{14,10},{16,20},{18,... | collective-permute-start | bytes 2359304 | tf_op jit(solution)/shard_map/ppermute | solution.py:774
  803.8 4.5 collective-permute-start.31
  806.1 10.3 %collective-permute-start.33 = (bf16[4,64,768]{2,1,0:T(8,128)(2,1)S(1)}, bf16[4,64,768]{2,1,0:T(8,128)(2,1)S(1)}, u32[]{:S(2)}, u32[]{:S(2)}) collective-permute-start(bf16[4,64,768]{2,1,0:T(8,128)(2,1)S(1)} %select_bitcast_fusion.3), channel_id=1, source_target_pairs={{0,4},{2,6},{4,0},{6,2},{8,12},{10,14},{12,8},{14,10},{16,20},{18,... | collective-permute-start | bytes 1179656 | tf_op jit(solution)/shard_map/ppermute | solution.py:774
  808.3 9.7 %collective-permute-start.35 = (bf16[4,64,768]{2,1,0:T(8,128)(2,1)S(1)}, bf16[4,64,768]{2,1,0:T(8,128)(2,1)S(1)}, u32[]{:S(2)}, u32[]{:S(2)}) collective-permute-start(bf16[4,64,768]{2,1,0:T(8,128)(2,1)S(1)} %select_bitcast_fusion.2), channel_id=1, source_target_pairs={{0,2},{2,0},{4,6},{6,4},{8,10},{10,8},{12,14},{14,12},{16,18},{18,... | collective-permute-start | bytes 1179656 | tf_op jit(solution)/shard_map/ppermute | solution.py:774
  831.6 5.2 collective-permute-start.39
  831.7 14.8 %collective-permute-start.40 = (bf16[64,1536]{1,0:T(8,128)(2,1)S(1)}, bf16[64,1536]{1,0:T(8,128)(2,1)S(1)}, u32[]{:S(2)}, u32[]{:S(2)}) collective-permute-start(bf16[64,1536]{1,0:T(8,128)(2,1)S(1)} %get-tuple-element.212), channel_id=1, source_target_pairs={{0,16},{2,18},{4,20},{6,22},{8,24},{10,26},{12,28},{14,30},{16,0},... | collective-permute-start | bytes 589832 | tf_op jit(solution)/shard_map/ppermute | solution.py:774
  834.8 16.0 %collective-permute-start.41 = (bf16[64,1536]{1,0:T(8,128)(2,1)S(1)}, bf16[64,1536]{1,0:T(8,128)(2,1)S(1)}, u32[]{:S(2)}, u32[]{:S(2)}) collective-permute-start(bf16[64,1536]{1,0:T(8,128)(2,1)S(1)} %get-tuple-element.211), channel_id=1, source_target_pairs={{0,24},{2,26},{4,28},{6,30},{8,16},{10,18},{12,20},{14,22},{16,8},... | collective-permute-start | bytes 589832 | tf_op jit(solution)/shard_map/ppermute | solution.py:774
  (73 other events, 524.3 us)
Sparse Core Ops, SparseCore 0:
  42.4 46.3 all-gather.4
  90.6 126.8 all-gather.6
  587.1 95.4 reduce-scatter.1

commit v12 on v10

--- a/solution.py
+++ b/solution.py
@@ -986,7 +986,7 @@
         second_all,
         second_all,
         hidden,
-        rows,
+        rows // 2,
         transposed=True,
         columns=(0, 1),
     )
@@ -1090,7 +1090,7 @@
         second_all,
         second_all,
         ffn_slope,
-        rows,
+        rows // 2,
         transposed=False,
         columns=(0, 1),
     )

time: 874 us -> 874 us (level)
  no operation moved by 1% of the time
where the time goes in v12:
time: 874 us; the launch traced here: 864 us
  waiting for transfers between devices  289 us (33%)
  Pallas kernels  255 us (29%)
  starting transfers between devices  104 us (12%)
  matrix products  99.7 us (11%)
  other arithmetic  57.2 us (7%)
  local copies, waits for them, and re-layouts  44.9 us (5%)
  between operations  15.4 us (2%)
    ppermute x14, waiting for transfers between devices, from_bit(): lax.ppermute(value, 'dp', [(i, i ^ bit) for i in range(lax.axis_size('dp'...  84.2 us
    pallas_call x1, Pallas kernels, attn_backward(): pl.pallas_call(functools.partial(attn_bwd_kernel, head=head, factor=head...  84.1 us
    dot_general x8, matrix products, matmul_tn(): lax.dot_general(left, right, (((0,), (0,)), ((), ())), preferred_element_...  66.1 us
    all_to_all x1, waiting for transfers between devices, body_paired(): lax.all_to_all(qkv_t, 'dp', split_axis=0, concat_axis=0, tiled=True)  63.9 us
    pallas_call x3, Pallas kernels, mlp_forward(): pl.pallas_call(functools.partial(mlp_kernel, kinds=kinds, transposed=tran...  62.6 us
    pallas_call x3, Pallas kernels, mlp_backward(): pl.pallas_call(functools.partial(mlp_back_kernel, kinds=kinds, transposed...  60.4 us
    all_to_all x4, waiting for transfers between devices, to_experts(): return lax.all_to_all(value, 'dp', split_axis=0, concat_axis=0, tiled=True)  51.3 us
    pallas_call x1, Pallas kernels, attn_forward(): pl.pallas_call(functools.partial(attn_fwd_kernel, head=head, factor=head...  47.7 us
  transfers between devices with their start and end apart: 53, of which 30 were waited for; matrix products, arithmetic and copies ran while one was open for 20% of the time, Pallas kernels for 26%

profile of v12, /device:TPU:9, one launch (start us, length us, event | category | flops | bytes accessed | tf_op | source)
XLA Modules:
  0.0 864.4 jit_solution(15868424100246349217)
XLA Ops:
  17.2 6.7 collective-permute-done.2
  23.9 7.0 collective-permute-done.3
  30.9 5.8 collective-permute-done.4
  42.3 6.7 collective-permute-done.5
  54.3 15.4 %collective-permute-done.6 = bf16[4,2,72,768]{3,2,0,1:T(8,128)(2,1)S(1)} collective-permute-done((bf16[4,2,72,768]{3,2,0,1:T(8,128)(2,1)S(1)}, bf16[4,2,72,768]{3,2,0,1:T(8,128)(2,1)S(1)}, u32[]{:S(2)}, u32[]{:S(2)}) %collective-permute-start.6) | collective-permute-done | bytes 884768 | tf_op jit(solution)/shard_map/ppermute | solution.py:774
  88.8 6.5 all-to-all-start
  99.3 63.9 %all-to-all-done = bf16[16,192,512]{2,1,0:T(8,128)(2,1)S(1)} async-done(((bf16[16,192,512]{2,1,0:T(8,128)(2,1)}), bf16[16,192,512]{2,1,0:T(8,128)(2,1)S(1)}, u32[]{:S(2)}, u32[]{:S(2)}) %all-to-all-start) | async-done | bytes 3145760 | tf_op jit(solution)/shard_map/all_to_all | solution.py:929
  164.7 3.8 collective-permute-start.10
  172.3 47.7 %attn_fwd.1 = (bf16[20,64,512]{2,1,0:T(8,128)(2,1)S(1)}, f32[20,1,512]{2,1,0:T(1,128)S(1)}) custom-call(s32[4,20]{1,0:T(4,128)S(1)} %add_select_fusion.2.plan, bf16[20,192,512]{2,1,0:T(8,128)(2,1)S(1)} %constant_dynamic-update-slice_fusion.own, bf16[16,128,512]{2,1,0:T(8,128)(2,1)S(1)} %broadcast_select_fusion.prompts), custom_call_target="tpu_custom_call" | custom-call | flops 26843545600 | bytes 8388608 | tf_op jit(solution)/shard_map/attn_fwd/pallas_call | solution.py:552
  221.5 9.6 %collective-permute-done.12 = bf16[4,64,512]{2,1,0:T(8,128)(2,1)S(1)} collective-permute-done((bf16[4,64,512]{2,1,0:T(8,128)(2,1)S(1)}, bf16[4,64,512]{2,1,0:T(8,128)(2,1)S(1)}, u32[]{:S(2)}, u32[]{:S(2)}) %collective-permute-start.12) | collective-permute-done | bytes 262176 | tf_op jit(solution)/shard_map/ppermute | solution.py:609
  232.2 7.8 all-to-all-start.1
  239.9 8.1 copy.131
  253.7 10.5 %all-to-all-done.1 = bf16[16,64,512]{2,1,0:T(8,128)(2,1)S(1)} async-done(((bf16[16,64,512]{2,1,0:T(8,128)(2,1)}), bf16[16,64,512]{2,1,0:T(8,128)(2,1)S(1)}, u32[]{:S(2)}, u32[]{:S(2)}) %all-to-all-start.1) | async-done | bytes 1048608 | tf_op jit(solution)/shard_map/all_to_all | solution.py:966
  276.1 17.3 %mlp_fwd.3 = (bf16[1024,1024]{1,0:T(8,128)(2,1)}, bf16[1024,2048]{1,0:T(8,128)(2,1)}, bf16[1024,2048]{1,0:T(8,128)(2,1)}, bf16[512,1024]{1,0:T(8,128)(2,1)}, bf16[512,1024]{1,0:T(8,128)(2,1)}) custom-call(bf16[512,1024]{1,0:T(8,128)(2,1)} %copy-done.15, bf16[512,1024]{1,0:T(8,128)(2,1)} %copy-done.33, bf16[1024,4608]{1,0:T(8,128)(2,1)} %bitcast.140, ...), custom_call_target="tpu_custom_call" | custom-call | flops 2147483648 | bytes 5242880 | tf_op jit(solution)/shard_map/mlp_fwd/pallas_call | solution.py:717
  296.5 3.8 convolution_convert_fusion.5
  300.3 4.8 all-to-all-start.2
  306.0 34.9 %all-to-all-done.2 = bf16[16,48,1024]{2,1,0:T(8,128)(2,1)} async-done(((bf16[16,48,1024]{2,1,0:T(8,128)(2,1)}), bf16[16,48,1024]{2,1,0:T(8,128)(2,1)}, u32[]{:S(2)}, u32[]{:S(2)}) %all-to-all-start.2) | async-done | bytes 1572896 | tf_op jit(solution)/shard_map/all_to_all | solution.py:52
  343.3 5.2 all-to-all-start.3
  348.5 22.0 %mlp_fwd.4 = (bf16[1536,1024]{1,0:T(8,128)(2,1)}, bf16[1536,2048]{1,0:T(8,128)(2,1)}, bf16[1536,2048]{1,0:T(8,128)(2,1)}, bf16[768,1024]{1,0:T(8,128)(2,1)}, bf1...) custom-call(bf16[768,1024]{1,0:T(8,128)(2,1)} %bitcast.31.refs_0_, bf16[768,1024]{1,0:T(8,128)(2,1)} %collective-permute-done.16.refs_1_, ...), custom_call_target="tpu_custom_call" | custom-call | flops 3221225472 | bytes 6815744 | tf_op jit(solution)/shard_map/mlp_fwd/pallas_call | solution.py:717
  377.8 23.3 %mlp_fwd.5 = (bf16[1536,1024]{1,0:T(8,128)(2,1)}, bf16[1536,2048]{1,0:T(8,128)(2,1)}, bf16[1536,2048]{1,0:T(8,128)(2,1)}, bf16[768,1024]{1,0:T(8,128)(2,1)}, bf16[768,1024]{1,0:T(8,128)(2,1)}) custom-call(bf16[1536,1024]{1,0:T(8,128)(2,1)} %get-tuple-element.121.refs_0_, bf16[768,1024]{1,0:T(8,128)(2,1)} %get-tuple-element.101.refs_1_, ...), custom_call_target="tpu_custom_call" | custom-call | flops 3221225472 | bytes 6815744 | tf_op jit(solution)/shard_map/mlp_fwd/pallas_call | solution.py:717
  404.9 21.6 %mlp_bwd.3 = (bf16[1536,1024]{1,0:T(8,128)(2,1)}, bf16[1536,2048]{1,0:T(8,128)(2,1)}, bf16[768,1024]{1,0:T(8,128)(2,1)}, bf16[768,1024]{1,0:T(8,128)(2,1)}) custom-call(f32[1536,1]{1,0:T(8,128)} %broadcast_select_fusion.9.refs_0_, bf16[768,1024]{1,0:T(8,128)(2,1)} %bitcast.36.refs_1_, bf16[768,1024]{1,0:T(8,128)(2,1)} %collective-permute-done.19.refs_2_, ...), custom_call_target="tpu_custom_call" | custom-call | flops 12884901888 | bytes 27262976 | tf_op jit(solution)/shard_map/mlp_bwd/pallas_call | solution.py:751
  432.4 6.8 all-to-all-start.4
  439.2 23.4 %mlp_bwd.4 = (bf16[1536,1024]{1,0:T(8,128)(2,1)}, bf16[1536,2048]{1,0:T(8,128)(2,1)}, bf16[768,1024]{1,0:T(8,128)(2,1)}, bf16[768,1024]{1,0:T(8,128)(2,1)}) custom-call(f32[1536,1]{1,0:T(8,128)} %broadcast_select_fusion.9.refs_0_, bf16[768,1024]{1,0:T(8,128)(2,1)} %bitcast.36.refs_1_, bf16[768,1024]{1,0:T(8,128)(2,1)} %collective-permute-done.19.refs_2_, ...), custom_call_target="tpu_custom_call" | custom-call | flops 12884901888 | bytes 27262976 | tf_op jit(solution)/shard_map/mlp_bwd/pallas_call | solution.py:751
  466.9 4.0 add_convert_fusion.1
  470.9 3.8 all-to-all-done.4
  474.7 5.9 all-to-all-start.5
  480.7 12.0 %fusion.58 = f32[1024,2048]{1,0:T(8,128)} fusion(bf16[1536,1024]{1,0:T(8,128)(2,1)} %get-tuple-element.121.refs_0_, bf16[1536,2048]{1,0:T(8,128)(2,1)} %get-tuple-element.122), kind=kOutput, calls=%fused_computation.206 | convolution fusion | flops 6442450944 | bytes 17825792 | tf_op jit(solution)/shard_map/dot_general | solution.py:60
  492.6 11.1 %fusion.57 = f32[2048,1024]{1,0:T(8,128)} fusion(bf16[1536,2048]{1,0:T(8,128)(2,1)} %get-tuple-element.119, bf16[1536,1024]{1,0:T(8,128)(2,1)S(1)} %copy-done.62), kind=kOutput, calls=%fused_computation.205 | convolution fusion | flops 6442450944 | bytes 17825792 | tf_op jit(solution)/shard_map/dot_general | solution.py:60
  503.7 12.5 %all-to-all-done.5 = bf16[16,48,1024]{2,1,0:T(8,128)(2,1)} async-done(((bf16[16,48,1024]{2,1,0:T(8,128)(2,1)}), bf16[16,48,1024]{2,1,0:T(8,128)(2,1)}, u32[]{:S(2)}, u32[]{:S(2)}) %all-to-all-start.5) | async-done | bytes 1572896 | tf_op jit(solution)/shard_map/all_to_all | solution.py:52
  525.1 15.4 %mlp_bwd.5 = (bf16[1024,1024]{1,0:T(8,128)(2,1)}, bf16[1024,2048]{1,0:T(8,128)(2,1)}, bf16[512,1024]{1,0:T(8,128)(2,1)}, bf16[512,1024]{1,0:T(8,128)(2,1)}) custom-call(bf16[512,1024]{1,0:T(8,128)(2,1)} %copy-done.58, bf16[512,1024]{1,0:T(8,128)(2,1)} %copy-done.59, bf16[1024,4608]{1,0:T(8,128)(2,1)} %bitcast.142, bf16[1024,4608]{1,0:T(8,128)(2,1)} %bitcast.143, ...), custom_call_target="tpu_custom_call" | custom-call | flops 8589934592 | bytes 20971520 | tf_op jit(solution)/shard_map/mlp_bwd/pallas_call | solution.py:751
  553.9 4.3 all-to-all-start.6
  558.2 7.5 convolution_convert_fusion.2
  565.8 5.1 convolution_convert_fusion.1
  573.0 5.2 pad_maximum_fusion
  578.2 8.0 copy.139
  593.0 84.1 %attn_bwd.1 = (bf16[20,192,512]{2,1,0:T(8,128)(2,1)}, bf16[16,128,512]{2,1,0:T(8,128)(2,1)S(1)}) custom-call(s32[4,20]{1,0:T(4,128)S(1)} %add_select_fusion.2.plan, bf16[20,192,512]{2,1,0:T(8,128)(2,1)} %copy-done, bf16[16,128,512]{2,1,0:T(8,128)(2,1)} %copy-done.1, bf16[20,64,512]{2,1,0:T(8,128)(2,1)S(1)} %pad_maximum_fusion.7.grad, ...), custom_call_target="tpu_custom_call" | custom-call | flops 67108864000 | bytes 16777216 | tf_op jit(solution)/shard_map/attn_bwd/pallas_call | solution.py:579
  677.0 5.1 collective-permute-start.28
  690.6 6.3 all-to-all-start.7
  697.0 12.0 %fusion.60 = f32[1024,2048]{1,0:T(8,128)} fusion(bf16[1536,1024]{1,0:T(8,128)(2,1)} %get-tuple-element.147, bf16[1536,2048]{1,0:T(8,128)(2,1)} %get-tuple-element.148), kind=kOutput, calls=%fused_computation.208 | convolution fusion | flops 6442450944 | bytes 17825792 | tf_op jit(solution)/shard_map/dot_general | solution.py:60
  709.0 11.1 %fusion.59 = f32[2048,1024]{1,0:T(8,128)} fusion(bf16[1536,2048]{1,0:T(8,128)(2,1)} %get-tuple-element.145, bf16[1536,1024]{1,0:T(8,128)(2,1)S(1)} %copy-done.63), kind=kOutput, calls=%fused_computation.207 | convolution fusion | flops 6442450944 | bytes 17825792 | tf_op jit(solution)/shard_map/dot_general | solution.py:60
  720.0 43.9 %all-to-all-done.7 = bf16[16,192,512]{2,1,0:T(8,128)(2,1)} async-done(((bf16[16,192,512]{2,1,0:T(8,128)(2,1)}), bf16[16,192,512]{2,1,0:T(8,128)(2,1)}, u32[]{:S(2)}, u32[]{:S(2)}) %all-to-all-start.7) | async-done | bytes 3145760 | tf_op jit(solution)/shard_map/all_to_all | solution.py:1165
  772.3 4.0 add_convert_fusion.4
  776.3 3.9 convolution_convert_fusion
  787.0 6.3 fusion.2
  794.5 8.2 collective-permute-done.34
  808.8 5.3 collective-permute-done.35
  821.1 11.5 %collective-permute-done.36 = bf16[64,1536]{1,0:T(8,128)(2,1)S(1)} collective-permute-done((bf16[64,1536]{1,0:T(8,128)(2,1)S(1)}, bf16[64,1536]{1,0:T(8,128)(2,1)S(1)}, u32[]{:S(2)}, u32[]{:S(2)}) %collective-permute-start.36) | collective-permute-done | bytes 196640 | tf_op jit(solution)/shard_map/ppermute | solution.py:774
  836.3 11.6 %collective-permute-done.38 = bf16[64,1536]{1,0:T(8,128)(2,1)S(1)} collective-permute-done((bf16[64,1536]{1,0:T(8,128)(2,1)S(1)}, bf16[64,1536]{1,0:T(8,128)(2,1)S(1)}, u32[]{:S(2)}, u32[]{:S(2)}) %collective-permute-start.38) | collective-permute-done | bytes 196640 | tf_op jit(solution)/shard_map/ppermute | solution.py:774
  (361 shorter events, 178.1 us)
Async XLA Ops:
  7.2 81.6 %all-gather.5.cloned.1.call-start = ((), (), s32[]{:S(2)}) async-start(), calls=%async_computation.12 | async-start | bytes 2949120 | tf_op jit(solution)/shard_map/all_gather | solution.py:900
  8.1 6.2 collective-permute-start.1
  14.5 9.4 %collective-permute-start.2 = (bf16[72,1536]{1,0:T(8,128)(2,1)S(1)}, bf16[72,1536]{1,0:T(8,128)(2,1)S(1)}, u32[]{:S(2)}, u32[]{:S(2)}) collective-permute-start(bf16[72,1536]{1,0:T(8,128)(2,1)S(1)} %fusion.23), channel_id=1, source_target_pairs={{0,8},{2,10},{4,12},{6,14},{8,0},{10,2},{12,4},{14,6},{16,24},{18,... | collective-permute-start | bytes 663560 | tf_op jit(solution)/shard_map/ppermute | solution.py:774
  14.5 16.4 %collective-permute-start.3 = (bf16[72,1536]{1,0:T(8,128)(2,1)S(1)}, bf16[72,1536]{1,0:T(8,128)(2,1)S(1)}, u32[]{:S(2)}, u32[]{:S(2)}) collective-permute-start(bf16[72,1536]{1,0:T(8,128)(2,1)S(1)} %fusion.23), channel_id=1, source_target_pairs={{0,16},{2,18},{4,20},{6,22},{8,24},{10,26},{12,28},{14,30},{16,0},... | collective-permute-start | bytes 663560 | tf_op jit(solution)/shard_map/ppermute | solution.py:774
  17.0 19.7 %collective-permute-start.4 = (bf16[72,1536]{1,0:T(8,128)(2,1)S(1)}, bf16[72,1536]{1,0:T(8,128)(2,1)S(1)}, u32[]{:S(2)}, u32[]{:S(2)}) collective-permute-start(bf16[72,1536]{1,0:T(8,128)(2,1)S(1)} %fusion.23), channel_id=1, source_target_pairs={{0,24},{2,26},{4,28},{6,30},{8,16},{10,18},{12,20},{14,22},{16,8},... | collective-permute-start | bytes 663560 | tf_op jit(solution)/shard_map/ppermute | solution.py:774
  38.1 10.9 %collective-permute-start.5 = (bf16[4,72,768]{2,1,0:T(8,128)(2,1)}, bf16[4,72,768]{2,1,0:T(8,128)(2,1)}, u32[]{:S(2)}, u32[]{:S(2)}) collective-permute-start(bf16[4,72,768]{2,1,0:T(8,128)(2,1)} %get-tuple-element.191), channel_id=1, source_target_pairs={{0,4},{2,6},{4,0},{6,2},{8,12},{10,14},{12,8},{14,10},{16,20},{18,... | collective-permute-start | bytes 1327112 | tf_op jit(solution)/shard_map/ppermute | solution.py:774
  39.3 12.3 %collective-permute-start.7 = (bf16[4,72,768]{2,1,0:T(8,128)(2,1)}, bf16[4,72,768]{2,1,0:T(8,128)(2,1)S(1)}, u32[]{:S(2)}, u32[]{:S(2)}) collective-permute-start(bf16[4,72,768]{2,1,0:T(8,128)(2,1)} %get-tuple-element.190), channel_id=1, source_target_pairs={{0,2},{2,0},{4,6},{6,4},{8,10},{10,8},{12,14},{14,12},{16,18},{18,... | collective-permute-start | bytes 1327112 | tf_op jit(solution)/shard_map/ppermute | solution.py:774
  40.5 12.7 %collective-permute-start = (bf16[512,1024]{1,0:T(8,128)(2,1)S(1)}, bf16[512,1024]{1,0:T(8,128)(2,1)S(1)}, u32[]{:S(2)}, u32[]{:S(2)}) collective-permute-start(bf16[512,1024]{1,0:T(8,128)(2,1)S(1)} %copy-done.3), channel_id=1, source_target_pairs={{0,1},{1,0},{2,3},{3,2},{4,5},{5,4},{6,7},{7,6},{8,9},{9,8},{10,11... | collective-permute-start | bytes 3145736 | tf_op jit(solution)/shard_map/ppermute | solution.py:605
  42.2 197.7 %all-gather.7.cloned.1.call-start = ((), (), s32[]{:S(2)}) async-start(), calls=%async_computation.13 | async-start | bytes 11796480 | tf_op jit(solution)/shard_map/all_gather | solution.py:932
  50.3 19.4 %collective-permute-start.6 = (bf16[4,2,72,768]{3,2,0,1:T(8,128)(2,1)S(1)}, bf16[4,2,72,768]{3,2,0,1:T(8,128)(2,1)S(1)}, u32[]{:S(2)}, u32[]{:S(2)}) collective-permute-start(bf16[4,2,72,768]{3,2,0,1:T(8,128)(2,1)S(1)} %maximum_select_fusion.3), channel_id=1, source_target_pairs={{0,2},{2,0},{4,6},{6,4},{8,10},{10,8},{12,14},{14,12},{16,18},{18,... | collective-permute-start | bytes 2654216 | tf_op jit(solution)/shard_map/ppermute | solution.py:774
  51.7 19.6 %collective-permute-start.8 = (bf16[4,2,72,768]{3,2,0,1:T(8,128)(2,1)S(1)}, bf16[4,2,72,768]{3,2,0,1:T(8,128)(2,1)S(1)}, u32[]{:S(2)}, u32[]{:S(2)}) collective-permute-start(bf16[4,2,72,768]{3,2,0,1:T(8,128)(2,1)S(1)} %maximum_select_fusion.4), channel_id=1, source_target_pairs={{0,4},{2,6},{4,0},{6,2},{8,12},{10,14},{12,8},{14,10},{16,20},{18,... | collective-permute-start | bytes 2654216 | tf_op jit(solution)/shard_map/ppermute | solution.py:774
  78.3 5.9 collective-permute-start.9
  88.8 74.3 %all-to-all-start = ((bf16[16,192,512]{2,1,0:T(8,128)(2,1)}), bf16[16,192,512]{2,1,0:T(8,128)(2,1)S(1)}, u32[]{:S(2)}, u32[]{:S(2)}) async-start(bf16[16,192,512]{2,1,0:T(8,128)(2,1)} %bitcast.147), calls=%async_computation | async-start | bytes 6291456 | tf_op jit(solution)/shard_map/all_to_all | solution.py:929
  163.3 7.2 collective-permute-start.11
  164.7 5.7 collective-permute-start.10
  220.1 11.0 %collective-permute-start.12 = (bf16[4,64,512]{2,1,0:T(8,128)(2,1)S(1)}, bf16[4,64,512]{2,1,0:T(8,128)(2,1)S(1)}, u32[]{:S(2)}, u32[]{:S(2)}) collective-permute-start(bf16[4,64,512]{2,1,0:T(8,128)(2,1)S(1)} %slice.198), channel_id=1, source_target_pairs={{0,1},{2,3},{4,5},{6,7},{8,9},{10,11},{12,13},{14,15},{16,17},{18,... | collective-permute-start | bytes 786440 | tf_op jit(solution)/shard_map/ppermute | solution.py:609
  232.2 32.1 %all-to-all-start.1 = ((bf16[16,64,512]{2,1,0:T(8,128)(2,1)}), bf16[16,64,512]{2,1,0:T(8,128)(2,1)S(1)}, u32[]{:S(2)}, u32[]{:S(2)}) async-start(bf16[16,64,512]{2,1,0:T(8,128)(2,1)} %pad_maximum_fusion.8), calls=%async_computation.1 | async-start | bytes 2097152 | tf_op jit(solution)/shard_map/all_to_all | solution.py:966
  250.5 16.3 %collective-permute-start.13 = (bf16[1024,512]{1,0:T(8,128)(2,1)}, bf16[1024,512]{1,0:T(8,128)(2,1)S(1)}, u32[]{:S(2)}, u32[]{:S(2)}) collective-permute-start(bf16[1024,512]{1,0:T(8,128)(2,1)} %slice.249), channel_id=1, source_target_pairs={{0,1},{1,0},{2,3},{3,2},{4,5},{5,4},{6,7},{7,6},{8,9},{9,8},{10,11... | collective-permute-start | bytes 3145736 | tf_op jit(solution)/shard_map/ppermute | solution.py:605
  270.6 4.6 collective-permute-start.14
  300.3 40.6 %all-to-all-start.2 = ((bf16[16,48,1024]{2,1,0:T(8,128)(2,1)}), bf16[16,48,1024]{2,1,0:T(8,128)(2,1)}, u32[]{:S(2)}, u32[]{:S(2)}) async-start(bf16[16,48,1024]{2,1,0:T(8,128)(2,1)} %bitcast.170), calls=%async_computation.2 | async-start | bytes 3145728 | tf_op jit(solution)/shard_map/all_to_all | solution.py:52
  340.9 7.6 collective-permute-start.16
  343.3 57.8 %all-to-all-start.3 = ((bf16[16,48,1024]{2,1,0:T(8,128)(2,1)}), bf16[16,48,1024]{2,1,0:T(8,128)(2,1)}, u32[]{:S(2)}, u32[]{:S(2)}) async-start(bf16[16,48,1024]{2,1,0:T(8,128)(2,1)} %bitcast.169), calls=%async_computation.3 | async-start | bytes 3145728 | tf_op jit(solution)/shard_map/all_to_all | solution.py:52
  370.5 3.9 collective-permute-start.17
  371.2 5.5 collective-permute-start.18
  401.1 3.8 collective-permute-start.19
  404.8 22.4 %collective-permute-start.23 = (bf16[768,1024]{1,0:T(8,128)(2,1)}, bf16[768,1024]{1,0:T(8,128)(2,1)S(1)}, u32[]{:S(2)}, u32[]{:S(2)}) collective-permute-start(bf16[768,1024]{1,0:T(8,128)(2,1)} %get-tuple-element.113), channel_id=1, source_target_pairs={{0,1},{1,0},{2,3},{3,2},{4,5},{5,4},{6,7},{7,6},{8,9},{9,8},{10,11... | collective-permute-start | bytes 4718600 | tf_op jit(solution)/shard_map/ppermute | solution.py:605
  426.5 12.6 %collective-permute-start.20 = (bf16[768,1024]{1,0:T(8,128)(2,1)}, bf16[768,1024]{1,0:T(8,128)(2,1)}, u32[]{:S(2)}, u32[]{:S(2)}) collective-permute-start(bf16[768,1024]{1,0:T(8,128)(2,1)} %get-tuple-element.108.refs_4_), channel_id=1, source_target_pairs={{0,1},{1,0},{2,3},{3,2},{4,5},{5,4},{6,7},{7,6},{8,9},{9,8},{10,11... | collective-permute-start | bytes 4718600 | tf_op jit(solution)/shard_map/ppermute | solution.py:605
  426.9 12.3 %collective-permute-start.21 = (bf16[768,1024]{1,0:T(8,128)(2,1)}, bf16[768,1024]{1,0:T(8,128)(2,1)}, u32[]{:S(2)}, u32[]{:S(2)}) collective-permute-start(bf16[768,1024]{1,0:T(8,128)(2,1)} %get-tuple-element.107.refs_3_), channel_id=1, source_target_pairs={{0,1},{1,0},{2,3},{3,2},{4,5},{5,4},{6,7},{7,6},{8,9},{9,8},{10,11... | collective-permute-start | bytes 4718600 | tf_op jit(solution)/shard_map/ppermute | solution.py:605
  432.4 42.3 %all-to-all-start.4 = ((bf16[16,48,1024]{2,1,0:T(8,128)(2,1)}), bf16[16,48,1024]{2,1,0:T(8,128)(2,1)}, u32[]{:S(2)}, u32[]{:S(2)}) async-start(bf16[16,48,1024]{2,1,0:T(8,128)(2,1)} %bitcast.150), calls=%async_computation.4 | async-start | bytes 3145728 | tf_op jit(solution)/shard_map/all_to_all | solution.py:52
  462.6 4.2 collective-permute-start.22
  474.7 41.5 %all-to-all-start.5 = ((bf16[16,48,1024]{2,1,0:T(8,128)(2,1)}), bf16[16,48,1024]{2,1,0:T(8,128)(2,1)}, u32[]{:S(2)}, u32[]{:S(2)}) async-start(bf16[16,48,1024]{2,1,0:T(8,128)(2,1)} %bitcast.149), calls=%async_computation.5 | async-start | bytes 3145728 | tf_op jit(solution)/shard_map/all_to_all | solution.py:52
  519.0 5.2 collective-permute-start.24
  553.5 17.4 %collective-permute-start.26 = (bf16[1024,512]{1,0:T(8,128)(2,1)}, bf16[1024,512]{1,0:T(8,128)(2,1)}, u32[]{:S(2)}, u32[]{:S(2)}) collective-permute-start(bf16[1024,512]{1,0:T(8,128)(2,1)} %convolution_convert_fusion.7), channel_id=1, source_target_pairs={{0,1},{1,0},{2,3},{3,2},{4,5},{5,4},{6,7},{7,6},{8,9},{9,8},{10,11... | collective-permute-start | bytes 3145736 | tf_op jit(solution)/shard_map/ppermute | solution.py:605
  553.9 32.3 %all-to-all-start.6 = ((bf16[16,64,512]{2,1,0:T(8,128)(2,1)}), bf16[16,64,512]{2,1,0:T(8,128)(2,1)}, u32[]{:S(2)}, u32[]{:S(2)}) async-start(bf16[16,64,512]{2,1,0:T(8,128)(2,1)} %bitcast.155), calls=%async_computation.6 | async-start | bytes 2097152 | tf_op jit(solution)/shard_map/all_to_all | solution.py:1119
  558.1 228.9 %reduce-scatter.3.cloned.1.call-start = ((), (), s32[]{:S(2)}) async-start(), calls=%async_computation.10 | async-start | bytes 11796480 | tf_op jit(solution)/shard_map/reduce_scatter | solution.py:1134
  677.0 9.9 %collective-permute-start.28 = (bf16[16,128,512]{2,1,0:T(8,128)(2,1)S(1)}, bf16[16,128,512]{2,1,0:T(8,128)(2,1)S(1)}, u32[]{:S(2)}, u32[]{:S(2)}) collective-permute-start(bf16[16,128,512]{2,1,0:T(8,128)(2,1)S(1)} %get-tuple-element.139), channel_id=1, source_target_pairs={{1,0},{3,2},{5,4},{7,6},{9,8},{11,10},{13,12},{15,14},{17,16},{19,... | collective-permute-start | bytes 6291464 | tf_op jit(solution)/shard_map/ppermute | solution.py:613
  683.4 4.5 collective-permute-start.29
  690.6 73.3 %all-to-all-start.7 = ((bf16[16,192,512]{2,1,0:T(8,128)(2,1)}), bf16[16,192,512]{2,1,0:T(8,128)(2,1)}, u32[]{:S(2)}, u32[]{:S(2)}) async-start(bf16[16,192,512]{2,1,0:T(8,128)(2,1)} %maximum_select_fusion), calls=%async_computation.7 | async-start | bytes 6291456 | tf_op jit(solution)/shard_map/all_to_all | solution.py:1165
  696.9 154.6 %reduce-scatter.5.cloned.1.call-start = ((), (), s32[]{:S(2)}) async-start(), calls=%async_computation.11 | async-start | bytes 2949120 | tf_op jit(solution)/shard_map/reduce_scatter | solution.py:1141
  766.1 10.2 %collective-permute-start.30 = (bf16[1536,512]{1,0:T(8,128)(2,1)S(1)}, bf16[1536,512]{1,0:T(8,128)(2,1)S(1)}, u32[]{:S(2)}, u32[]{:S(2)}) collective-permute-start(bf16[1536,512]{1,0:T(8,128)(2,1)S(1)} %bitcast.173), channel_id=1, source_target_pairs={{0,1},{1,0},{2,3},{3,2},{4,5},{5,4},{6,7},{7,6},{8,9},{9,8},{10,11... | collective-permute-start | bytes 4718600 | tf_op jit(solution)/shard_map/ppermute | solution.py:605
  781.3 21.4 %collective-permute-start.34 = (bf16[4,2,64,768]{3,2,0,1:T(8,128)(2,1)}, bf16[4,2,64,768]{3,2,0,1:T(8,128)(2,1)}, u32[]{:S(2)}, u32[]{:S(2)}) collective-permute-start(bf16[4,2,64,768]{3,2,0,1:T(8,128)(2,1)} %select_bitcast_fusion), channel_id=1, source_target_pairs={{0,4},{2,6},{4,0},{6,2},{8,12},{10,14},{12,8},{14,10},{16,20},{18,... | collective-permute-start | bytes 2359304 | tf_op jit(solution)/shard_map/ppermute | solution.py:774
  785.9 19.6 %collective-permute-start.32 = (bf16[4,2,64,768]{3,2,0,1:T(8,128)(2,1)}, bf16[4,2,64,768]{3,2,0,1:T(8,128)(2,1)}, u32[]{:S(2)}, u32[]{:S(2)}) collective-permute-start(bf16[4,2,64,768]{3,2,0,1:T(8,128)(2,1)} %select_bitcast_fusion.1), channel_id=1, source_target_pairs={{0,2},{2,0},{4,6},{6,4},{8,10},{10,8},{12,14},{14,12},{16,18},{18,... | collective-permute-start | bytes 2359304 | tf_op jit(solution)/shard_map/ppermute | solution.py:774
  793.5 14.7 %collective-permute-start.31 = (bf16[512,1024]{1,0:T(8,128)(2,1)S(1)}, bf16[512,1024]{1,0:T(8,128)(2,1)S(1)}, u32[]{:S(2)}, u32[]{:S(2)}) collective-permute-start(bf16[512,1024]{1,0:T(8,128)(2,1)S(1)} %slice.335), channel_id=1, source_target_pairs={{0,1},{1,0},{2,3},{3,2},{4,5},{5,4},{6,7},{7,6},{8,9},{9,8},{10,11... | collective-permute-start | bytes 3145736 | tf_op jit(solution)/shard_map/ppermute | solution.py:605
  804.2 9.9 %collective-permute-start.35 = (bf16[4,64,768]{2,1,0:T(8,128)(2,1)S(1)}, bf16[4,64,768]{2,1,0:T(8,128)(2,1)S(1)}, u32[]{:S(2)}, u32[]{:S(2)}) collective-permute-start(bf16[4,64,768]{2,1,0:T(8,128)(2,1)S(1)} %select_bitcast_fusion.2), channel_id=1, source_target_pairs={{0,2},{2,0},{4,6},{6,4},{8,10},{10,8},{12,14},{14,12},{16,18},{18,... | collective-permute-start | bytes 1179656 | tf_op jit(solution)/shard_map/ppermute | solution.py:774
  806.9 9.7 %collective-permute-start.33 = (bf16[4,64,768]{2,1,0:T(8,128)(2,1)S(1)}, bf16[4,64,768]{2,1,0:T(8,128)(2,1)S(1)}, u32[]{:S(2)}, u32[]{:S(2)}) collective-permute-start(bf16[4,64,768]{2,1,0:T(8,128)(2,1)S(1)} %select_bitcast_fusion.3), channel_id=1, source_target_pairs={{0,4},{2,6},{4,0},{6,2},{8,12},{10,14},{12,8},{14,10},{16,20},{18,... | collective-permute-start | bytes 1179656 | tf_op jit(solution)/shard_map/ppermute | solution.py:774
  816.8 15.9 %collective-permute-start.36 = (bf16[64,1536]{1,0:T(8,128)(2,1)S(1)}, bf16[64,1536]{1,0:T(8,128)(2,1)S(1)}, u32[]{:S(2)}, u32[]{:S(2)}) collective-permute-start(bf16[64,1536]{1,0:T(8,128)(2,1)S(1)} %get-tuple-element.196), channel_id=1, source_target_pairs={{0,8},{2,10},{4,12},{6,14},{8,0},{10,2},{12,4},{14,6},{16,24},{18,... | collective-permute-start | bytes 589832 | tf_op jit(solution)/shard_map/ppermute | solution.py:774
  816.9 19.4 %collective-permute-start.37 = (bf16[64,1536]{1,0:T(8,128)(2,1)S(1)}, bf16[64,1536]{1,0:T(8,128)(2,1)S(1)}, u32[]{:S(2)}, u32[]{:S(2)}) collective-permute-start(bf16[64,1536]{1,0:T(8,128)(2,1)S(1)} %get-tuple-element.197), channel_id=1, source_target_pairs={{0,16},{2,18},{4,20},{6,22},{8,24},{10,26},{12,28},{14,30},{16,0},... | collective-permute-start | bytes 589832 | tf_op jit(solution)/shard_map/ppermute | solution.py:774
  818.9 29.0 %collective-permute-start.38 = (bf16[64,1536]{1,0:T(8,128)(2,1)S(1)}, bf16[64,1536]{1,0:T(8,128)(2,1)S(1)}, u32[]{:S(2)}, u32[]{:S(2)}) collective-permute-start(bf16[64,1536]{1,0:T(8,128)(2,1)S(1)} %get-tuple-element.198), channel_id=1, source_target_pairs={{0,24},{2,26},{4,28},{6,30},{8,16},{10,18},{12,20},{14,22},{16,8},... | collective-permute-start | bytes 589832 | tf_op jit(solution)/shard_map/ppermute | solution.py:774
  (70 other events, 623.2 us)
Sparse Core Ops, SparseCore 0:
  42.4 46.3 all-gather.4
  90.6 126.5 all-gather.6
  590.9 95.3 reduce-scatter.2
  787.1 51.9 reduce-scatter.4
